TPU v7x, 32 devices: a whole 2x2x4 slice. The times are simulated.
32 devices in a mesh: dp: 16 (over z, x, core), mp: 2 (over y).
Axes of the slice: x: 2, y: 2, z: 4, core: 2. Of those that a mesh axis runs over, the one named last changes fastest.
Arguments:
- source_rows: bfloat16 [2048, 16, 512], P('mp', 'dp'), may hold values from -6 to 6
- target_rows: bfloat16 [2048, 16, 512], P('mp', 'dp'), may hold values from -6 to 6
- source_segment: int32 [16, 2048], P('dp'), may hold values from 0 to 7, as said below
- target_segment: int32 [16, 2048], P('dp'), may hold values from 0 to 7, as said below
- running: int32 [2, 16, 2048], P(None, 'dp', 'mp'), may hold values 0 or 1
- enc_qkv: bfloat16 [3, 512, 512], P(None, None, 'mp'), may hold values from -0.25 to 0.25
- enc_proj: bfloat16 [512, 512], P('mp'), may hold values from -1 to 1
- enc_up: bfloat16 [512, 2048], P(None, 'mp'), may hold values from -0.25 to 0.25
- enc_down: bfloat16 [2048, 512], P('mp'), may hold values from -0.1875 to 0.1875
- enc_gains: float32 [2, 512], replicated, may hold values from 0.25 to 1.75
- enc_shifts: float32 [2, 512], replicated, may hold values from -1.8 to 1.8
- dec_qkv: bfloat16 [3, 512, 512], P(None, None, 'mp'), may hold values from -0.25 to 0.25
- dec_proj: bfloat16 [512, 512], P('mp'), may hold values from -1 to 1
- cross_query: bfloat16 [512, 512], P(None, 'mp'), may hold values from -0.25 to 0.25
- cross_kv: bfloat16 [2, 512, 512], P(None, None, 'mp'), may hold values from -0.25 to 0.25
- cross_proj: bfloat16 [512, 512], P('mp'), may hold values from -1 to 1
- dec_up: bfloat16 [512, 2048], P(None, 'mp'), may hold values from -0.25 to 0.25
- dec_down: bfloat16 [2048, 512], P('mp'), may hold values from -0.1875 to 0.1875
- dec_gains: float32 [3, 512], replicated, may hold values from 0.25 to 1.75
- dec_shifts: float32 [3, 512], replicated, may hold values from -1.8 to 1.8
- halt_weight: float32 [2, 512], replicated, may hold values from -0.25 to 0.25
- enc_cotangent: float32 [2048, 16, 512], P('mp', 'dp'), may hold values from -6 to 6
- dec_cotangent: float32 [2048, 16, 512], P('mp', 'dp'), may hold values from -6 to 6
Outputs:
- enc_states: bfloat16 [2048, 16, 512], P('mp', 'dp')
- dec_states: bfloat16 [2048, 16, 512], P('mp', 'dp')
- source_grad: float32 [2048, 16, 512], P('mp', 'dp')
- target_grad: float32 [2048, 16, 512], P('mp', 'dp')
- enc_qkv_grad: float32 [3, 512, 512], P(None, None, 'mp')
- enc_proj_grad: float32 [512, 512], P('mp')
- enc_up_grad: float32 [512, 2048], P(None, 'mp')
- enc_down_grad: float32 [2048, 512], P('mp')
- enc_gains_grad: float32 [2, 512], replicated
- enc_shifts_grad: float32 [2, 512], replicated
- dec_qkv_grad: float32 [3, 512, 512], P(None, None, 'mp')
- dec_proj_grad: float32 [512, 512], P('mp')
- cross_query_grad: float32 [512, 512], P(None, 'mp')
- cross_kv_grad: float32 [2, 512, 512], P(None, None, 'mp')
- cross_proj_grad: float32 [512, 512], P('mp')
- dec_up_grad: float32 [512, 2048], P(None, 'mp')
- dec_down_grad: float32 [2048, 512], P('mp')
- dec_gains_grad: float32 [3, 512], replicated
- dec_shifts_grad: float32 [3, 512], replicated
- halt_weight_grad: float32 [2, 512], replicated
Inputs may be any that keep to these rules, and one draw needn't show every extreme that they name: Each row holds 8 sentences numbered 0 to 7 in order, each one position or more, in both source_segment and target_segment; a target sentence is paired with the source sentence of the same number. In every row one sentence begins within the first 256 positions and ends within the last 256. `target_segment`: as for source_segment, drawn independently.
All inputs are finite; a program needn't handle non-finite values. No bound on the sum of `running` on one device may be relied on, other than what follows from the above.
Results may differ from a plain program's by a relative error of at most 0.04.
Values may be sent and summed in bfloat16 or wider, within the bound.
No kernel may reach another device: no remote copies, remote signals or barrier semaphores. Data moves between devices by JAX's collectives and lax.ppermute only.
A program may use at most 256 MiB of HBM per device.

v0:
```python
from functools import partial

import jax
import jax.numpy as jnp
from jax import lax
from jax.sharding import PartitionSpec as P

D = 512
DH = 64


EPS = 1e-05
NEGATIVE = -1000000000.0


def signal(position):
    half_width = D // 2
    inverse_rates = jnp.exp(
        jnp.arange(half_width, dtype=jnp.float32) * (-jnp.log(10000.0) / (half_width - 1))
    )
    angles = position[:, None] * inverse_rates[None, :]
    return jnp.concatenate([jnp.sin(angles), jnp.cos(angles)], axis=1)


def normalize(values, norm_gain, norm_shift):
    centred = values - jnp.mean(values, axis=-1, keepdims=True)
    spread = jnp.mean(centred * centred, axis=-1, keepdims=True)
    return centred * lax.rsqrt(spread + EPS) * norm_gain + norm_shift


def halting(running_now, initial, updated, weight):
    halt_prob = jax.nn.sigmoid(jnp.sum(updated * weight, axis=-1, keepdims=True))
    return initial + running_now * halt_prob * (updated - initial)


def dot_last(left, right):
    return lax.dot_general(
        left, right, (((left.ndim - 1,), (1,)), ((), ())), preferred_element_type=jnp.float32
    )


def collect(piece_rows):
    return lax.all_gather(piece_rows, "mp", axis=0, tiled=True)


def collect_grad(piece_rows):
    return lax.all_gather(piece_rows.astype(jnp.bfloat16), "mp", axis=0, tiled=True)


def project_out(hidden, weight, rows):

    def partial_term(begin_row, row_count):
        return jnp.dot(hidden, weight, preferred_element_type=jnp.float32)

    return lax.psum_scatter(
        partial_term(jnp.int32(0), lax.axis_size("mp") * rows).astype(jnp.bfloat16),
        "mp",
        scatter_dimension=0,
        tiled=True,
    ).astype(jnp.float32)


def project_back(gradients, matrices, rows):

    def partial_term(begin_row, row_count):
        summed = jnp.zeros(
            (row_count,) + gradients[0].shape[1:-1] + (matrices[0].shape[0],), jnp.float32
        )
        for gradient, matrix in zip(gradients, matrices):
            summed = summed + dot_last(gradient, matrix)
        return summed

    return lax.psum_scatter(
        partial_term(jnp.int32(0), lax.axis_size("mp") * rows).astype(jnp.bfloat16),
        "mp",
        scatter_dimension=0,
        tiled=True,
    ).astype(jnp.float32)


def to_pairs(values):
    length, row_count, width = values.shape
    return (
        values.reshape(length, row_count, width // DH, DH)
        .transpose(1, 2, 0, 3)
        .reshape(-1, length, DH)
    )


def from_pairs(values, row_count):
    pairs, length, unused = values.shape
    heads_here = pairs // row_count
    return (
        values.reshape(row_count, heads_here, length, DH)
        .transpose(2, 0, 1, 3)
        .reshape(length, row_count, heads_here * DH)
    )


def per_pair(segments, width):
    return jnp.repeat(segments, width // DH, axis=0)


def pair_scores(query_block, key_rows, segment_block, segment_keys, first_row, causal):
    scores = lax.dot_general(
        query_block, key_rows, (((1,), (1,)), ((), ())), preferred_element_type=jnp.float32
    )
    scores = scores * DH ** (-0.5)
    allowed = segment_block[:, None] == segment_keys[None, :]
    if causal:
        query_place = first_row + jnp.arange(query_block.shape[0], dtype=jnp.int32)
        key_place = jnp.arange(key_rows.shape[0], dtype=jnp.int32)
        allowed = allowed & (key_place[None, :] <= query_place[:, None])
    return jnp.where(allowed, scores, NEGATIVE)


def attend_pair(inputs, causal):
    query_rows, key_rows, value_rows, segment_query, segment_keys = inputs
    length = query_rows.shape[0]
    block_rows = min(512, length)
    blocks = length // block_rows
    firsts = jnp.arange(blocks, dtype=jnp.int32) * block_rows

    def one_block(pieces):
        query_block, segment_block, first_row = pieces
        scores = pair_scores(query_block, key_rows, segment_block, segment_keys, first_row, causal)
        highest = jnp.max(scores, axis=1, keepdims=True)
        exponent = jnp.exp(scores - highest)
        totals = jnp.sum(exponent, axis=1, keepdims=True)
        weights = (exponent / totals).astype(jnp.bfloat16)
        mixed = jnp.dot(weights, value_rows, preferred_element_type=jnp.float32)
        return (mixed.astype(jnp.bfloat16), (highest + jnp.log(totals))[:, 0])

    mixed, log_total = lax.map(
        one_block,
        (
            query_rows.reshape(blocks, block_rows, -1),
            segment_query.reshape(blocks, block_rows),
            firsts,
        ),
    )
    return (mixed.reshape(length, -1), log_total.reshape(length))


def attend_pair_back(inputs, causal):
    query_rows, key_rows, value_rows, mixed_grad, log_total, segment_query, segment_keys = inputs
    length = query_rows.shape[0]
    block_rows = min(512, length)
    blocks = length // block_rows
    firsts = jnp.arange(blocks, dtype=jnp.int32) * block_rows

    def one_block(carry, pieces):
        key_total, value_total = carry
        query_block, grad_block, log_block, segment_block, first_row = pieces
        scores = pair_scores(query_block, key_rows, segment_block, segment_keys, first_row, causal)
        probs = jnp.exp(scores - log_block[:, None])
        weights = probs.astype(jnp.bfloat16)
        prob_grad = lax.dot_general(
            grad_block, value_rows, (((1,), (1,)), ((), ())), preferred_element_type=jnp.float32
        )
        inner = jnp.sum(probs * prob_grad, axis=1, keepdims=True)
        score_grad = (probs * (prob_grad - inner)).astype(jnp.bfloat16)
        query_grad = jnp.dot(score_grad, key_rows, preferred_element_type=jnp.float32) * DH ** (
            -0.5
        )
        key_total = key_total + lax.dot_general(
            score_grad, query_block, (((0,), (0,)), ((), ())), preferred_element_type=jnp.float32
        ) * DH ** (-0.5)
        value_total = value_total + lax.dot_general(
            weights, grad_block, (((0,), (0,)), ((), ())), preferred_element_type=jnp.float32
        )
        return ((key_total, value_total), query_grad.astype(jnp.bfloat16))

    zeros_start = jnp.zeros(key_rows.shape, jnp.float32)
    (key_total, value_total), query_grad = lax.scan(
        one_block,
        (zeros_start, zeros_start),
        (
            query_rows.reshape(blocks, block_rows, -1),
            mixed_grad.reshape(blocks, block_rows, -1),
            log_total.reshape(blocks, block_rows),
            segment_query.reshape(blocks, block_rows),
            firsts,
        ),
    )
    return (
        query_grad.reshape(length, -1),
        key_total.astype(jnp.bfloat16),
        value_total.astype(jnp.bfloat16),
    )


def attention_forward(
    query_full,
    key_full,
    weight_query,
    weight_key,
    weight_value,
    weight_out,
    segment_query,
    segment_keys,
    causal,
    rows,
):
    queries = jnp.dot(query_full, weight_query, preferred_element_type=jnp.float32).astype(
        jnp.bfloat16
    )
    keys_low = jnp.dot(key_full, weight_key, preferred_element_type=jnp.float32).astype(
        jnp.bfloat16
    )
    values_low = jnp.dot(key_full, weight_value, preferred_element_type=jnp.float32).astype(
        jnp.bfloat16
    )
    width = queries.shape[2]
    row_count = queries.shape[1]
    mixed, log_total = lax.map(
        partial(attend_pair, causal=causal),
        (
            to_pairs(queries),
            to_pairs(keys_low),
            to_pairs(values_low),
            per_pair(segment_query, width),
            per_pair(segment_keys, width),
        ),
    )
    mixed = from_pairs(mixed, row_count)
    branch = project_out(mixed, weight_out, rows)
    return (branch, (queries, keys_low, values_low, mixed, log_total))


def attention_backward(
    branch_grad, kept, query_full, key_full, weight_out, segment_query, segment_keys, causal
):
    queries, keys_low, values_low, kept_mixed, log_total = kept
    grad_full = collect_grad(branch_grad)
    out_weight_grad = jnp.einsum(
        "lrc,lrd->cd", kept_mixed, grad_full, preferred_element_type=jnp.float32
    )
    mixed_grad = dot_last(grad_full, weight_out).astype(jnp.bfloat16)
    width = queries.shape[2]
    row_count = queries.shape[1]
    query_grad, key_grad, value_grad = lax.map(
        partial(attend_pair_back, causal=causal),
        (
            to_pairs(queries),
            to_pairs(keys_low),
            to_pairs(values_low),
            to_pairs(mixed_grad),
            log_total,
            per_pair(segment_query, width),
            per_pair(segment_keys, width),
        ),
    )
    query_grad = from_pairs(query_grad, row_count)
    key_grad = from_pairs(key_grad, row_count)
    value_grad = from_pairs(value_grad, row_count)
    weight_grads = (
        jnp.einsum("lrd,lrc->dc", query_full, query_grad, preferred_element_type=jnp.float32),
        jnp.einsum("lrd,lrc->dc", key_full, key_grad, preferred_element_type=jnp.float32),
        jnp.einsum("lrd,lrc->dc", key_full, value_grad, preferred_element_type=jnp.float32),
    )
    return (query_grad, key_grad, value_grad, weight_grads, out_weight_grad)


def feed_forward(source_full, weight_up, weight_down, rows):
    hidden = jnp.dot(source_full, weight_up, preferred_element_type=jnp.float32)
    active = jax.nn.gelu(hidden).astype(jnp.bfloat16)
    return (project_out(active, weight_down, rows), hidden)


def feed_backward(branch_grad, source_full, hidden, weight_up, weight_down, rows):
    grad_full = collect_grad(branch_grad)
    active, gelu_back = jax.vjp(jax.nn.gelu, hidden)
    active = active.astype(jnp.bfloat16)
    down_grad = jnp.einsum("lrf,lrd->fd", active, grad_full, preferred_element_type=jnp.float32)
    hidden_grad = gelu_back(dot_last(grad_full, weight_down))[0].astype(jnp.bfloat16)
    up_grad = jnp.einsum(
        "lrd,lrf->df", source_full, hidden_grad, preferred_element_type=jnp.float32
    )
    input_grad = project_back((hidden_grad,), (weight_up,), rows)
    return (input_grad, up_grad, down_grad)


def local(
    source_rows,
    target_rows,
    source_segment,
    target_segment,
    running,
    enc_qkv,
    enc_proj,
    enc_up,
    enc_down,
    enc_gains,
    enc_shifts,
    dec_qkv,
    dec_proj,
    cross_query,
    cross_kv,
    cross_proj,
    dec_up,
    dec_down,
    dec_gains,
    dec_shifts,
    halt_weight,
    enc_cotangent,
    dec_cotangent,
):
    rows = source_rows.shape[0]
    position = (lax.axis_index("mp") * rows + jnp.arange(rows, dtype=jnp.int32)).astype(jnp.float32)
    embedding = (signal(position) + signal(jnp.ones((1,), jnp.float32)))[:, None, :]
    runs_now = jnp.transpose(running, (0, 2, 1)).astype(jnp.float32)[..., None]
    enc_start = source_rows.astype(jnp.float32) + embedding
    enc_start_low = enc_start.astype(jnp.bfloat16)
    enc_start_full = collect(enc_start_low)
    enc_attn, enc_attn_kept = attention_forward(
        enc_start_full,
        enc_start_full,
        enc_qkv[0],
        enc_qkv[1],
        enc_qkv[2],
        enc_proj,
        source_segment,
        source_segment,
        False,
        rows,
    )
    enc_sum_one = enc_start + enc_attn
    enc_middle = normalize(enc_sum_one, enc_gains[0], enc_shifts[0])
    enc_middle_low = enc_middle.astype(jnp.bfloat16)
    enc_middle_full = collect(enc_middle_low)
    enc_ffn, enc_hidden = feed_forward(enc_middle_full, enc_up, enc_down, rows)
    enc_sum_two = enc_middle + enc_ffn
    enc_last = normalize(enc_sum_two, enc_gains[1], enc_shifts[1])
    enc_final = halting(runs_now[0], enc_start, enc_last, halt_weight[0])
    enc_states = enc_final.astype(jnp.bfloat16)
    enc_states_full = collect(enc_states)
    dec_start = target_rows.astype(jnp.float32) + embedding
    dec_start_low = dec_start.astype(jnp.bfloat16)
    dec_start_full = collect(dec_start_low)
    dec_self, dec_self_kept = attention_forward(
        dec_start_full,
        dec_start_full,
        dec_qkv[0],
        dec_qkv[1],
        dec_qkv[2],
        dec_proj,
        target_segment,
        target_segment,
        True,
        rows,
    )
    dec_sum_one = dec_start + dec_self
    dec_middle = normalize(dec_sum_one, dec_gains[0], dec_shifts[0])
    dec_middle_low = dec_middle.astype(jnp.bfloat16)
    dec_middle_full = collect(dec_middle_low)
    dec_cross, dec_cross_kept = attention_forward(
        dec_middle_full,
        enc_states_full,
        cross_query,
        cross_kv[0],
        cross_kv[1],
        cross_proj,
        target_segment,
        source_segment,
        False,
        rows,
    )
    dec_sum_two = dec_middle + dec_cross
    dec_mixed = normalize(dec_sum_two, dec_gains[1], dec_shifts[1])
    dec_mixed_low = dec_mixed.astype(jnp.bfloat16)
    dec_mixed_full = collect(dec_mixed_low)
    dec_ffn, dec_hidden = feed_forward(dec_mixed_full, dec_up, dec_down, rows)
    dec_sum_three = dec_mixed + dec_ffn
    dec_last = normalize(dec_sum_three, dec_gains[2], dec_shifts[2])
    dec_final = halting(runs_now[1], dec_start, dec_last, halt_weight[1])
    dec_states = dec_final.astype(jnp.bfloat16)
    unused, halt_back = jax.vjp(partial(halting, runs_now[1]), dec_start, dec_last, halt_weight[1])
    dec_start_grad, last_grad, dec_halt_grad = halt_back(dec_cotangent)
    unused, norm_back = jax.vjp(normalize, dec_sum_three, dec_gains[2], dec_shifts[2])
    sum_grad, dec_gain_three, dec_shift_three = norm_back(last_grad)
    ffn_input_grad, dec_up_grad, dec_down_grad = feed_backward(
        sum_grad, dec_mixed_full, dec_hidden, dec_up, dec_down, rows
    )
    mixed_grad = sum_grad + ffn_input_grad
    unused, norm_back = jax.vjp(normalize, dec_sum_two, dec_gains[1], dec_shifts[1])
    sum_grad, dec_gain_two, dec_shift_two = norm_back(mixed_grad)
    query_grad, key_grad, value_grad, cross_grads, cross_proj_grad = attention_backward(
        sum_grad,
        dec_cross_kept,
        dec_middle_full,
        enc_states_full,
        cross_proj,
        target_segment,
        source_segment,
        False,
    )
    middle_grad = sum_grad + project_back((query_grad,), (cross_query,), rows)
    enc_extra = project_back((key_grad, value_grad), (cross_kv[0], cross_kv[1]), rows)
    unused, norm_back = jax.vjp(normalize, dec_sum_one, dec_gains[0], dec_shifts[0])
    sum_grad, dec_gain_one, dec_shift_one = norm_back(middle_grad)
    query_grad, key_grad, value_grad, self_grads, dec_proj_grad = attention_backward(
        sum_grad,
        dec_self_kept,
        dec_start_full,
        dec_start_full,
        dec_proj,
        target_segment,
        target_segment,
        True,
    )
    target_grad = (
        sum_grad
        + dec_start_grad
        + project_back(
            (query_grad, key_grad, value_grad), (dec_qkv[0], dec_qkv[1], dec_qkv[2]), rows
        )
    )
    dec_qkv_grad = jnp.stack(self_grads)
    cross_query_grad = cross_grads[0]
    cross_kv_grad = jnp.stack([cross_grads[1], cross_grads[2]])
    enc_final_grad = enc_cotangent + enc_extra
    unused, halt_back = jax.vjp(partial(halting, runs_now[0]), enc_start, enc_last, halt_weight[0])
    enc_start_grad, last_grad, enc_halt_grad = halt_back(enc_final_grad)
    unused, norm_back = jax.vjp(normalize, enc_sum_two, enc_gains[1], enc_shifts[1])
    sum_grad, enc_gain_two, enc_shift_two = norm_back(last_grad)
    ffn_input_grad, enc_up_grad, enc_down_grad = feed_backward(
        sum_grad, enc_middle_full, enc_hidden, enc_up, enc_down, rows
    )
    middle_grad = sum_grad + ffn_input_grad
    unused, norm_back = jax.vjp(normalize, enc_sum_one, enc_gains[0], enc_shifts[0])
    sum_grad, enc_gain_one, enc_shift_one = norm_back(middle_grad)
    query_grad, key_grad, value_grad, self_grads, enc_proj_grad = attention_backward(
        sum_grad,
        enc_attn_kept,
        enc_start_full,
        enc_start_full,
        enc_proj,
        source_segment,
        source_segment,
        False,
    )
    source_grad = (
        sum_grad
        + enc_start_grad
        + project_back(
            (query_grad, key_grad, value_grad), (enc_qkv[0], enc_qkv[1], enc_qkv[2]), rows
        )
    )
    enc_qkv_grad = jnp.stack(self_grads)
    (
        enc_qkv_grad,
        enc_proj_grad,
        enc_up_grad,
        enc_down_grad,
        dec_qkv_grad,
        dec_proj_grad,
        cross_query_grad,
        cross_kv_grad,
        cross_proj_grad,
        dec_up_grad,
        dec_down_grad,
    ) = (
        lax.psum(enc_qkv_grad.astype(jnp.bfloat16), "dp").astype(jnp.float32),
        lax.psum(enc_proj_grad.astype(jnp.bfloat16), "dp").astype(jnp.float32),
        lax.psum(enc_up_grad.astype(jnp.bfloat16), "dp").astype(jnp.float32),
        lax.psum(enc_down_grad.astype(jnp.bfloat16), "dp").astype(jnp.float32),
        lax.psum(dec_qkv_grad.astype(jnp.bfloat16), "dp").astype(jnp.float32),
        lax.psum(dec_proj_grad.astype(jnp.bfloat16), "dp").astype(jnp.float32),
        lax.psum(cross_query_grad.astype(jnp.bfloat16), "dp").astype(jnp.float32),
        lax.psum(cross_kv_grad.astype(jnp.bfloat16), "dp").astype(jnp.float32),
        lax.psum(cross_proj_grad.astype(jnp.bfloat16), "dp").astype(jnp.float32),
        lax.psum(dec_up_grad.astype(jnp.bfloat16), "dp").astype(jnp.float32),
        lax.psum(dec_down_grad.astype(jnp.bfloat16), "dp").astype(jnp.float32),
    )
    enc_gains_grad, enc_shifts_grad, dec_gains_grad, dec_shifts_grad, halt_weight_grad = lax.psum(
        (
            jnp.stack([enc_gain_one, enc_gain_two]),
            jnp.stack([enc_shift_one, enc_shift_two]),
            jnp.stack([dec_gain_one, dec_gain_two, dec_gain_three]),
            jnp.stack([dec_shift_one, dec_shift_two, dec_shift_three]),
            jnp.stack([enc_halt_grad, dec_halt_grad]),
        ),
        ("dp", "mp"),
    )
    return (
        enc_states,
        dec_states,
        source_grad,
        target_grad,
        enc_qkv_grad,
        enc_proj_grad,
        enc_up_grad,
        enc_down_grad,
        enc_gains_grad,
        enc_shifts_grad,
        dec_qkv_grad,
        dec_proj_grad,
        cross_query_grad,
        cross_kv_grad,
        cross_proj_grad,
        dec_up_grad,
        dec_down_grad,
        dec_gains_grad,
        dec_shifts_grad,
        halt_weight_grad,
    )


def solution(mesh):
    return jax.shard_map(
        local,
        mesh=mesh,
        in_specs=(
            P("mp", "dp", None),
            P("mp", "dp", None),
            P("dp", None),
            P("dp", None),
            P(None, "dp", "mp"),
            P(None, None, "mp"),
            P("mp", None),
            P(None, "mp"),
            P("mp", None),
            P(),
            P(),
            P(None, None, "mp"),
            P("mp", None),
            P(None, "mp"),
            P(None, None, "mp"),
            P("mp", None),
            P(None, "mp"),
            P("mp", None),
            P(),
            P(),
            P(),
            P("mp", "dp", None),
            P("mp", "dp", None),
        ),
        out_specs=(
            P("mp", "dp", None),
            P("mp", "dp", None),
            P("mp", "dp", None),
            P("mp", "dp", None),
            P(None, None, "mp"),
            P("mp", None),
            P(None, "mp"),
            P("mp", None),
            P(),
            P(),
            P(None, None, "mp"),
            P("mp", None),
            P(None, "mp"),
            P(None, None, "mp"),
            P("mp", None),
            P(None, "mp"),
            P("mp", None),
            P(),
            P(),
            P(),
        ),
        check_vma=False,
    )
```

profile of v0, /device:TPU:0, one launch (start us, length us, event | category | flops | bytes accessed | tf_op | source)
XLA Modules:
  0.0 1557.1 jit_solution(7749468721323809490)
XLA Ops:
  14.2 35.0 %all-gather.12.cloned.1.call-done = bf16[2048,1,512]{2,0,1:T(8,128)(2,1)} async-done(((bf16[1024,1,512]{2,0,1:T(8,128)(2,1)}), bf16[2048,1,512]{2,0,1:T(8,128)(2,1)}) %all-gather.12.cloned.1.call-update) | async-done | bytes 2097168 | tf_op jit(solution)/shard_map/all_gather | solution.py:43
  102.6 90.6 %while.184 = (s32[]{:T(128)}, bf16[4,2048,64]{1,2,0:T(8,128)(2,1)}, f32[4,2048]{1,0:T(4,128)S(1)}, bf16[4,2048,64]{2,1,0:T(8,128)(2,1)}, s32[4,2048]{1,0:T(4,128...) while((s32[]{:T(128)}, bf16[4,2048,64]{1,2,0:T(8,128)(2,1)}, ...), condition=%wide.region_18.19_spmd, body=%wide.region_13.18_spmd.sunk | while | flops 280002560 | bytes 17086872 | solution.py:216
  198.3 64.1 %while.182 = (s32[]{:T(128)}, bf16[4,2048,64]{1,2,0:T(8,128)(2,1)}, f32[4,2048]{1,0:T(4,128)S(1)}, bf16[4,2048,64]{2,1,0:T(8,128)(2,1)}, s32[4,2048]{1,0:T(4,128...) while((s32[]{:T(128)}, bf16[4,2048,64]{1,2,0:T(8,128)(2,1)}, ...), condition=%wide.region_5.6_spmd, body=%wide.region_0.5_spmd.sunk | while | flops 277904896 | bytes 17082728 | solution.py:216
  266.5 31.2 %reduce-scatter.12.cloned.1.call-done = bf16[1024,1,512]{2,0,1:T(8,128)(2,1)} async-done(((bf16[2048,1,512]{2,0,1:T(8,128)(2,1)}), bf16[1024,1,512]{2,0,1:T(8,128)(2,1)}) %reduce-scatter.12.cloned.1.call-update) | async-done | bytes 1048592 | tf_op jit(solution)/shard_map/reduce_scatter | solution.py:55
  304.1 33.2 %all-gather.14.cloned.1.call-done = bf16[2048,1,512]{2,0,1:T(8,128)(2,1)} async-done(((bf16[1024,1,512]{2,0,1:T(8,128)(2,1)}), bf16[2048,1,512]{2,0,1:T(8,128)(2,1)}) %all-gather.14.cloned.1.call-update) | async-done | bytes 2097168 | tf_op jit(solution)/shard_map/all_gather | solution.py:43
  356.1 25.0 %reduce-scatter.14.cloned.1.call-done = bf16[1024,1,512]{2,0,1:T(8,128)(2,1)} async-done(((bf16[2048,1,512]{2,0,1:T(8,128)(2,1)}), bf16[1024,1,512]{2,0,1:T(8,128)(2,1)}) %reduce-scatter.14.cloned.1.call-update) | async-done | bytes 1048592 | tf_op jit(solution)/shard_map/reduce_scatter | solution.py:55
  388.8 27.6 %all-gather.18.cloned.1.call-done = bf16[2048,1,512]{2,0,1:T(8,128)(2,1)} async-done(((bf16[1024,1,512]{2,0,1:T(8,128)(2,1)}), bf16[2048,1,512]{2,0,1:T(8,128)(2,1)}) %all-gather.18.cloned.1.call-update) | async-done | bytes 2097168 | tf_op jit(solution)/shard_map/all_gather | solution.py:43
  420.6 31.1 %all-gather.20.cloned.1.call-done = bf16[2048,1,512]{2,0,1:T(8,128)(2,1)} async-done(((bf16[1024,1,512]{2,0,1:T(8,128)(2,1)}), bf16[2048,1,512]{2,0,1:T(8,128)(2,1)}) %all-gather.20.cloned.1.call-update) | async-done | bytes 2097168 | tf_op jit(solution)/shard_map/all_gather | solution.py:43
  464.5 59.4 %while.186 = (s32[]{:T(128)}, bf16[4,2048,64]{1,2,0:T(8,128)(2,1)}, f32[4,2048]{1,0:T(4,128)S(1)}, bf16[4,2048,64]{2,1,0:T(8,128)(2,1)}, s32[4,2048]{1,0:T(4,128...) while((s32[]{:T(128)}, bf16[4,2048,64]{1,2,0:T(8,128)(2,1)}, ...), condition=%wide.region_27.28_spmd, body=%wide.region_22.27_spmd.sunk | while | flops 277904896 | bytes 17090916 | solution.py:216
  527.3 31.9 %reduce-scatter.18.cloned.1.call-done = bf16[1024,1,512]{2,0,1:T(8,128)(2,1)} async-done(((bf16[2048,1,512]{2,0,1:T(8,128)(2,1)}), bf16[1024,1,512]{2,0,1:T(8,128)(2,1)}) %reduce-scatter.18.cloned.1.call-update) | async-done | bytes 1048592 | tf_op jit(solution)/shard_map/reduce_scatter | solution.py:55
  564.1 33.1 %all-gather.22.cloned.1.call-done = bf16[2048,1,512]{2,0,1:T(8,128)(2,1)} async-done(((bf16[1024,1,512]{2,0,1:T(8,128)(2,1)}), bf16[2048,1,512]{2,0,1:T(8,128)(2,1)}) %all-gather.22.cloned.1.call-update) | async-done | bytes 2097168 | tf_op jit(solution)/shard_map/all_gather | solution.py:43
  608.6 31.9 %reduce-scatter.20.cloned.1.call-done = bf16[1024,1,512]{2,0,1:T(8,128)(2,1)} async-done(((bf16[2048,1,512]{2,0,1:T(8,128)(2,1)}), bf16[1024,1,512]{2,0,1:T(8,128)(2,1)}) %reduce-scatter.20.cloned.1.call-update) | async-done | bytes 1048592 | tf_op jit(solution)/shard_map/reduce_scatter | solution.py:55
  653.5 33.2 %all-gather.24.cloned.1.call-done = bf16[2048,1,512]{2,0,1:T(8,128)(2,1)} async-done(((bf16[1024,1,512]{2,0,1:T(8,128)(2,1)}), bf16[2048,1,512]{2,0,1:T(8,128)(2,1)}) %all-gather.24.cloned.1.call-update) | async-done | bytes 2097168 | tf_op jit(solution)/shard_map/all_gather | solution.py:47
  702.7 31.9 %reduce-scatter.22.cloned.1.call-done = bf16[1024,1,512]{2,0,1:T(8,128)(2,1)} async-done(((bf16[2048,1,512]{2,0,1:T(8,128)(2,1)}), bf16[1024,1,512]{2,0,1:T(8,128)(2,1)}) %reduce-scatter.22.cloned.1.call-update) | async-done | bytes 1048592 | tf_op jit(solution)/shard_map/reduce_scatter | solution.py:73
  742.4 32.8 %all-gather.26.cloned.1.call-done = bf16[2048,1,512]{2,0,1:T(8,128)(2,1)} async-done(((bf16[1024,1,512]{2,0,1:T(8,128)(2,1)}), bf16[2048,1,512]{2,0,1:T(8,128)(2,1)}) %all-gather.26.cloned.1.call-update) | async-done | bytes 2097168 | tf_op jit(solution)/shard_map/all_gather | solution.py:47
  782.7 96.0 %while.188 = (s32[]{:T(128)}, bf16[4,2048,64]{1,2,0:T(8,128)(2,1)}, bf16[4,2048,64]{1,2,0:T(8,128)(2,1)}, bf16[4,2048,64]{1,2,0:T(8,128)(2,1)}, bf16[4,2048,64]{...) while((s32[]{:T(128)}, bf16[4,2048,64]{1,2,0:T(8,128)(2,1)}, ...), condition=%wide.region_45.46_spmd, body=%wide.region_41.45_spmd.sunk | while | flops 682556928 | bytes 41066952 | solution.py:242
  809.4 18.6 %while.196 = (s32[]{:T(128)}, f32[2048,64]{0,1:T(8,128)S(1)}, f32[2048,64]{0,1:T(8,128)S(1)}, bf16[4,512,64]{1,2,0:T(8,128)(2,1)S(1)}, s32[4,512]{1,0:T(4,128)S(...) while((s32[]{:T(128)}, f32[2048,64]{0,1:T(8,128)S(1)}, ...), condition=%wide.region_44.44_spmd.clone, body=%wide.region_42.43_spmd.clone.sunk | while | flops 682294784 | bytes 35741864 | solution.py:175
  833.4 18.6 %while.196 = (s32[]{:T(128)}, f32[2048,64]{0,1:T(8,128)S(1)}, f32[2048,64]{0,1:T(8,128)S(1)}, bf16[4,512,64]{1,2,0:T(8,128)(2,1)S(1)}, s32[4,512]{1,0:T(4,128)S(...) while((s32[]{:T(128)}, f32[2048,64]{0,1:T(8,128)S(1)}, ...), condition=%wide.region_44.44_spmd.clone, body=%wide.region_42.43_spmd.clone.sunk | while | flops 682294784 | bytes 35741864 | solution.py:175
  887.7 27.3 %reduce-scatter.24.cloned.1.call-done = bf16[1024,1,512]{2,0,1:T(8,128)(2,1)} async-done(((bf16[2048,1,512]{2,0,1:T(8,128)(2,1)}), bf16[1024,1,512]{2,0,1:T(8,128)(2,1)}) %reduce-scatter.24.cloned.1.call-update) | async-done | bytes 1048592 | tf_op jit(solution)/shard_map/reduce_scatter | solution.py:73
  918.4 30.7 %reduce-scatter.30.cloned.1.call-done = bf16[1024,1,512]{2,0,1:T(8,128)(2,1)} async-done(((bf16[2048,1,512]{2,0,1:T(8,128)(2,1)}), bf16[1024,1,512]{2,0,1:T(8,128)(2,1)}) %reduce-scatter.30.cloned.1.call-update) | async-done | bytes 1048592 | tf_op jit(solution)/shard_map/reduce_scatter | solution.py:73
  964.9 27.0 %all-gather.28.cloned.1.call-done = bf16[2048,1,512]{2,0,1:T(8,128)(2,1)} async-done(((bf16[1024,1,512]{2,0,1:T(8,128)(2,1)}), bf16[2048,1,512]{2,0,1:T(8,128)(2,1)}) %all-gather.28.cloned.1.call-update) | async-done | bytes 2097168 | tf_op jit(solution)/shard_map/all_gather | solution.py:47
  1033.6 28.0 %reduce-scatter.26.cloned.1.call-done = bf16[1024,1,512]{2,0,1:T(8,128)(2,1)} async-done(((bf16[2048,1,512]{2,0,1:T(8,128)(2,1)}), bf16[1024,1,512]{2,0,1:T(8,128)(2,1)}) %reduce-scatter.26.cloned.1.call-update) | async-done | bytes 1048592 | tf_op jit(solution)/shard_map/reduce_scatter | solution.py:73
  1072.4 129.8 %while.192 = (s32[]{:T(128)}, bf16[4,2048,64]{1,2,0:T(8,128)(2,1)}, bf16[4,2048,64]{1,2,0:T(8,128)(2,1)}, bf16[4,2048,64]{1,2,0:T(8,128)(2,1)}, bf16[4,2048,64]{...) while((s32[]{:T(128)}, bf16[4,2048,64]{1,2,0:T(8,128)(2,1)}, ...), condition=%wide.region_66.67_spmd, body=%wide.region_62.66_spmd.sunk | while | flops 684654592 | bytes 41062908 | solution.py:242
  1077.2 25.1 %while.198 = (s32[]{:T(128)}, f32[2048,64]{0,1:T(8,128)S(1)}, f32[2048,64]{0,1:T(8,128)S(1)}, bf16[4,512,64]{1,2,0:T(8,128)(2,1)S(1)}, s32[4,512]{1,0:T(4,128)S(...) while((s32[]{:T(128)}, f32[2048,64]{0,1:T(8,128)S(1)}, ...), condition=%wide.region_65.65_spmd.clone, body=%wide.region_63.64_spmd.clone.sunk | while | flops 684392448 | bytes 35745984 | solution.py:175
  1109.6 25.1 %while.198 = (s32[]{:T(128)}, f32[2048,64]{0,1:T(8,128)S(1)}, f32[2048,64]{0,1:T(8,128)S(1)}, bf16[4,512,64]{1,2,0:T(8,128)(2,1)S(1)}, s32[4,512]{1,0:T(4,128)S(...) while((s32[]{:T(128)}, f32[2048,64]{0,1:T(8,128)S(1)}, ...), condition=%wide.region_65.65_spmd.clone, body=%wide.region_63.64_spmd.clone.sunk | while | flops 684392448 | bytes 35745984 | solution.py:175
  1142.0 25.1 %while.198 = (s32[]{:T(128)}, f32[2048,64]{0,1:T(8,128)S(1)}, f32[2048,64]{0,1:T(8,128)S(1)}, bf16[4,512,64]{1,2,0:T(8,128)(2,1)S(1)}, s32[4,512]{1,0:T(4,128)S(...) while((s32[]{:T(128)}, f32[2048,64]{0,1:T(8,128)S(1)}, ...), condition=%wide.region_65.65_spmd.clone, body=%wide.region_63.64_spmd.clone.sunk | while | flops 684392448 | bytes 35745984 | solution.py:175
  1174.4 25.1 %while.198 = (s32[]{:T(128)}, f32[2048,64]{0,1:T(8,128)S(1)}, f32[2048,64]{0,1:T(8,128)S(1)}, bf16[4,512,64]{1,2,0:T(8,128)(2,1)S(1)}, s32[4,512]{1,0:T(4,128)S(...) while((s32[]{:T(128)}, f32[2048,64]{0,1:T(8,128)S(1)}, ...), condition=%wide.region_65.65_spmd.clone, body=%wide.region_63.64_spmd.clone.sunk | while | flops 684392448 | bytes 35745984 | solution.py:175
  1234.3 107.0 %while.190 = (s32[]{:T(128)}, bf16[4,2048,64]{1,2,0:T(8,128)(2,1)}, bf16[4,2048,64]{1,2,0:T(8,128)(2,1)}, bf16[4,2048,64]{1,2,0:T(8,128)(2,1)}, bf16[4,2048,64]{...) while((s32[]{:T(128)}, bf16[4,2048,64]{1,2,0:T(8,128)(2,1)}, ...), condition=%wide.region_57.58_spmd, body=%wide.region_53.57_spmd.sunk | while | flops 682556928 | bytes 41058764 | solution.py:242
  1266.5 18.6 %while.197 = (s32[]{:T(128)}, f32[2048,64]{0,1:T(8,128)S(1)}, f32[2048,64]{0,1:T(8,128)S(1)}, bf16[4,512,64]{1,2,0:T(8,128)(2,1)S(1)}, s32[4,512]{1,0:T(4,128)S(...) while((s32[]{:T(128)}, f32[2048,64]{0,1:T(8,128)S(1)}, ...), condition=%wide.region_56.56_spmd.clone, body=%wide.region_54.55_spmd.clone.sunk | while | flops 682294784 | bytes 35741864 | solution.py:175
  1320.0 18.6 %while.197 = (s32[]{:T(128)}, f32[2048,64]{0,1:T(8,128)S(1)}, f32[2048,64]{0,1:T(8,128)S(1)}, bf16[4,512,64]{1,2,0:T(8,128)(2,1)S(1)}, s32[4,512]{1,0:T(4,128)S(...) while((s32[]{:T(128)}, f32[2048,64]{0,1:T(8,128)S(1)}, ...), condition=%wide.region_56.56_spmd.clone, body=%wide.region_54.55_spmd.clone.sunk | while | flops 682294784 | bytes 35741864 | solution.py:175
  1362.0 42.0 %all-reduce = (f32[2,512]{1,0:T(2,128)}, f32[2,512]{1,0:T(2,128)}, f32[3,512]{1,0:T(4,128)}, f32[3,512]{1,0:T(4,128)}, f32[2,512]{1,0:T(2,128)}) all-reduce(f32[2,512]{1,0:T(2,128)S(1)} %pad_maximum_fusion.5, f32[2,512]{1,0:T(2,128)S(1)} %pad_maximum_fusion.6, ...), channel_id=1, replica_groups=mesh['dp'=16,'mp'=2] {'dp','mp'}, use_global_device_ids=true, to_apply=%region_74.75 | all-reduce | flops 6144 | bytes 49152 | tf_op jit(solution)/shard_map/psum | solution.py:476
  1404.0 105.0 %all-reduce.4.cloned.1.call-done = (bf16[3,512,256]{2,1,0:T(8,128)(2,1)}, bf16[256,512]{1,0:T(8,128)(2,1)}, bf16[512,1024]{1,0:T(8,128)(2,1)}, bf16[1024,512]{1,...) async-done(((bf16[3,512,256]{2,1,0:T(8,128)(2,1)}, ...) | async-done | bytes 7340048 | tf_op jit(solution)/shard_map/psum | solution.py:464
  (1645 shorter events, 1130.0 us)
Async XLA Ops:
  7.2 597.3 %copy-start = (bf16[1024,512]{1,0:T(8,128)(2,1)S(1)}, bf16[1024,512]{1,0:T(8,128)(2,1)}, u32[]{:S(2)}) copy-start(bf16[1024,512]{1,0:T(8,128)(2,1)} %param.64) | copy-start | bytes 3145732
  7.2 42.0 %all-gather.12.cloned.1.call-start = ((), (), s32[]{:S(2)}) async-start(), calls=%async_computation.11 | async-start | bytes 3145728 | tf_op jit(solution)/shard_map/all_gather | solution.py:43
  13.2 71.2 %all-gather.16.cloned.1.call-start = ((), (), s32[]{:S(2)}) async-start(), calls=%async_computation.15 | async-start | bytes 3145728 | tf_op jit(solution)/shard_map/all_gather | solution.py:43
  14.0 252.5 %reduce-scatter.16.cloned.1.call-start = ((), (), s32[]{:S(2)}) async-start(), calls=%async_computation.16 | async-start | bytes 3145728 | tf_op jit(solution)/shard_map/reduce_scatter | solution.py:55
  102.6 90.6 %copy-start.73 = (bf16[256,512]{1,0:T(8,128)(2,1)S(1)}, bf16[256,512]{1,0:T(8,128)(2,1)}, u32[]{:S(2)}) copy-start(bf16[256,512]{1,0:T(8,128)(2,1)} %param.59) | copy-start | bytes 786436
  196.5 101.2 %reduce-scatter.12.cloned.1.call-start = ((), (), s32[]{:S(2)}) async-start(), calls=%async_computation.12 | async-start | bytes 3145728 | tf_op jit(solution)/shard_map/reduce_scatter | solution.py:55
  198.3 64.1 %copy-start.75 = (bf16[256,512]{1,0:T(8,128)(2,1)S(1)}, bf16[256,512]{1,0:T(8,128)(2,1)}, u32[]{:S(2)}) copy-start(bf16[256,512]{1,0:T(8,128)(2,1)} %param.53) | copy-start | bytes 786436
  265.7 71.6 %all-gather.14.cloned.1.call-start = ((), (), s32[]{:S(2)}) async-start(), calls=%async_computation.13 | async-start | bytes 3145728 | tf_op jit(solution)/shard_map/all_gather | solution.py:43
  266.4 114.7 %copy-start.109 = (f32[1,512]{1,0:T(1,128)}, f32[1,512]{1,0:T(1,128)S(1)}, u32[]{:S(2)}) copy-start(f32[1,512]{1,0:T(1,128)S(1)} %get-tuple-element.1284) | copy-start | bytes 6148
  266.4 118.3 %copy-start.98 = (f32[1,512]{1,0:T(1,128)}, f32[1,512]{1,0:T(1,128)S(1)}, u32[]{:S(2)}) copy-start(f32[1,512]{1,0:T(1,128)S(1)} %get-tuple-element.1283) | copy-start | bytes 6148
  266.4 118.3 %copy-start.107 = (f32[1,512]{1,0:T(1,128)}, f32[1,512]{1,0:T(1,128)S(1)}, u32[]{:S(2)}) copy-start(f32[1,512]{1,0:T(1,128)S(1)} %get-tuple-element.1285) | copy-start | bytes 6148
  302.2 78.8 %copy-start.4 = (f32[1024,1,512]{2,0,1:T(8,128)}, f32[1024,1,512]{2,0,1:T(8,128)S(1)}, u32[]{:S(2)}) copy-start(f32[1024,1,512]{2,0,1:T(8,128)S(1)} %get-tuple-element.1266) | copy-start | bytes 6291460
  302.2 78.8 %copy-start.87 = (f32[1024]{0:T(1024)}, f32[1024]{0:T(1024)S(1)}, u32[]{:S(2)}) copy-start(f32[1024]{0:T(1024)S(1)} %broadcast_multiply_fusion.4) | copy-start | bytes 12292
  302.7 78.4 %copy-start.92 = (f32[1024]{0:T(1024)}, f32[1024]{0:T(1024)S(1)}, u32[]{:S(2)}) copy-start(f32[1024]{0:T(1024)S(1)} %fusion.279) | copy-start | bytes 12292
  304.1 77.0 %reduce-scatter.14.cloned.1.call-start = ((), (), s32[]{:S(2)}) async-start(), calls=%async_computation.14 | async-start | bytes 3145728 | tf_op jit(solution)/shard_map/reduce_scatter | solution.py:55
  349.1 67.3 %all-gather.18.cloned.1.call-start = ((), (), s32[]{:S(2)}) async-start(), calls=%async_computation.17 | async-start | bytes 3145728 | tf_op jit(solution)/shard_map/all_gather | solution.py:43
  354.5 97.3 %all-gather.20.cloned.1.call-start = ((), (), s32[]{:S(2)}) async-start(), calls=%async_computation.18 | async-start | bytes 3145728 | tf_op jit(solution)/shard_map/all_gather | solution.py:43
  388.8 170.5 %reduce-scatter.18.cloned.1.call-start = ((), (), s32[]{:S(2)}) async-start(), calls=%async_computation.19 | async-start | bytes 3145728 | tf_op jit(solution)/shard_map/reduce_scatter | solution.py:55
  527.3 69.9 %all-gather.22.cloned.1.call-start = ((), (), s32[]{:S(2)}) async-start(), calls=%async_computation.20 | async-start | bytes 3145728 | tf_op jit(solution)/shard_map/all_gather | solution.py:43
  563.9 76.7 %reduce-scatter.20.cloned.1.call-start = ((), (), s32[]{:S(2)}) async-start(), calls=%async_computation.21 | async-start | bytes 3145728 | tf_op jit(solution)/shard_map/reduce_scatter | solution.py:55
  608.6 78.1 %all-gather.24.cloned.1.call-start = ((), (), s32[]{:S(2)}) async-start(), calls=%async_computation.22 | async-start | bytes 3145728 | tf_op jit(solution)/shard_map/all_gather | solution.py:47
  653.4 81.2 %reduce-scatter.22.cloned.1.call-start = ((), (), s32[]{:S(2)}) async-start(), calls=%async_computation.23 | async-start | bytes 3145728 | tf_op jit(solution)/shard_map/reduce_scatter | solution.py:73
  702.7 72.6 %all-gather.26.cloned.1.call-start = ((), (), s32[]{:S(2)}) async-start(), calls=%async_computation.24 | async-start | bytes 3145728 | tf_op jit(solution)/shard_map/all_gather | solution.py:47
  741.9 173.1 %reduce-scatter.24.cloned.1.call-start = ((), (), s32[]{:S(2)}) async-start(), calls=%async_computation.25 | async-start | bytes 3145728 | tf_op jit(solution)/shard_map/reduce_scatter | solution.py:73
  883.1 66.0 %reduce-scatter.30.cloned.1.call-start = ((), (), s32[]{:S(2)}) async-start(), calls=%async_computation.30 | async-start | bytes 3145728 | tf_op jit(solution)/shard_map/reduce_scatter | solution.py:73
  887.7 104.2 %all-gather.28.cloned.1.call-start = ((), (), s32[]{:S(2)}) async-start(), calls=%async_computation.26 | async-start | bytes 3145728 | tf_op jit(solution)/shard_map/all_gather | solution.py:47
  958.6 70.9 %all-gather.32.cloned.1.call-start = ((), (), s32[]{:S(2)}) async-start(), calls=%async_computation.31 | async-start | bytes 3145728 | tf_op jit(solution)/shard_map/all_gather | solution.py:47
  964.7 97.0 %reduce-scatter.26.cloned.1.call-start = ((), (), s32[]{:S(2)}) async-start(), calls=%async_computation.27 | async-start | bytes 3145728 | tf_op jit(solution)/shard_map/reduce_scatter | solution.py:73
  1007.8 219.0 %all-gather.30.cloned.1.call-start = ((), (), s32[]{:S(2)}) async-start(), calls=%async_computation.28 | async-start | bytes 3145728 | tf_op jit(solution)/shard_map/all_gather | solution.py:47
  1068.9 285.7 %reduce-scatter.32.cloned.1.call-start = ((), (), s32[]{:S(2)}) async-start(), calls=%async_computation.32 | async-start | bytes 3145728 | tf_op jit(solution)/shard_map/reduce_scatter | solution.py:73
  1207.8 301.3 %all-reduce.4.cloned.1.call-start = ((), (), s32[]{:S(2)}) async-start(), calls=%async_computation.33 | async-start | bytes 14680064 | tf_op jit(solution)/shard_map/psum | solution.py:464
  1348.8 195.1 %reduce-scatter.28.cloned.1.call-start = ((), (), s32[]{:S(2)}) async-start(), calls=%async_computation.29 | async-start | bytes 3145728 | tf_op jit(solution)/shard_map/reduce_scatter | solution.py:73
  (166 other events, 1731.1 us)
Sparse Core Ops, SparseCore 0:
  13.3 35.8 all-gather.11
  51.3 33.1 all-gather.15
  196.7 31.8 reduce-scatter.15
  265.9 31.8 reduce-scatter.11
  304.2 33.1 all-gather.13
  349.2 31.8 reduce-scatter.13
  383.3 33.1 all-gather.17
  418.6 33.1 all-gather.19
  527.4 31.8 reduce-scatter.17
  564.0 33.1 all-gather.21
  608.7 31.8 reduce-scatter.19
  653.5 33.1 all-gather.23
  702.8 31.8 reduce-scatter.21
  742.0 33.1 all-gather.25
  883.2 31.8 reduce-scatter.23
  917.3 31.8 reduce-scatter.29
  958.7 33.1 all-gather.27
  993.8 33.1 all-gather.31
  1029.8 31.8 reduce-scatter.25
  1069.0 33.1 all-gather.29
  1207.9 31.8 reduce-scatter.31
  1348.9 160.0 all-reduce.3
  1511.9 31.9 reduce-scatter.27
where the time goes:
time: 1570 us; the launch traced here: 1560 us
  waiting for transfers between devices  634 us (40%)
  matrix products  447 us (28%)
  local copies, waits for them, and re-layouts  228 us (15%)
  other arithmetic  180 us (11%)
  blocking collectives  42 us (3%)
  between operations  16 us (1%)
    all_gather x6, waiting for transfers between devices, collect(): return lax.all_gather(piece_rows, 'mp', axis=0, tiled=True)  178 us
    reduce_scatter x6, waiting for transfers between devices, project_back(): lax.psum_scatter(partial_term(jnp.int32(0), lax.axis_size('mp') * rows).a...  136 us
    dot_general x96, matrix products, pair_scores(): lax.dot_general(query_block, key_rows, (((1,), (1,)), ((), ())), preferre...  127 us
    reduce_scatter x5, waiting for transfers between devices, project_out(): lax.psum_scatter(partial_term(jnp.int32(0), lax.axis_size('mp') * rows).a...  120 us
    psum x1, waiting for transfers between devices, local(): lax.psum(enc_qkv_grad.astype(jnp.bfloat16), 'dp').astype(jnp.float32)  105 us
    all_gather x5, waiting for transfers between devices, collect_grad(): lax.all_gather(piece_rows.astype(jnp.bfloat16), 'mp', axis=0, tiled=True)  93 us
    dot_general x16, matrix products, dot_last(): lax.dot_general(left, right, (((left.ndim - 1,), (1,)), ((), ())), prefer...  52.2 us
    dot_general x48, matrix products, one_block(): mixed = jnp.dot(weights, value_rows, preferred_element_type=jnp.float32)  51.8 us
  transfers between devices with their start and end apart: 23, of which 19 were waited for; matrix products, arithmetic and copies ran while one was open for 29% of the time, Pallas kernels for 0%

commit v1 on v0

--- a/solution.py
+++ b/solution.py
@@ -1,8 +1,11 @@
+import math
 from functools import partial
 
 import jax
 import jax.numpy as jnp
 from jax import lax
+from jax.experimental import pallas as pl
+from jax.experimental.pallas import tpu as pltpu
 from jax.sharding import PartitionSpec as P
 
 D = 512
@@ -507,9 +510,649 @@
     )
 
 
+BIG=-1e30
+BF=jnp.bfloat16; F32=jnp.float32
+NT=(((1,),(1,)),((),()))
+NN=(((1,),(0,)),((),()))
+TN=(((0,),(0,)),((),()))
+def dg(a,b,d): return lax.dot_general(a,b,d,preferred_element_type=F32)
+
+def fwd_kernel(c_ref,q_ref,ko_ref,kx_ref,vo_ref,vx_ref,qe_ref,ke_ref,o_ref,lse_ref,K,V,*,causal,bq,n,sub):
+    qb=pl.program_id(1)
+    half=n//2
+    L=2*n
+    c=c_ref[0]
+    lane=lax.broadcasted_iota(jnp.int32,(1,128),1)
+    left=lane<64
+    @pl.when(qb==0)
+    def _():
+        for src_k,src_v,base in ((ko_ref,vo_ref,c),(kx_ref,vx_ref,1-c)):
+            for j in range(2):
+                pos=jnp.where(base==0,0 if j==0 else 3,1 if j==0 else 2)*half
+                pos=pl.multiple_of(pos,half)
+                kk=src_k[pl.ds(j*half,half),:]; vv=src_v[pl.ds(j*half,half),:]
+                ke=ke_ref[pl.ds(pos,half),:]
+                one=jnp.ones_like(vv)
+                K[0,pl.ds(pos,half),:]=jnp.where(left,kk,ke)
+                K[1,pl.ds(pos,half),:]=jnp.where(left,ke,kk)
+                V[0,pl.ds(pos,half),:]=jnp.where(left,vv,one)
+                V[1,pl.ds(pos,half),:]=jnp.where(left,one,vv)
+    qp=q_ref[...]; qe=qe_ref[...]
+    def finish(R,m,r0,rows):
+        Re,Ro=R; me,mo=m
+        lb=jnp.where(left,Ro,Re)
+        O=jnp.where(left,Re,Ro)/pltpu.roll(lb,64,1)
+        o_ref[pl.ds(r0,rows),:]=O.astype(BF)
+        lse_ref[pl.ds(r0,rows),:]=jnp.where(left,mo,me)+jnp.log2(lb)
+    def block(nk,diag_row):
+        for r0 in range(0,bq,sub):
+            R=[];M=[]
+            for e in range(2):
+                qq=(jnp.where(left,qp,qe) if e==0 else jnp.where(left,qe,qp))[r0:r0+sub]
+                if diag_row is None:
+                    S=dg(qq,K[e,:nk,:],NT)
+                    m=jnp.max(S,axis=1,keepdims=True)
+                    p=jnp.exp2(S-m).astype(BF)
+                    R.append(dg(p,V[e,:nk,:],NN)); M.append(m)
+                else:
+                    S2=dg(qq,K[e,nk-half:nk,:],NT)
+                    ri=lax.broadcasted_iota(jnp.int32,(sub,half),0)+(diag_row+r0)
+                    ci=lax.broadcasted_iota(jnp.int32,(sub,half),1)
+                    S2=jnp.where(ci<=ri,S2,BIG)
+                    m=jnp.max(S2,axis=1,keepdims=True)
+                    if nk>half:
+                        S1=dg(qq,K[e,:nk-half,:],NT)
+                        m=jnp.maximum(m,jnp.max(S1,axis=1,keepdims=True))
+                        r=dg(jnp.exp2(S2-m).astype(BF),V[e,nk-half:nk,:],NN)+dg(jnp.exp2(S1-m).astype(BF),V[e,:nk-half,:],NN)
+                    else:
+                        r=dg(jnp.exp2(S2-m).astype(BF),V[e,nk-half:nk,:],NN)
+                    R.append(r); M.append(m)
+            finish(R,M,r0,sub)
+    if not causal:
+        block(L,None)
+    else:
+        per=half//bq
+        chunk=qb//per
+        pos=jnp.where(c==0,chunk*3,chunk+1)
+        drow=(qb-chunk*per)*bq
+        for t in range(4):
+            @pl.when(pos==t)
+            def _(t=t): block((t+1)*half,drow)
+
+def attn_fwd(c,q,ko,kx,vo,vx,qe,ke,*,causal,bq=256,sub=None,vmem=100):
+    n,D=q.shape; L=2*n
+    sub=sub or bq
+    np_=D//128
+    kern=partial(fwd_kernel,causal=causal,bq=bq,n=n,sub=sub)
+    full=pl.BlockSpec((n,128),lambda p,b:(0,p))
+    qs=pl.BlockSpec((bq,128),lambda p,b:(b,p))
+    return pl.pallas_call(kern,grid=(np_,n//bq),
+        in_specs=[pl.BlockSpec(memory_space=pltpu.SMEM),qs,full,full,full,full,
+            pl.BlockSpec((bq,128),lambda p,b:(b,0)),pl.BlockSpec((L,128),lambda p,b:(0,0))],
+        out_specs=[qs,qs],
+        out_shape=[jax.ShapeDtypeStruct((n,D),BF),jax.ShapeDtypeStruct((n,D),F32)],
+        scratch_shapes=[pltpu.VMEM((2,L,128),BF),pltpu.VMEM((2,L,128),BF)],
+        compiler_params=pltpu.CompilerParams(vmem_limit_bytes=56*1024*1024),
+        cost_estimate=pl.CostEstimate(flops=4*n*L*D,bytes_accessed=n*D*2*8,transcendentals=n*L*8),
+        name="attn_fwd_causal" if causal else "attn_fwd")(c,q,ko,kx,vo,vx,qe,ke)
+
+def bwd_kernel(c_ref,q_ref,ko_ref,kx_ref,vo_ref,vx_ref,qe_ref,keo_ref,kex_ref,do_ref,o_ref,lse_ref,
+     dq_ref,dko_ref,dkx_ref,dvo_ref,dvx_ref,Q,DO,DQT,*,causal,bk,n,sub,dqt):
+    kb=pl.program_id(1); nb=n//bk
+    half=n//2; L=2*n
+    c=c_ref[0]
+    lane=lax.broadcasted_iota(jnp.int32,(1,128),1)
+    left=lane<64
+    l64=lane%64
+    @pl.when(kb==0)
+    def _():
+        lse=lse_ref[...]
+        h=lse.astype(BF).astype(F32); r=lse-h; h2=r.astype(BF).astype(F32); h3=r-h2
+        ext=jnp.where(l64==8,-h,jnp.where(l64==9,-h2,jnp.where(l64==10,-h3,qe_ref[...].astype(F32)))).astype(BF)
+        qp=q_ref[...]
+        Q[0]=jnp.where(left,qp,ext); Q[1]=jnp.where(left,ext,qp)
+        dop=do_ref[...]
+        pr=dop.astype(F32)*o_ref[...].astype(F32)
+        hi=pr.astype(BF); lo=(pr-hi.astype(F32)).astype(BF)
+        ii=lax.broadcasted_iota(jnp.int32,(128,128),0); jj=lax.broadcasted_iota(jnp.int32,(128,128),1)
+        J=((ii<64)!=(jj<64)).astype(BF)
+        dl=dg(hi,J,NN)+dg(lo,J,NN)
+        h=dl.astype(BF).astype(F32); r=dl-h
+        ext=jnp.where(l64==8,-h,jnp.where(l64==9,-r,0.0)).astype(BF)
+        DO[0]=jnp.where(left,dop,ext); DO[1]=jnp.where(left,ext,dop)
+        DQT[...]=jnp.zeros_like(DQT)
+    own=kb<nb
+    kp=jnp.where(own,ko_ref[...],kx_ref[...]); vp=jnp.where(own,vo_ref[...],vx_ref[...]); ke=jnp.where(own,keo_ref[...],kex_ref[...])
+    one=jnp.ones_like(vp)
+    Kx=(jnp.where(left,kp,ke),jnp.where(left,ke,kp))
+    Vx=(jnp.where(left,vp,one),jnp.where(left,one,vp))
+    if dqt: KT=kp.T
+    def body(q0,rows,diag_off):
+        acck=[];accv=[]
+        for e in range(2):
+            qq=Q[e,pl.ds(q0,rows),:]; dd=DO[e,pl.ds(q0,rows),:]
+            S=dg(Kx[e],qq,NT)
+            if diag_off is not None:
+                ki=lax.broadcasted_iota(jnp.int32,S.shape,0)+diag_off
+                qi=lax.broadcasted_iota(jnp.int32,S.shape,1)
+                S=jnp.where(ki<=qi,S,BIG)
+            p=jnp.exp2(S)
+            dp=dg(Vx[e],dd,NT)
+            ds=(p*dp).astype(BF)
+            accv.append(dg(p.astype(BF),dd,NN))
+            acck.append(dg(ds,qq,NN))
+            if dqt:
+                DQT[64*e:64*e+64,pl.ds(q0,rows)]+=dg(KT[64*e:64*e+64],ds,NN)
+            else:
+                DQT[e,pl.ds(q0,rows),:]+=dg(ds,Kx[e],TN)
+        return jnp.where(left,acck[0],acck[1]),jnp.where(left,accv[0],accv[1])
+    def put(dk,dv):
+        dk=(dk*math.log(2.0)).astype(BF); dv=dv.astype(BF)
+        @pl.when(own)
+        def _(): dko_ref[...]=dk; dvo_ref[...]=dv
+        @pl.when(jnp.logical_not(own))
+        def _(): dkx_ref[...]=dk; dvx_ref[...]=dv
+    if not causal:
+        dk=dv=0
+        for q0 in range(0,n,sub):
+            a,b=body(q0,sub,None); dk=dk+a; dv=dv+b
+        put(dk,dv)
+    else:
+        per=half//bk
+        kbl=jnp.where(own,kb,kb-nb)
+        j=kbl//per
+        base=jnp.where(own,c,1-c)
+        kpos=jnp.where(base==0,j*3,j+1)
+        koff=(kbl-j*per)*bk
+        pa=jnp.where(c==0,0,1); pb=jnp.where(c==0,3,2)
+        def case(am,bm):
+            dk=dv=0
+            for q0,mode in ((0,am),(half,bm)):
+                if mode==0: continue
+                a,b=body(q0,half,koff if mode==1 else None); dk=dk+a; dv=dv+b
+            if am==0 and bm==0: dk=dv=jnp.zeros((bk,128),F32)
+            put(dk,dv)
+        for am in range(3):
+            for bm in range(3):
+                if am>bm or (am==bm==1): continue
+                if am>0 and bm!=2: continue
+                ca=(kpos>pa,kpos==pa,kpos<pa)[am]; cb=(kpos>pb,kpos==pb,kpos<pb)[bm]
+                @pl.when(jnp.logical_and(ca,cb))
+                def _(am=am,bm=bm): case(am,bm)
+    @pl.when(kb==2*nb-1)
+    def _():
+        if dqt:
+            dq_ref[...]=(DQT[...]*0.125).T.astype(BF)
+        else:
+            dq_ref[...]=(jnp.where(left,DQT[0],DQT[1])*0.125).astype(BF)
+
+def attn_bwd(c,q,ko,kx,vo,vx,qe,keo,kex,do,o,lse,*,causal,bk=256,sub=None,dqt=True):
+    n,D=q.shape; L=2*n; np_=D//128; nb=n//bk
+    sub=sub or n
+    kern=partial(bwd_kernel,causal=causal,bk=bk,n=n,sub=sub,dqt=dqt)
+    full=pl.BlockSpec((n,128),lambda p,b:(0,p))
+    ow=pl.BlockSpec((bk,128),lambda p,b:(jnp.minimum(b,nb-1),p)); ot=pl.BlockSpec((bk,128),lambda p,b:(jnp.maximum(b-nb,0),p))
+    keo_s=pl.BlockSpec((bk,128),lambda p,b:(jnp.minimum(b,nb-1),0)); kex_s=pl.BlockSpec((bk,128),lambda p,b:(jnp.maximum(b-nb,0),0))
+    sh=jax.ShapeDtypeStruct((n,D),BF)
+    return pl.pallas_call(kern,grid=(np_,2*nb),
+        in_specs=[pl.BlockSpec(memory_space=pltpu.SMEM),full,ow,ot,ow,ot,
+            pl.BlockSpec((n,128),lambda p,b:(0,0)),keo_s,kex_s,full,full,full],
+        out_specs=[full,ow,ot,ow,ot],
+        out_shape=[sh]*5,
+        scratch_shapes=[pltpu.VMEM((2,n,128),BF),pltpu.VMEM((2,n,128),BF),pltpu.VMEM((128,n) if dqt else (2,n,128),F32)],
+        compiler_params=pltpu.CompilerParams(vmem_limit_bytes=56*1024*1024),
+        cost_estimate=pl.CostEstimate(flops=10*n*L*D,bytes_accessed=n*D*2*12,transcendentals=n*L*8),
+        name="attn_bwd_causal" if causal else "attn_bwd")(c,q,ko,kx,vo,vx,qe,keo,kex,do,o,lse)
+
+
+def split_rows(values, bit):
+    half = values.shape[0] // 2
+    keep = lax.dynamic_slice_in_dim(values, bit * half, half, 0)
+    send = lax.dynamic_slice_in_dim(values, (1 - bit) * half, half, 0)
+    return keep, send
+
+
+def join_rows(mine, other, bit):
+    return jnp.where(bit == 0, jnp.concatenate([mine, other]), jnp.concatenate([other, mine]))
+
+
+class Place:
+    def __init__(self, dp_size):
+        self.dp_size = dp_size
+        self.dp = lax.axis_index("dp")
+        self.y = lax.axis_index("mp")
+        self.c = self.dp % 2
+        self.bits = [1 << b for b in range(1, dp_size.bit_length() - 1)]
+
+    def flip(self, values, mask):
+        return lax.ppermute(values, "dp", [(d, d ^ mask) for d in range(self.dp_size)])
+
+    def core_swap(self, values):
+        return self.flip(values, 1)
+
+    def y_swap(self, values):
+        return lax.ppermute(values, "mp", [(0, 1), (1, 0)])
+
+    def move(self, values, pairs):
+        perm = []
+        for d in range(0, self.dp_size, 2):
+            for (y0, c0), (y1, c1) in pairs:
+                perm.append(((d + c0) * 2 + y0, (d + c1) * 2 + y1))
+        return lax.ppermute(values, ("dp", "mp"), perm)
+
+    def pick(self, v00, v01, v10, v11):
+        return jnp.where(
+            self.y == 0, jnp.where(self.c == 0, v00, v01), jnp.where(self.c == 0, v10, v11)
+        )
+
+    def to_row(self, low, high):
+        a = self.move(high, [((0, 0), (0, 1)), ((1, 1), (1, 0))])
+        b = self.move(low, [((1, 0), (0, 1)), ((0, 1), (1, 0))])
+        e = self.move(high, [((1, 0), (0, 0)), ((0, 1), (1, 1))])
+        return self.pick(low, a, b, e), self.pick(e, b, a, low)
+
+    def from_row(self, first, second):
+        a = self.move(
+            jnp.where(self.y == 0, first, second), [((0, 1), (0, 0)), ((1, 0), (1, 1))]
+        )
+        by_core = jnp.where(self.c == 0, first, second)
+        b = self.move(by_core, [((0, 1), (1, 0)), ((1, 0), (0, 1))])
+        e = self.move(
+            jnp.where(self.c == 0, second, first), [((0, 0), (1, 0)), ((1, 1), (0, 1))]
+        )
+        return a, b, e
+
+    def native(self, first, second, a, b, e):
+        return jnp.concatenate([self.pick(first, b, b, second), self.pick(a, e, e, a)])
+
+    def other_half(self, weight, axis):
+        size = weight.shape[axis] // 2
+        piece = lax.dynamic_slice_in_dim(weight, self.c * size, size, axis)
+        near = self.y_swap(piece)
+        far = self.core_swap(near)
+        return jnp.where(
+            self.c == 0,
+            jnp.concatenate([near, far], axis=axis),
+            jnp.concatenate([far, near], axis=axis),
+        )
+
+    def reduce_bucket(self, own, other):
+        rows = own.shape[0]
+        own_keep, own_send = split_rows(own, self.c)
+        other_keep, other_send = split_rows(other, self.c)
+        got = self.core_swap(jnp.concatenate([own_send, other_send]).astype(BF))
+        own_keep = own_keep + got[: rows // 2].astype(F32)
+        other_keep = other_keep + got[rows // 2 :].astype(F32)
+        total = own_keep + self.y_swap(other_keep.astype(BF)).astype(F32)
+        for mask in self.bits:
+            keep, send = split_rows(total, (self.dp // mask) % 2)
+            total = keep + self.flip(send.astype(BF), mask).astype(F32)
+        total = total.astype(BF)
+        for mask in self.bits[::-1] + [1]:
+            total = join_rows(total, self.flip(total, mask), (self.dp // mask) % 2)
+        return total.astype(F32)
+
+    def reduce_all(self, values):
+        for mask in [1] + self.bits:
+            values = values + self.flip(values, mask)
+        return values + self.y_swap(values)
+
+
+def rows_of(grad):
+    if grad.ndim == 3:
+        kinds, depth, width = grad.shape
+        folded = jnp.concatenate([grad[:, : depth // 2], grad[:, depth // 2 :]], axis=2)
+        return folded.reshape(kinds * depth // 2, 2 * width)
+    depth, width = grad.shape
+    if width == D:
+        return grad
+    if width < D:
+        return jnp.concatenate([grad[: depth // 2], grad[depth // 2 :]], axis=1)
+    return jnp.concatenate([grad[:, :D], grad[:, D:]], axis=0)
+
+
+def rows_back(rows, shape):
+    if len(shape) == 3:
+        kinds, depth, width = shape
+        folded = rows.reshape(kinds, depth // 2, 2 * width)
+        return jnp.concatenate([folded[..., :width], folded[..., width:]], axis=1)
+    depth, width = shape
+    if width == D:
+        return rows
+    if width < D:
+        return jnp.concatenate([rows[:, :width], rows[:, width:]], axis=0)
+    return jnp.concatenate([rows[:depth], rows[depth:]], axis=1)
+
+
+def extensions(segments):
+    lane = jnp.arange(128, dtype=jnp.int32)[None, :] % DH
+    same = segments[:, None] == lane
+    for_query = jnp.where((lane < 8) & ~same, BIG, 0.0).astype(BF)
+    for_key = jnp.where(lane < 8, same.astype(F32), jnp.where(lane < 11, 1.0, 0.0)).astype(BF)
+    return for_query, for_key
+
+
+def dots(left, right):
+    return jnp.dot(left, right, preferred_element_type=F32)
+
+
+def dots_t(left, right):
+    return lax.dot_general(left, right, (((1,), (1,)), ((), ())), preferred_element_type=F32)
+
+
+def weight_dots(left, right):
+    return lax.dot_general(left, right, (((0,), (0,)), ((), ())), preferred_element_type=F32)
+
+
+Q_SCALE = DH**-0.5 * math.log2(math.e)
+
+
+def chip_rows(
+    source_rows,
+    target_rows,
+    source_segment,
+    target_segment,
+    running,
+    enc_qkv,
+    enc_proj,
+    enc_up,
+    enc_down,
+    enc_gains,
+    enc_shifts,
+    dec_qkv,
+    dec_proj,
+    cross_query,
+    cross_kv,
+    cross_proj,
+    dec_up,
+    dec_down,
+    dec_gains,
+    dec_shifts,
+    halt_weight,
+    enc_cotangent,
+    dec_cotangent,
+    *,
+    dp_size,
+):
+    at = Place(dp_size)
+    rows = source_rows.shape[0]
+    quarter = rows // 2
+    length = 2 * rows
+    core = at.c.astype(jnp.int32).reshape(1)
+
+    def to_row(values):
+        first, second = at.to_row(values[:quarter], values[quarter:])
+        return jnp.concatenate([first, second])
+
+    source = to_row(source_rows[:, 0]).astype(F32)
+    enc_qkv_other = at.other_half(enc_qkv, 1)
+    segments = jnp.concatenate([source_segment, target_segment])
+    segments = jnp.where(at.c == at.y, segments, at.core_swap(segments))
+    runs = jnp.transpose(running[:, 0]).astype(F32)
+    runs = to_row(jnp.concatenate([runs, jnp.zeros((rows, 126), F32)], axis=1))
+    runs_enc, runs_dec = runs[:, :1], runs[:, 1:2]
+    target = to_row(target_rows[:, 0]).astype(F32)
+
+    place = jnp.arange(rows, dtype=jnp.int32)
+    first_place = at.c * quarter + place
+    second_place = jnp.where(at.c == 0, 3 * quarter, 2 * quarter) + place - quarter
+    place = jnp.where(place < quarter, first_place, second_place)
+    embedding = signal(place.astype(F32)) + signal(jnp.ones((1,), F32))
+
+    def own_part(rows_all, core_of):
+        first = lax.dynamic_slice_in_dim(rows_all, core_of * quarter, quarter, 0)
+        second = lax.dynamic_slice_in_dim(
+            rows_all, jnp.where(core_of == 0, 3, 2) * quarter, quarter, 0
+        )
+        return jnp.concatenate([first, second])
+
+    source_q_all, source_k_all = extensions(segments[0])
+    target_q_all, target_k_all = extensions(segments[1])
+    source_q = own_part(source_q_all, at.c)
+    target_q = own_part(target_q_all, at.c)
+    source_k = (source_k_all, own_part(source_k_all, at.c), own_part(source_k_all, 1 - at.c))
+    target_k = (target_k_all, own_part(target_k_all, at.c), own_part(target_k_all, 1 - at.c))
+
+    def full(own, axis, other=None):
+        other = at.other_half(own, axis) if other is None else other
+        return other
+
+    enc_proj_other = at.other_half(enc_proj, 0)
+    enc_up_other = at.other_half(enc_up, 0)
+    enc_down_other = at.other_half(enc_down, 0)
+    dec_qkv_other = at.other_half(dec_qkv, 1)
+    dec_proj_other = at.other_half(dec_proj, 0)
+    cross_query_other = at.other_half(cross_query, 0)
+    cross_kv_other = at.other_half(cross_kv, 1)
+    cross_proj_other = at.other_half(cross_proj, 0)
+    dec_up_other = at.other_half(dec_up, 0)
+    dec_down_other = at.other_half(dec_down, 0)
+    enc_qkv = jnp.concatenate([enc_qkv, enc_qkv_other], axis=2)
+    enc_proj = jnp.concatenate([enc_proj, enc_proj_other], axis=0)
+    enc_up = jnp.concatenate([enc_up, enc_up_other], axis=1)
+    enc_down = jnp.concatenate([enc_down, enc_down_other], axis=0)
+    dec_qkv = jnp.concatenate([dec_qkv, dec_qkv_other], axis=2)
+    dec_proj = jnp.concatenate([dec_proj, dec_proj_other], axis=0)
+    cross_query = jnp.concatenate([cross_query, cross_query_other], axis=1)
+    cross_kv = jnp.concatenate([cross_kv, cross_kv_other], axis=2)
+    cross_proj = jnp.concatenate([cross_proj, cross_proj_other], axis=0)
+    dec_up = jnp.concatenate([dec_up, dec_up_other], axis=1)
+    dec_down = jnp.concatenate([dec_down, dec_down_other], axis=0)
+    cotangents = jnp.concatenate([enc_cotangent[:, 0], dec_cotangent[:, 0]], axis=1)
+    cotangents = to_row(cotangents.astype(BF)).astype(F32)
+    enc_cot, dec_cot = cotangents[:, :D], cotangents[:, D:]
+
+    def attend(query_in, key_in, w_query, w_key, w_value, query_ext, key_ext, causal):
+        queries = (dots(query_in, w_query) * Q_SCALE).astype(BF)
+        keys_own = dots(key_in, w_key).astype(BF)
+        values_own = dots(key_in, w_value).astype(BF)
+        keys_other = at.core_swap(keys_own)
+        values_other = at.core_swap(values_own)
+        mixed, log_total = attn_fwd(
+            core, queries, keys_own, keys_other, values_own, values_other, query_ext, key_ext[0],
+            causal=causal, bq=512, sub=256,
+        )
+        return mixed, (queries, keys_own, keys_other, values_own, values_other, query_ext, key_ext, mixed, log_total)
+
+    def attend_back(kept, out_grad, w_out, causal):
+        queries, keys_own, keys_other, values_own, values_other, query_ext, key_ext, mixed, log_total = kept
+        mixed_grad = dots_t(out_grad, w_out).astype(BF)
+        out_weight_grad = weight_dots(mixed, out_grad)
+        query_grad, key_own, key_other, value_own, value_other = attn_bwd(
+            core, queries, keys_own, keys_other, values_own, values_other, query_ext,
+            key_ext[1], key_ext[2], mixed_grad, mixed, log_total, causal=causal, bk=512,
+        )
+        key_grad = (key_own.astype(F32) + at.core_swap(key_other).astype(F32)).astype(BF)
+        value_grad = (value_own.astype(F32) + at.core_swap(value_other).astype(F32)).astype(BF)
+        return query_grad, key_grad, value_grad, out_weight_grad
+
+    def feed(low, up, down):
+        hidden = dots(low, up)
+        return dots(jax.nn.gelu(hidden).astype(BF), down), hidden
+
+    def feed_back(low, hidden, up, down, out_grad):
+        active, gelu_back = jax.vjp(jax.nn.gelu, hidden)
+        down_grad = weight_dots(active.astype(BF), out_grad)
+        hidden_grad = gelu_back(dots_t(out_grad, down))[0].astype(BF)
+        up_grad = weight_dots(low, hidden_grad)
+        return dots_t(hidden_grad, up), up_grad, down_grad
+
+    enc_start = source + embedding
+    enc_start_low = enc_start.astype(BF)
+    enc_mixed, enc_kept = attend(
+        enc_start_low, enc_start_low, enc_qkv[0], enc_qkv[1], enc_qkv[2], source_q, source_k, False
+    )
+    enc_sum_one = enc_start + dots(enc_mixed, enc_proj)
+    enc_middle = normalize(enc_sum_one, enc_gains[0], enc_shifts[0])
+    enc_middle_low = enc_middle.astype(BF)
+    enc_ffn, enc_hidden = feed(enc_middle_low, enc_up, enc_down)
+    enc_sum_two = enc_middle + enc_ffn
+    enc_last = normalize(enc_sum_two, enc_gains[1], enc_shifts[1])
+    enc_states = halting(runs_enc, enc_start, enc_last, halt_weight[0]).astype(BF)
+    enc_states_moved = at.from_row(enc_states[:quarter], enc_states[quarter:])
+
+    dec_start = target + embedding
+    dec_start_low = dec_start.astype(BF)
+    dec_mixed_heads, self_kept = attend(
+        dec_start_low, dec_start_low, dec_qkv[0], dec_qkv[1], dec_qkv[2], target_q, target_k, True
+    )
+    dec_sum_one = dec_start + dots(dec_mixed_heads, dec_proj)
+    dec_middle = normalize(dec_sum_one, dec_gains[0], dec_shifts[0])
+    dec_middle_low = dec_middle.astype(BF)
+    cross_mixed, cross_kept = attend(
+        dec_middle_low, enc_states, cross_query, cross_kv[0], cross_kv[1], target_q, source_k, False
+    )
+    dec_sum_two = dec_middle + dots(cross_mixed, cross_proj)
+    dec_mixed = normalize(dec_sum_two, dec_gains[1], dec_shifts[1])
+    dec_mixed_low = dec_mixed.astype(BF)
+    dec_ffn, dec_hidden = feed(dec_mixed_low, dec_up, dec_down)
+    dec_sum_three = dec_mixed + dec_ffn
+    dec_last = normalize(dec_sum_three, dec_gains[2], dec_shifts[2])
+    dec_states = halting(runs_dec, dec_start, dec_last, halt_weight[1]).astype(BF)
+    dec_states_moved = at.from_row(dec_states[:quarter], dec_states[quarter:])
+
+    _, halt_back = jax.vjp(partial(halting, runs_dec), dec_start, dec_last, halt_weight[1])
+    dec_start_grad, last_grad, dec_halt_grad = halt_back(dec_cot)
+    _, norm_back = jax.vjp(normalize, dec_sum_three, dec_gains[2], dec_shifts[2])
+    sum_grad, dec_gain_three, dec_shift_three = norm_back(last_grad)
+    ffn_input_grad, dec_up_grad, dec_down_grad = feed_back(
+        dec_mixed_low, dec_hidden, dec_up, dec_down, sum_grad.astype(BF)
+    )
+
+    def halves(grad, axis):
+        size = grad.shape[axis] // 2
+        return (
+            rows_of(lax.slice_in_dim(grad, 0, size, axis=axis)),
+            rows_of(lax.slice_in_dim(grad, size, 2 * size, axis=axis)),
+        )
+
+    def reduced(grads, axes, shapes):
+        parts = [halves(grad, axis) for grad, axis in zip(grads, axes)]
+        total = at.reduce_bucket(
+            jnp.concatenate([p[0] for p in parts]), jnp.concatenate([p[1] for p in parts])
+        )
+        outs, begin = [], 0
+        for part, shape in zip(parts, shapes):
+            count = part[0].shape[0]
+            outs.append(rows_back(total[begin : begin + count], shape))
+            begin += count
+        return outs
+
+    half_of = lambda shape, axis: tuple(s // 2 if i == axis else s for i, s in enumerate(shape))
+
+    def bucket(grads, axes):
+        return reduced(grads, axes, [half_of(g.shape, a) for g, a in zip(grads, axes)])
+
+    dec_up_grad, dec_down_grad = bucket((dec_up_grad, dec_down_grad), (1, 0))
+    mixed_grad = sum_grad + ffn_input_grad
+    _, norm_back = jax.vjp(normalize, dec_sum_two, dec_gains[1], dec_shifts[1])
+    sum_grad, dec_gain_two, dec_shift_two = norm_back(mixed_grad)
+    query_grad, key_grad, value_grad, cross_proj_grad = attend_back(
+        cross_kept, sum_grad.astype(BF), cross_proj, False
+    )
+    cross_query_grad = weight_dots(dec_middle_low, query_grad)
+    cross_kv_grad = jnp.stack(
+        [weight_dots(enc_states, key_grad), weight_dots(enc_states, value_grad)]
+    )
+    cross_query_grad, cross_kv_grad, cross_proj_grad = bucket(
+        (cross_query_grad, cross_kv_grad, cross_proj_grad), (1, 2, 0)
+    )
+    middle_grad = sum_grad + dots_t(query_grad, cross_query)
+    enc_extra = dots_t(key_grad, cross_kv[0]) + dots_t(value_grad, cross_kv[1])
+    _, norm_back = jax.vjp(normalize, dec_sum_one, dec_gains[0], dec_shifts[0])
+    self_sum_grad, dec_gain_one, dec_shift_one = norm_back(middle_grad)
+
+    enc_final_grad = enc_cot + enc_extra
+    _, halt_back = jax.vjp(partial(halting, runs_enc), enc_start, enc_last, halt_weight[0])
+    enc_start_grad, last_grad, enc_halt_grad = halt_back(enc_final_grad)
+    _, norm_back = jax.vjp(normalize, enc_sum_two, enc_gains[1], enc_shifts[1])
+    sum_grad, enc_gain_two, enc_shift_two = norm_back(last_grad)
+    ffn_input_grad, enc_up_grad, enc_down_grad = feed_back(
+        enc_middle_low, enc_hidden, enc_up, enc_down, sum_grad.astype(BF)
+    )
+    enc_up_grad, enc_down_grad = bucket((enc_up_grad, enc_down_grad), (1, 0))
+    middle_grad = sum_grad + ffn_input_grad
+    _, norm_back = jax.vjp(normalize, enc_sum_one, enc_gains[0], enc_shifts[0])
+    enc_sum_grad, enc_gain_one, enc_shift_one = norm_back(middle_grad)
+    small = at.reduce_all(
+        jnp.stack(
+            [
+                enc_gain_one, enc_gain_two, enc_shift_one, enc_shift_two,
+                dec_gain_one, dec_gain_two, dec_gain_three,
+                dec_shift_one, dec_shift_two, dec_shift_three,
+                enc_halt_grad, dec_halt_grad,
+            ]
+        )
+    )
+
+    query_grad, key_grad, value_grad, enc_proj_grad = attend_back(
+        enc_kept, enc_sum_grad.astype(BF), enc_proj, False
+    )
+    enc_qkv_grad = jnp.stack(
+        [weight_dots(enc_start_low, g) for g in (query_grad, key_grad, value_grad)]
+    )
+    enc_qkv_grad, enc_proj_grad = bucket((enc_qkv_grad, enc_proj_grad), (2, 0))
+    source_grad = (
+        enc_sum_grad
+        + enc_start_grad
+        + dots_t(query_grad, enc_qkv[0])
+        + dots_t(key_grad, enc_qkv[1])
+        + dots_t(value_grad, enc_qkv[2])
+    )
+    source_low = source_grad.astype(BF)
+    source_moved = at.from_row(source_low[:quarter], source_low[quarter:])
+
+    query_grad, key_grad, value_grad, dec_proj_grad = attend_back(
+        self_kept, self_sum_grad.astype(BF), dec_proj, True
+    )
+    dec_qkv_grad = jnp.stack(
+        [weight_dots(dec_start_low, g) for g in (query_grad, key_grad, value_grad)]
+    )
+    dec_qkv_grad, dec_proj_grad = bucket((dec_qkv_grad, dec_proj_grad), (2, 0))
+    target_grad = (
+        self_sum_grad
+        + dec_start_grad
+        + dots_t(query_grad, dec_qkv[0])
+        + dots_t(key_grad, dec_qkv[1])
+        + dots_t(value_grad, dec_qkv[2])
+    )
+    target_low = target_grad.astype(BF)
+    target_moved = at.from_row(target_low[:quarter], target_low[quarter:])
+
+    def back_home(values, moved):
+        moved = [m.astype(values.dtype) for m in moved]
+        return at.native(values[:quarter], values[quarter:], *moved)[:, None]
+
+    return (
+        back_home(enc_states, enc_states_moved),
+        back_home(dec_states, dec_states_moved),
+        back_home(source_grad, source_moved),
+        back_home(target_grad, target_moved),
+        enc_qkv_grad,
+        enc_proj_grad,
+        enc_up_grad,
+        enc_down_grad,
+        small[0:2],
+        small[2:4],
+        dec_qkv_grad,
+        dec_proj_grad,
+        cross_query_grad,
+        cross_kv_grad,
+        cross_proj_grad,
+        dec_up_grad,
+        dec_down_grad,
+        small[4:7],
+        small[7:10],
+        small[10:12],
+    )
+
+
 def solution(mesh):
+    dp_size, mp_size = mesh.shape["dp"], mesh.shape["mp"]
+    by_chip = mp_size == 2 and dp_size >= 4 and dp_size & (dp_size - 1) == 0
+    body = partial(chip_rows, dp_size=dp_size) if by_chip else local
     return jax.shard_map(
-        local,
+        body,
         mesh=mesh,
         in_specs=(
             P("mp", "dp", None),

time: 1570 us -> 953 us (0.61)
  waiting for transfers between devices: 634 us -> 161 us
  matrix products: 447 us -> 133 us
  Pallas kernels: 0 us -> 228 us
  starting transfers between devices: 3.33 us -> 149 us
  local copies, waits for them, and re-layouts: 228 us -> 142 us
  other arithmetic: 180 us -> 124 us
  blocking collectives: 42 us -> 0 us
    dot_general x384 -> x48, matrix products: 447 us -> 133 us  [the longest x16 54.5 us: dots_t(): lax.dot_general(left, right, (((1,), (1,)), ((), ())), preferred_element_...]
    all_gather x11 -> x0, waiting for transfers between devices: 271 us -> none  [the longest x6 178 us: collect(): return lax.all_gather(piece_rows, 'mp', axis=0, tiled=True)]
    reduce_scatter x11 -> x0, waiting for transfers between devices: 257 us -> none  [the longest x6 136 us: project_back(): lax.psum_scatter(partial_term(jnp.int32(0), lax.axis_size('mp') * rows).a...]
    pallas_call x0 -> x6, Pallas kernels: none -> 228 us  [the longest x3 147 us: attn_bwd(): pl.pallas_call(kern, grid=(np_, 2 * nb), in_specs=[pl.BlockSpec(memory_sp...]
    ppermute x0 -> x109, waiting for transfers between devices: none -> 161 us  [the longest x17 79.9 us: y_swap(): return lax.ppermute(values, 'mp', [(0, 1), (1, 0)])]
    ppermute x0 -> x109, starting transfers between devices: none -> 149 us  [the longest x68 76.7 us: flip(): lax.ppermute(values, 'dp', [(d, d ^ mask) for d in range(self.dp_size)])]
    psum x1 -> x0, waiting for transfers between devices: 105 us -> none  [local(): lax.psum(enc_qkv_grad.astype(jnp.bfloat16), 'dp').astype(jnp.float32)]
    dynamic_slice x252 -> x14, local copies, waits for them, and re-layouts: 78.2 us -> 15.3 us  [the longest x11 15.1 us: other_half(): piece = lax.dynamic_slice_in_dim(weight, self.c * size, size, axis)]
  transfers between devices with their start and end apart: 23 -> 109, of which waited for: 19 -> 29; matrix products, arithmetic and copies ran while one was open for 29% -> 37% of each run, Pallas kernels for 0% -> 21%
where the time goes in v1:
time: 953 us; the launch traced here: 942 us
  Pallas kernels  228 us (24%)
  waiting for transfers between devices  161 us (17%)
  starting transfers between devices  149 us (16%)
  local copies, waits for them, and re-layouts  142 us (15%)
  matrix products  133 us (14%)
  other arithmetic  124 us (13%)
    pallas_call x3, Pallas kernels, attn_bwd(): pl.pallas_call(kern, grid=(np_, 2 * nb), in_specs=[pl.BlockSpec(memory_sp...  147 us
    pallas_call x3, Pallas kernels, attn_fwd(): pl.pallas_call(kern, grid=(np_, n // bq), in_specs=[pl.BlockSpec(memory_s...  81.6 us
    ppermute x17, waiting for transfers between devices, y_swap(): return lax.ppermute(values, 'mp', [(0, 1), (1, 0)])  79.9 us
    ppermute x68, starting transfers between devices, flip(): lax.ppermute(values, 'dp', [(d, d ^ mask) for d in range(self.dp_size)])  76.7 us
    ppermute x68, waiting for transfers between devices, flip(): lax.ppermute(values, 'dp', [(d, d ^ mask) for d in range(self.dp_size)])  74.7 us
    unnamed x431, local copies, waits for them, and re-layouts  64.5 us
    dot_general x16, matrix products, dots_t(): lax.dot_general(left, right, (((1,), (1,)), ((), ())), preferred_element_...  54.5 us
    ppermute x24, starting transfers between devices, move(): return lax.ppermute(values, ('dp', 'mp'), perm)  53.6 us
  transfers between devices with their start and end apart: 109, of which 29 were waited for; matrix products, arithmetic and copies ran while one was open for 37% of the time, Pallas kernels for 21%

profile of v1, /device:TPU:0, one launch (start us, length us, event | category | flops | bytes accessed | tf_op | source)
XLA Modules:
  0.0 942.1 jit_solution(8522805380409519008)
XLA Ops:
  3.7 6.5 collective-permute-start.3
  100.2 20.8 %collective-permute-done.31 = bf16[2,256,256]{2,1,0:T(8,128)(2,1)S(1)} collective-permute-done((bf16[2,256,256]{2,1,0:T(8,128)(2,1)S(1)}, bf16[2,256,256]{2,1,0:T(8,128)(2,1)S(1)}, u32[]{:S(2)}, u32[]{:S(2)}) %collective-permute-start.31) | collective-permute-done | bytes 262176 | tf_op jit(solution)/shard_map/ppermute | solution.py:734
  126.1 7.1 collective-permute-done.23
  136.2 8.2 collective-permute-done.39
  144.4 11.2 %collective-permute-done.15 = bf16[512,512]{1,0:T(8,128)(2,1)S(1)} collective-permute-done((bf16[512,512]{1,0:T(8,128)(2,1)S(1)}, bf16[512,512]{1,0:T(8,128)(2,1)S(1)}, u32[]{:S(2)}, u32[]{:S(2)}) %collective-permute-start.15) | collective-permute-done | bytes 524320 | tf_op jit(solution)/shard_map/ppermute | solution.py:734
  157.2 9.6 %collective-permute-done.13 = bf16[256,1024]{0,1:T(8,128)(2,1)S(1)} collective-permute-done((bf16[256,1024]{0,1:T(8,128)(2,1)S(1)}, bf16[256,1024]{0,1:T(8,128)(2,1)S(1)}, u32[]{:S(2)}, u32[]{:S(2)}) %collective-permute-start.13) | collective-permute-done | bytes 524320 | tf_op jit(solution)/shard_map/ppermute | solution.py:734
  168.2 7.2 collective-permute-done.37
  195.4 29.3 %attn_fwd.2 = (bf16[1024,512]{1,0:T(8,128)(2,1)}, f32[1024,512]{1,0:T(8,128)}) custom-call(s32[1]{0:T(128)} %bitcast.4.c_ref, bf16[1024,512]{1,0:T(8,128)(2,1)} %multiply_convert_fusion.4.q_ref, bf16[1024,512]{1,0:T(8,128)(2,1)} %copy-done.195, bf16[1024,512]{1,0:T(8,128)(2,1)} %copy-done.196, bf16[1024,512]{1,0:T(8,128)(2,1)} %copy-done.194, ...), custom_call_target="tpu_custom_call" | custom-call | flops 4294967296 | bytes 8388608 | tf_op jit(solution)/shard_map/attn_fwd/pallas_call | solution.py:589
  241.6 12.7 %collective-permute-start.25 = (bf16[1024,512]{1,0:T(8,128)(2,1)S(1)}, bf16[1024,512]{1,0:T(8,128)(2,1)S(1)}, u32[]{:S(2)}, u32[]{:S(2)}) collective-permute-start(bf16[1024,512]{1,0:T(8,128)(2,1)S(1)} %convolution_convert_fusion.6.ko_ref), channel_id=1, source_target_pairs={{0,2},{2,0},{4,6},{6,4},{8,10},{10,8},{12,14},{14,12},{16,18},{18,... | collective-permute-start | bytes 3145736 | tf_op jit(solution)/shard_map/ppermute | solution.py:728
  263.8 6.0 collective-permute-start.19
  269.8 22.9 %attn_fwd_causal.1 = (bf16[1024,512]{1,0:T(8,128)(2,1)}, f32[1024,512]{1,0:T(8,128)}) custom-call(s32[1]{0:T(128)} %bitcast.4.c_ref, bf16[1024,512]{1,0:T(8,128)(2,1)} %multiply_convert_fusion.3.q_ref, bf16[1024,512]{1,0:T(8,128)(2,1)} %copy-done.199, bf16[1024,512]{1,0:T(8,128)(2,1)} %copy-done.200, bf16[1024,512]{1,0:T(8,128)(2,1)} %copy-done.198, ...), custom_call_target="tpu_custom_call" | custom-call | flops 4294967296 | bytes 8388608 | tf_op jit(solution)/shard_map/attn_fwd_causal/pallas_call | solution.py:589
  298.9 29.4 %attn_fwd.3 = (bf16[1024,512]{1,0:T(8,128)(2,1)}, f32[1024,512]{1,0:T(8,128)}) custom-call(s32[1]{0:T(128)} %bitcast.4.c_ref, bf16[1024,512]{1,0:T(8,128)(2,1)} %multiply_convert_fusion.2.q_ref, bf16[1024,512]{1,0:T(8,128)(2,1)} %convolution_convert_fusion.4.ko_ref, bf16[1024,512]{1,0:T(8,128)(2,1)} %collective-permute-done.33.kx_ref, ...), custom_call_target="tpu_custom_call" | custom-call | flops 4294967296 | bytes 8388608 | tf_op jit(solution)/shard_map/attn_fwd/pallas_call | solution.py:589
  347.8 9.5 %fusion.13 = bf16[1024,2048]{1,0:T(8,128)(2,1)S(1)} fusion(f32[1024,2048]{1,0:T(8,128)S(1)} %fusion.22, bf16[1024,512]{1,0:T(8,128)(2,1)S(1)} %copy-done.114, bf16[1024,512]{1,0:T(8,128)(2,1)S(1)} %copy-done.153, f32[1024,512]{0,1:T(8,128)S(1)} %get-tuple-element.130, f32[1024]{0:T(1024)S(1)} %negate_multiply_fusion.4), kind=kOutput, calls=%fused_computation.17 | convolution fusion | flops 2194669568 | bytes 16781312 | tf_op jit(solution)/shard_map/dot_general | solution.py:840
  357.3 5.1 fusion.82
  370.1 53.0 %attn_bwd.2 = (bf16[1024,512]{1,0:T(8,128)(2,1)}, bf16[1024,512]{1,0:T(8,128)(2,1)}, bf16[1024,512]{1,0:T(8,128)(2,1)}, bf16[1024,512]{1,0:T(8,128)(2,1)}, bf16[1024,512]{1,0:T(8,128)(2,1)}) custom-call(s32[1]{0:T(128)} %bitcast.4.c_ref, bf16[1024,512]{1,0:T(8,128)(2,1)} %multiply_convert_fusion.2.q_ref, bf16[1024,512]{1,0:T(8,128)(2,1)} %convolution_convert_fusion.4.ko_ref, ...), custom_call_target="tpu_custom_call" | custom-call | flops 10737418240 | bytes 12582912 | tf_op jit(solution)/shard_map/attn_bwd/pallas_call | solution.py:697
  465.0 40.4 %attn_bwd_causal.1 = (bf16[1024,512]{1,0:T(8,128)(2,1)}, bf16[1024,512]{1,0:T(8,128)(2,1)}, bf16[1024,512]{1,0:T(8,128)(2,1)}, bf16[1024,512]{1,0:T(8,128)(2,1)}, bf16[1024,512]{1,0:T(8,128)(2,1)}) custom-call(s32[1]{0:T(128)} %bitcast.4.c_ref, bf16[1024,512]{1,0:T(8,128)(2,1)} %multiply_convert_fusion.3.q_ref, bf16[1024,512]{1,0:T(8,128)(2,1)} %copy-done.199, ...), custom_call_target="tpu_custom_call" | custom-call | flops 10737418240 | bytes 12582912 | tf_op jit(solution)/shard_map/attn_bwd_causal/pallas_call | solution.py:697
  518.8 5.1 collective-permute-start.43
  543.9 11.4 %fusion.6 = bf16[1024,2048]{1,0:T(8,128)(2,1)S(1)} fusion(f32[1024,2048]{1,0:T(8,128)} %copy-done.204, bf16[1024,512]{1,0:T(8,128)(2,1)S(1)} %copy-done.113, bf16[1024,512]{1,0:T(8,128)(2,1)S(1)} %copy-done.155, f32[1024,512]{0,1:T(8,128)S(1)} %get-tuple-element.126, f32[1024]{0:T(1024)S(1)} %negate_multiply_fusion.2), kind=kOutput, calls=%fused_computation.10 | convolution fusion | flops 2194669568 | bytes 16781312 | tf_op jit(solution)/shard_map/dot_general | solution.py:840
  570.3 5.4 fusion.84
  594.4 7.1 collective-permute-start.58
  626.0 53.3 %attn_bwd.3 = (bf16[1024,512]{1,0:T(8,128)(2,1)}, bf16[1024,512]{1,0:T(8,128)(2,1)}, bf16[1024,512]{1,0:T(8,128)(2,1)}, bf16[1024,512]{1,0:T(8,128)(2,1)}, bf16[1024,512]{1,0:T(8,128)(2,1)}) custom-call(s32[1]{0:T(128)} %bitcast.4.c_ref, bf16[1024,512]{1,0:T(8,128)(2,1)} %multiply_convert_fusion.4.q_ref, bf16[1024,512]{1,0:T(8,128)(2,1)} %copy-done.195, ...), custom_call_target="tpu_custom_call" | custom-call | flops 10737418240 | bytes 12582912 | tf_op jit(solution)/shard_map/attn_bwd/pallas_call | solution.py:697
  719.4 6.2 copy.102
  769.7 7.6 collective-permute-done.92
  790.8 6.3 copy.101
  831.8 5.2 collective-permute-done.89
  855.6 5.8 collective-permute-done.104
  869.6 10.3 %collective-permute-done.70 = bf16[512,512]{1,0:T(8,128)(2,1)S(1)} collective-permute-done((bf16[512,512]{1,0:T(8,128)(2,1)S(1)}, bf16[512,512]{1,0:T(8,128)(2,1)S(1)}, u32[]{:S(2)}, u32[]{:S(2)}) %collective-permute-start.70) | collective-permute-done | bytes 524320 | tf_op jit(solution)/shard_map/ppermute | solution.py:728
  884.1 6.3 collective-permute-done.64
  894.1 6.0 collective-permute-done.65
  902.9 6.9 collective-permute-done.73
  910.3 6.2 collective-permute-done.107
  923.1 8.5 collective-permute-done.75
  (927 shorter events, 501.2 us)
Async XLA Ops:
  2.4 81.3 %collective-permute-start.5 = (f32[512,128]{0,1:T(8,128)}, f32[512,128]{0,1:T(8,128)}, u32[]{:S(2)}, u32[]{:S(2)}) collective-permute-start(f32[512,128]{0,1:T(8,128)} %get-tuple-element.235), channel_id=1, source_target_pairs={{1,0},{2,3},{5,4},{6,7},{9,8},{10,11},{13,12},{14,15},{17,16},{18,... | collective-permute-start | bytes 786440 | tf_op jit(solution)/shard_map/ppermute | solution.py:741
  3.7 81.5 %collective-permute-start.3 = (f32[512,128]{0,1:T(8,128)}, f32[512,128]{0,1:T(8,128)}, u32[]{:S(2)}, u32[]{:S(2)}) collective-permute-start(f32[512,128]{0,1:T(8,128)} %get-tuple-element.235), channel_id=1, source_target_pairs={{0,2},{3,1},{4,6},{7,5},{8,10},{11,9},{12,14},{15,13},{16,18},{19,... | collective-permute-start | bytes 786440 | tf_op jit(solution)/shard_map/ppermute | solution.py:741
  11.5 53.2 %collective-permute-start.10 = (s32[2,2048]{1,0:T(2,128)}, s32[2,2048]{1,0:T(2,128)}, u32[]{:S(2)}, u32[]{:S(2)}) collective-permute-start(s32[2,2048]{1,0:T(2,128)} %pad_add_fusion), channel_id=1, source_target_pairs={{0,2},{2,0},{4,6},{6,4},{8,10},{10,8},{12,14},{14,12},{16,18},{18,... | collective-permute-start | bytes 49160 | tf_op jit(solution)/shard_map/ppermute | solution.py:728
  13.0 57.7 %collective-permute-start.29 = (bf16[256,256]{1,0:T(8,128)(2,1)}, bf16[256,256]{1,0:T(8,128)(2,1)S(1)}, u32[]{:S(2)}, u32[]{:S(2)}) collective-permute-start(bf16[256,256]{1,0:T(8,128)(2,1)} %constant_dynamic-slice_fusion.12), channel_id=1, source_target_pairs={{0,1},{1,0},{2,3},{3,2},{4,5},{5,4},{6,7},{7,6},{8,9},{9,8},{10,11... | collective-permute-start | bytes 393224 | tf_op jit(solution)/shard_map/ppermute | solution.py:734
  14.9 57.4 %collective-permute-start.35 = (bf16[128,512]{1,0:T(8,128)(2,1)}, bf16[128,512]{1,0:T(8,128)(2,1)}, u32[]{:S(2)}, u32[]{:S(2)}) collective-permute-start(bf16[128,512]{1,0:T(8,128)(2,1)} %constant_dynamic-slice_fusion.10), channel_id=1, source_target_pairs={{0,1},{1,0},{2,3},{3,2},{4,5},{5,4},{6,7},{7,6},{8,9},{9,8},{10,11... | collective-permute-start | bytes 393224 | tf_op jit(solution)/shard_map/ppermute | solution.py:734
  90.3 32.8 %collective-permute-start.22 = (bf16[512,512]{0,1:T(8,128)(2,1)S(1)}, bf16[512,512]{0,1:T(8,128)(2,1)S(1)}, u32[]{:S(2)}, u32[]{:S(2)}) collective-permute-start(bf16[512,512]{0,1:T(8,128)(2,1)S(1)} %bitcast.180), channel_id=1, source_target_pairs={{1,0},{2,3},{5,4},{6,7},{9,8},{10,11},{13,12},{14,15},{17,16},{18,... | collective-permute-start | bytes 1572872 | tf_op jit(solution)/shard_map/ppermute | solution.py:741
  91.6 31.6 %collective-permute-start.20 = (bf16[512,512]{0,1:T(8,128)(2,1)S(1)}, bf16[512,512]{0,1:T(8,128)(2,1)S(1)}, u32[]{:S(2)}, u32[]{:S(2)}) collective-permute-start(bf16[512,512]{0,1:T(8,128)(2,1)S(1)} %bitcast.181), channel_id=1, source_target_pairs={{0,2},{3,1},{4,6},{7,5},{8,10},{11,9},{12,14},{15,13},{16,18},{19,... | collective-permute-start | bytes 1572872 | tf_op jit(solution)/shard_map/ppermute | solution.py:741
  95.3 27.9 %collective-permute-start.21 = (bf16[512,512]{0,1:T(8,128)(2,1)}, bf16[512,512]{0,1:T(8,128)(2,1)S(1)}, u32[]{:S(2)}, u32[]{:S(2)}) collective-permute-start(bf16[512,512]{0,1:T(8,128)(2,1)} %bitcast.17), channel_id=1, source_target_pairs={{1,2},{2,1},{5,6},{6,5},{9,10},{10,9},{13,14},{14,13},{17,18},{18,... | collective-permute-start | bytes 1572872 | tf_op jit(solution)/shard_map/ppermute | solution.py:741
  123.1 32.5 %collective-permute-start.15 = (bf16[512,512]{1,0:T(8,128)(2,1)S(1)}, bf16[512,512]{1,0:T(8,128)(2,1)S(1)}, u32[]{:S(2)}, u32[]{:S(2)}) collective-permute-start(bf16[512,512]{1,0:T(8,128)(2,1)S(1)} %copy-done.141), channel_id=1, source_target_pairs={{0,1},{1,0},{2,3},{3,2},{4,5},{5,4},{6,7},{7,6},{8,9},{9,8},{10,11... | collective-permute-start | bytes 1572872 | tf_op jit(solution)/shard_map/ppermute | solution.py:734
  123.2 32.4 %collective-permute-start.7 = (bf16[3,256,256]{2,1,0:T(8,128)(2,1)S(1)}, bf16[3,256,256]{2,1,0:T(8,128)(2,1)S(1)}, u32[]{:S(2)}, u32[]{:S(2)}) collective-permute-start(bf16[3,256,256]{2,1,0:T(8,128)(2,1)S(1)} %collective-permute-done.6), channel_id=1, source_target_pairs={{0,2},{2,0},{4,6},{6,4},{8,10},{10,8},{12,14},{14,12},{16,18},{18,... | collective-permute-start | bytes 1179656 | tf_op jit(solution)/shard_map/ppermute | solution.py:728
  133.1 33.7 %collective-permute-start.13 = (bf16[256,1024]{0,1:T(8,128)(2,1)S(1)}, bf16[256,1024]{0,1:T(8,128)(2,1)S(1)}, u32[]{:S(2)}, u32[]{:S(2)}) collective-permute-start(bf16[256,1024]{0,1:T(8,128)(2,1)S(1)} %copy-done.140), channel_id=1, source_target_pairs={{0,1},{1,0},{2,3},{3,2},{4,5},{5,4},{6,7},{7,6},{8,9},{9,8},{10,11... | collective-permute-start | bytes 1572872 | tf_op jit(solution)/shard_map/ppermute | solution.py:734
  133.1 42.3 %collective-permute-start.37 = (bf16[256,1024]{0,1:T(8,128)(2,1)S(1)}, bf16[256,1024]{0,1:T(8,128)(2,1)S(1)}, u32[]{:S(2)}, u32[]{:S(2)}) collective-permute-start(bf16[256,1024]{0,1:T(8,128)(2,1)S(1)} %copy-done.139), channel_id=1, source_target_pairs={{0,1},{1,0},{2,3},{3,2},{4,5},{5,4},{6,7},{7,6},{8,9},{9,8},{10,11... | collective-permute-start | bytes 1572872 | tf_op jit(solution)/shard_map/ppermute | solution.py:734
  144.3 32.3 %collective-permute-start.24 = (bf16[3,256,256]{2,1,0:T(8,128)(2,1)S(1)}, bf16[3,256,256]{2,1,0:T(8,128)(2,1)S(1)}, u32[]{:S(2)}, u32[]{:S(2)}) collective-permute-start(bf16[3,256,256]{2,1,0:T(8,128)(2,1)S(1)} %collective-permute-done.23), channel_id=1, source_target_pairs={{0,2},{2,0},{4,6},{6,4},{8,10},{10,8},{12,14},{14,12},{16,18},{18,... | collective-permute-start | bytes 1179656 | tf_op jit(solution)/shard_map/ppermute | solution.py:728
  256.2 42.7 %collective-permute-start.33 = (bf16[1024,512]{1,0:T(8,128)(2,1)}, bf16[1024,512]{1,0:T(8,128)(2,1)}, u32[]{:S(2)}, u32[]{:S(2)}) collective-permute-start(bf16[1024,512]{1,0:T(8,128)(2,1)} %convolution_convert_fusion.4.ko_ref), channel_id=1, source_target_pairs={{0,2},{2,0},{4,6},{6,4},{8,10},{10,8},{12,14},{14,12},{16,18},{18,... | collective-permute-start | bytes 3145736 | tf_op jit(solution)/shard_map/ppermute | solution.py:728
  258.4 40.6 %collective-permute-start.34 = (bf16[1024,512]{1,0:T(8,128)(2,1)}, bf16[1024,512]{1,0:T(8,128)(2,1)}, u32[]{:S(2)}, u32[]{:S(2)}) collective-permute-start(bf16[1024,512]{1,0:T(8,128)(2,1)} %convolution_convert_fusion.3.vo_ref), channel_id=1, source_target_pairs={{0,2},{2,0},{4,6},{6,4},{8,10},{10,8},{12,14},{14,12},{16,18},{18,... | collective-permute-start | bytes 3145736 | tf_op jit(solution)/shard_map/ppermute | solution.py:728
  261.4 177.4 %collective-permute-start.18 = (bf16[512,512]{0,1:T(8,128)(2,1)}, bf16[512,512]{0,1:T(8,128)(2,1)}, u32[]{:S(2)}, u32[]{:S(2)}) collective-permute-start(bf16[512,512]{0,1:T(8,128)(2,1)} %get-tuple-element.203), channel_id=1, source_target_pairs={{2,0},{1,3},{6,4},{5,7},{10,8},{9,11},{14,12},{13,15},{18,16},{17,... | collective-permute-start | bytes 1572872 | tf_op jit(solution)/shard_map/ppermute | solution.py:741
  263.8 175.1 %collective-permute-start.19 = (bf16[512,512]{0,1:T(8,128)(2,1)}, bf16[512,512]{0,1:T(8,128)(2,1)}, u32[]{:S(2)}, u32[]{:S(2)}) collective-permute-start(bf16[512,512]{0,1:T(8,128)(2,1)} %get-tuple-element.204), channel_id=1, source_target_pairs={{0,1},{3,2},{4,5},{7,6},{8,9},{11,10},{12,13},{15,14},{16,17},{19,... | collective-permute-start | bytes 1572872 | tf_op jit(solution)/shard_map/ppermute | solution.py:741
  445.5 69.6 %collective-permute-start.41 = (bf16[512,512]{0,1:T(8,128)(2,1)}, bf16[512,512]{0,1:T(8,128)(2,1)}, u32[]{:S(2)}, u32[]{:S(2)}) collective-permute-start(bf16[512,512]{0,1:T(8,128)(2,1)} %broadcast_select_fusion.2), channel_id=1, source_target_pairs={{2,1},{1,2},{6,5},{5,6},{10,9},{9,10},{14,13},{13,14},{18,17},{17,... | collective-permute-start | bytes 1572872 | tf_op jit(solution)/shard_map/ppermute | solution.py:741
  505.4 61.0 %collective-permute-start.54 = (bf16[1024,512]{1,0:T(8,128)(2,1)}, bf16[1024,512]{1,0:T(8,128)(2,1)}, u32[]{:S(2)}, u32[]{:S(2)}) collective-permute-start(bf16[1024,512]{1,0:T(8,128)(2,1)} %get-tuple-element.59), channel_id=1, source_target_pairs={{0,2},{2,0},{4,6},{6,4},{8,10},{10,8},{12,14},{14,12},{16,18},{18,... | collective-permute-start | bytes 3145736 | tf_op jit(solution)/shard_map/ppermute | solution.py:728
  508.6 28.3 %collective-permute-start.47 = (bf16[1024,512]{1,0:T(8,128)(2,1)}, bf16[1024,512]{1,0:T(8,128)(2,1)}, u32[]{:S(2)}, u32[]{:S(2)}) collective-permute-start(bf16[1024,512]{1,0:T(8,128)(2,1)} %get-tuple-element.46), channel_id=1, source_target_pairs={{0,2},{2,0},{4,6},{6,4},{8,10},{10,8},{12,14},{14,12},{16,18},{18,... | collective-permute-start | bytes 3145736 | tf_op jit(solution)/shard_map/ppermute | solution.py:728
  525.8 49.9 %collective-permute-start.55 = (bf16[1024,512]{1,0:T(8,128)(2,1)}, bf16[1024,512]{1,0:T(8,128)(2,1)}, u32[]{:S(2)}, u32[]{:S(2)}) collective-permute-start(bf16[1024,512]{1,0:T(8,128)(2,1)} %get-tuple-element.61), channel_id=1, source_target_pairs={{0,2},{2,0},{4,6},{6,4},{8,10},{10,8},{12,14},{14,12},{16,18},{18,... | collective-permute-start | bytes 3145736 | tf_op jit(solution)/shard_map/ppermute | solution.py:728
  530.6 194.9 %collective-permute-start.100 = (bf16[2048,512]{1,0:T(8,128)(2,1)}, bf16[2048,512]{1,0:T(8,128)(2,1)}, u32[]{:S(2)}, u32[]{:S(2)}) collective-permute-start(bf16[2048,512]{1,0:T(8,128)(2,1)} %pad_maximum_fusion.14), channel_id=1, source_target_pairs={{0,2},{2,0},{4,6},{6,4},{8,10},{10,8},{12,14},{14,12},{16,18},{18,... | collective-permute-start | bytes 6291464 | tf_op jit(solution)/shard_map/ppermute | solution.py:728
  591.7 122.4 %collective-permute-start.56 = (bf16[512,512]{0,1:T(8,128)(2,1)}, bf16[512,512]{0,1:T(8,128)(2,1)}, u32[]{:S(2)}, u32[]{:S(2)}) collective-permute-start(bf16[512,512]{0,1:T(8,128)(2,1)} %get-tuple-element.191), channel_id=1, source_target_pairs={{2,1},{1,2},{6,5},{5,6},{10,9},{9,10},{14,13},{13,14},{18,17},{17,... | collective-permute-start | bytes 1572872 | tf_op jit(solution)/shard_map/ppermute | solution.py:741
  593.1 122.8 %collective-permute-start.57 = (bf16[512,512]{0,1:T(8,128)(2,1)}, bf16[512,512]{0,1:T(8,128)(2,1)}, u32[]{:S(2)}, u32[]{:S(2)}) collective-permute-start(bf16[512,512]{0,1:T(8,128)(2,1)} %get-tuple-element.192), channel_id=1, source_target_pairs={{2,0},{1,3},{6,4},{5,7},{10,8},{9,11},{14,12},{13,15},{18,16},{17,... | collective-permute-start | bytes 1572872 | tf_op jit(solution)/shard_map/ppermute | solution.py:741
  594.4 121.6 %collective-permute-start.58 = (bf16[512,512]{0,1:T(8,128)(2,1)}, bf16[512,512]{0,1:T(8,128)(2,1)}, u32[]{:S(2)}, u32[]{:S(2)}) collective-permute-start(bf16[512,512]{0,1:T(8,128)(2,1)} %get-tuple-element.193), channel_id=1, source_target_pairs={{0,1},{3,2},{4,5},{7,6},{8,9},{11,10},{12,13},{15,14},{16,17},{19,... | collective-permute-start | bytes 1572872 | tf_op jit(solution)/shard_map/ppermute | solution.py:741
  625.9 70.2 %collective-permute-start.77 = (f32[12,512]{1,0:T(8,128)S(1)}, f32[12,512]{1,0:T(8,128)S(1)}, u32[]{:S(2)}, u32[]{:S(2)}) collective-permute-start(f32[12,512]{1,0:T(8,128)S(1)} %stack.52), channel_id=1, source_target_pairs={{0,2},{2,0},{4,6},{6,4},{8,10},{10,8},{12,14},{14,12},{16,18},{18,... | collective-permute-start | bytes 73736 | tf_op jit(solution)/shard_map/ppermute | solution.py:728
  725.6 103.9 %collective-permute-start.68 = (bf16[2048,512]{1,0:T(8,128)(2,1)}, bf16[2048,512]{1,0:T(8,128)(2,1)}, u32[]{:S(2)}, u32[]{:S(2)}) collective-permute-start(bf16[2048,512]{1,0:T(8,128)(2,1)} %pad_maximum_fusion.10), channel_id=1, source_target_pairs={{0,2},{2,0},{4,6},{6,4},{8,10},{10,8},{12,14},{14,12},{16,18},{18,... | collective-permute-start | bytes 6291464 | tf_op jit(solution)/shard_map/ppermute | solution.py:728
  728.9 86.7 %collective-permute-start.101 = (bf16[1024,512]{1,0:T(8,128)(2,1)}, bf16[1024,512]{1,0:T(8,128)(2,1)}, u32[]{:S(2)}, u32[]{:S(2)}) collective-permute-start(bf16[1024,512]{1,0:T(8,128)(2,1)} %add_convert_fusion), channel_id=1, source_target_pairs={{0,1},{1,0},{2,3},{3,2},{4,5},{5,4},{6,7},{7,6},{8,9},{9,8},{10,11... | collective-permute-start | bytes 3145736 | tf_op jit(solution)/shard_map/ppermute | solution.py:734
  732.4 34.1 %collective-permute-start.83 = (bf16[512,512]{1,0:T(8,128)(2,1)}, bf16[512,512]{1,0:T(8,128)(2,1)}, u32[]{:S(2)}, u32[]{:S(2)}) collective-permute-start(bf16[512,512]{1,0:T(8,128)(2,1)} %fusion.37), channel_id=1, source_target_pairs={{0,1},{1,0},{2,3},{3,2},{4,5},{5,4},{6,7},{7,6},{8,9},{9,8},{10,11... | collective-permute-start | bytes 1572872 | tf_op jit(solution)/shard_map/ppermute | solution.py:734
  735.6 41.6 %collective-permute-start.92 = (bf16[512,512]{1,0:T(8,128)(2,1)}, bf16[512,512]{1,0:T(8,128)(2,1)}, u32[]{:S(2)}, u32[]{:S(2)}) collective-permute-start(bf16[512,512]{1,0:T(8,128)(2,1)} %add_convert_fusion.15), channel_id=1, source_target_pairs={{0,1},{1,0},{2,3},{3,2},{4,5},{5,4},{6,7},{7,6},{8,9},{9,8},{10,11... | collective-permute-start | bytes 1572872 | tf_op jit(solution)/shard_map/ppermute | solution.py:734
  783.4 39.5 %collective-permute-start.59 = (bf16[1024,512]{1,0:T(8,128)(2,1)}, bf16[1024,512]{1,0:T(8,128)(2,1)}, u32[]{:S(2)}, u32[]{:S(2)}) collective-permute-start(bf16[1024,512]{1,0:T(8,128)(2,1)} %pad_maximum_fusion.31), channel_id=1, source_target_pairs={{0,2},{2,0},{4,6},{6,4},{8,10},{10,8},{12,14},{14,12},{16,18},{18,... | collective-permute-start | bytes 3145736 | tf_op jit(solution)/shard_map/ppermute | solution.py:728
  831.0 35.3 %collective-permute-start.69 = (bf16[1024,512]{1,0:T(8,128)(2,1)S(1)}, bf16[1024,512]{1,0:T(8,128)(2,1)S(1)}, u32[]{:S(2)}, u32[]{:S(2)}) collective-permute-start(bf16[1024,512]{1,0:T(8,128)(2,1)S(1)} %add_convert_fusion.1), channel_id=1, source_target_pairs={{0,1},{1,0},{2,3},{3,2},{4,5},{5,4},{6,7},{7,6},{8,9},{9,8},{10,11... | collective-permute-start | bytes 3145736 | tf_op jit(solution)/shard_map/ppermute | solution.py:734
  (287 other events, 2994.0 us)

commit v2 on v0

--- a/solution.py
+++ b/solution.py
@@ -1,8 +1,11 @@
+import math
 from functools import partial
 
 import jax
 import jax.numpy as jnp
 from jax import lax
+from jax.experimental import pallas as pl
+from jax.experimental.pallas import tpu as pltpu
 from jax.sharding import PartitionSpec as P
 
 D = 512
@@ -507,9 +510,1016 @@
     )
 
 
+BIG = -1e30
+BF = jnp.bfloat16
+F32 = jnp.float32
+NN = (((1,), (0,)), ((), ()))
+NT = (((1,), (1,)), ((), ()))
+TN = (((0,), (0,)), ((), ()))
+HALF = D // 2
+VMEM_BYTES = 56 * 1024 * 1024
+NO_COST = pl.CostEstimate(flops=1, bytes_accessed=1, transcendentals=0)
+
+
+def dot_nn(a, b):
+    return lax.dot_general(a, b, NN, preferred_element_type=F32)
+
+
+def dot_nt(a, b):
+    return lax.dot_general(a, b, NT, preferred_element_type=F32)
+
+
+def dot_tn(a, b):
+    return lax.dot_general(a, b, TN, preferred_element_type=F32)
+
+
+def lanes():
+    lane = lax.broadcasted_iota(jnp.int32, (1, 128), 1)
+    return lane < DH, lane % DH
+
+
+def forward_kernel(
+    core_ref, q_ref, own_ref, got_ref, query_ext_ref, key_ext_ref, o_ref, log_ref, keys, values,
+    *, causal, rows,
+):
+    step = pl.program_id(1)
+    block = q_ref.shape[0]
+    quarter = own_ref.shape[1] // 2
+    core = core_ref[0]
+    left, _ = lanes()
+
+    @pl.when(step == 0)
+    def _():
+        n = own_ref.shape[1]
+        for ref, of in ((own_ref, core), (got_ref, 1 - core)):
+            here = pl.ds(pl.multiple_of(of * n, n), n)
+            k, v, ext = ref[0], ref[1], key_ext_ref[here, :]
+            ones = jnp.ones_like(v)
+            keys[0, here, :] = jnp.where(left, k, ext)
+            keys[1, here, :] = jnp.where(left, ext, k)
+            values[0, here, :] = jnp.where(left, v, ones)
+            values[1, here, :] = jnp.where(left, ones, v)
+
+    def attend(count, first_row):
+        for begin in range(0, block, rows):
+            here = slice(begin, begin + rows)
+            pair, ext = q_ref[here, :], query_ext_ref[here, :]
+            mixed, highest = [], []
+            for head in range(2):
+                q = jnp.where(left, pair, ext) if head == 0 else jnp.where(left, ext, pair)
+                clear = count - quarter if causal else count
+                parts = []
+                if clear:
+                    parts.append((dot_nt(q, keys[head, :clear, :]), values[head, :clear, :]))
+                if causal:
+                    scores = dot_nt(q, keys[head, clear:count, :])
+                    row = lax.broadcasted_iota(jnp.int32, scores.shape, 0) + (first_row + begin)
+                    column = lax.broadcasted_iota(jnp.int32, scores.shape, 1)
+                    scores = jnp.where(column <= row, scores, BIG)
+                    parts.append((scores, values[head, clear:count, :]))
+                top = jnp.max(parts[0][0], axis=1, keepdims=True)
+                for scores, _ in parts[1:]:
+                    top = jnp.maximum(top, jnp.max(scores, axis=1, keepdims=True))
+                total = 0.0
+                for scores, v in parts:
+                    total = total + dot_nn(jnp.exp2(scores - top).astype(BF), v)
+                mixed.append(total)
+                highest.append(top)
+            sums = jnp.where(left, mixed[1], mixed[0])
+            out = jnp.where(left, mixed[0], mixed[1]) / pltpu.roll(sums, DH, 1)
+            o_ref[here, :] = out.astype(BF)
+            log_ref[here, :] = jnp.where(left, highest[1], highest[0]) + jnp.log2(sums)
+
+    if not causal:
+        attend(2 * own_ref.shape[1], None)
+    else:
+        each = quarter // block
+        piece = step // each
+        place = 2 * core + piece
+        for case in range(4):
+
+            @pl.when(place == case)
+            def _(case=case):
+                attend((case + 1) * quarter, (step - piece * each) * block)
+
+
+def attention_forward_half(core, q, own, got, query_ext, key_ext, causal):
+    n, width = q.shape
+    length = 2 * n
+    block, rows = 512, 256
+    keys = pl.BlockSpec((2, n, 128), lambda p, b: (0, 0, p))
+    queries = pl.BlockSpec((block, 128), lambda p, b: (b, p))
+    return pl.pallas_call(
+        partial(forward_kernel, causal=causal, rows=rows),
+        grid=(width // 128, n // block),
+        in_specs=[
+            pl.BlockSpec(memory_space=pltpu.SMEM),
+            queries,
+            keys,
+            keys,
+            pl.BlockSpec((block, 128), lambda p, b: (b, 0)),
+            pl.BlockSpec((length, 128), lambda p, b: (0, 0)),
+        ],
+        out_specs=[queries, queries],
+        out_shape=[jax.ShapeDtypeStruct((n, width), BF), jax.ShapeDtypeStruct((n, width), F32)],
+        scratch_shapes=[pltpu.VMEM((2, length, 128), BF), pltpu.VMEM((2, length, 128), BF)],
+        compiler_params=pltpu.CompilerParams(vmem_limit_bytes=VMEM_BYTES),
+        cost_estimate=NO_COST,
+        name="attention_causal" if causal else "attention",
+    )(core, q, own, got, query_ext, key_ext)
+
+
+def backward_kernel(
+    core_ref, q_ref, own_ref, got_ref, query_ext_ref, own_ext_ref, got_ext_ref, grad_ref, o_ref, log_ref,
+    q_grad_ref, own_grad_ref, got_grad_ref, queries, grads, q_total, *, causal,
+):
+    step = pl.program_id(1)
+    n, block = q_ref.shape[0], own_ref.shape[1]
+    quarter = n // 2
+    blocks = n // block
+    core = core_ref[0]
+    left, lane = lanes()
+
+    @pl.when(step == 0)
+    def _():
+        log = log_ref[...]
+        high = log.astype(BF).astype(F32)
+        middle = (log - high).astype(BF).astype(F32)
+        low = log - high - middle
+        ext = query_ext_ref[...].astype(F32)
+        ext = jnp.where(lane == 10, -low, ext)
+        ext = jnp.where(lane == 9, -middle, jnp.where(lane == 8, -high, ext)).astype(BF)
+        pair = q_ref[...]
+        queries[0] = jnp.where(left, pair, ext)
+        queries[1] = jnp.where(left, ext, pair)
+        pair = grad_ref[...]
+        product = pair.astype(F32) * o_ref[...].astype(F32)
+        high = product.astype(BF)
+        low = (product - high.astype(F32)).astype(BF)
+        row = lax.broadcasted_iota(jnp.int32, (128, 128), 0)
+        column = lax.broadcasted_iota(jnp.int32, (128, 128), 1)
+        across = ((row < DH) != (column < DH)).astype(BF)
+        inner = dot_nn(high, across) + dot_nn(low, across)
+        high = inner.astype(BF).astype(F32)
+        ext = jnp.where(lane == 8, -high, jnp.where(lane == 9, high - inner, 0.0)).astype(BF)
+        grads[0] = jnp.where(left, pair, ext)
+        grads[1] = jnp.where(left, ext, pair)
+        q_total[...] = jnp.zeros_like(q_total)
+
+    own = step < blocks
+    k = jnp.where(own, own_ref[0], got_ref[0])
+    v = jnp.where(own, own_ref[1], got_ref[1])
+    ext = jnp.where(own, own_ext_ref[...], got_ext_ref[...])
+    ones = jnp.ones_like(v)
+    keys = (jnp.where(left, k, ext), jnp.where(left, ext, k))
+    values = (jnp.where(left, v, ones), jnp.where(left, ones, v))
+    k_turned = k.T
+
+    def part(begin, rows, diagonal):
+        k_grads, v_grads = [], []
+        here = slice(begin, begin + rows)
+        for head in range(2):
+            q, grad = queries[head, here, :], grads[head, here, :]
+            scores = dot_nt(keys[head], q)
+            if diagonal is not None:
+                key = lax.broadcasted_iota(jnp.int32, scores.shape, 0) + diagonal
+                query = lax.broadcasted_iota(jnp.int32, scores.shape, 1)
+                scores = jnp.where(key <= query, scores, BIG)
+            probs = jnp.exp2(scores)
+            score_grad = (probs * dot_nt(values[head], grad)).astype(BF)
+            v_grads.append(dot_nn(probs.astype(BF), grad))
+            k_grads.append(dot_nn(score_grad, q))
+            mine = slice(DH * head, DH * (head + 1))
+            q_total[mine, here] += dot_nn(k_turned[mine], score_grad)
+        return jnp.where(left, k_grads[0], k_grads[1]), jnp.where(left, v_grads[0], v_grads[1])
+
+    def put(k_grad, v_grad):
+        k_grad = (k_grad * math.log(2.0)).astype(BF)
+        v_grad = v_grad.astype(BF)
+
+        @pl.when(own)
+        def _():
+            own_grad_ref[0] = k_grad
+            own_grad_ref[1] = v_grad
+
+        @pl.when(jnp.logical_not(own))
+        def _():
+            got_grad_ref[0] = k_grad
+            got_grad_ref[1] = v_grad
+
+    if not causal:
+        put(*part(0, n, None))
+    else:
+        each = quarter // block
+        local_step = jnp.where(own, step, step - blocks)
+        piece = local_step // each
+        key_place = 2 * jnp.where(own, core, 1 - core) + piece
+        diagonal = (local_step - piece * each) * block
+        first, second = 2 * core, 2 * core + 1
+        skip, cut, whole = 0, 1, 2
+
+        def kind(query_place):
+            return jnp.where(key_place > query_place, skip, jnp.where(key_place == query_place, cut, whole))
+
+        for kinds in ((skip, skip), (skip, cut), (cut, whole), (whole, whole)):
+
+            @pl.when(jnp.logical_and(kind(first) == kinds[0], kind(second) == kinds[1]))
+            def _(kinds=kinds):
+                k_grad = v_grad = jnp.zeros((block, 128), F32)
+                for begin, how in zip((0, quarter), kinds):
+                    if how != skip:
+                        more = part(begin, quarter, diagonal if how == cut else None)
+                        k_grad, v_grad = k_grad + more[0], v_grad + more[1]
+                put(k_grad, v_grad)
+
+    @pl.when(step == 2 * blocks - 1)
+    def _():
+        q_grad_ref[...] = (q_total[...] * DH**-0.5).T.astype(BF)
+
+
+def attention_backward_half(core, kept, grad, causal):
+    q, own, got, query_ext, own_ext, got_ext, o, log = kept
+    n, width = q.shape
+    block = 512
+    blocks = n // block
+    first = lambda b: jnp.minimum(b, blocks - 1)
+    second = lambda b: jnp.maximum(b - blocks, 0)
+    whole = pl.BlockSpec((n, 128), lambda p, b: (0, p))
+    own_keys = pl.BlockSpec((2, block, 128), lambda p, b: (0, first(b), p))
+    got_keys = pl.BlockSpec((2, block, 128), lambda p, b: (0, second(b), p))
+    return pl.pallas_call(
+        partial(backward_kernel, causal=causal),
+        grid=(width // 128, 2 * blocks),
+        in_specs=[
+            pl.BlockSpec(memory_space=pltpu.SMEM),
+            whole,
+            own_keys,
+            got_keys,
+            pl.BlockSpec((n, 128), lambda p, b: (0, 0)),
+            pl.BlockSpec((block, 128), lambda p, b: (first(b), 0)),
+            pl.BlockSpec((block, 128), lambda p, b: (second(b), 0)),
+            whole,
+            whole,
+            whole,
+        ],
+        out_specs=[whole, own_keys, got_keys],
+        out_shape=[jax.ShapeDtypeStruct(s, BF) for s in ((n, width), own.shape, own.shape)],
+        scratch_shapes=[
+            pltpu.VMEM((2, n, 128), BF),
+            pltpu.VMEM((2, n, 128), BF),
+            pltpu.VMEM((128, n), F32),
+        ],
+        compiler_params=pltpu.CompilerParams(vmem_limit_bytes=VMEM_BYTES),
+        cost_estimate=NO_COST,
+        name="attention_causal_back" if causal else "attention_back",
+    )(core, q, own, got, query_ext, own_ext, got_ext, grad, o, log)
+
+
+def fold_dot(x, w):
+    return dot_nn(x[:, :HALF], w[:, :HALF]) + dot_nn(x[:, HALF:], w[:, HALF:])
+
+
+def fold_dot_t(g, w):
+    return jnp.concatenate([dot_nt(g, w[:, :HALF]), dot_nt(g, w[:, HALF:])], axis=1)
+
+
+def fold_grad(x, g):
+    return jnp.concatenate([dot_tn(x[:, :HALF], g), dot_tn(x[:, HALF:], g)], axis=1)
+
+
+def norm(v, gain, shift):
+    centred = v - jnp.mean(v, axis=-1, keepdims=True)
+    scale = lax.rsqrt(jnp.mean(centred * centred, axis=-1, keepdims=True) + EPS)
+    unit = centred * scale
+    return unit * gain + shift, unit, scale
+
+
+def norm_back(grad, unit, scale, gain):
+    inner = grad * gain
+    mean_inner = jnp.mean(inner, axis=-1, keepdims=True)
+    mean_unit = jnp.mean(inner * unit, axis=-1, keepdims=True)
+    return scale * (inner - mean_inner - unit * mean_unit)
+
+
+def over_rows(v):
+    return jnp.sum(v, axis=0, keepdims=True)
+
+
+GELU_C = math.sqrt(2.0 / math.pi)
+
+
+def gelu(u):
+    return 0.5 * u * (1.0 + jnp.tanh(GELU_C * u * (1.0 + 0.044715 * u * u)))
+
+
+def gelu_both(u):
+    square = u * u
+    t = jnp.tanh(GELU_C * u * (1.0 + 0.044715 * square))
+    half = 0.5 * (1.0 + t)
+    slope = half + 0.5 * u * (1.0 - t * t) * (GELU_C * (1.0 + 3 * 0.044715 * square))
+    return u * half, slope
+
+
+def halt_gate(last, weight):
+    logit = jnp.sum(last * weight, axis=-1, keepdims=True)
+    return 1.0 / (1.0 + jnp.exp(-logit))
+
+
+def halt_back(grad, start, last, runs, weight):
+    gate = halt_gate(last, weight)
+    used = runs * gate
+    logit_grad = used * (1.0 - gate) * jnp.sum(grad * (last - start), axis=-1, keepdims=True)
+    return grad * (1.0 - used), used * grad + logit_grad * weight, over_rows(logit_grad * last)
+
+
+def ffn_blocks(own_ref, other_ref, begin):
+    for which, ref in ((0, own_ref), (1, other_ref)):
+        for j in range(2):
+            up = begin + j * D
+            down = up + 2 * D
+            yield which, ref[up : up + D, :], ref[down : down + D, :], up, down
+
+
+def ffn(low, own_ref, other_ref, begin):
+    total = 0.0
+    for _, up, down, _, _ in ffn_blocks(own_ref, other_ref, begin):
+        total = total + dot_nn(gelu(dot_nn(low, up)).astype(BF), down)
+    return total
+
+
+def ffn_back(low, out_low, own_ref, other_ref, begin, acc, shift):
+    total = 0.0
+    for which, up, down, up_at, down_at in ffn_blocks(own_ref, other_ref, begin):
+        active, slope = gelu_both(dot_nn(low, up))
+        hidden = (dot_nt(out_low, down) * slope).astype(BF)
+        up_at, down_at = up_at + shift, down_at + shift
+        acc[which, down_at : down_at + D, :] += dot_tn(active.astype(BF), out_low)
+        acc[which, up_at : up_at + D, :] += dot_tn(low, hidden)
+        total = total + dot_nt(hidden, up)
+    return total
+
+
+def proj_back(o_refs, out_low, projs, acc, begin, o_grad_refs):
+    for which in range(2):
+        o_grad_refs[which][...] = dot_nt(out_low, projs[which]).astype(BF)
+        acc[which, begin : begin + HALF, :] += dot_tn(o_refs[which][...], out_low)
+
+
+def first_step(*refs):
+    @pl.when(pl.program_id(0) == 0)
+    def _():
+        for ref in refs:
+            ref[...] = jnp.zeros_like(ref)
+
+
+def last_step(core_ref, acc, keep_ref, send_ref, small_acc=None, small_ref=None):
+    @pl.when(pl.program_id(0) == pl.num_programs(0) - 1)
+    def _():
+        rows = acc.shape[1] // 2
+        for part, ref in ((core_ref[0], keep_ref), (1 - core_ref[0], send_ref)):
+            here = pl.ds(pl.multiple_of(part * rows, 16), rows)
+            for which in range(acc.shape[0]):
+                ref[which] = acc[which, here, :].astype(BF)
+        if small_ref is not None:
+            small_ref[...] = small_acc[...]
+
+
+def pre_kernel(
+    rows_ref, place_ref, own_ref, other_ref,
+    start_ref, q0_ref, q1_ref, kv0_ref, kv1_ref,
+):
+    start = rows_ref[...].astype(F32) + place_ref[...]
+    start_ref[...] = start
+    low = start.astype(BF)
+    for ref, q_ref, kv_ref in ((own_ref, q0_ref, kv0_ref), (other_ref, q1_ref, kv1_ref)):
+        q_ref[...] = (fold_dot(low, ref[0:HALF, :]) * Q_SCALE).astype(BF)
+        for kind in range(2):
+            w = ref[(kind + 1) * HALF : (kind + 2) * HALF, :]
+            kv_ref[kind] = fold_dot(low, w).astype(BF)
+
+
+def enc_post_kernel(
+    o0_ref, o1_ref, start_ref, runs_ref, own_ref, other_ref, small_ref,
+    sum_one_ref, sum_two_ref, states_ref,
+):
+    start = start_ref[...]
+    sum_one = start + dot_nn(o0_ref[...], own_ref[:HALF, :]) + dot_nn(o1_ref[...], other_ref[:HALF, :])
+    sum_one_ref[...] = sum_one
+    middle, _, _ = norm(sum_one, small_ref[0:1, :], small_ref[1:2, :])
+    sum_two = middle + ffn(middle.astype(BF), own_ref, other_ref, HALF)
+    sum_two_ref[...] = sum_two
+    last, _, _ = norm(sum_two, small_ref[2:3, :], small_ref[3:4, :])
+    gate = halt_gate(last, small_ref[4:5, :])
+    states_ref[...] = (start + runs_ref[:, 0:1] * gate * (last - start)).astype(BF)
+
+
+def dec_mid_kernel(
+    o0_ref, o1_ref, start_ref, states_ref, proj_own_ref, proj_other_ref, own_ref, other_ref, small_ref,
+    sum_ref, q0_ref, q1_ref, kv0_ref, kv1_ref,
+):
+    total = start_ref[...] + dot_nn(o0_ref[...], proj_own_ref[...])
+    total = total + dot_nn(o1_ref[...], proj_other_ref[...])
+    sum_ref[...] = total
+    middle, _, _ = norm(total, small_ref[0:1, :], small_ref[1:2, :])
+    low = middle.astype(BF)
+    states = states_ref[...]
+    for ref, q_ref, kv_ref in ((own_ref, q0_ref, kv0_ref), (other_ref, q1_ref, kv1_ref)):
+        q_ref[...] = (fold_dot(low, ref[0:HALF, :]) * Q_SCALE).astype(BF)
+        for kind in range(2):
+            w = ref[(kind + 1) * HALF : (kind + 2) * HALF, :]
+            kv_ref[kind] = fold_dot(states, w).astype(BF)
+
+
+def dec_post_kernel(
+    core_ref, o0_ref, o1_ref, sum_one_ref, start_ref, runs_ref, cot_ref, own_ref, other_ref, small_ref,
+    states_ref, start_grad_ref, sum_grad_ref, o0_grad_ref, o1_grad_ref,
+    keep_ref, send_ref, small_grad_ref,
+    acc, small_acc,
+):
+    first_step(acc, small_acc)
+    start = start_ref[...]
+    projs = own_ref[:HALF, :], other_ref[:HALF, :]
+    middle, _, _ = norm(sum_one_ref[...], small_ref[0:1, :], small_ref[1:2, :])
+    sum_two = middle + dot_nn(o0_ref[...], projs[0]) + dot_nn(o1_ref[...], projs[1])
+    gain_two = small_ref[2:3, :]
+    mixed, unit_two, scale_two = norm(sum_two, gain_two, small_ref[3:4, :])
+    low = mixed.astype(BF)
+    sum_three = mixed + ffn(low, own_ref, other_ref, HALF)
+    gain_three = small_ref[4:5, :]
+    last, unit_three, scale_three = norm(sum_three, gain_three, small_ref[5:6, :])
+    weight = small_ref[6:7, :]
+    runs = runs_ref[:, 1:2]
+    states_ref[...] = (start + runs * halt_gate(last, weight) * (last - start)).astype(BF)
+    start_grad, last_grad, weight_grad = halt_back(
+        cot_ref[...].astype(F32), start, last, runs, weight
+    )
+    start_grad_ref[...] = start_grad
+    small_acc[4:5, :] += weight_grad
+    small_acc[2:3, :] += over_rows(last_grad * unit_three)
+    small_acc[3:4, :] += over_rows(last_grad)
+    grad = norm_back(last_grad, unit_three, scale_three, gain_three)
+    grad = grad + ffn_back(low, grad.astype(BF), own_ref, other_ref, HALF, acc, 0)
+    small_acc[0:1, :] += over_rows(grad * unit_two)
+    small_acc[1:2, :] += over_rows(grad)
+    grad = norm_back(grad, unit_two, scale_two, gain_two)
+    sum_grad_ref[...] = grad
+    proj_back((o0_ref, o1_ref), grad.astype(BF), projs, acc, 0, (o0_grad_ref, o1_grad_ref))
+    last_step(core_ref, acc, keep_ref, send_ref, small_acc, small_grad_ref)
+
+
+def dec_mid_back_kernel(
+    core_ref, q0_grad_ref, q1_grad_ref, sum_grad_ref, sum_one_ref, start_grad_ref, o0_ref, o1_ref,
+    cq_own_ref, cq_other_ref, proj_own_ref, proj_other_ref, small_ref,
+    out_ref, o0_grad_ref, o1_grad_ref, keep_ref, send_ref, small_grad_ref,
+    acc, small_acc,
+):
+    first_step(acc, small_acc)
+    gain = small_ref[0:1, :]
+    middle, unit, scale = norm(sum_one_ref[...], gain, small_ref[1:2, :])
+    low = middle.astype(BF)
+    grad = sum_grad_ref[...]
+    for which, (ref, part_ref) in enumerate(((cq_own_ref, q0_grad_ref), (cq_other_ref, q1_grad_ref))):
+        grad = grad + fold_dot_t(part_ref[...], ref[...])
+        acc[which, :HALF, :] += fold_grad(low, part_ref[...])
+    small_acc[0:1, :] += over_rows(grad * unit)
+    small_acc[1:2, :] += over_rows(grad)
+    grad = norm_back(grad, unit, scale, gain)
+    out_ref[...] = start_grad_ref[...] + grad
+    projs = proj_own_ref[...], proj_other_ref[...]
+    proj_back((o0_ref, o1_ref), grad.astype(BF), projs, acc, HALF, (o0_grad_ref, o1_grad_ref))
+    last_step(core_ref, acc, keep_ref, send_ref, small_acc, small_grad_ref)
+
+
+def kv_total(own_ref, got_ref, kind):
+    return (own_ref[kind].astype(F32) + got_ref[kind].astype(F32)).astype(BF)
+
+
+def enc_back_kernel(
+    core_ref, kv0_ref, kv1_ref, got0_ref, got1_ref, states_ref, cot_ref, start_ref, sum_one_ref, sum_two_ref,
+    o0_ref, o1_ref, runs_ref, cross_own_ref, cross_other_ref, own_ref, other_ref, small_ref,
+    out_ref, o0_grad_ref, o1_grad_ref, keep_ref, send_ref, small_grad_ref,
+    acc, small_acc,
+):
+    first_step(acc, small_acc)
+    states = states_ref[...]
+    grad = cot_ref[...].astype(F32)
+    crosses = (cross_own_ref, kv0_ref, got0_ref), (cross_other_ref, kv1_ref, got1_ref)
+    for which, (ref, kv_ref, got_ref) in enumerate(crosses):
+        for kind in range(2):
+            part = kv_total(kv_ref, got_ref, kind)
+            at = kind * HALF
+            grad = grad + fold_dot_t(part, ref[at + HALF : at + 2 * HALF, :])
+            acc[which, at : at + HALF, :] += fold_grad(states, part)
+    gain_one, gain_two, weight = small_ref[0:1, :], small_ref[2:3, :], small_ref[4:5, :]
+    last, unit_two, scale_two = norm(sum_two_ref[...], gain_two, small_ref[3:4, :])
+    start_grad, last_grad, weight_grad = halt_back(
+        grad, start_ref[...], last, runs_ref[:, 0:1], weight
+    )
+    small_acc[4:5, :] += weight_grad
+    small_acc[2:3, :] += over_rows(last_grad * unit_two)
+    small_acc[3:4, :] += over_rows(last_grad)
+    grad = norm_back(last_grad, unit_two, scale_two, gain_two)
+    middle, unit_one, scale_one = norm(sum_one_ref[...], gain_one, small_ref[1:2, :])
+    grad = grad + ffn_back(middle.astype(BF), grad.astype(BF), own_ref, other_ref, HALF, acc, 2 * HALF)
+    small_acc[0:1, :] += over_rows(grad * unit_one)
+    small_acc[1:2, :] += over_rows(grad)
+    grad = norm_back(grad, unit_one, scale_one, gain_one)
+    out_ref[...] = start_grad + grad
+    projs = own_ref[:HALF, :], other_ref[:HALF, :]
+    proj_back((o0_ref, o1_ref), grad.astype(BF), projs, acc, 2 * HALF, (o0_grad_ref, o1_grad_ref))
+    last_step(core_ref, acc, keep_ref, send_ref, small_acc, small_grad_ref)
+
+
+def qkv_back_kernel(
+    core_ref, q_grad_ref, kv_ref, got_ref, start_ref, base_ref, w_ref,
+    out_ref, keep_ref, send_ref,
+    acc,
+):
+    first_step(acc)
+    low = start_ref[...].astype(BF)
+    grad = base_ref[...]
+    parts = q_grad_ref[...], kv_total(kv_ref, got_ref, 0), kv_total(kv_ref, got_ref, 1)
+    for kind, part in enumerate(parts):
+        rows = slice(kind * HALF, (kind + 1) * HALF)
+        grad = grad + fold_dot_t(part, w_ref[rows, :])
+        acc[0, rows, :] += fold_grad(low, part)
+    out_ref[...] = grad
+    last_step(core_ref, acc, keep_ref, send_ref)
+
+
+def rows_call(kernel, name, by_rows, whole, row_outs, whole_outs=(), scratch=(), core=None, block=512):
+    n = by_rows[0].shape[-2]
+
+    def row_spec(shape):
+        if len(shape) == 3:
+            return pl.BlockSpec((shape[0], block, shape[2]), lambda i: (0, i, 0))
+        return pl.BlockSpec((block, shape[1]), lambda i: (i, 0))
+
+    def whole_spec(entry):
+        array, rows, index = entry if isinstance(entry, tuple) else (entry, entry.shape[0], 0)
+        return pl.BlockSpec((rows, array.shape[1]), lambda i: (index, 0), pipeline_mode=pl.Buffered(1))
+
+    arrays = [e[0] if isinstance(e, tuple) else e for e in whole]
+    return pl.pallas_call(
+        kernel,
+        grid=(n // block,),
+        in_specs=([] if core is None else [pl.BlockSpec(memory_space=pltpu.SMEM)])
+        + [row_spec(a.shape) for a in by_rows]
+        + [whole_spec(e) for e in whole],
+        out_specs=[row_spec(s) for s, _ in row_outs]
+        + [pl.BlockSpec(s, lambda i, s=s: (0,) * len(s)) for s, _ in whole_outs],
+        out_shape=[jax.ShapeDtypeStruct(s, t) for s, t in [*row_outs, *whole_outs]],
+        scratch_shapes=[pltpu.VMEM(s, F32) for s in scratch],
+        compiler_params=pltpu.CompilerParams(vmem_limit_bytes=VMEM_BYTES),
+        cost_estimate=NO_COST,
+        name=name,
+    )(*([] if core is None else [core]), *by_rows, *arrays)
+
+
+def in_order_kernel(place_ref, mine_ref, got_ref, out_ref):
+    piece, core = place_ref[0], place_ref[1]
+    pieces, rows, _ = mine_ref.shape
+    for ref, of in ((mine_ref, core), (got_ref, 1 - core)):
+        for k in range(pieces):
+            begin = (of * pieces + (piece ^ k)) * rows
+            out_ref[pl.ds(pl.multiple_of(begin, 16), rows), :] = ref[k]
+
+
+def in_order(place, mine, got):
+    pieces, rows, width = mine.shape
+    return pl.pallas_call(
+        in_order_kernel,
+        in_specs=[pl.BlockSpec(memory_space=pltpu.SMEM)] + [pl.BlockSpec(memory_space=pltpu.VMEM)] * 2,
+        out_specs=pl.BlockSpec(memory_space=pltpu.VMEM),
+        out_shape=jax.ShapeDtypeStruct((2 * pieces * rows, width), mine.dtype),
+        compiler_params=pltpu.CompilerParams(vmem_limit_bytes=VMEM_BYTES),
+        cost_estimate=NO_COST,
+        name="in_order",
+    )(place, mine, got)
+
+
+class Place:
+    def __init__(self, dp_size):
+        self.dp_size = dp_size
+        dp = lax.axis_index("dp")
+        self.c = dp % 2
+        self.stays = self.c == lax.axis_index("mp")
+        self.masks = [1 << b for b in range(1, dp_size.bit_length() - 1)]
+        self.bits = [(dp // mask) % 2 for mask in self.masks]
+        self.core = self.c.astype(jnp.int32).reshape(1)
+        piece = jnp.int32(0)
+        for bit in self.bits:
+            piece = 2 * piece + bit.astype(jnp.int32)
+        self.order = jnp.concatenate([piece.reshape(1), self.core])
+        self.pair = jnp.concatenate([jnp.zeros((1,), jnp.int32), self.core])
+
+    def flip(self, values, mask):
+        return lax.ppermute(values, "dp", [(d, d ^ mask) for d in range(self.dp_size)])
+
+    def core_swap(self, values):
+        return self.flip(values, 1)
+
+    def y_swap(self, values):
+        return lax.ppermute(values, "mp", [(0, 1), (1, 0)])
+
+    def cross(self, values):
+        perm = []
+        for d in range(0, self.dp_size, 2):
+            perm += [(2 * d + 1, 2 * d + 2), (2 * d + 2, 2 * d + 1)]
+        return lax.ppermute(values, ("dp", "mp"), perm)
+
+
+class Flow:
+    def __init__(self):
+        self.fresh = []
+        self.chains = []
+        self.results = {}
+
+    def add(self, name, chain):
+        self.fresh.append((name, chain, next(chain)))
+
+    def go_on(self, name, chain, arrived):
+        try:
+            self.fresh.append((name, chain, chain.send(arrived)))
+        except StopIteration as stop:
+            self.results[name] = stop.value
+
+    def step(self, values):
+        due = [chain for chain in self.chains if chain[3] == 1]
+        self.chains = [(*chain[:3], chain[3] - 1) for chain in self.chains if chain[3] > 1]
+        values, arrived = lax.optimization_barrier((values, [chain[2] for chain in due]))
+        for (name, chain, _, _), got in zip(due, arrived):
+            self.go_on(name, chain, got)
+        fresh, self.fresh = self.fresh, []
+        values, operands = lax.optimization_barrier((values, [op[1] for _, _, op in fresh]))
+        for (name, chain, (send, _, steps)), operand in zip(fresh, operands):
+            self.chains.append((name, chain, send(operand), steps))
+        return values
+
+    def finish(self):
+        while self.chains:
+            name, chain, pending, _ = self.chains.pop(0)
+            self.go_on(name, chain, pending)
+        while self.fresh:
+            name, chain, (send, operand, _) = self.fresh.pop(0)
+            self.go_on(name, chain, send(operand))
+
+
+def gathered(at, own, first=1, second=1):
+    rows = own.shape[0] // 2
+    near = yield at.y_swap, lax.dynamic_slice_in_dim(own, at.c * rows, rows, 0), first
+    far = yield at.core_swap, near, second
+    return in_order(at.pair, near[None], far[None])
+
+
+def moved(at, values, steps):
+    got = yield at.cross, values, steps
+    return jnp.where(at.stays, values, got)
+
+
+def plus(*values):
+    return sum(v.astype(F32) for v in values).astype(BF)
+
+
+def over_chips(at, total, steps, last_steps):
+    for mask, bit in zip(at.masks, at.bits):
+        rows = total.shape[0] // 2
+        half = lax.dynamic_slice_in_dim(total, (1 - bit) * rows, rows, 0)
+        got = yield partial(at.flip, mask=mask), half, steps
+        total = plus(lax.dynamic_slice_in_dim(total, bit * rows, rows, 0), got)
+    total = total[None]
+    for mask in at.masks[::-1]:
+        got = yield partial(at.flip, mask=mask), total, steps
+        total = jnp.concatenate([total, got])
+    far = yield at.core_swap, total, last_steps
+    return in_order(at.order, total, far)
+
+
+def summed(at, keep, send, core_steps=1, y_steps=1, steps=1, last_steps=1):
+    got = yield at.core_swap, send, core_steps
+    near = yield at.y_swap, plus(keep[1], got[1]), y_steps
+    return (yield from over_chips(at, plus(keep[0], got[0], near), steps, last_steps))
+
+
+def summed_other(at, keep, got, y_steps):
+    near = yield at.y_swap, plus(keep[0], got[0]), y_steps
+    return near
+
+
+def summed_own(at, keep, send, near):
+    got = yield at.core_swap, send, 1
+    return (yield from over_chips(at, plus(keep[0], got[0], near), 1, 1))
+
+
+def summed_small(at, values):
+    for mask in [1, *at.masks]:
+        values = values + (yield partial(at.flip, mask=mask), values, 1)
+    return values + (yield at.y_swap, values, 1)
+
+
+def rows_of(weight):
+    if weight.ndim == 3:
+        kinds, depth, width = weight.shape
+        folded = jnp.concatenate([weight[:, : depth // 2], weight[:, depth // 2 :]], axis=2)
+        return folded.reshape(kinds * depth // 2, 2 * width)
+    depth, width = weight.shape
+    if width == D:
+        return weight
+    if width < D:
+        return jnp.concatenate([weight[: depth // 2], weight[depth // 2 :]], axis=1)
+    return jnp.concatenate([weight[:, :D], weight[:, D:]], axis=0)
+
+
+def rows_back(rows, shape):
+    if len(shape) == 3:
+        kinds, depth, width = shape
+        folded = rows.reshape(kinds, depth // 2, 2 * width)
+        return jnp.concatenate([folded[..., :width], folded[..., width:]], axis=1)
+    depth, width = shape
+    if width == D:
+        return rows
+    if width < D:
+        return jnp.concatenate([rows[:, :width], rows[:, width:]], axis=0)
+    return jnp.concatenate([rows[:depth], rows[depth:]], axis=1)
+
+
+def unpack(rows, *weights):
+    outs, begin = [], 0
+    for weight in weights:
+        count = weight.size // D
+        outs.append(rows_back(rows[begin : begin + count].astype(F32), weight.shape))
+        begin += count
+    return outs
+
+
+def extensions(segments):
+    lane = jnp.arange(128, dtype=jnp.int32)[None, :] % DH
+    same = segments[:, None] == lane
+    for_query = jnp.where((lane < 8) & ~same, BIG, 0.0).astype(BF)
+    for_key = jnp.where(lane < 8, same.astype(F32), jnp.where(lane < 11, 1.0, 0.0)).astype(BF)
+    return for_query, for_key
+
+
+Q_SCALE = DH**-0.5 * math.log2(math.e)
+
+
+def chip_rows(
+    source_rows,
+    target_rows,
+    source_segment,
+    target_segment,
+    running,
+    enc_qkv,
+    enc_proj,
+    enc_up,
+    enc_down,
+    enc_gains,
+    enc_shifts,
+    dec_qkv,
+    dec_proj,
+    cross_query,
+    cross_kv,
+    cross_proj,
+    dec_up,
+    dec_down,
+    dec_gains,
+    dec_shifts,
+    halt_weight,
+    enc_cotangent,
+    dec_cotangent,
+    *,
+    dp_size,
+):
+    at = Place(dp_size)
+    flow = Flow()
+    n = source_rows.shape[0]
+    row = ((n, D), F32)
+    row_low = ((n, D), BF)
+    half_low = ((n, HALF), BF)
+    kv_low = ((2, n, HALF), BF)
+
+    ints = jnp.concatenate([source_segment[0], target_segment[0], running[0, 0], running[1, 0]])
+    w_enc_qkv = rows_of(enc_qkv)
+    flow.add("source", moved(at, source_rows[:, 0], 1))
+    flow.add("w_enc_qkv", gathered(at, w_enc_qkv))
+    flow.add("ints", moved(at, ints.reshape(6, n), 1))
+    (target_rows,) = flow.step((target_rows,))
+
+    w_dec_self = jnp.concatenate([rows_of(dec_qkv), rows_of(dec_proj)])
+    w_enc = jnp.concatenate([rows_of(enc_proj), rows_of(enc_up), rows_of(enc_down)])
+    w_cross = jnp.concatenate([rows_of(cross_query), rows_of(cross_kv)])
+    w_dec = jnp.concatenate([rows_of(cross_proj), rows_of(dec_up), rows_of(dec_down)])
+    cots = jnp.concatenate([enc_cotangent[:, 0].astype(BF), dec_cotangent[:, 0].astype(BF)], axis=1)
+    pad = jnp.zeros((3, D), F32)
+    small_enc = jnp.stack(
+        [enc_gains[0], enc_shifts[0], enc_gains[1], enc_shifts[1], halt_weight[0]]
+    )
+    small_enc = jnp.concatenate([small_enc, pad])
+    small_dec = jnp.stack(
+        [dec_gains[0], dec_shifts[0], dec_gains[1], dec_shifts[1], dec_gains[2], dec_shifts[2], halt_weight[1]]
+    )
+    small_dec = jnp.concatenate([small_dec, pad[:1]])
+    place = at.core[0] * n + jnp.arange(n, dtype=jnp.int32)
+    embedding = signal(place.astype(F32)) + signal(jnp.ones((1,), F32))
+
+    flow.add("target", moved(at, target_rows[:, 0], 2))
+    flow.add("w_dec_self", gathered(at, w_dec_self, 2, 1))
+    w_enc, w_cross, w_dec, embedding, cots = flow.step((w_enc, w_cross, w_dec, embedding, cots))
+    source, ints = flow.results["source"], flow.results["ints"]
+    source_segments, target_segments = ints[:2].reshape(-1), ints[2:4].reshape(-1)
+    runs = jnp.transpose(jnp.pad(ints[4:].astype(F32), ((0, 126), (0, 0))))
+
+    def tables(segments):
+        for_query, for_key = extensions(segments)
+        own = lax.dynamic_slice_in_dim(for_query, at.c * n, n, 0)
+        own_keys = lax.dynamic_slice_in_dim(for_key, at.c * n, n, 0)
+        got_keys = lax.dynamic_slice_in_dim(for_key, (1 - at.c) * n, n, 0)
+        return own, (for_key, own_keys, got_keys)
+
+    source_q, source_keys = tables(source_segments)
+    target_q, target_keys = tables(target_segments)
+    source_q, source_keys, target_q, target_keys = flow.step((source_q, source_keys, target_q, target_keys))
+
+    def pre(rows, own, other):
+        whole = [(own, 3 * HALF, 0), (other, 3 * HALF, 0)]
+        return rows_call(
+            pre_kernel, "project", [rows, embedding], whole,
+            [row, half_low, half_low, kv_low, kv_low],
+        )
+
+    def attend(q, kv, got, query_ext, key_ext, causal=False):
+        o, log = attention_forward_half(at.core, q, kv, got, query_ext, key_ext[0], causal)
+        return o, (q, kv, got, query_ext, key_ext[1], key_ext[2], o, log)
+
+    def attend_back(kept, grad, causal=False):
+        return attention_backward_half(at.core, kept, grad, causal)
+
+    w_enc_qkv_got = flow.results["w_enc_qkv"]
+    enc_start, q0, q1, kv0, kv1 = pre(source, w_enc_qkv, w_enc_qkv_got)
+    got0, got1 = at.core_swap(kv0), at.core_swap(kv1)
+    enc_o0, enc_kept0 = attend(q0, kv0, got0, source_q, source_keys)
+    flow.add("w_enc", gathered(at, w_enc, 2, 1))
+    enc_o0, q1, kv1, got1 = flow.step((enc_o0, q1, kv1, got1))
+    target = flow.results["target"]
+    enc_o1, enc_kept1 = attend(q1, kv1, got1, source_q, source_keys)
+    enc_o1, target = flow.step((enc_o1, target))
+
+    w_dec_self_got = flow.results["w_dec_self"]
+    dec_start, q0, q1, kv0, kv1 = pre(target, w_dec_self, w_dec_self_got)
+    got0, got1 = at.core_swap(kv0), at.core_swap(kv1)
+    self_o0, self_kept0 = attend(q0, kv0, got0, target_q, target_keys, True)
+    flow.add("w_cross", gathered(at, w_cross))
+    self_o0, q1, kv1, got1 = flow.step((self_o0, q1, kv1, got1))
+    self_o1, self_kept1 = attend(q1, kv1, got1, target_q, target_keys, True)
+    flow.add("w_dec", gathered(at, w_dec, 3, 1))
+    self_o1, enc_o1 = flow.step((self_o1, enc_o1))
+    w_enc_got = flow.results["w_enc"]
+    enc_sum_one, enc_sum_two, enc_states = rows_call(
+        enc_post_kernel, "encoder_feed", [enc_o0, enc_o1, enc_start, runs], [w_enc, w_enc_got, small_enc],
+        [row, row, row_low],
+    )
+    flow.add("cots", moved(at, cots, 3))
+    (enc_states,) = flow.step((enc_states,))
+    w_cross_got = flow.results["w_cross"]
+    dec_sum_one, q0, q1, kv0, kv1 = rows_call(
+        dec_mid_kernel, "cross_project", [self_o0, self_o1, dec_start, enc_states],
+        [(w_dec_self, HALF, 3), (w_dec_self_got, HALF, 3), w_cross, w_cross_got, small_dec],
+        [row, half_low, half_low, kv_low, kv_low],
+    )
+    got0, got1 = at.core_swap(kv0), at.core_swap(kv1)
+    q0, q1, kv0, kv1 = flow.step((q0, q1, kv0, kv1))
+    cross_o0, cross_kept0 = attend(q0, kv0, got0, target_q, source_keys)
+    cross_o0, q1, kv1, got1 = flow.step((cross_o0, q1, kv1, got1))
+    cross_o1, cross_kept1 = attend(q1, kv1, got1, target_q, source_keys)
+    flow.add("enc_states", moved(at, enc_states, 1))
+    (cross_o1,) = flow.step((cross_o1,))
+    cots = flow.results["cots"]
+    enc_cot, dec_cot = cots[:, :D], cots[:, D:]
+
+    def grad_outs(rows):
+        return [((2, rows // 2, D), BF)] * 2 + [((8, D), F32)]
+
+    w_dec_got = flow.results["w_dec"]
+    (
+        dec_states, start_grad, sum_grad, o0_grad, o1_grad, *dec_parts, small_two,
+    ) = rows_call(
+        dec_post_kernel, "decoder_feed",
+        [cross_o0, cross_o1, dec_sum_one, dec_start, runs, dec_cot], [w_dec, w_dec_got, small_dec],
+        [row_low, row, row, half_low, half_low], grad_outs(9 * HALF),
+        [(2, 9 * HALF, D), (8, D)], at.core,
+    )
+    flow.add("dec", summed(at, *dec_parts))
+    flow.add("dec_states", moved(at, dec_states, 1))
+    o0_grad, o1_grad = flow.step((o0_grad, o1_grad))
+
+    q0_grad, kv0_grad, kv0_send = attend_back(cross_kept0, o0_grad)
+    q0_grad, kv0_grad, kv0_send, o1_grad = flow.step((q0_grad, kv0_grad, kv0_send, o1_grad))
+    kv0_got = at.core_swap(kv0_send)
+    q1_grad, kv1_grad, kv1_send = attend_back(cross_kept1, o1_grad)
+    q1_grad, kv1_grad, kv1_send, kv0_got = flow.step((q1_grad, kv1_grad, kv1_send, kv0_got))
+    kv1_got = at.core_swap(kv1_send)
+
+    (
+        enc_base, enc_o0_grad, enc_o1_grad, *enc_parts, small_enc_grad,
+    ) = rows_call(
+        enc_back_kernel, "encoder_feed_back",
+        [kv0_grad, kv1_grad, kv0_got, kv1_got, enc_states, enc_cot, enc_start, enc_sum_one, enc_sum_two,
+         enc_o0, enc_o1, runs],
+        [w_cross, w_cross_got, w_enc, w_enc_got, small_enc],
+        [row, half_low, half_low], grad_outs(11 * HALF), [(2, 11 * HALF, D), (8, D)], at.core,
+    )
+    flow.add("enc", summed(at, *enc_parts))
+    enc_o0_grad, enc_o1_grad, q0_grad = flow.step((enc_o0_grad, enc_o1_grad, q0_grad))
+    (
+        dec_base, self_o0_grad, self_o1_grad, *mid_parts, small_one,
+    ) = rows_call(
+        dec_mid_back_kernel, "cross_project_back",
+        [q0_grad, q1_grad, sum_grad, dec_sum_one, start_grad, self_o0, self_o1],
+        [(w_cross, HALF, 0), (w_cross_got, HALF, 0), (w_dec_self, HALF, 3), (w_dec_self_got, HALF, 3), small_dec],
+        [row, half_low, half_low], grad_outs(2 * HALF), [(2, 2 * HALF, D), (8, D)], at.core,
+    )
+    flow.add("small", summed_small(at, jnp.concatenate([small_enc_grad, small_one, small_two])))
+    enc_o1_grad, mid_parts = flow.step((enc_o1_grad, mid_parts))
+
+    def project_back(q_grad, kv_grad, got, start, base, weight):
+        return rows_call(
+            qkv_back_kernel, "project_back", [q_grad, kv_grad, got, start, base], [(weight, 3 * HALF, 0)],
+            [row], [((1, 3 * HALF // 2, D), BF)] * 2, [(1, 3 * HALF, D)], at.core,
+        )
+
+    q1_grad, kv1_grad, kv1_send = attend_back(enc_kept1, enc_o1_grad)
+    kv1_got = at.core_swap(kv1_send)
+    q1_grad, kv1_grad, enc_o0_grad = flow.step((q1_grad, kv1_grad, enc_o0_grad))
+    q0_grad, kv0_grad, kv0_send = attend_back(enc_kept0, enc_o0_grad)
+    kv0_got = at.core_swap(kv0_send)
+    q0_grad, kv0_grad, kv1_got, q1_grad = flow.step((q0_grad, kv0_grad, kv1_got, q1_grad))
+    source_grad, keep1, send1 = project_back(q1_grad, kv1_grad, kv1_got, enc_start, enc_base, w_enc_qkv_got)
+    source_grad, keep0, send0 = project_back(q0_grad, kv0_grad, kv0_got, enc_start, source_grad, w_enc_qkv)
+    keep = jnp.concatenate([jnp.concatenate([keep0, keep1]), mid_parts[0]], axis=1)
+    send = jnp.concatenate([jnp.concatenate([send0, send1]), mid_parts[1]], axis=1)
+    source_low = source_grad.astype(BF)
+    flow.add("enc_qkv", summed(at, keep, send, 1, 2))
+    flow.add("source_grad", moved(at, source_low, 1))
+    (self_o1_grad,) = flow.step((self_o1_grad,))
+
+    q1_grad, kv1_grad, kv1_send = attend_back(self_kept1, self_o1_grad, True)
+    q1_grad, kv1_grad, kv1_send, self_o0_grad = flow.step((q1_grad, kv1_grad, kv1_send, self_o0_grad))
+    kv1_got = at.core_swap(kv1_send)
+    target_grad, keep1, send1 = project_back(q1_grad, kv1_grad, kv1_got, dec_start, dec_base, w_dec_self_got)
+    flow.add("dec_qkv_other", summed_other(at, keep1, at.core_swap(send1), 1))
+    target_grad, self_o0_grad = flow.step((target_grad, self_o0_grad))
+    q0_grad, kv0_grad, kv0_send = attend_back(self_kept0, self_o0_grad, True)
+    q0_grad, kv0_grad, kv0_send, target_grad = flow.step((q0_grad, kv0_grad, kv0_send, target_grad))
+    kv0_got = at.core_swap(kv0_send)
+    target_grad, keep0, send0 = project_back(q0_grad, kv0_grad, kv0_got, dec_start, target_grad, w_dec_self)
+    target_grad, keep0, send0 = flow.step((target_grad, keep0, send0))
+    flow.add("dec_qkv", summed_own(at, keep0, send0, flow.results["dec_qkv_other"]))
+    flow.add("target_grad", moved(at, target_grad.astype(BF), 1))
+    flow.finish()
+
+    done = flow.results
+    cross_proj_grad, dec_up_grad, dec_down_grad = unpack(done["dec"], cross_proj, dec_up, dec_down)
+    cross_kv_grad, enc_proj_grad, enc_up_grad, enc_down_grad = unpack(
+        done["enc"], cross_kv, enc_proj, enc_up, enc_down
+    )
+    both = done["enc_qkv"].reshape(2, -1, D)
+    (enc_qkv_grad,) = unpack(both[:, : 3 * HALF // 2].reshape(-1, D), enc_qkv)
+    cross_query_grad, dec_proj_grad = unpack(
+        both[:, 3 * HALF // 2 :].reshape(-1, D), cross_query, dec_proj
+    )
+    (dec_qkv_grad,) = unpack(done["dec_qkv"], dec_qkv)
+    small = done["small"]
+    enc_small, one, two = small[:8], small[8:16], small[16:]
+    return (
+        done["enc_states"][:, None],
+        done["dec_states"][:, None],
+        done["source_grad"].astype(F32)[:, None],
+        done["target_grad"].astype(F32)[:, None],
+        enc_qkv_grad,
+        enc_proj_grad,
+        enc_up_grad,
+        enc_down_grad,
+        enc_small[0:3:2],
+        enc_small[1:4:2],
+        dec_qkv_grad,
+        dec_proj_grad,
+        cross_query_grad,
+        cross_kv_grad,
+        cross_proj_grad,
+        dec_up_grad,
+        dec_down_grad,
+        jnp.concatenate([one[0:1], two[0:3:2]]),
+        jnp.concatenate([one[1:2], two[1:4:2]]),
+        jnp.stack([enc_small[4], two[4]]),
+    )
+
+
 def solution(mesh):
+    dp_size, mp_size = mesh.shape["dp"], mesh.shape["mp"]
+    by_chip = mp_size == 2 and dp_size in (4, 8, 16)
+    body = partial(chip_rows, dp_size=dp_size) if by_chip else local
     return jax.shard_map(
-        local,
+        body,
         mesh=mesh,
         in_specs=(
             P("mp", "dp", None),

time: 1570 us -> 680 us (0.43)
  waiting for transfers between devices: 634 us -> 59.1 us
  matrix products: 447 us -> 0 us
  Pallas kernels: 0 us -> 377 us
  local copies, waits for them, and re-layouts: 228 us -> 53.1 us
  other arithmetic: 180 us -> 83.1 us
  starting transfers between devices: 3.33 us -> 97.5 us
  blocking collectives: 42 us -> 0 us
    dot_general x384 -> x0, matrix products: 447 us -> none  [the longest x96 127 us: pair_scores(): lax.dot_general(query_block, key_rows, (((1,), (1,)), ((), ())), preferre...]
    pallas_call x0 -> x32, Pallas kernels: none -> 377 us  [the longest x6 145 us: attention_backward_half(): pl.pallas_call(partial(backward_kernel, causal=causal), grid=(width // 12...]
    all_gather x11 -> x0, waiting for transfers between devices: 271 us -> none  [the longest x6 178 us: collect(): return lax.all_gather(piece_rows, 'mp', axis=0, tiled=True)]
    reduce_scatter x11 -> x0, waiting for transfers between devices: 257 us -> none  [the longest x6 136 us: project_back(): lax.psum_scatter(partial_term(jnp.int32(0), lax.axis_size('mp') * rows).a...]
    psum x1 -> x0, waiting for transfers between devices: 105 us -> none  [local(): lax.psum(enc_qkv_grad.astype(jnp.bfloat16), 'dp').astype(jnp.float32)]
    ppermute x0 -> x72, starting transfers between devices: none -> 97.5 us  [the longest x54 70.8 us: flip(): lax.ppermute(values, 'dp', [(d, d ^ mask) for d in range(self.dp_size)])]
    reduce_sum x69 -> x0, other arithmetic: 77.2 us -> none  [the longest x48 34.1 us: one_block(): totals = jnp.sum(exponent, axis=1, keepdims=True)]
    dynamic_slice x252 -> x18, local copies, waits for them, and re-layouts: 78.2 us -> 8.34 us  [the longest x12 3.93 us: over_chips(): half = lax.dynamic_slice_in_dim(total, (1 - bit) * rows, rows, 0)]
  transfers between devices with their start and end apart: 23 -> 72, of which waited for: 19 -> 19; matrix products, arithmetic and copies ran while one was open for 29% -> 13% of each run, Pallas kernels for 0% -> 55%
where the time goes in v2:
time: 680 us; the launch traced here: 672 us
  Pallas kernels  377 us (55%)
  starting transfers between devices  97.5 us (14%)
  other arithmetic  83.1 us (12%)
  waiting for transfers between devices  59.1 us (9%)
  local copies, waits for them, and re-layouts  53.1 us (8%)
    pallas_call x6, Pallas kernels, attention_backward_half(): pl.pallas_call(partial(backward_kernel, causal=causal), grid=(width // 12...  145 us
    pallas_call x11, Pallas kernels, rows_call(): pl.pallas_call(kernel, grid=(n // block,), in_specs=([] if core is None e...  124 us
    pallas_call x6, Pallas kernels, attention_forward_half(): pl.pallas_call(partial(forward_kernel, causal=causal, rows=rows), grid=(w...  83.4 us
    ppermute x54, starting transfers between devices, flip(): lax.ppermute(values, 'dp', [(d, d ^ mask) for d in range(self.dp_size)])  70.8 us
    ppermute x54, waiting for transfers between devices, flip(): lax.ppermute(values, 'dp', [(d, d ^ mask) for d in range(self.dp_size)])  45.3 us
    unnamed x224, local copies, waits for them, and re-layouts  28.8 us
    pallas_call x9, Pallas kernels, in_order(): pl.pallas_call(in_order_kernel, in_specs=[pl.BlockSpec(memory_space=pltpu...  24.4 us
    ppermute x10, starting transfers between devices, y_swap(): return lax.ppermute(values, 'mp', [(0, 1), (1, 0)])  16.3 us
  transfers between devices with their start and end apart: 72, of which 19 were waited for; matrix products, arithmetic and copies ran while one was open for 13% of the time, Pallas kernels for 55%

profile of v2, /device:TPU:0, one launch (start us, length us, event | category | flops | bytes accessed | tf_op | source)
XLA Modules:
  0.0 672.3 jit_solution(4494511888964517978)
XLA Ops:
  9.3 5.5 collective-permute-start.1
  17.6 4.7 multiply_sine_fusion
  32.6 4.5 collective-permute-done.1
  49.9 4.8 project.2
  60.5 15.5 %attention.4 = (bf16[1024,256]{1,0:T(8,128)(2,1)}, f32[1024,256]{1,0:T(8,128)}) custom-call(s32[1]{0:T(128)} %bitcast.core_ref, bf16[1024,256]{1,0:T(8,128)(2,1)} %get-tuple-element.340.q_ref, bf16[2,1024,256]{2,1,0:T(8,128)(2,1)} %get-tuple-element.341.own_ref, bf16[2,1024,256]{2,1,0:T(8,128)(2,1)} %copy-done.20, ...), custom_call_target="tpu_custom_call" | custom-call | flops 1 | bytes 1 | tf_op jit(solution)/shard_map/attention/pallas_call | solution.py:612
  76.0 7.4 %collective-permute-done.7 = bf16[512,512]{1,0:T(8,128)(2,1)} collective-permute-done((bf16[512,512]{1,0:T(8,128)(2,1)}, bf16[512,512]{1,0:T(8,128)(2,1)}, u32[]{:S(2)}, u32[]{:S(2)}) %collective-permute-start.7) | collective-permute-done | bytes 524320 | tf_op jit(solution)/shard_map/ppermute | solution.py:1123
  87.1 15.6 %attention.5 = (bf16[1024,256]{1,0:T(8,128)(2,1)}, f32[1024,256]{1,0:T(8,128)}) custom-call(s32[1]{0:T(128)} %bitcast.core_ref, bf16[1024,256]{1,0:T(8,128)(2,1)} %get-tuple-element.364.q_ref, bf16[2,1024,256]{2,1,0:T(8,128)(2,1)} %get-tuple-element.365.own_ref, bf16[2,1024,256]{2,1,0:T(8,128)(2,1)} %collective-permute-done.5.got_ref, ...), custom_call_target="tpu_custom_call" | custom-call | flops 1 | bytes 1 | tf_op jit(solution)/shard_map/attention/pallas_call | solution.py:612
  105.8 4.9 project.3
  114.7 10.5 %attention_causal.2 = (bf16[1024,256]{1,0:T(8,128)(2,1)}, f32[1024,256]{1,0:T(8,128)}) custom-call(s32[1]{0:T(128)} %bitcast.core_ref, bf16[1024,256]{1,0:T(8,128)(2,1)} %get-tuple-element.374.q_ref, bf16[2,1024,256]{2,1,0:T(8,128)(2,1)} %get-tuple-element.375.own_ref, bf16[2,1024,256]{2,1,0:T(8,128)(2,1)} %copy-done.18, ...), custom_call_target="tpu_custom_call" | custom-call | flops 1 | bytes 1 | tf_op jit(solution)/shard_map/attention_causal/pallas_call | solution.py:612
  125.2 5.0 collective-permute-start.13
  133.6 10.5 %attention_causal.3 = (bf16[1024,256]{1,0:T(8,128)(2,1)}, f32[1024,256]{1,0:T(8,128)}) custom-call(s32[1]{0:T(128)} %bitcast.core_ref, bf16[1024,256]{1,0:T(8,128)(2,1)} %get-tuple-element.388.q_ref, bf16[2,1024,256]{2,1,0:T(8,128)(2,1)} %get-tuple-element.389.own_ref, bf16[2,1024,256]{2,1,0:T(8,128)(2,1)} %copy-done.19, ...), custom_call_target="tpu_custom_call" | custom-call | flops 1 | bytes 1 | tf_op jit(solution)/shard_map/attention_causal/pallas_call | solution.py:612
  155.6 12.4 %encoder_feed.1 = (f32[1024,512]{1,0:T(8,128)}, f32[1024,512]{1,0:T(8,128)}, bf16[1024,512]{1,0:T(8,128)(2,1)}) custom-call(bf16[1024,256]{1,0:T(8,128)(2,1)} %get-tuple-element.363.o0_ref.o_ref, bf16[1024,256]{1,0:T(8,128)(2,1)} %get-tuple-element.399.o1_ref.o_ref, f32[1024,512]{1,0:T(8,128)} %get-tuple-element.400.start_ref, ...), custom_call_target="tpu_custom_call" | custom-call | flops 1 | bytes 1 | tf_op jit(solution)/shard_map/encoder_feed/pallas_call | solution.py:1063
  170.9 6.5 cross_project.1
  181.3 15.7 %attention.6 = (bf16[1024,256]{1,0:T(8,128)(2,1)}, f32[1024,256]{1,0:T(8,128)}) custom-call(s32[1]{0:T(128)} %bitcast.core_ref, bf16[1024,256]{1,0:T(8,128)(2,1)} %get-tuple-element.415.q_ref, bf16[2,1024,256]{2,1,0:T(8,128)(2,1)} %get-tuple-element.416.own_ref, bf16[2,1024,256]{2,1,0:T(8,128)(2,1)} %copy-done.22, ...), custom_call_target="tpu_custom_call" | custom-call | flops 1 | bytes 1 | tf_op jit(solution)/shard_map/attention/pallas_call | solution.py:612
  198.3 15.6 %attention.7 = (bf16[1024,256]{1,0:T(8,128)(2,1)}, f32[1024,256]{1,0:T(8,128)}) custom-call(s32[1]{0:T(128)} %bitcast.core_ref, bf16[1024,256]{1,0:T(8,128)(2,1)} %get-tuple-element.422.q_ref, bf16[2,1024,256]{2,1,0:T(8,128)(2,1)} %get-tuple-element.423.own_ref, bf16[2,1024,256]{2,1,0:T(8,128)(2,1)} %copy-done.21, ...), custom_call_target="tpu_custom_call" | custom-call | flops 1 | bytes 1 | tf_op jit(solution)/shard_map/attention/pallas_call | solution.py:612
  220.5 33.8 %decoder_feed.1 = (bf16[1024,512]{1,0:T(8,128)(2,1)}, f32[1024,512]{1,0:T(8,128)}, f32[1024,512]{1,0:T(8,128)}, bf16[1024,256]{1,0:T(8,128)(2,1)}, bf16[1024,256...) custom-call(s32[1]{0:T(128)} %bitcast.core_ref, ...), custom_call_target="tpu_custom_call" | custom-call | flops 1 | bytes 1 | tf_op jit(solution)/shard_map/decoder_feed/pallas_call | solution.py:1063
  258.3 27.6 %attention_back.4 = (bf16[1024,256]{1,0:T(8,128)(2,1)}, bf16[2,1024,256]{2,1,0:T(8,128)(2,1)}, bf16[2,1024,256]{2,1,0:T(8,128)(2,1)}) custom-call(s32[1]{0:T(128)} %bitcast.core_ref, bf16[1024,256]{1,0:T(8,128)(2,1)} %get-tuple-element.415.q_ref, bf16[2,1024,256]{2,1,0:T(8,128)(2,1)} %get-tuple-element.416.own_ref, bf16[2,1024,256]{2,1,0:T(8,128)(2,1)} %copy-done.22, ...), custom_call_target="tpu_custom_call" | custom-call | flops 1 | bytes 1 | tf_op jit(solution)/shard_map/attention_back/pallas_call | solution.py:750
  290.6 27.6 %attention_back.5 = (bf16[1024,256]{1,0:T(8,128)(2,1)}, bf16[2,1024,256]{2,1,0:T(8,128)(2,1)}, bf16[2,1024,256]{2,1,0:T(8,128)(2,1)}) custom-call(s32[1]{0:T(128)} %bitcast.core_ref, bf16[1024,256]{1,0:T(8,128)(2,1)} %get-tuple-element.422.q_ref, bf16[2,1024,256]{2,1,0:T(8,128)(2,1)} %get-tuple-element.423.own_ref, bf16[2,1024,256]{2,1,0:T(8,128)(2,1)} %copy-done.21, ...), custom_call_target="tpu_custom_call" | custom-call | flops 1 | bytes 1 | tf_op jit(solution)/shard_map/attention_back/pallas_call | solution.py:750
  324.1 29.4 %encoder_feed_back.1 = (f32[1024,512]{1,0:T(8,128)}, bf16[1024,256]{1,0:T(8,128)(2,1)}, bf16[1024,256]{1,0:T(8,128)(2,1)}, bf16[2,1408,512]{2,1,0:T(8,128)(2,1)}...) custom-call(s32[1]{0:T(128)} %bitcast.core_ref, bf16[2,1024,256]{2,1,0:T(8,128)(2,1)} %get-tuple-element.459.kv0_ref, ...), custom_call_target="tpu_custom_call" | custom-call | flops 1 | bytes 1 | tf_op jit(solution)/shard_map/encoder_feed_back/pallas_call | solution.py:1063
  358.3 8.7 %cross_project_back.1 = (f32[1024,512]{1,0:T(8,128)}, bf16[1024,256]{1,0:T(8,128)(2,1)}, bf16[1024,256]{1,0:T(8,128)(2,1)}, bf16[2,256,512]{2,1,0:T(8,128)(2,1)}...) custom-call(s32[1]{0:T(128)} %bitcast.core_ref, bf16[1024,256]{1,0:T(8,128)(2,1)} %get-tuple-element.487.q0_grad_ref, ...), custom_call_target="tpu_custom_call" | custom-call | flops 1 | bytes 1 | tf_op jit(solution)/shard_map/cross_project_back/pallas_call | solution.py:1063
  373.5 27.6 %attention_back.6 = (bf16[1024,256]{1,0:T(8,128)(2,1)}, bf16[2,1024,256]{2,1,0:T(8,128)(2,1)}, bf16[2,1024,256]{2,1,0:T(8,128)(2,1)}) custom-call(s32[1]{0:T(128)} %bitcast.core_ref, bf16[1024,256]{1,0:T(8,128)(2,1)} %get-tuple-element.364.q_ref, bf16[2,1024,256]{2,1,0:T(8,128)(2,1)} %get-tuple-element.365.own_ref, ...), custom_call_target="tpu_custom_call" | custom-call | flops 1 | bytes 1 | tf_op jit(solution)/shard_map/attention_back/pallas_call | solution.py:750
  408.5 27.4 %attention_back.7 = (bf16[1024,256]{1,0:T(8,128)(2,1)}, bf16[2,1024,256]{2,1,0:T(8,128)(2,1)}, bf16[2,1024,256]{2,1,0:T(8,128)(2,1)}) custom-call(s32[1]{0:T(128)} %bitcast.core_ref, bf16[1024,256]{1,0:T(8,128)(2,1)} %get-tuple-element.340.q_ref, bf16[2,1024,256]{2,1,0:T(8,128)(2,1)} %get-tuple-element.341.own_ref, bf16[2,1024,256]{2,1,0:T(8,128)(2,1)} %copy-done.20, ...), custom_call_target="tpu_custom_call" | custom-call | flops 1 | bytes 1 | tf_op jit(solution)/shard_map/attention_back/pallas_call | solution.py:750
  452.0 6.1 project_back.4
  458.1 5.8 project_back.5
  477.0 17.5 %attention_causal_back.2 = (bf16[1024,256]{1,0:T(8,128)(2,1)}, bf16[2,1024,256]{2,1,0:T(8,128)(2,1)}, bf16[2,1024,256]{2,1,0:T(8,128)(2,1)}) custom-call(s32[1]{0:T(128)} %bitcast.core_ref, bf16[1024,256]{1,0:T(8,128)(2,1)} %get-tuple-element.388.q_ref, bf16[2,1024,256]{2,1,0:T(8,128)(2,1)} %get-tuple-element.389.own_ref, bf16[2,1024,256]{2,1,0:T(8,128)(2,1)} %copy-done.19, ...), custom_call_target="tpu_custom_call" | custom-call | flops 1 | bytes 1 | tf_op jit(solution)/shard_map/attention_causal_back/pallas_call | solution.py:750
  500.1 9.9 %collective-permute-start.45 = (bf16[2,1024,256]{2,1,0:T(8,128)(2,1)}, bf16[2,1024,256]{2,1,0:T(8,128)(2,1)}, u32[]{:S(2)}, u32[]{:S(2)}) collective-permute-start(bf16[2,1024,256]{2,1,0:T(8,128)(2,1)} %get-tuple-element.581), channel_id=1, source_target_pairs={{0,2},{2,0},{4,6},{6,4},{8,10},{10,8},{12,14},{14,12},{16,18},{18,... | collective-permute-start | bytes 3145736 | tf_op jit(solution)/shard_map/ppermute | solution.py:1117
  515.6 6.0 project_back.6
  536.6 17.3 %attention_causal_back.3 = (bf16[1024,256]{1,0:T(8,128)(2,1)}, bf16[2,1024,256]{2,1,0:T(8,128)(2,1)}, bf16[2,1024,256]{2,1,0:T(8,128)(2,1)}) custom-call(s32[1]{0:T(128)} %bitcast.core_ref, bf16[1024,256]{1,0:T(8,128)(2,1)} %get-tuple-element.374.q_ref, bf16[2,1024,256]{2,1,0:T(8,128)(2,1)} %get-tuple-element.375.own_ref, bf16[2,1024,256]{2,1,0:T(8,128)(2,1)} %copy-done.18, ...), custom_call_target="tpu_custom_call" | custom-call | flops 1 | bytes 1 | tf_op jit(solution)/shard_map/attention_causal_back/pallas_call | solution.py:750
  557.8 9.9 %collective-permute-start.53 = (bf16[2,1024,256]{2,1,0:T(8,128)(2,1)}, bf16[2,1024,256]{2,1,0:T(8,128)(2,1)S(1)}, u32[]{:S(2)}, u32[]{:S(2)}) collective-permute-start(bf16[2,1024,256]{2,1,0:T(8,128)(2,1)} %get-tuple-element.610), channel_id=1, source_target_pairs={{0,2},{2,0},{4,6},{6,4},{8,10},{10,8},{12,14},{14,12},{16,18},{18,... | collective-permute-start | bytes 3145736 | tf_op jit(solution)/shard_map/ppermute | solution.py:1117
  575.5 5.7 project_back.7
  581.2 12.0 %collective-permute-done.54 = bf16[320,512]{1,0:T(8,128)(2,1)S(1)} collective-permute-done((bf16[320,512]{1,0:T(8,128)(2,1)S(1)}, bf16[320,512]{1,0:T(8,128)(2,1)S(1)}, u32[]{:S(2)}, u32[]{:S(2)}) %collective-permute-start.54) | collective-permute-done | bytes 327712 | tf_op jit(solution)/shard_map/ppermute | solution.py:1117
  607.6 5.2 collective-permute-done.58
  (511 shorter events, 253.1 us)
Async XLA Ops:
  5.1 32.0 %collective-permute-start = (bf16[1024,512]{1,0:T(8,128)(2,1)}, bf16[1024,512]{1,0:T(8,128)(2,1)}, u32[]{:S(2)}, u32[]{:S(2)}) collective-permute-start(bf16[1024,512]{1,0:T(8,128)(2,1)} %bitcast.1), channel_id=1, source_target_pairs={{1,2},{2,1},{5,6},{6,5},{9,10},{10,9},{13,14},{14,13},{17,18},{18,... | collective-permute-start | bytes 3145736 | tf_op jit(solution)/shard_map/ppermute | solution.py:1129
  7.8 24.8 %collective-permute-start.2 = (s32[6,1024]{0,1:T(8,128)}, s32[6,1024]{0,1:T(8,128)}, u32[]{:S(2)}, u32[]{:S(2)}) collective-permute-start(s32[6,1024]{0,1:T(8,128)} %copy.49), channel_id=1, source_target_pairs={{1,2},{2,1},{5,6},{6,5},{9,10},{10,9},{13,14},{14,13},{17,18},{18,... | collective-permute-start | bytes 73736 | tf_op jit(solution)/shard_map/ppermute | solution.py:1129
  9.3 27.8 %collective-permute-start.1 = (bf16[384,512]{1,0:T(8,128)(2,1)}, bf16[384,512]{1,0:T(8,128)(2,1)}, u32[]{:S(2)}, u32[]{:S(2)}) collective-permute-start(bf16[384,512]{1,0:T(8,128)(2,1)} %constant_dynamic-slice_fusion.19), channel_id=1, source_target_pairs={{0,1},{1,0},{2,3},{3,2},{4,5},{5,4},{6,7},{7,6},{8,9},{9,8},{10,11... | collective-permute-start | bytes 1179656 | tf_op jit(solution)/shard_map/ppermute | solution.py:1123
  55.5 27.9 %collective-permute-start.6 = (bf16[1024,512]{1,0:T(8,128)(2,1)}, bf16[1024,512]{1,0:T(8,128)(2,1)}, u32[]{:S(2)}, u32[]{:S(2)}) collective-permute-start(bf16[1024,512]{1,0:T(8,128)(2,1)} %bitcast.11), channel_id=1, source_target_pairs={{1,2},{2,1},{5,6},{6,5},{9,10},{10,9},{13,14},{14,13},{17,18},{18,... | collective-permute-start | bytes 3145736 | tf_op jit(solution)/shard_map/ppermute | solution.py:1129
  57.3 26.1 %collective-permute-start.5 = (bf16[2,1024,256]{2,1,0:T(8,128)(2,1)}, bf16[2,1024,256]{2,1,0:T(8,128)(2,1)}, u32[]{:S(2)}, u32[]{:S(2)}) collective-permute-start(bf16[2,1024,256]{2,1,0:T(8,128)(2,1)} %get-tuple-element.365.own_ref), channel_id=1, source_target_pairs={{0,2},{2,0},{4,6},{6,4},{8,10},{10,8},{12,14},{14,12},{16,18},{18,... | collective-permute-start | bytes 3145736 | tf_op jit(solution)/shard_map/ppermute | solution.py:1117
  58.5 24.8 %collective-permute-start.7 = (bf16[512,512]{1,0:T(8,128)(2,1)}, bf16[512,512]{1,0:T(8,128)(2,1)}, u32[]{:S(2)}, u32[]{:S(2)}) collective-permute-start(bf16[512,512]{1,0:T(8,128)(2,1)} %fusion.9), channel_id=1, source_target_pairs={{0,1},{1,0},{2,3},{3,2},{4,5},{5,4},{6,7},{7,6},{8,9},{9,8},{10,11... | collective-permute-start | bytes 1572872 | tf_op jit(solution)/shard_map/ppermute | solution.py:1123
  84.4 40.8 %collective-permute-start.11 = (bf16[1152,512]{1,0:T(8,128)(2,1)S(1)}, bf16[1152,512]{1,0:T(8,128)(2,1)S(1)}, u32[]{:S(2)}, u32[]{:S(2)}) collective-permute-start(bf16[1152,512]{1,0:T(8,128)(2,1)S(1)} %constant_dynamic-slice_fusion.14), channel_id=1, source_target_pairs={{0,1},{1,0},{2,3},{3,2},{4,5},{5,4},{6,7},{7,6},{8,9},{9,8},{10,11... | collective-permute-start | bytes 3538952 | tf_op jit(solution)/shard_map/ppermute | solution.py:1123
  145.3 22.8 %collective-permute-start.14 = (bf16[384,512]{1,0:T(8,128)(2,1)S(1)}, bf16[384,512]{1,0:T(8,128)(2,1)S(1)}, u32[]{:S(2)}, u32[]{:S(2)}) collective-permute-start(bf16[384,512]{1,0:T(8,128)(2,1)S(1)} %collective-permute-done.12), channel_id=1, source_target_pairs={{0,2},{2,0},{4,6},{6,4},{8,10},{10,8},{12,14},{14,12},{16,18},{18,... | collective-permute-start | bytes 1179656 | tf_op jit(solution)/shard_map/ppermute | solution.py:1117
  149.6 47.4 %collective-permute-start.17 = (bf16[1152,512]{1,0:T(8,128)(2,1)}, bf16[1152,512]{1,0:T(8,128)(2,1)}, u32[]{:S(2)}, u32[]{:S(2)}) collective-permute-start(bf16[1152,512]{1,0:T(8,128)(2,1)} %constant_dynamic-slice_fusion.12), channel_id=1, source_target_pairs={{0,1},{1,0},{2,3},{3,2},{4,5},{5,4},{6,7},{7,6},{8,9},{9,8},{10,11... | collective-permute-start | bytes 3538952 | tf_op jit(solution)/shard_map/ppermute | solution.py:1123
  178.0 35.9 %collective-permute-start.18 = (bf16[1024,1024]{1,0:T(8,128)(2,1)S(1)}, bf16[1024,1024]{1,0:T(8,128)(2,1)S(1)}, u32[]{:S(2)}, u32[]{:S(2)}) collective-permute-start(bf16[1024,1024]{1,0:T(8,128)(2,1)S(1)} %copy-done.8), channel_id=1, source_target_pairs={{1,2},{2,1},{5,6},{6,5},{9,10},{10,9},{13,14},{14,13},{17,18},{18,... | collective-permute-start | bytes 6291464 | tf_op jit(solution)/shard_map/ppermute | solution.py:1129
  213.9 40.4 %collective-permute-start.20 = (bf16[1024,512]{1,0:T(8,128)(2,1)S(1)}, bf16[1024,512]{1,0:T(8,128)(2,1)S(1)}, u32[]{:S(2)}, u32[]{:S(2)}) collective-permute-start(bf16[1024,512]{1,0:T(8,128)(2,1)S(1)} %copy-done.6), channel_id=1, source_target_pairs={{1,2},{2,1},{5,6},{6,5},{9,10},{10,9},{13,14},{14,13},{17,18},{18,... | collective-permute-start | bytes 3145736 | tf_op jit(solution)/shard_map/ppermute | solution.py:1129
  254.3 31.6 %collective-permute-start.21 = (bf16[2,1152,512]{2,1,0:T(8,128)(2,1)}, bf16[2,1152,512]{2,1,0:T(8,128)(2,1)S(1)}, u32[]{:S(2)}, u32[]{:S(2)}) collective-permute-start(bf16[2,1152,512]{2,1,0:T(8,128)(2,1)} %get-tuple-element.450), channel_id=1, source_target_pairs={{0,2},{2,0},{4,6},{6,4},{8,10},{10,8},{12,14},{14,12},{16,18},{18,... | collective-permute-start | bytes 7077896 | tf_op jit(solution)/shard_map/ppermute | solution.py:1117
  257.6 28.4 %collective-permute-start.22 = (bf16[1024,512]{1,0:T(8,128)(2,1)}, bf16[1024,512]{1,0:T(8,128)(2,1)S(1)}, u32[]{:S(2)}, u32[]{:S(2)}) collective-permute-start(bf16[1024,512]{1,0:T(8,128)(2,1)} %get-tuple-element.451), channel_id=1, source_target_pairs={{1,2},{2,1},{5,6},{6,5},{9,10},{10,9},{13,14},{14,13},{17,18},{18,... | collective-permute-start | bytes 3145736 | tf_op jit(solution)/shard_map/ppermute | solution.py:1129
  287.7 30.5 %collective-permute-start.24 = (bf16[1152,512]{1,0:T(8,128)(2,1)S(1)}, bf16[1152,512]{1,0:T(8,128)(2,1)}, u32[]{:S(2)}, u32[]{:S(2)}) collective-permute-start(bf16[1152,512]{1,0:T(8,128)(2,1)S(1)} %fusion.4), channel_id=1, source_target_pairs={{0,1},{1,0},{2,3},{3,2},{4,5},{5,4},{6,7},{7,6},{8,9},{9,8},{10,11... | collective-permute-start | bytes 3538952 | tf_op jit(solution)/shard_map/ppermute | solution.py:1123
  290.6 27.6 %collective-permute-start.23 = (bf16[2,1024,256]{2,1,0:T(8,128)(2,1)}, bf16[2,1024,256]{2,1,0:T(8,128)(2,1)}, u32[]{:S(2)}, u32[]{:S(2)}) collective-permute-start(bf16[2,1024,256]{2,1,0:T(8,128)(2,1)} %get-tuple-element.465), channel_id=1, source_target_pairs={{0,2},{2,0},{4,6},{6,4},{8,10},{10,8},{12,14},{14,12},{16,18},{18,... | collective-permute-start | bytes 3145736 | tf_op jit(solution)/shard_map/ppermute | solution.py:1117
  320.6 32.9 %collective-permute-start.26 = (bf16[576,512]{1,0:T(8,128)(2,1)S(1)}, bf16[576,512]{1,0:T(8,128)(2,1)S(1)}, u32[]{:S(2)}, u32[]{:S(2)}) collective-permute-start(bf16[576,512]{1,0:T(8,128)(2,1)S(1)} %constant_dynamic-slice_fusion.11), channel_id=1, source_target_pairs={{0,4},{2,6},{4,0},{6,2},{8,12},{10,14},{12,8},{14,10},{16,20},{18,... | collective-permute-start | bytes 1769480 | tf_op jit(solution)/shard_map/ppermute | solution.py:1117
  369.9 33.7 %collective-permute-start.30 = (bf16[1408,512]{1,0:T(8,128)(2,1)}, bf16[1408,512]{1,0:T(8,128)(2,1)}, u32[]{:S(2)}, u32[]{:S(2)}) collective-permute-start(bf16[1408,512]{1,0:T(8,128)(2,1)} %fusion.2), channel_id=1, source_target_pairs={{0,1},{1,0},{2,3},{3,2},{4,5},{5,4},{6,7},{7,6},{8,9},{9,8},{10,11... | collective-permute-start | bytes 4325384 | tf_op jit(solution)/shard_map/ppermute | solution.py:1123
  370.9 30.7 %collective-permute-start.31 = (bf16[144,512]{1,0:T(8,128)(2,1)S(1)}, bf16[144,512]{1,0:T(8,128)(2,1)S(1)}, u32[]{:S(2)}, u32[]{:S(2)}) collective-permute-start(bf16[144,512]{1,0:T(8,128)(2,1)S(1)} %constant_dynamic-slice_fusion.9), channel_id=1, source_target_pairs={{0,16},{2,18},{4,20},{6,22},{8,24},{10,26},{12,28},{14,30},{16,0},... | collective-permute-start | bytes 442376 | tf_op jit(solution)/shard_map/ppermute | solution.py:1117
  373.5 28.1 %collective-permute-start.29 = (f32[24,512]{1,0:T(8,128)S(1)}, f32[24,512]{1,0:T(8,128)S(1)}, u32[]{:S(2)}, u32[]{:S(2)}) collective-permute-start(f32[24,512]{1,0:T(8,128)S(1)} %constant_dynamic-update-slice_fusion), channel_id=1, source_target_pairs={{0,2},{2,0},{4,6},{6,4},{8,10},{10,8},{12,14},{14,12},{16,18},{18,... | collective-permute-start | bytes 147464 | tf_op jit(solution)/shard_map/ppermute | solution.py:1117
  401.1 38.1 %collective-permute-start.32 = (bf16[2,1024,256]{2,1,0:T(8,128)(2,1)}, bf16[2,1024,256]{2,1,0:T(8,128)(2,1)S(1)}, u32[]{:S(2)}, u32[]{:S(2)}) collective-permute-start(bf16[2,1024,256]{2,1,0:T(8,128)(2,1)} %get-tuple-element.522), channel_id=1, source_target_pairs={{0,2},{2,0},{4,6},{6,4},{8,10},{10,8},{12,14},{14,12},{16,18},{18,... | collective-permute-start | bytes 3145736 | tf_op jit(solution)/shard_map/ppermute | solution.py:1117
  407.0 39.3 %collective-permute-start.34 = (bf16[704,512]{1,0:T(8,128)(2,1)}, bf16[704,512]{1,0:T(8,128)(2,1)}, u32[]{:S(2)}, u32[]{:S(2)}) collective-permute-start(bf16[704,512]{1,0:T(8,128)(2,1)} %constant_dynamic-slice_fusion.8), channel_id=1, source_target_pairs={{0,4},{2,6},{4,0},{6,2},{8,12},{10,14},{12,8},{14,10},{16,20},{18,... | collective-permute-start | bytes 2162696 | tf_op jit(solution)/shard_map/ppermute | solution.py:1117
  436.0 22.1 %collective-permute-start.36 = (bf16[2,1024,256]{2,1,0:T(8,128)(2,1)}, bf16[2,1024,256]{2,1,0:T(8,128)(2,1)}, u32[]{:S(2)}, u32[]{:S(2)}) collective-permute-start(bf16[2,1024,256]{2,1,0:T(8,128)(2,1)} %get-tuple-element.536), channel_id=1, source_target_pairs={{0,2},{2,0},{4,6},{6,4},{8,10},{10,8},{12,14},{14,12},{16,18},{18,... | collective-permute-start | bytes 3145736 | tf_op jit(solution)/shard_map/ppermute | solution.py:1117
  470.5 24.1 %collective-permute-start.40 = (bf16[2,640,512]{2,1,0:T(8,128)(2,1)}, bf16[2,640,512]{2,1,0:T(8,128)(2,1)}, u32[]{:S(2)}, u32[]{:S(2)}) collective-permute-start(bf16[2,640,512]{2,1,0:T(8,128)(2,1)} %pad_maximum_fusion.9), channel_id=1, source_target_pairs={{0,2},{2,0},{4,6},{6,4},{8,10},{10,8},{12,14},{14,12},{16,18},{18,... | collective-permute-start | bytes 3932168 | tf_op jit(solution)/shard_map/ppermute | solution.py:1117
  470.5 24.0 %collective-permute-start.41 = (bf16[1024,512]{1,0:T(8,128)(2,1)}, bf16[1024,512]{1,0:T(8,128)(2,1)}, u32[]{:S(2)}, u32[]{:S(2)}) collective-permute-start(bf16[1024,512]{1,0:T(8,128)(2,1)} %convert_element_type.349), channel_id=1, source_target_pairs={{1,2},{2,1},{5,6},{6,5},{9,10},{10,9},{13,14},{14,13},{17,18},{18,... | collective-permute-start | bytes 3145736 | tf_op jit(solution)/shard_map/ppermute | solution.py:1129
  472.1 22.4 %collective-permute-start.44 = (bf16[4,144,512]{2,1,0:T(8,128)(2,1)S(1)}, bf16[4,144,512]{2,1,0:T(8,128)(2,1)}, u32[]{:S(2)}, u32[]{:S(2)}) collective-permute-start(bf16[4,144,512]{2,1,0:T(8,128)(2,1)S(1)} %pad_maximum_fusion.18), channel_id=1, source_target_pairs={{0,4},{2,6},{4,0},{6,2},{8,12},{10,14},{12,8},{14,10},{16,20},{18,... | collective-permute-start | bytes 1769480 | tf_op jit(solution)/shard_map/ppermute | solution.py:1117
  522.9 30.9 %collective-permute-start.50 = (bf16[640,512]{1,0:T(8,128)(2,1)S(1)}, bf16[640,512]{1,0:T(8,128)(2,1)S(1)}, u32[]{:S(2)}, u32[]{:S(2)}) collective-permute-start(bf16[640,512]{1,0:T(8,128)(2,1)S(1)} %copy-done.78), channel_id=1, source_target_pairs={{0,1},{1,0},{2,3},{3,2},{4,5},{5,4},{6,7},{7,6},{8,9},{9,8},{10,11... | collective-permute-start | bytes 1966088 | tf_op jit(solution)/shard_map/ppermute | solution.py:1123
  525.6 28.3 %collective-permute-start.51 = (bf16[384,512]{1,0:T(8,128)(2,1)S(1)}, bf16[384,512]{1,0:T(8,128)(2,1)S(1)}, u32[]{:S(2)}, u32[]{:S(2)}) collective-permute-start(bf16[384,512]{1,0:T(8,128)(2,1)S(1)} %fusion.12), channel_id=1, source_target_pairs={{0,1},{1,0},{2,3},{3,2},{4,5},{5,4},{6,7},{7,6},{8,9},{9,8},{10,11... | collective-permute-start | bytes 1179656 | tf_op jit(solution)/shard_map/ppermute | solution.py:1123
  525.9 28.0 %collective-permute-start.52 = (bf16[2,176,512]{2,1,0:T(8,128)(2,1)}, bf16[2,176,512]{2,1,0:T(8,128)(2,1)S(1)}, u32[]{:S(2)}, u32[]{:S(2)}) collective-permute-start(bf16[2,176,512]{2,1,0:T(8,128)(2,1)} %pad_maximum_fusion.22), channel_id=1, source_target_pairs={{0,8},{2,10},{4,12},{6,14},{8,0},{10,2},{12,4},{14,6},{16,24},{18,... | collective-permute-start | bytes 1081352 | tf_op jit(solution)/shard_map/ppermute | solution.py:1117
  567.8 25.4 %collective-permute-start.55 = (bf16[4,176,512]{2,1,0:T(8,128)(2,1)}, bf16[4,176,512]{2,1,0:T(8,128)(2,1)}, u32[]{:S(2)}, u32[]{:S(2)}) collective-permute-start(bf16[4,176,512]{2,1,0:T(8,128)(2,1)} %pad_maximum_fusion.16), channel_id=1, source_target_pairs={{0,4},{2,6},{4,0},{6,2},{8,12},{10,14},{12,8},{14,10},{16,20},{18,... | collective-permute-start | bytes 2162696 | tf_op jit(solution)/shard_map/ppermute | solution.py:1117
  570.6 22.5 %collective-permute-start.54 = (bf16[320,512]{1,0:T(8,128)(2,1)S(1)}, bf16[320,512]{1,0:T(8,128)(2,1)S(1)}, u32[]{:S(2)}, u32[]{:S(2)}) collective-permute-start(bf16[320,512]{1,0:T(8,128)(2,1)S(1)} %constant_dynamic-slice_fusion.5), channel_id=1, source_target_pairs={{0,4},{2,6},{4,0},{6,2},{8,12},{10,14},{12,8},{14,10},{16,20},{18,... | collective-permute-start | bytes 983048 | tf_op jit(solution)/shard_map/ppermute | solution.py:1117
  601.3 46.2 %collective-permute-start.63 = (bf16[8,176,512]{2,1,0:T(8,128)(2,1)S(1)}, bf16[8,176,512]{2,1,0:T(8,128)(2,1)}, u32[]{:S(2)}, u32[]{:S(2)}) collective-permute-start(bf16[8,176,512]{2,1,0:T(8,128)(2,1)S(1)} %pad_maximum_fusion.7.mine_ref), channel_id=1, source_target_pairs={{0,2},{2,0},{4,6},{6,4},{8,10},{10,8},{12,14},{14,12},{16,18},{18,... | collective-permute-start | bytes 4325384 | tf_op jit(solution)/shard_map/ppermute | solution.py:1117
  602.8 38.6 %collective-permute-start.56 = (bf16[1024,512]{1,0:T(8,128)(2,1)}, bf16[1024,512]{1,0:T(8,128)(2,1)}, u32[]{:S(2)}, u32[]{:S(2)}) collective-permute-start(bf16[1024,512]{1,0:T(8,128)(2,1)} %convert_element_type.371), channel_id=1, source_target_pairs={{1,2},{2,1},{5,6},{6,5},{9,10},{10,9},{13,14},{14,13},{17,18},{18,... | collective-permute-start | bytes 3145736 | tf_op jit(solution)/shard_map/ppermute | solution.py:1129
  (150 other events, 1421.7 us)

commit v3 on v2

--- a/solution.py
+++ b/solution.py
@@ -518,7 +518,7 @@
 TN = (((0,), (0,)), ((), ()))
 HALF = D // 2
 VMEM_BYTES = 56 * 1024 * 1024
-NO_COST = pl.CostEstimate(flops=1, bytes_accessed=1, transcendentals=0)
+COST = pl.CostEstimate(flops=1, bytes_accessed=1, transcendentals=0)
 
 
 def dot_nn(a, b):
@@ -538,104 +538,120 @@
     return lane < DH, lane % DH
 
 
+def softmax_tasks(tasks, scores_of, after):
+    ahead = scores_of(*tasks[0])
+    for i, task in enumerate(tasks):
+        now = ahead
+        if i + 1 < len(tasks):
+            ahead = scores_of(*tasks[i + 1])
+        after(now, *task)
+
+
 def forward_kernel(
-    core_ref, q_ref, own_ref, got_ref, query_ext_ref, key_ext_ref, o_ref, log_ref, keys, values,
-    *, causal, rows,
+    core_ref, q_ref, own_ref, got_ref, hot_ref, key_hot_ref, o_ref, log_ref, keys, values, *, causal
 ):
-    step = pl.program_id(1)
-    block = q_ref.shape[0]
-    quarter = own_ref.shape[1] // 2
+    n = q_ref.shape[0]
+    chunk = n // 2
     core = core_ref[0]
-    left, _ = lanes()
-
-    @pl.when(step == 0)
-    def _():
-        n = own_ref.shape[1]
-        for ref, of in ((own_ref, core), (got_ref, 1 - core)):
-            here = pl.ds(pl.multiple_of(of * n, n), n)
-            k, v, ext = ref[0], ref[1], key_ext_ref[here, :]
-            ones = jnp.ones_like(v)
-            keys[0, here, :] = jnp.where(left, k, ext)
-            keys[1, here, :] = jnp.where(left, ext, k)
-            values[0, here, :] = jnp.where(left, v, ones)
-            values[1, here, :] = jnp.where(left, ones, v)
-
-    def attend(count, first_row):
-        for begin in range(0, block, rows):
-            here = slice(begin, begin + rows)
-            pair, ext = q_ref[here, :], query_ext_ref[here, :]
-            mixed, highest = [], []
-            for head in range(2):
-                q = jnp.where(left, pair, ext) if head == 0 else jnp.where(left, ext, pair)
-                clear = count - quarter if causal else count
-                parts = []
-                if clear:
-                    parts.append((dot_nt(q, keys[head, :clear, :]), values[head, :clear, :]))
-                if causal:
-                    scores = dot_nt(q, keys[head, clear:count, :])
-                    row = lax.broadcasted_iota(jnp.int32, scores.shape, 0) + (first_row + begin)
-                    column = lax.broadcasted_iota(jnp.int32, scores.shape, 1)
-                    scores = jnp.where(column <= row, scores, BIG)
-                    parts.append((scores, values[head, clear:count, :]))
-                top = jnp.max(parts[0][0], axis=1, keepdims=True)
-                for scores, _ in parts[1:]:
-                    top = jnp.maximum(top, jnp.max(scores, axis=1, keepdims=True))
-                total = 0.0
-                for scores, v in parts:
-                    total = total + dot_nn(jnp.exp2(scores - top).astype(BF), v)
-                mixed.append(total)
-                highest.append(top)
-            sums = jnp.where(left, mixed[1], mixed[0])
-            out = jnp.where(left, mixed[0], mixed[1]) / pltpu.roll(sums, DH, 1)
-            o_ref[here, :] = out.astype(BF)
-            log_ref[here, :] = jnp.where(left, highest[1], highest[0]) + jnp.log2(sums)
+    left, lane = lanes()
+    for ref, of in ((own_ref, core), (got_ref, 1 - core)):
+        here = pl.ds(pl.multiple_of(of * n, n), n)
+        k, hot = ref[0], key_hot_ref[here, :]
+        ext = jnp.where((lane >= 8) & (lane < 11), jnp.ones_like(hot), hot)
+        keys[0, here, :] = jnp.where(left, k, ext)
+        keys[1, here, :] = jnp.where(left, ext, k)
+        turned = ref[1].T
+        ones = jnp.ones((DH, n), BF)
+        values[0, :, here] = jnp.concatenate([turned[:DH], ones])
+        values[1, :, here] = jnp.concatenate([ones, turned[DH:]])
+    pair = q_ref[...]
+    mine = hot_ref[pl.ds(pl.multiple_of(core * n, n), n), :].astype(F32)
+    ext = jnp.where(lane < 8, (1.0 - mine) * BIG, 0.0).astype(BF)
+    queries = jnp.where(left, pair, ext), jnp.where(left, ext, pair)
+
+    def run(tasks, rows):
+        state = {}
+
+        def scores_of(head, query, key, cut):
+            q = queries[head][query * rows : (query + 1) * rows]
+            scores = dot_nt(keys[head, key * chunk : (key + 1) * chunk, :], q)
+            if cut:
+                at = lax.broadcasted_iota(jnp.int32, scores.shape, 0)
+                to = lax.broadcasted_iota(jnp.int32, scores.shape, 1)
+                scores = jnp.where(at <= to, scores, BIG)
+            return scores
+
+        def after(scores, head, query, key, cut):
+            top = jnp.max(scores, axis=0, keepdims=True)
+            total = 0.0
+            if (head, query) in state:
+                old_top, total = state[head, query]
+                top = jnp.maximum(top, old_top)
+                total = total * jnp.exp2(old_top - top)
+            probs = jnp.exp2(scores - top).astype(BF)
+            total = total + dot_nn(values[head, :, key * chunk : (key + 1) * chunk], probs)
+            state[head, query] = top, total
+
+        softmax_tasks(tasks, scores_of, after)
+        for query in range(n // rows):
+            (top0, total0), (top1, total1) = state[0, query], state[1, query]
+            out = jnp.concatenate([total0[:DH] / total0[DH:], total1[DH:] / total1[:DH]])
+            logs = jnp.concatenate([top1 + jnp.log2(total1[:DH]), top0 + jnp.log2(total0[DH:])])
+            here = slice(query * rows, (query + 1) * rows)
+            o_ref[here, :] = out.T.astype(BF)
+            log_ref[here, :] = logs.T
 
     if not causal:
-        attend(2 * own_ref.shape[1], None)
+        run([(head, 0, key, False) for head in range(2) for key in range(4)], n)
     else:
-        each = quarter // block
-        piece = step // each
-        place = 2 * core + piece
-        for case in range(4):
-
-            @pl.when(place == case)
+        for case in range(2):
+
+            @pl.when(core == case)
             def _(case=case):
-                attend((case + 1) * quarter, (step - piece * each) * block)
-
-
-def attention_forward_half(core, q, own, got, query_ext, key_ext, causal):
+                run(
+                    [
+                        (head, query, key, key == 2 * case + query)
+                        for head in range(2)
+                        for query in range(2)
+                        for key in range(2 * case + query + 1)
+                    ],
+                    chunk,
+                )
+
+
+def heads_forward(core, q, own, got, hot, key_hot, causal):
     n, width = q.shape
     length = 2 * n
-    block, rows = 512, 256
-    keys = pl.BlockSpec((2, n, 128), lambda p, b: (0, 0, p))
-    queries = pl.BlockSpec((block, 128), lambda p, b: (b, p))
+    keys = pl.BlockSpec((2, n, 128), lambda p: (0, 0, p))
+    queries = pl.BlockSpec((n, 128), lambda p: (0, p))
+    table = pl.BlockSpec((length, 128), lambda p: (0, 0))
     return pl.pallas_call(
-        partial(forward_kernel, causal=causal, rows=rows),
-        grid=(width // 128, n // block),
+        partial(forward_kernel, causal=causal),
+        grid=(width // 128,),
         in_specs=[
             pl.BlockSpec(memory_space=pltpu.SMEM),
             queries,
             keys,
             keys,
-            pl.BlockSpec((block, 128), lambda p, b: (b, 0)),
-            pl.BlockSpec((length, 128), lambda p, b: (0, 0)),
+            table,
+            table,
         ],
         out_specs=[queries, queries],
         out_shape=[jax.ShapeDtypeStruct((n, width), BF), jax.ShapeDtypeStruct((n, width), F32)],
-        scratch_shapes=[pltpu.VMEM((2, length, 128), BF), pltpu.VMEM((2, length, 128), BF)],
+        scratch_shapes=[pltpu.VMEM((2, length, 128), BF), pltpu.VMEM((2, 128, length), BF)],
         compiler_params=pltpu.CompilerParams(vmem_limit_bytes=VMEM_BYTES),
-        cost_estimate=NO_COST,
+        cost_estimate=COST,
         name="attention_causal" if causal else "attention",
-    )(core, q, own, got, query_ext, key_ext)
+    )(core, q, own, got, hot, key_hot)
 
 
 def backward_kernel(
-    core_ref, q_ref, own_ref, got_ref, query_ext_ref, own_ext_ref, got_ext_ref, grad_ref, o_ref, log_ref,
-    q_grad_ref, own_grad_ref, got_grad_ref, queries, grads, q_total, *, causal,
+    core_ref, q_ref, own_ref, got_ref, hot_ref, key_hot_ref, grad_ref, o_ref, log_ref,
+    q_grad_ref, own_grad_ref, got_grad_ref, queries, grads, q_turned, grad_turned, q_total, *, causal,
 ):
     step = pl.program_id(1)
     n, block = q_ref.shape[0], own_ref.shape[1]
-    quarter = n // 2
+    chunk = n // 2
     blocks = n // block
     core = core_ref[0]
     left, lane = lanes()
@@ -646,12 +662,14 @@
         high = log.astype(BF).astype(F32)
         middle = (log - high).astype(BF).astype(F32)
         low = log - high - middle
-        ext = query_ext_ref[...].astype(F32)
+        mine = hot_ref[pl.ds(pl.multiple_of(core * n, n), n), :].astype(F32)
+        ext = jnp.where(lane < 8, (1.0 - mine) * BIG, 0.0)
         ext = jnp.where(lane == 10, -low, ext)
         ext = jnp.where(lane == 9, -middle, jnp.where(lane == 8, -high, ext)).astype(BF)
         pair = q_ref[...]
         queries[0] = jnp.where(left, pair, ext)
         queries[1] = jnp.where(left, ext, pair)
+        q_turned[...] = pair.T
         pair = grad_ref[...]
         product = pair.astype(F32) * o_ref[...].astype(F32)
         high = product.astype(BF)
@@ -664,39 +682,45 @@
         ext = jnp.where(lane == 8, -high, jnp.where(lane == 9, high - inner, 0.0)).astype(BF)
         grads[0] = jnp.where(left, pair, ext)
         grads[1] = jnp.where(left, ext, pair)
+        grad_turned[...] = pair.T
         q_total[...] = jnp.zeros_like(q_total)
 
     own = step < blocks
     k = jnp.where(own, own_ref[0], got_ref[0])
     v = jnp.where(own, own_ref[1], got_ref[1])
-    ext = jnp.where(own, own_ext_ref[...], got_ext_ref[...])
+    place = jnp.where(own, core * n + step * block, (1 - core) * n + (step - blocks) * block)
+    hot = key_hot_ref[pl.ds(pl.multiple_of(place, block), block), :]
     ones = jnp.ones_like(v)
+    ext = jnp.where((lane >= 8) & (lane < 11), ones, hot)
     keys = (jnp.where(left, k, ext), jnp.where(left, ext, k))
     values = (jnp.where(left, v, ones), jnp.where(left, ones, v))
-    k_turned = k.T
-
-    def part(begin, rows, diagonal):
-        k_grads, v_grads = [], []
-        here = slice(begin, begin + rows)
-        for head in range(2):
-            q, grad = queries[head, here, :], grads[head, here, :]
-            scores = dot_nt(keys[head], q)
-            if diagonal is not None:
-                key = lax.broadcasted_iota(jnp.int32, scores.shape, 0) + diagonal
-                query = lax.broadcasted_iota(jnp.int32, scores.shape, 1)
-                scores = jnp.where(key <= query, scores, BIG)
-            probs = jnp.exp2(scores)
-            score_grad = (probs * dot_nt(values[head], grad)).astype(BF)
-            v_grads.append(dot_nn(probs.astype(BF), grad))
-            k_grads.append(dot_nn(score_grad, q))
-            mine = slice(DH * head, DH * (head + 1))
-            q_total[mine, here] += dot_nn(k_turned[mine], score_grad)
-        return jnp.where(left, k_grads[0], k_grads[1]), jnp.where(left, v_grads[0], v_grads[1])
+
+    def run(tasks):
+        k_grads, v_grads = [0.0, 0.0], [0.0, 0.0]
+
+        def scores_of(head, query, cut):
+            here = slice(query * chunk, (query + 1) * chunk)
+            scores = dot_nt(queries[head, here, :], keys[head])
+            if cut:
+                to = lax.broadcasted_iota(jnp.int32, scores.shape, 0)
+                at = lax.broadcasted_iota(jnp.int32, scores.shape, 1)
+                scores = jnp.where(at <= to, scores, BIG)
+            return scores, dot_nt(grads[head, here, :], values[head])
+
+        def after(products, head, query, cut):
+            here = slice(query * chunk, (query + 1) * chunk)
+            probs = jnp.exp2(products[0])
+            score_grad = (probs * products[1]).astype(BF)
+            v_grads[head] = v_grads[head] + dot_nn(grad_turned[:, here], probs.astype(BF))
+            k_grads[head] = k_grads[head] + dot_nn(q_turned[:, here], score_grad)
+            q_total[head, here, :] += dot_nn(score_grad, keys[head])
+
+        softmax_tasks(tasks, scores_of, after)
+        k_grad = jnp.concatenate([k_grads[0][:DH], k_grads[1][DH:]]).T
+        v_grad = jnp.concatenate([v_grads[0][:DH], v_grads[1][DH:]]).T
+        put((k_grad * math.log(2.0)).astype(BF), v_grad.astype(BF))
 
     def put(k_grad, v_grad):
-        k_grad = (k_grad * math.log(2.0)).astype(BF)
-        v_grad = v_grad.astype(BF)
-
         @pl.when(own)
         def _():
             own_grad_ref[0] = k_grad
@@ -708,71 +732,69 @@
             got_grad_ref[1] = v_grad
 
     if not causal:
-        put(*part(0, n, None))
+        run([(head, query, False) for head in range(2) for query in range(2)])
     else:
-        each = quarter // block
-        local_step = jnp.where(own, step, step - blocks)
-        piece = local_step // each
-        key_place = 2 * jnp.where(own, core, 1 - core) + piece
-        diagonal = (local_step - piece * each) * block
-        first, second = 2 * core, 2 * core + 1
-        skip, cut, whole = 0, 1, 2
-
-        def kind(query_place):
-            return jnp.where(key_place > query_place, skip, jnp.where(key_place == query_place, cut, whole))
-
-        for kinds in ((skip, skip), (skip, cut), (cut, whole), (whole, whole)):
-
-            @pl.when(jnp.logical_and(kind(first) == kinds[0], kind(second) == kinds[1]))
-            def _(kinds=kinds):
-                k_grad = v_grad = jnp.zeros((block, 128), F32)
-                for begin, how in zip((0, quarter), kinds):
-                    if how != skip:
-                        more = part(begin, quarter, diagonal if how == cut else None)
-                        k_grad, v_grad = k_grad + more[0], v_grad + more[1]
-                put(k_grad, v_grad)
+        @pl.when(jnp.logical_not(own) & (core == 0))
+        def _():
+            put(jnp.zeros((block, 128), BF), jnp.zeros((block, 128), BF))
+
+        @pl.when(jnp.logical_not(own) & (core == 1))
+        def _():
+            run([(head, query, False) for head in range(2) for query in range(2)])
+
+        for case in range(2):
+
+            @pl.when(step == case)
+            def _(case=case):
+                run([(head, query, query == case) for head in range(2) for query in range(case, 2)])
 
     @pl.when(step == 2 * blocks - 1)
     def _():
-        q_grad_ref[...] = (q_total[...] * DH**-0.5).T.astype(BF)
-
-
-def attention_backward_half(core, kept, grad, causal):
-    q, own, got, query_ext, own_ext, got_ext, o, log = kept
-    n, width = q.shape
-    block = 512
-    blocks = n // block
+        q_grad_ref[...] = (jnp.where(left, q_total[0], q_total[1]) * DH**-0.5).astype(BF)
+
+
+def heads_backward(core, kept, grad, causal, begin=0, width=HALF):
+    q, own, got, hot, key_hot, o, log = kept
+    n = q.shape[0]
+    skip = begin // 128
+    block = n // 2
+    blocks = 2
     first = lambda b: jnp.minimum(b, blocks - 1)
     second = lambda b: jnp.maximum(b - blocks, 0)
-    whole = pl.BlockSpec((n, 128), lambda p, b: (0, p))
-    own_keys = pl.BlockSpec((2, block, 128), lambda p, b: (0, first(b), p))
-    got_keys = pl.BlockSpec((2, block, 128), lambda p, b: (0, second(b), p))
+    whole = pl.BlockSpec((n, 128), lambda p, b: (0, skip + p))
+    whole_out = pl.BlockSpec((n, 128), lambda p, b: (0, p))
+    table = pl.BlockSpec((2 * n, 128), lambda p, b: (0, 0))
+
+    def keys(part, skip):
+        return pl.BlockSpec((2, block, 128), lambda p, b: (0, part(b), skip + p))
+
     return pl.pallas_call(
         partial(backward_kernel, causal=causal),
         grid=(width // 128, 2 * blocks),
         in_specs=[
             pl.BlockSpec(memory_space=pltpu.SMEM),
             whole,
-            own_keys,
-            got_keys,
-            pl.BlockSpec((n, 128), lambda p, b: (0, 0)),
-            pl.BlockSpec((block, 128), lambda p, b: (first(b), 0)),
-            pl.BlockSpec((block, 128), lambda p, b: (second(b), 0)),
+            keys(first, skip),
+            keys(second, skip),
+            table,
+            table,
             whole,
             whole,
             whole,
         ],
-        out_specs=[whole, own_keys, got_keys],
-        out_shape=[jax.ShapeDtypeStruct(s, BF) for s in ((n, width), own.shape, own.shape)],
+        out_specs=[whole_out, keys(first, 0), keys(second, 0)],
+        out_shape=[jax.ShapeDtypeStruct(s, BF) for s in ((n, width), (2, n, width), (2, n, width))],
         scratch_shapes=[
             pltpu.VMEM((2, n, 128), BF),
             pltpu.VMEM((2, n, 128), BF),
-            pltpu.VMEM((128, n), F32),
+            pltpu.VMEM((128, n), BF),
+            pltpu.VMEM((128, n), BF),
+            pltpu.VMEM((2, n, 128), F32),
         ],
         compiler_params=pltpu.CompilerParams(vmem_limit_bytes=VMEM_BYTES),
-        cost_estimate=NO_COST,
+        cost_estimate=COST,
         name="attention_causal_back" if causal else "attention_back",
-    )(core, q, own, got, query_ext, own_ext, got_ext, grad, o, log)
+    )(core, q, own, got, hot, key_hot, grad, o, log)
 
 
 def fold_dot(x, w):
@@ -884,11 +906,27 @@
             small_ref[...] = small_acc[...]
 
 
+def join(core_ref, *triples):
+    @pl.when(pl.program_id(0) == 0)
+    def _():
+        for near_ref, far_ref, whole in triples:
+            rows = near_ref.shape[0]
+            for part, ref in ((core_ref[0], near_ref), (1 - core_ref[0], far_ref)):
+                whole[pl.ds(pl.multiple_of(part * rows, 16), rows), :] = ref[...]
+
+
+def second_part(core_ref, near_ref, far_ref):
+    return jnp.where(core_ref[0] == 1, near_ref[...], far_ref[...])
+
+
 def pre_kernel(
-    rows_ref, place_ref, own_ref, other_ref,
+    core_ref, rows_ref, got_ref, place_ref, own_ref, near_ref, far_ref,
     start_ref, q0_ref, q1_ref, kv0_ref, kv1_ref,
+    other_ref,
 ):
-    start = rows_ref[...].astype(F32) + place_ref[...]
+    join(core_ref, (near_ref, far_ref, other_ref))
+    rows = jnp.where(core_ref[1] == 1, rows_ref[...].astype(F32), got_ref[...].astype(F32))
+    start = rows + place_ref[...]
     start_ref[...] = start
     low = start.astype(BF)
     for ref, q_ref, kv_ref in ((own_ref, q0_ref, kv0_ref), (other_ref, q1_ref, kv1_ref)):
@@ -899,9 +937,11 @@
 
 
 def enc_post_kernel(
-    o0_ref, o1_ref, start_ref, runs_ref, own_ref, other_ref, small_ref,
+    core_ref, o0_ref, o1_ref, start_ref, runs_ref, own_ref, near_ref, far_ref, small_ref,
     sum_one_ref, sum_two_ref, states_ref,
+    other_ref,
 ):
+    join(core_ref, (near_ref, far_ref, other_ref))
     start = start_ref[...]
     sum_one = start + dot_nn(o0_ref[...], own_ref[:HALF, :]) + dot_nn(o1_ref[...], other_ref[:HALF, :])
     sum_one_ref[...] = sum_one
@@ -914,11 +954,14 @@
 
 
 def dec_mid_kernel(
-    o0_ref, o1_ref, start_ref, states_ref, proj_own_ref, proj_other_ref, own_ref, other_ref, small_ref,
+    core_ref, o0_ref, o1_ref, start_ref, states_ref, proj_own_ref, proj_near_ref, proj_far_ref,
+    own_ref, near_ref, far_ref, small_ref,
     sum_ref, q0_ref, q1_ref, kv0_ref, kv1_ref,
+    other_ref,
 ):
+    join(core_ref, (near_ref, far_ref, other_ref))
     total = start_ref[...] + dot_nn(o0_ref[...], proj_own_ref[...])
-    total = total + dot_nn(o1_ref[...], proj_other_ref[...])
+    total = total + dot_nn(o1_ref[...], second_part(core_ref, proj_near_ref, proj_far_ref))
     sum_ref[...] = total
     middle, _, _ = norm(total, small_ref[0:1, :], small_ref[1:2, :])
     low = middle.astype(BF)
@@ -931,11 +974,12 @@
 
 
 def dec_post_kernel(
-    core_ref, o0_ref, o1_ref, sum_one_ref, start_ref, runs_ref, cot_ref, own_ref, other_ref, small_ref,
+    core_ref, o0_ref, o1_ref, sum_one_ref, start_ref, runs_ref, cot_ref, own_ref, near_ref, far_ref, small_ref,
     states_ref, start_grad_ref, sum_grad_ref, o0_grad_ref, o1_grad_ref,
     keep_ref, send_ref, small_grad_ref,
-    acc, small_acc,
+    acc, small_acc, other_ref,
 ):
+    join(core_ref, (near_ref, far_ref, other_ref))
     first_step(acc, small_acc)
     start = start_ref[...]
     projs = own_ref[:HALF, :], other_ref[:HALF, :]
@@ -969,23 +1013,24 @@
 
 def dec_mid_back_kernel(
     core_ref, q0_grad_ref, q1_grad_ref, sum_grad_ref, sum_one_ref, start_grad_ref, o0_ref, o1_ref,
-    cq_own_ref, cq_other_ref, proj_own_ref, proj_other_ref, small_ref,
+    cq_own_ref, cq_near_ref, cq_far_ref, proj_own_ref, proj_near_ref, proj_far_ref, small_ref,
     out_ref, o0_grad_ref, o1_grad_ref, keep_ref, send_ref, small_grad_ref,
     acc, small_acc,
 ):
+    cq_other = jnp.where(core_ref[0] == 0, cq_near_ref[:HALF, :], cq_far_ref[:HALF, :])
     first_step(acc, small_acc)
     gain = small_ref[0:1, :]
     middle, unit, scale = norm(sum_one_ref[...], gain, small_ref[1:2, :])
     low = middle.astype(BF)
     grad = sum_grad_ref[...]
-    for which, (ref, part_ref) in enumerate(((cq_own_ref, q0_grad_ref), (cq_other_ref, q1_grad_ref))):
-        grad = grad + fold_dot_t(part_ref[...], ref[...])
+    for which, (w, part_ref) in enumerate(((cq_own_ref[...], q0_grad_ref), (cq_other, q1_grad_ref))):
+        grad = grad + fold_dot_t(part_ref[...], w)
         acc[which, :HALF, :] += fold_grad(low, part_ref[...])
     small_acc[0:1, :] += over_rows(grad * unit)
     small_acc[1:2, :] += over_rows(grad)
     grad = norm_back(grad, unit, scale, gain)
     out_ref[...] = start_grad_ref[...] + grad
-    projs = proj_own_ref[...], proj_other_ref[...]
+    projs = proj_own_ref[...], second_part(core_ref, proj_near_ref, proj_far_ref)
     proj_back((o0_ref, o1_ref), grad.astype(BF), projs, acc, HALF, (o0_grad_ref, o1_grad_ref))
     last_step(core_ref, acc, keep_ref, send_ref, small_acc, small_grad_ref)
 
@@ -996,10 +1041,11 @@
 
 def enc_back_kernel(
     core_ref, kv0_ref, kv1_ref, got0_ref, got1_ref, states_ref, cot_ref, start_ref, sum_one_ref, sum_two_ref,
-    o0_ref, o1_ref, runs_ref, cross_own_ref, cross_other_ref, own_ref, other_ref, small_ref,
+    o0_ref, o1_ref, runs_ref, cross_own_ref, cross_near_ref, cross_far_ref, own_ref, near_ref, far_ref, small_ref,
     out_ref, o0_grad_ref, o1_grad_ref, keep_ref, send_ref, small_grad_ref,
-    acc, small_acc,
+    acc, small_acc, cross_other_ref, other_ref,
 ):
+    join(core_ref, (near_ref, far_ref, other_ref), (cross_near_ref, cross_far_ref, cross_other_ref))
     first_step(acc, small_acc)
     states = states_ref[...]
     grad = cot_ref[...].astype(F32)
@@ -1030,24 +1076,74 @@
     last_step(core_ref, acc, keep_ref, send_ref, small_acc, small_grad_ref)
 
 
-def qkv_back_kernel(
-    core_ref, q_grad_ref, kv_ref, got_ref, start_ref, base_ref, w_ref,
+def qkv_back(low, parts, w_ref, acc, which):
+    grad = 0.0
+    for kind, part in enumerate(parts):
+        rows = slice(kind * HALF, (kind + 1) * HALF)
+        grad = grad + fold_dot_t(part, w_ref[rows, :])
+        acc[which, rows, :] += fold_grad(low, part)
+    return grad
+
+
+def qkv_parts(*triples):
+    def beside(parts):
+        return parts[0] if len(parts) == 1 else jnp.concatenate(parts, axis=1)
+
+    return (
+        beside([q_ref[...] for q_ref, _, _ in triples]),
+        beside([kv_total(kv_ref, got_ref, 0) for _, kv_ref, got_ref in triples]),
+        beside([kv_total(kv_ref, got_ref, 1) for _, kv_ref, got_ref in triples]),
+    )
+
+
+def own_qkv_back_kernel(
+    core_ref, qa_ref, kva_ref, gota_ref, qb_ref, kvb_ref, gotb_ref, start_ref, base_ref, w_ref,
     out_ref, keep_ref, send_ref,
     acc,
 ):
     first_step(acc)
     low = start_ref[...].astype(BF)
-    grad = base_ref[...]
-    parts = q_grad_ref[...], kv_total(kv_ref, got_ref, 0), kv_total(kv_ref, got_ref, 1)
-    for kind, part in enumerate(parts):
-        rows = slice(kind * HALF, (kind + 1) * HALF)
-        grad = grad + fold_dot_t(part, w_ref[rows, :])
-        acc[0, rows, :] += fold_grad(low, part)
-    out_ref[...] = grad
+    parts = qkv_parts((qa_ref, kva_ref, gota_ref), (qb_ref, kvb_ref, gotb_ref))
+    out_ref[...] = base_ref[...] + qkv_back(low, parts, w_ref, acc, 0)
     last_step(core_ref, acc, keep_ref, send_ref)
 
 
-def rows_call(kernel, name, by_rows, whole, row_outs, whole_outs=(), scratch=(), core=None, block=512):
+def other_qkv_back_kernel(
+    core_ref, qa_ref, kva_ref, gota_ref, qb_ref, kvb_ref, gotb_ref, start_ref, base_ref, near_ref, far_ref,
+    out_ref, keep_ref, send_ref,
+    acc, other_ref,
+):
+    join(core_ref, (near_ref, far_ref, other_ref))
+    own_qkv_back_kernel(
+        core_ref, qa_ref, kva_ref, gota_ref, qb_ref, kvb_ref, gotb_ref, start_ref, base_ref, other_ref,
+        out_ref, keep_ref, send_ref, acc,
+    )
+
+
+def both_qkv_back_kernel(
+    core_ref, q0_grad_ref, kv0_ref, got0_ref, q1_grad_ref, kv1_ref, got1_ref, start_ref, base_ref,
+    own_ref, near_ref, far_ref, more_keep_ref, more_send_ref,
+    out_ref, keep_ref, send_ref,
+    acc, other_ref,
+):
+    first_step(acc)
+    join(core_ref, (near_ref, far_ref, other_ref))
+    low = start_ref[...].astype(BF)
+    grad = base_ref[...] + qkv_back(low, qkv_parts((q0_grad_ref, kv0_ref, got0_ref)), own_ref, acc, 0)
+    out_ref[...] = grad + qkv_back(low, qkv_parts((q1_grad_ref, kv1_ref, got1_ref)), other_ref, acc, 1)
+
+    @pl.when(pl.program_id(0) == pl.num_programs(0) - 1)
+    def _():
+        rows = acc.shape[1] // 2
+        ends = (core_ref[0], keep_ref, more_keep_ref), (1 - core_ref[0], send_ref, more_send_ref)
+        for part, ref, more_ref in ends:
+            here = pl.ds(pl.multiple_of(part * rows, 16), rows)
+            for which in range(2):
+                ref[which, :rows, :] = acc[which, here, :].astype(BF)
+                ref[which, rows:, :] = more_ref[which]
+
+
+def rows_call(kernel, name, core, by_rows, whole, row_outs, whole_outs=(), scratch=(), block=512):
     n = by_rows[0].shape[-2]
 
     def row_spec(shape):
@@ -1056,46 +1152,76 @@
         return pl.BlockSpec((block, shape[1]), lambda i: (i, 0))
 
     def whole_spec(entry):
-        array, rows, index = entry if isinstance(entry, tuple) else (entry, entry.shape[0], 0)
+        if not isinstance(entry, tuple):
+            return pl.BlockSpec(entry.shape, lambda i: (0,) * entry.ndim, pipeline_mode=pl.Buffered(1))
+        array, rows, index = entry
         return pl.BlockSpec((rows, array.shape[1]), lambda i: (index, 0), pipeline_mode=pl.Buffered(1))
 
     arrays = [e[0] if isinstance(e, tuple) else e for e in whole]
     return pl.pallas_call(
         kernel,
         grid=(n // block,),
-        in_specs=([] if core is None else [pl.BlockSpec(memory_space=pltpu.SMEM)])
+        in_specs=[pl.BlockSpec(memory_space=pltpu.SMEM)]
         + [row_spec(a.shape) for a in by_rows]
         + [whole_spec(e) for e in whole],
         out_specs=[row_spec(s) for s, _ in row_outs]
         + [pl.BlockSpec(s, lambda i, s=s: (0,) * len(s)) for s, _ in whole_outs],
         out_shape=[jax.ShapeDtypeStruct(s, t) for s, t in [*row_outs, *whole_outs]],
-        scratch_shapes=[pltpu.VMEM(s, F32) for s in scratch],
+        scratch_shapes=[pltpu.VMEM(*s) for s in scratch],
         compiler_params=pltpu.CompilerParams(vmem_limit_bytes=VMEM_BYTES),
-        cost_estimate=NO_COST,
+        cost_estimate=COST,
         name=name,
-    )(*([] if core is None else [core]), *by_rows, *arrays)
-
-
-def in_order_kernel(place_ref, mine_ref, got_ref, out_ref):
-    piece, core = place_ref[0], place_ref[1]
+    )(core, *by_rows, *arrays)
+
+
+def put_rows(out_ref, at, values):
+    count = values.shape[0]
+    if len(out_ref.shape) == 3 or out_ref.shape[1] < D:
+        width = out_ref.shape[-1]
+        folds = D // width
+        depth = out_ref.shape[-2] // folds
+        for begin in range(at // depth * depth, at + count, depth):
+            low, high = max(begin, at), min(begin + depth, at + count)
+            if low < high:
+                kind = begin // depth
+                ref = out_ref.at[kind] if len(out_ref.shape) == 3 else out_ref
+                for fold in range(folds):
+                    rows = slice(fold * depth + low - begin, fold * depth + high - begin)
+                    ref[rows, :] = values[low - at : high - at, fold * width : (fold + 1) * width]
+        return
+    depth = out_ref.shape[0]
+    for begin in range(0, at + count, depth):
+        low, high = max(begin, at), min(begin + depth, at + count)
+        if low < high:
+            column = begin // depth * D
+            out_ref[low - begin : high - begin, column : column + D] = values[low - at : high - at]
+
+
+def unpack_kernel(order_ref, mine_ref, got_ref, *refs, places):
+    outs, rows_in = refs[:-1], refs[-1]
+    piece, core = order_ref[0], order_ref[1]
     pieces, rows, _ = mine_ref.shape
     for ref, of in ((mine_ref, core), (got_ref, 1 - core)):
         for k in range(pieces):
             begin = (of * pieces + (piece ^ k)) * rows
-            out_ref[pl.ds(pl.multiple_of(begin, 16), rows), :] = ref[k]
-
-
-def in_order(place, mine, got):
+            rows_in[pl.ds(pl.multiple_of(begin, 16), rows), :] = ref[k].astype(F32)
+    for out, begin, at, count in places:
+        put_rows(outs[out], at, rows_in[begin : begin + count, :])
+
+
+def unpack(order, mine, got, shapes, places):
     pieces, rows, width = mine.shape
+    vmem = pl.BlockSpec(memory_space=pltpu.VMEM)
     return pl.pallas_call(
-        in_order_kernel,
-        in_specs=[pl.BlockSpec(memory_space=pltpu.SMEM)] + [pl.BlockSpec(memory_space=pltpu.VMEM)] * 2,
-        out_specs=pl.BlockSpec(memory_space=pltpu.VMEM),
-        out_shape=jax.ShapeDtypeStruct((2 * pieces * rows, width), mine.dtype),
+        partial(unpack_kernel, places=places),
+        in_specs=[pl.BlockSpec(memory_space=pltpu.SMEM), vmem, vmem],
+        out_specs=[vmem] * len(shapes),
+        out_shape=[jax.ShapeDtypeStruct(s, F32) for s in shapes],
+        scratch_shapes=[pltpu.VMEM((2 * pieces * rows, width), F32)],
         compiler_params=pltpu.CompilerParams(vmem_limit_bytes=VMEM_BYTES),
-        cost_estimate=NO_COST,
-        name="in_order",
-    )(place, mine, got)
+        cost_estimate=COST,
+        name="unpack",
+    )(order, mine, got)
 
 
 class Place:
@@ -1106,12 +1232,11 @@
         self.stays = self.c == lax.axis_index("mp")
         self.masks = [1 << b for b in range(1, dp_size.bit_length() - 1)]
         self.bits = [(dp // mask) % 2 for mask in self.masks]
-        self.core = self.c.astype(jnp.int32).reshape(1)
+        self.core = jnp.stack([self.c, self.stays]).astype(jnp.int32)
         piece = jnp.int32(0)
         for bit in self.bits:
             piece = 2 * piece + bit.astype(jnp.int32)
-        self.order = jnp.concatenate([piece.reshape(1), self.core])
-        self.pair = jnp.concatenate([jnp.zeros((1,), jnp.int32), self.core])
+        self.order = jnp.stack([piece, self.c.astype(jnp.int32)])
 
     def flip(self, values, mask):
         return lax.ppermute(values, "dp", [(d, d ^ mask) for d in range(self.dp_size)])
@@ -1169,12 +1294,11 @@
     rows = own.shape[0] // 2
     near = yield at.y_swap, lax.dynamic_slice_in_dim(own, at.c * rows, rows, 0), first
     far = yield at.core_swap, near, second
-    return in_order(at.pair, near[None], far[None])
+    return near, far
 
 
 def moved(at, values, steps):
-    got = yield at.cross, values, steps
-    return jnp.where(at.stays, values, got)
+    return (yield at.cross, values, steps)
 
 
 def plus(*values):
@@ -1191,8 +1315,7 @@
     for mask in at.masks[::-1]:
         got = yield partial(at.flip, mask=mask), total, steps
         total = jnp.concatenate([total, got])
-    far = yield at.core_swap, total, last_steps
-    return in_order(at.order, total, far)
+    return total, (yield at.core_swap, total, last_steps)
 
 
 def summed(at, keep, send, core_steps=1, y_steps=1, steps=1, last_steps=1):
@@ -1228,36 +1351,6 @@
     if width < D:
         return jnp.concatenate([weight[: depth // 2], weight[depth // 2 :]], axis=1)
     return jnp.concatenate([weight[:, :D], weight[:, D:]], axis=0)
-
-
-def rows_back(rows, shape):
-    if len(shape) == 3:
-        kinds, depth, width = shape
-        folded = rows.reshape(kinds, depth // 2, 2 * width)
-        return jnp.concatenate([folded[..., :width], folded[..., width:]], axis=1)
-    depth, width = shape
-    if width == D:
-        return rows
-    if width < D:
-        return jnp.concatenate([rows[:, :width], rows[:, width:]], axis=0)
-    return jnp.concatenate([rows[:depth], rows[depth:]], axis=1)
-
-
-def unpack(rows, *weights):
-    outs, begin = [], 0
-    for weight in weights:
-        count = weight.size // D
-        outs.append(rows_back(rows[begin : begin + count].astype(F32), weight.shape))
-        begin += count
-    return outs
-
-
-def extensions(segments):
-    lane = jnp.arange(128, dtype=jnp.int32)[None, :] % DH
-    same = segments[:, None] == lane
-    for_query = jnp.where((lane < 8) & ~same, BIG, 0.0).astype(BF)
-    for_key = jnp.where(lane < 8, same.astype(F32), jnp.where(lane < 11, 1.0, 0.0)).astype(BF)
-    return for_query, for_key
 
 
 Q_SCALE = DH**-0.5 * math.log2(math.e)
@@ -1302,7 +1395,8 @@
     w_enc_qkv = rows_of(enc_qkv)
     flow.add("source", moved(at, source_rows[:, 0], 1))
     flow.add("w_enc_qkv", gathered(at, w_enc_qkv))
-    flow.add("ints", moved(at, ints.reshape(6, n), 1))
+    ints = ints.reshape(6, n)
+    flow.add("ints", moved(at, ints, 1))
     (target_rows,) = flow.step((target_rows,))
 
     w_dec_self = jnp.concatenate([rows_of(dec_qkv), rows_of(dec_proj)])
@@ -1325,88 +1419,85 @@
     flow.add("target", moved(at, target_rows[:, 0], 2))
     flow.add("w_dec_self", gathered(at, w_dec_self, 2, 1))
     w_enc, w_cross, w_dec, embedding, cots = flow.step((w_enc, w_cross, w_dec, embedding, cots))
-    source, ints = flow.results["source"], flow.results["ints"]
-    source_segments, target_segments = ints[:2].reshape(-1), ints[2:4].reshape(-1)
+    ints = jnp.where(at.stays, ints, flow.results["ints"])
     runs = jnp.transpose(jnp.pad(ints[4:].astype(F32), ((0, 126), (0, 0))))
-
-    def tables(segments):
-        for_query, for_key = extensions(segments)
-        own = lax.dynamic_slice_in_dim(for_query, at.c * n, n, 0)
-        own_keys = lax.dynamic_slice_in_dim(for_key, at.c * n, n, 0)
-        got_keys = lax.dynamic_slice_in_dim(for_key, (1 - at.c) * n, n, 0)
-        return own, (for_key, own_keys, got_keys)
-
-    source_q, source_keys = tables(source_segments)
-    target_q, target_keys = tables(target_segments)
-    source_q, source_keys, target_q, target_keys = flow.step((source_q, source_keys, target_q, target_keys))
-
-    def pre(rows, own, other):
-        whole = [(own, 3 * HALF, 0), (other, 3 * HALF, 0)]
+    lane = jnp.arange(128, dtype=jnp.int32) % DH
+    source_hot, target_hot = (ints[:4].reshape(2, 2 * n, 1) == lane).astype(BF)
+    source_hot, target_hot = flow.step((source_hot, target_hot))
+
+    def pre(rows, got, own, other):
         return rows_call(
-            pre_kernel, "project", [rows, embedding], whole,
-            [row, half_low, half_low, kv_low, kv_low],
+            pre_kernel, "project", at.core, [rows, got, embedding], [own, *other],
+            [row, half_low, half_low, kv_low, kv_low], scratch=[(own.shape, BF)],
         )
 
-    def attend(q, kv, got, query_ext, key_ext, causal=False):
-        o, log = attention_forward_half(at.core, q, kv, got, query_ext, key_ext[0], causal)
-        return o, (q, kv, got, query_ext, key_ext[1], key_ext[2], o, log)
-
-    def attend_back(kept, grad, causal=False):
-        return attention_backward_half(at.core, kept, grad, causal)
+    def attend(q, kv, got, hot, key_hot, causal=False):
+        o, log = heads_forward(at.core, q, kv, got, hot, key_hot, causal)
+        return o, (q, kv, got, hot, key_hot, o, log)
+
+    def attend_back(kept, grad):
+        return heads_backward(at.core, kept, grad, False)
+
+    def attend_back_pair(kept, grad, pair):
+        return heads_backward(at.core, kept, grad, True, 128 * pair, 128)
 
     w_enc_qkv_got = flow.results["w_enc_qkv"]
-    enc_start, q0, q1, kv0, kv1 = pre(source, w_enc_qkv, w_enc_qkv_got)
+    enc_start, q0, q1, kv0, kv1 = pre(source_rows[:, 0], flow.results["source"], w_enc_qkv, w_enc_qkv_got)
     got0, got1 = at.core_swap(kv0), at.core_swap(kv1)
-    enc_o0, enc_kept0 = attend(q0, kv0, got0, source_q, source_keys)
+    enc_o0, enc_kept0 = attend(q0, kv0, got0, source_hot, source_hot)
     flow.add("w_enc", gathered(at, w_enc, 2, 1))
     enc_o0, q1, kv1, got1 = flow.step((enc_o0, q1, kv1, got1))
     target = flow.results["target"]
-    enc_o1, enc_kept1 = attend(q1, kv1, got1, source_q, source_keys)
+    enc_o1, enc_kept1 = attend(q1, kv1, got1, source_hot, source_hot)
     enc_o1, target = flow.step((enc_o1, target))
 
     w_dec_self_got = flow.results["w_dec_self"]
-    dec_start, q0, q1, kv0, kv1 = pre(target, w_dec_self, w_dec_self_got)
+    dec_start, q0, q1, kv0, kv1 = pre(target_rows[:, 0], target, w_dec_self, w_dec_self_got)
     got0, got1 = at.core_swap(kv0), at.core_swap(kv1)
-    self_o0, self_kept0 = attend(q0, kv0, got0, target_q, target_keys, True)
+    self_o0, self_kept0 = attend(q0, kv0, got0, target_hot, target_hot, True)
     flow.add("w_cross", gathered(at, w_cross))
     self_o0, q1, kv1, got1 = flow.step((self_o0, q1, kv1, got1))
-    self_o1, self_kept1 = attend(q1, kv1, got1, target_q, target_keys, True)
+    self_o1, self_kept1 = attend(q1, kv1, got1, target_hot, target_hot, True)
     flow.add("w_dec", gathered(at, w_dec, 3, 1))
     self_o1, enc_o1 = flow.step((self_o1, enc_o1))
     w_enc_got = flow.results["w_enc"]
     enc_sum_one, enc_sum_two, enc_states = rows_call(
-        enc_post_kernel, "encoder_feed", [enc_o0, enc_o1, enc_start, runs], [w_enc, w_enc_got, small_enc],
-        [row, row, row_low],
+        enc_post_kernel, "encoder_feed", at.core, [enc_o0, enc_o1, enc_start, runs],
+        [w_enc, *w_enc_got, small_enc], [row, row, row_low], scratch=[(w_enc.shape, BF)],
     )
     flow.add("cots", moved(at, cots, 3))
     (enc_states,) = flow.step((enc_states,))
     w_cross_got = flow.results["w_cross"]
+    self_proj = [(w_dec_self, HALF, 3)] + [(w, HALF, 1) for w in w_dec_self_got]
     dec_sum_one, q0, q1, kv0, kv1 = rows_call(
-        dec_mid_kernel, "cross_project", [self_o0, self_o1, dec_start, enc_states],
-        [(w_dec_self, HALF, 3), (w_dec_self_got, HALF, 3), w_cross, w_cross_got, small_dec],
-        [row, half_low, half_low, kv_low, kv_low],
+        dec_mid_kernel, "cross_project", at.core, [self_o0, self_o1, dec_start, enc_states],
+        [*self_proj, w_cross, *w_cross_got, small_dec],
+        [row, half_low, half_low, kv_low, kv_low], scratch=[(w_cross.shape, BF)],
     )
     got0, got1 = at.core_swap(kv0), at.core_swap(kv1)
     q0, q1, kv0, kv1 = flow.step((q0, q1, kv0, kv1))
-    cross_o0, cross_kept0 = attend(q0, kv0, got0, target_q, source_keys)
+    cross_o0, cross_kept0 = attend(q0, kv0, got0, target_hot, source_hot)
     cross_o0, q1, kv1, got1 = flow.step((cross_o0, q1, kv1, got1))
-    cross_o1, cross_kept1 = attend(q1, kv1, got1, target_q, source_keys)
+    cross_o1, cross_kept1 = attend(q1, kv1, got1, target_hot, source_hot)
     flow.add("enc_states", moved(at, enc_states, 1))
     (cross_o1,) = flow.step((cross_o1,))
-    cots = flow.results["cots"]
+    cots = jnp.where(at.stays, cots, flow.results["cots"])
     enc_cot, dec_cot = cots[:, :D], cots[:, D:]
 
     def grad_outs(rows):
         return [((2, rows // 2, D), BF)] * 2 + [((8, D), F32)]
+
+    def grad_scratch(rows):
+        return [((2, rows, D), F32), ((8, D), F32)]
 
     w_dec_got = flow.results["w_dec"]
     (
         dec_states, start_grad, sum_grad, o0_grad, o1_grad, *dec_parts, small_two,
     ) = rows_call(
-        dec_post_kernel, "decoder_feed",
-        [cross_o0, cross_o1, dec_sum_one, dec_start, runs, dec_cot], [w_dec, w_dec_got, small_dec],
+        dec_post_kernel, "decoder_feed", at.core,
+        [cross_o0, cross_o1, dec_sum_one, dec_start, runs, dec_cot], [w_dec, *w_dec_got, small_dec],
         [row_low, row, row, half_low, half_low], grad_outs(9 * HALF),
-        [(2, 9 * HALF, D), (8, D)], at.core,
+        [*grad_scratch(9 * HALF), (w_dec.shape, BF)],
     )
     flow.add("dec", summed(at, *dec_parts))
     flow.add("dec_states", moved(at, dec_states, 1))
@@ -1422,30 +1513,25 @@
     (
         enc_base, enc_o0_grad, enc_o1_grad, *enc_parts, small_enc_grad,
     ) = rows_call(
-        enc_back_kernel, "encoder_feed_back",
+        enc_back_kernel, "encoder_feed_back", at.core,
         [kv0_grad, kv1_grad, kv0_got, kv1_got, enc_states, enc_cot, enc_start, enc_sum_one, enc_sum_two,
          enc_o0, enc_o1, runs],
-        [w_cross, w_cross_got, w_enc, w_enc_got, small_enc],
-        [row, half_low, half_low], grad_outs(11 * HALF), [(2, 11 * HALF, D), (8, D)], at.core,
+        [w_cross, *w_cross_got, w_enc, *w_enc_got, small_enc],
+        [row, half_low, half_low], grad_outs(11 * HALF),
+        [*grad_scratch(11 * HALF), (w_cross.shape, BF), (w_enc.shape, BF)],
     )
     flow.add("enc", summed(at, *enc_parts))
     enc_o0_grad, enc_o1_grad, q0_grad = flow.step((enc_o0_grad, enc_o1_grad, q0_grad))
     (
         dec_base, self_o0_grad, self_o1_grad, *mid_parts, small_one,
     ) = rows_call(
-        dec_mid_back_kernel, "cross_project_back",
+        dec_mid_back_kernel, "cross_project_back", at.core,
         [q0_grad, q1_grad, sum_grad, dec_sum_one, start_grad, self_o0, self_o1],
-        [(w_cross, HALF, 0), (w_cross_got, HALF, 0), (w_dec_self, HALF, 3), (w_dec_self_got, HALF, 3), small_dec],
-        [row, half_low, half_low], grad_outs(2 * HALF), [(2, 2 * HALF, D), (8, D)], at.core,
+        [(w_cross, HALF, 0), *w_cross_got, *self_proj, small_dec],
+        [row, half_low, half_low], grad_outs(2 * HALF), grad_scratch(2 * HALF),
     )
     flow.add("small", summed_small(at, jnp.concatenate([small_enc_grad, small_one, small_two])))
     enc_o1_grad, mid_parts = flow.step((enc_o1_grad, mid_parts))
-
-    def project_back(q_grad, kv_grad, got, start, base, weight):
-        return rows_call(
-            qkv_back_kernel, "project_back", [q_grad, kv_grad, got, start, base], [(weight, 3 * HALF, 0)],
-            [row], [((1, 3 * HALF // 2, D), BF)] * 2, [(1, 3 * HALF, D)], at.core,
-        )
 
     q1_grad, kv1_grad, kv1_send = attend_back(enc_kept1, enc_o1_grad)
     kv1_got = at.core_swap(kv1_send)
@@ -1453,48 +1539,88 @@
     q0_grad, kv0_grad, kv0_send = attend_back(enc_kept0, enc_o0_grad)
     kv0_got = at.core_swap(kv0_send)
     q0_grad, kv0_grad, kv1_got, q1_grad = flow.step((q0_grad, kv0_grad, kv1_got, q1_grad))
-    source_grad, keep1, send1 = project_back(q1_grad, kv1_grad, kv1_got, enc_start, enc_base, w_enc_qkv_got)
-    source_grad, keep0, send0 = project_back(q0_grad, kv0_grad, kv0_got, enc_start, source_grad, w_enc_qkv)
-    keep = jnp.concatenate([jnp.concatenate([keep0, keep1]), mid_parts[0]], axis=1)
-    send = jnp.concatenate([jnp.concatenate([send0, send1]), mid_parts[1]], axis=1)
+    source_grad, keep, send = rows_call(
+        both_qkv_back_kernel, "project_back", at.core,
+        [q0_grad, kv0_grad, kv0_got, q1_grad, kv1_grad, kv1_got, enc_start, enc_base],
+        [w_enc_qkv, *w_enc_qkv_got, *mid_parts], [row], [((2, 5 * HALF // 2, D), BF)] * 2,
+        [((2, 3 * HALF, D), F32), (w_enc_qkv.shape, BF)],
+    )
     source_low = source_grad.astype(BF)
-    flow.add("enc_qkv", summed(at, keep, send, 1, 2))
+    flow.add("enc_qkv", summed(at, keep, send))
     flow.add("source_grad", moved(at, source_low, 1))
     (self_o1_grad,) = flow.step((self_o1_grad,))
 
-    q1_grad, kv1_grad, kv1_send = attend_back(self_kept1, self_o1_grad, True)
-    q1_grad, kv1_grad, kv1_send, self_o0_grad = flow.step((q1_grad, kv1_grad, kv1_send, self_o0_grad))
-    kv1_got = at.core_swap(kv1_send)
-    target_grad, keep1, send1 = project_back(q1_grad, kv1_grad, kv1_got, dec_start, dec_base, w_dec_self_got)
+    def heads_back(kept, grad):
+        parts = []
+        for pair in range(2):
+            q_grad, kv_grad, kv_send = attend_back_pair(kept, grad, pair)
+            grad, q_grad, kv_grad, kv_send = flow.step((grad, q_grad, kv_grad, kv_send))
+            parts += [q_grad, kv_grad, at.core_swap(kv_send)]
+        return parts
+
+    parts = heads_back(self_kept1, self_o1_grad)
+    part_outs = [((1, 3 * HALF // 2, D), BF)] * 2
+    part_scratch = [((1, 3 * HALF, D), F32)]
+    target_grad, keep1, send1 = rows_call(
+        other_qkv_back_kernel, "project_back", at.core, [*parts, dec_start, dec_base],
+        [*w_dec_self_got], [row], part_outs, [*part_scratch, (w_dec_self.shape, BF)],
+    )
     flow.add("dec_qkv_other", summed_other(at, keep1, at.core_swap(send1), 1))
     target_grad, self_o0_grad = flow.step((target_grad, self_o0_grad))
-    q0_grad, kv0_grad, kv0_send = attend_back(self_kept0, self_o0_grad, True)
-    q0_grad, kv0_grad, kv0_send, target_grad = flow.step((q0_grad, kv0_grad, kv0_send, target_grad))
-    kv0_got = at.core_swap(kv0_send)
-    target_grad, keep0, send0 = project_back(q0_grad, kv0_grad, kv0_got, dec_start, target_grad, w_dec_self)
-    target_grad, keep0, send0 = flow.step((target_grad, keep0, send0))
+    parts = heads_back(self_kept0, self_o0_grad)
+    target_grad, keep0, send0 = rows_call(
+        own_qkv_back_kernel, "project_back", at.core, [*parts, dec_start, target_grad],
+        [(w_dec_self, 3 * HALF, 0)], [row], part_outs, part_scratch,
+    )
+    target_low = target_grad.astype(BF)
     flow.add("dec_qkv", summed_own(at, keep0, send0, flow.results["dec_qkv_other"]))
-    flow.add("target_grad", moved(at, target_grad.astype(BF), 1))
+    flow.add("target_grad", moved(at, target_low, 2))
+
+    done = flow.results
+
+    def weights(name, *weights):
+        places, begin = [], 0
+        for i, weight in enumerate(weights):
+            places.append((i, begin, 0, weight.size // D))
+            begin += weight.size // D
+        return unpack(at.order, *done[name], [w.shape for w in weights], places)
+
+    def home(values, name):
+        return jnp.where(at.stays, values, done[name].astype(values.dtype))[:, None]
+
+    def mixed_weights(name):
+        part, more = 3 * HALF // 2, HALF // 2
+        places = []
+        for c in range(2):
+            begin = c * (part + 2 * more)
+            places += [(0, begin, c * part, part), (1 + c, begin + part, 0, 2 * more)]
+        shapes = [enc_qkv.shape, cross_query.shape, dec_proj.shape]
+        return unpack(at.order, *done[name], shapes, places)
+
+    target_grad, done["dec"] = flow.step((target_grad, done["dec"]))
+    dec_grads = weights("dec", cross_proj, dec_up, dec_down)
+    dec_grads, done["enc"] = flow.step((dec_grads, done["enc"]))
+    enc_grads = weights("enc", cross_kv, enc_proj, enc_up, enc_down)
+    enc_grads, source_grad = flow.step((enc_grads, source_grad))
+    source_out = home(source_grad, "source_grad")
+    source_out, enc_states, dec_states = flow.step((source_out, enc_states, dec_states))
+    states_out = home(enc_states, "enc_states"), home(dec_states, "dec_states")
+    states_out, done["enc_qkv"] = flow.step((states_out, done["enc_qkv"]))
+    mixed_grads = mixed_weights("enc_qkv")
+    mixed_grads, target_grad = flow.step((mixed_grads, target_grad))
+    target_out = home(target_grad, "target_grad")
+    (target_out,) = flow.step((target_out,))
     flow.finish()
-
-    done = flow.results
-    cross_proj_grad, dec_up_grad, dec_down_grad = unpack(done["dec"], cross_proj, dec_up, dec_down)
-    cross_kv_grad, enc_proj_grad, enc_up_grad, enc_down_grad = unpack(
-        done["enc"], cross_kv, enc_proj, enc_up, enc_down
-    )
-    both = done["enc_qkv"].reshape(2, -1, D)
-    (enc_qkv_grad,) = unpack(both[:, : 3 * HALF // 2].reshape(-1, D), enc_qkv)
-    cross_query_grad, dec_proj_grad = unpack(
-        both[:, 3 * HALF // 2 :].reshape(-1, D), cross_query, dec_proj
-    )
-    (dec_qkv_grad,) = unpack(done["dec_qkv"], dec_qkv)
+    cross_proj_grad, dec_up_grad, dec_down_grad = dec_grads
+    cross_kv_grad, enc_proj_grad, enc_up_grad, enc_down_grad = enc_grads
+    enc_qkv_grad, cross_query_grad, dec_proj_grad = mixed_grads
+    (dec_qkv_grad,) = weights("dec_qkv", dec_qkv)
     small = done["small"]
     enc_small, one, two = small[:8], small[8:16], small[16:]
     return (
-        done["enc_states"][:, None],
-        done["dec_states"][:, None],
-        done["source_grad"].astype(F32)[:, None],
-        done["target_grad"].astype(F32)[:, None],
+        *states_out,
+        source_out,
+        target_out,
         enc_qkv_grad,
         enc_proj_grad,
         enc_up_grad,

time: 680 us -> 604 us (0.89)
  Pallas kernels: 377 us -> 347 us
  other arithmetic: 83.1 us -> 53.1 us
  starting transfers between devices: 97.5 us -> 83.4 us
  local copies, waits for them, and re-layouts: 53.1 us -> 43.4 us
  waiting for transfers between devices: 59.1 us -> 68.1 us
    pallas_call x32 -> x28, Pallas kernels: 377 us -> 347 us  [the longest x8 136 us: heads_backward(): pl.pallas_call(partial(backward_kernel, causal=causal), grid=(width // 12...]
    concatenate x10 -> x0, other arithmetic: 12.1 us -> none  [the longest x3 3.53 us: rows_back(): return jnp.concatenate([folded[..., :width], folded[..., width:]], axis=1)]
    convert_element_type x8 -> x2, other arithmetic: 14.8 us -> 3.61 us  [the longest x1 2.74 us: chip_rows(): target_low = target_grad.astype(BF)]
    ppermute x54 -> x56, starting transfers between devices: 70.8 us -> 60 us  [flip(): lax.ppermute(values, 'dp', [(d, d ^ mask) for d in range(self.dp_size)])]
    ppermute x10, waiting for transfers between devices: 13.8 us -> 21.9 us  [y_swap(): return lax.ppermute(values, 'mp', [(0, 1), (1, 0)])]
    unnamed x224 -> x176, local copies, waits for them, and re-layouts: 28.8 us -> 21.6 us
    ppermute x54 -> x56, waiting for transfers between devices: 45.3 us -> 46.2 us  [flip(): lax.ppermute(values, 'dp', [(d, d ^ mask) for d in range(self.dp_size)])]
  transfers between devices with their start and end apart: 72 -> 74, of which waited for: 19 -> 27; matrix products, arithmetic and copies ran while one was open for 13% -> 10% of each run, Pallas kernels for 55% -> 57%
where the time goes in v3:
time: 604 us; the launch traced here: 598 us
  Pallas kernels  347 us (57%)
  starting transfers between devices  83.4 us (14%)
  waiting for transfers between devices  68.1 us (11%)
  other arithmetic  53.1 us (9%)
  local copies, waits for them, and re-layouts  43.4 us (7%)
    pallas_call x8, Pallas kernels, heads_backward(): pl.pallas_call(partial(backward_kernel, causal=causal), grid=(width // 12...  136 us
    pallas_call x10, Pallas kernels, rows_call(): pl.pallas_call(kernel, grid=(n // block,), in_specs=[pl.BlockSpec(memory_...  124 us
    pallas_call x6, Pallas kernels, heads_forward(): pl.pallas_call(partial(forward_kernel, causal=causal), grid=(width // 128...  72.3 us
    ppermute x56, starting transfers between devices, flip(): lax.ppermute(values, 'dp', [(d, d ^ mask) for d in range(self.dp_size)])  60 us
    ppermute x56, waiting for transfers between devices, flip(): lax.ppermute(values, 'dp', [(d, d ^ mask) for d in range(self.dp_size)])  46.2 us
    ppermute x10, waiting for transfers between devices, y_swap(): return lax.ppermute(values, 'mp', [(0, 1), (1, 0)])  21.9 us
    unnamed x176, local copies, waits for them, and re-layouts  21.6 us
    pallas_call x4, Pallas kernels, unpack(): pl.pallas_call(partial(unpack_kernel, places=places), in_specs=[pl.BlockS...  14.6 us
  transfers between devices with their start and end apart: 74, of which 27 were waited for; matrix products, arithmetic and copies ran while one was open for 10% of the time, Pallas kernels for 57%

profile of v3, /device:TPU:0, one launch (start us, length us, event | category | flops | bytes accessed | tf_op | source)
XLA Modules:
  0.0 597.9 jit_solution(1256831020504650676)
XLA Ops:
  18.1 5.5 multiply_sine_fusion
  42.0 5.2 project.2
  52.6 14.1 %attention.4 = (bf16[1024,256]{1,0:T(8,128)(2,1)}, f32[1024,256]{1,0:T(8,128)}) custom-call(s32[2]{0:T(128)} %get-tuple-element.877.core_ref, bf16[1024,256]{1,0:T(8,128)(2,1)} %get-tuple-element.424.q_ref, bf16[2,1024,256]{2,1,0:T(8,128)(2,1)} %get-tuple-element.425.own_ref, bf16[2,1024,256]{2,1,0:T(8,128)(2,1)} %collective-permute-done.4.got_ref, ...), custom_call_target="tpu_custom_call" | custom-call | flops 1 | bytes 1 | tf_op jit(solution)/shard_map/attention/pallas_call | solution.py:628
  66.6 9.0 %collective-permute-done.7.near_ref.proj_near_ref = bf16[512,512]{1,0:T(8,128)(2,1)} collective-permute-done((bf16[512,512]{1,0:T(8,128)(2,1)}, bf16[512,512]{1,0:T(8,128)(2,1)}, u32[]{:S(2)}, u32[]{:S(2)}) %collective-permute-start.7) | collective-permute-done | bytes 524320 | tf_op jit(solution)/shard_map/ppermute | solution.py:1248
  77.9 13.9 %attention.5 = (bf16[1024,256]{1,0:T(8,128)(2,1)}, f32[1024,256]{1,0:T(8,128)}) custom-call(s32[2]{0:T(128)} %get-tuple-element.877.core_ref, bf16[1024,256]{1,0:T(8,128)(2,1)} %get-tuple-element.440.q_ref, bf16[2,1024,256]{2,1,0:T(8,128)(2,1)} %get-tuple-element.441.own_ref, bf16[2,1024,256]{2,1,0:T(8,128)(2,1)} %collective-permute-done.5.got_ref, ...), custom_call_target="tpu_custom_call" | custom-call | flops 1 | bytes 1 | tf_op jit(solution)/shard_map/attention/pallas_call | solution.py:628
  92.6 5.4 project.3
  101.9 8.3 %attention_causal.2 = (bf16[1024,256]{1,0:T(8,128)(2,1)}, f32[1024,256]{1,0:T(8,128)}) custom-call(s32[2]{0:T(128)} %get-tuple-element.877.core_ref, bf16[1024,256]{1,0:T(8,128)(2,1)} %get-tuple-element.450.q_ref, bf16[2,1024,256]{2,1,0:T(8,128)(2,1)} %get-tuple-element.451.own_ref, bf16[2,1024,256]{2,1,0:T(8,128)(2,1)} %copy-done.6, ...), custom_call_target="tpu_custom_call" | custom-call | flops 1 | bytes 1 | tf_op jit(solution)/shard_map/attention_causal/pallas_call | solution.py:628
  110.3 5.0 collective-permute-start.13
  117.3 8.5 %attention_causal.3 = (bf16[1024,256]{1,0:T(8,128)(2,1)}, f32[1024,256]{1,0:T(8,128)}) custom-call(s32[2]{0:T(128)} %get-tuple-element.877.core_ref, bf16[1024,256]{1,0:T(8,128)(2,1)} %get-tuple-element.464.q_ref, bf16[2,1024,256]{2,1,0:T(8,128)(2,1)} %get-tuple-element.465.own_ref, bf16[2,1024,256]{2,1,0:T(8,128)(2,1)} %copy-done.7, ...), custom_call_target="tpu_custom_call" | custom-call | flops 1 | bytes 1 | tf_op jit(solution)/shard_map/attention_causal/pallas_call | solution.py:628
  133.9 12.8 %encoder_feed.1 = (f32[1024,512]{1,0:T(8,128)}, f32[1024,512]{1,0:T(8,128)}, bf16[1024,512]{1,0:T(8,128)(2,1)}) custom-call(s32[2]{0:T(128)} %get-tuple-element.877.core_ref, bf16[1024,256]{1,0:T(8,128)(2,1)} %get-tuple-element.477.o0_ref.o_ref, bf16[1024,256]{1,0:T(8,128)(2,1)} %get-tuple-element.478.o1_ref.o_ref, ...), custom_call_target="tpu_custom_call" | custom-call | flops 1 | bytes 1 | tf_op jit(solution)/shard_map/encoder_feed/pallas_call | solution.py:1161
  147.5 7.1 %cross_project.1 = (f32[1024,512]{1,0:T(8,128)}, bf16[1024,256]{1,0:T(8,128)(2,1)}, bf16[1024,256]{1,0:T(8,128)(2,1)}, bf16[2,1024,256]{2,1,0:T(8,128)(2,1)}, bf16[2,1024,256]{2,1,0:T(8,128)(2,1)}) custom-call(s32[2]{0:T(128)} %get-tuple-element.877.core_ref, bf16[1024,256]{1,0:T(8,128)(2,1)} %get-tuple-element.463.o0_ref.o_ref, ...), custom_call_target="tpu_custom_call" | custom-call | flops 1 | bytes 1 | tf_op jit(solution)/shard_map/cross_project/pallas_call | solution.py:1161
  158.4 13.8 %attention.6 = (bf16[1024,256]{1,0:T(8,128)(2,1)}, f32[1024,256]{1,0:T(8,128)}) custom-call(s32[2]{0:T(128)} %get-tuple-element.877.core_ref, bf16[1024,256]{1,0:T(8,128)(2,1)} %get-tuple-element.491.q_ref, bf16[2,1024,256]{2,1,0:T(8,128)(2,1)} %get-tuple-element.492.own_ref, bf16[2,1024,256]{2,1,0:T(8,128)(2,1)} %copy-done.24, ...), custom_call_target="tpu_custom_call" | custom-call | flops 1 | bytes 1 | tf_op jit(solution)/shard_map/attention/pallas_call | solution.py:628
  173.2 13.8 %attention.7 = (bf16[1024,256]{1,0:T(8,128)(2,1)}, f32[1024,256]{1,0:T(8,128)}) custom-call(s32[2]{0:T(128)} %get-tuple-element.877.core_ref, bf16[1024,256]{1,0:T(8,128)(2,1)} %get-tuple-element.498.q_ref, bf16[2,1024,256]{2,1,0:T(8,128)(2,1)} %get-tuple-element.499.own_ref, bf16[2,1024,256]{2,1,0:T(8,128)(2,1)} %copy-done.23, ...), custom_call_target="tpu_custom_call" | custom-call | flops 1 | bytes 1 | tf_op jit(solution)/shard_map/attention/pallas_call | solution.py:628
  189.6 33.9 %decoder_feed.1 = (bf16[1024,512]{1,0:T(8,128)(2,1)}, f32[1024,512]{1,0:T(8,128)}, f32[1024,512]{1,0:T(8,128)}, bf16[1024,256]{1,0:T(8,128)(2,1)}, bf16[1024,256...) custom-call(s32[2]{0:T(128)} %get-tuple-element.877.core_ref, ...), custom_call_target="tpu_custom_call" | custom-call | flops 1 | bytes 1 | tf_op jit(solution)/shard_map/decoder_feed/pallas_call | solution.py:1161
  226.8 25.1 %attention_back.4 = (bf16[1024,256]{1,0:T(8,128)(2,1)}, bf16[2,1024,256]{2,1,0:T(8,128)(2,1)}, bf16[2,1024,256]{2,1,0:T(8,128)(2,1)}) custom-call(s32[2]{0:T(128)} %get-tuple-element.877.core_ref, bf16[1024,256]{1,0:T(8,128)(2,1)} %get-tuple-element.491.q_ref, bf16[2,1024,256]{2,1,0:T(8,128)(2,1)} %get-tuple-element.492.own_ref, ...), custom_call_target="tpu_custom_call" | custom-call | flops 1 | bytes 1 | tf_op jit(solution)/shard_map/attention_back/pallas_call | solution.py:771
  256.6 25.1 %attention_back.5 = (bf16[1024,256]{1,0:T(8,128)(2,1)}, bf16[2,1024,256]{2,1,0:T(8,128)(2,1)}, bf16[2,1024,256]{2,1,0:T(8,128)(2,1)}) custom-call(s32[2]{0:T(128)} %get-tuple-element.877.core_ref, bf16[1024,256]{1,0:T(8,128)(2,1)} %get-tuple-element.498.q_ref, bf16[2,1024,256]{2,1,0:T(8,128)(2,1)} %get-tuple-element.499.own_ref, ...), custom_call_target="tpu_custom_call" | custom-call | flops 1 | bytes 1 | tf_op jit(solution)/shard_map/attention_back/pallas_call | solution.py:771
  288.9 29.4 %encoder_feed_back.1 = (f32[1024,512]{1,0:T(8,128)}, bf16[1024,256]{1,0:T(8,128)(2,1)}, bf16[1024,256]{1,0:T(8,128)(2,1)}, bf16[2,1408,512]{2,1,0:T(8,128)(2,1)}...) custom-call(s32[2]{0:T(128)} %get-tuple-element.877.core_ref, bf16[2,1024,256]{2,1,0:T(8,128)(2,1)} %get-tuple-element.531.kv0_ref, ...), custom_call_target="tpu_custom_call" | custom-call | flops 1 | bytes 1 | tf_op jit(solution)/shard_map/encoder_feed_back/pallas_call | solution.py:1161
  321.0 9.0 %cross_project_back.1 = (f32[1024,512]{1,0:T(8,128)}, bf16[1024,256]{1,0:T(8,128)(2,1)}, bf16[1024,256]{1,0:T(8,128)(2,1)}, bf16[2,256,512]{2,1,0:T(8,128)(2,1)}...) custom-call(s32[2]{0:T(128)} %get-tuple-element.877.core_ref, bf16[1024,256]{1,0:T(8,128)(2,1)} %get-tuple-element.558.q0_grad_ref, ...), custom_call_target="tpu_custom_call" | custom-call | flops 1 | bytes 1 | tf_op jit(solution)/shard_map/cross_project_back/pallas_call | solution.py:1161
  337.3 25.0 %attention_back.6 = (bf16[1024,256]{1,0:T(8,128)(2,1)}, bf16[2,1024,256]{2,1,0:T(8,128)(2,1)}, bf16[2,1024,256]{2,1,0:T(8,128)(2,1)}) custom-call(s32[2]{0:T(128)} %get-tuple-element.877.core_ref, bf16[1024,256]{1,0:T(8,128)(2,1)} %get-tuple-element.440.q_ref, bf16[2,1024,256]{2,1,0:T(8,128)(2,1)} %get-tuple-element.441.own_ref, ...), custom_call_target="tpu_custom_call" | custom-call | flops 1 | bytes 1 | tf_op jit(solution)/shard_map/attention_back/pallas_call | solution.py:771
  362.8 4.6 collective-permute-done.30
  371.2 25.0 %attention_back.7 = (bf16[1024,256]{1,0:T(8,128)(2,1)}, bf16[2,1024,256]{2,1,0:T(8,128)(2,1)}, bf16[2,1024,256]{2,1,0:T(8,128)(2,1)}) custom-call(s32[2]{0:T(128)} %get-tuple-element.877.core_ref, bf16[1024,256]{1,0:T(8,128)(2,1)} %get-tuple-element.424.q_ref, bf16[2,1024,256]{2,1,0:T(8,128)(2,1)} %get-tuple-element.425.own_ref, ...), custom_call_target="tpu_custom_call" | custom-call | flops 1 | bytes 1 | tf_op jit(solution)/shard_map/attention_back/pallas_call | solution.py:771
  409.6 9.6 %project_back.3 = (f32[1024,512]{1,0:T(8,128)}, bf16[2,640,512]{2,1,0:T(8,128)(2,1)}, bf16[2,640,512]{2,1,0:T(8,128)(2,1)}) custom-call(s32[2]{0:T(128)} %get-tuple-element.877.core_ref, bf16[1024,256]{1,0:T(8,128)(2,1)} %get-tuple-element.611.q0_grad_ref, bf16[2,1024,256]{2,1,0:T(8,128)(2,1)} %get-tuple-element.612.kv0_ref, ...), custom_call_target="tpu_custom_call" | custom-call | flops 1 | bytes 1 | tf_op jit(solution)/shard_map/project_back/pallas_call | solution.py:1161
  432.0 8.8 %attention_causal_back.4 = (bf16[1024,128]{1,0:T(8,128)(2,1)}, bf16[2,1024,128]{2,1,0:T(8,128)(2,1)}, bf16[2,1024,128]{2,1,0:T(8,128)(2,1)}) custom-call(s32[2]{0:T(128)} %get-tuple-element.877.core_ref, bf16[1024,256]{1,0:T(8,128)(2,1)} %get-tuple-element.464.q_ref, bf16[2,1024,256]{2,1,0:T(8,128)(2,1)} %get-tuple-element.465.own_ref, ...), custom_call_target="tpu_custom_call" | custom-call | flops 1 | bytes 1 | tf_op jit(solution)/shard_map/attention_causal_back/pallas_call | solution.py:771
  453.0 9.1 %attention_causal_back.5 = (bf16[1024,128]{1,0:T(8,128)(2,1)}, bf16[2,1024,128]{2,1,0:T(8,128)(2,1)}, bf16[2,1024,128]{2,1,0:T(8,128)(2,1)}) custom-call(s32[2]{0:T(128)} %get-tuple-element.877.core_ref, bf16[1024,256]{1,0:T(8,128)(2,1)} %get-tuple-element.464.q_ref, bf16[2,1024,256]{2,1,0:T(8,128)(2,1)} %get-tuple-element.465.own_ref, ...), custom_call_target="tpu_custom_call" | custom-call | flops 1 | bytes 1 | tf_op jit(solution)/shard_map/attention_causal_back/pallas_call | solution.py:771
  462.1 5.8 collective-permute-done.47
  472.4 5.9 project_back.4
  485.2 9.1 %attention_causal_back.6 = (bf16[1024,128]{1,0:T(8,128)(2,1)}, bf16[2,1024,128]{2,1,0:T(8,128)(2,1)}, bf16[2,1024,128]{2,1,0:T(8,128)(2,1)}) custom-call(s32[2]{0:T(128)} %get-tuple-element.877.core_ref, bf16[1024,256]{1,0:T(8,128)(2,1)} %get-tuple-element.450.q_ref, bf16[2,1024,256]{2,1,0:T(8,128)(2,1)} %get-tuple-element.451.own_ref, ...), custom_call_target="tpu_custom_call" | custom-call | flops 1 | bytes 1 | tf_op jit(solution)/shard_map/attention_causal_back/pallas_call | solution.py:771
  494.8 5.8 collective-permute-done.56
  506.0 9.2 %attention_causal_back.7 = (bf16[1024,128]{1,0:T(8,128)(2,1)}, bf16[2,1024,128]{2,1,0:T(8,128)(2,1)}, bf16[2,1024,128]{2,1,0:T(8,128)(2,1)}) custom-call(s32[2]{0:T(128)} %get-tuple-element.877.core_ref, bf16[1024,256]{1,0:T(8,128)(2,1)} %get-tuple-element.450.q_ref, bf16[2,1024,256]{2,1,0:T(8,128)(2,1)} %get-tuple-element.451.own_ref, ...), custom_call_target="tpu_custom_call" | custom-call | flops 1 | bytes 1 | tf_op jit(solution)/shard_map/attention_causal_back/pallas_call | solution.py:771
  522.5 5.7 project_back.5
  543.2 4.9 unpack.5
  548.1 6.9 %collective-permute-done.65 = bf16[192,512]{1,0:T(8,128)(2,1)} collective-permute-done((bf16[192,512]{1,0:T(8,128)(2,1)}, bf16[192,512]{1,0:T(8,128)(2,1)}, u32[]{:S(2)}, u32[]{:S(2)}) %collective-permute-start.65) | collective-permute-done | bytes 196640 | tf_op jit(solution)/shard_map/ppermute | solution.py:1242
  (433 shorter events, 215.1 us)
Async XLA Ops:
  4.3 30.3 %collective-permute-start = (bf16[1024,512]{1,0:T(8,128)(2,1)}, bf16[1024,512]{1,0:T(8,128)(2,1)}, u32[]{:S(2)}, u32[]{:S(2)}) collective-permute-start(bf16[1024,512]{1,0:T(8,128)(2,1)} %bitcast.71), channel_id=1, source_target_pairs={{1,2},{2,1},{5,6},{6,5},{9,10},{10,9},{13,14},{14,13},{17,18},{18,... | collective-permute-start | bytes 3145736 | tf_op jit(solution)/shard_map/ppermute | solution.py:1254
  6.0 28.6 %collective-permute-start.1 = (bf16[384,512]{1,0:T(8,128)(2,1)}, bf16[384,512]{1,0:T(8,128)(2,1)}, u32[]{:S(2)}, u32[]{:S(2)}) collective-permute-start(bf16[384,512]{1,0:T(8,128)(2,1)} %constant_dynamic-slice_fusion.15), channel_id=1, source_target_pairs={{0,1},{1,0},{2,3},{3,2},{4,5},{5,4},{6,7},{7,6},{8,9},{9,8},{10,11... | collective-permute-start | bytes 1179656 | tf_op jit(solution)/shard_map/ppermute | solution.py:1248
  10.3 24.3 %collective-permute-start.2 = (s32[6,1024]{0,1:T(8,128)}, s32[6,1024]{0,1:T(8,128)}, u32[]{:S(2)}, u32[]{:S(2)}) collective-permute-start(s32[6,1024]{0,1:T(8,128)} %copy.49), channel_id=1, source_target_pairs={{1,2},{2,1},{5,6},{6,5},{9,10},{10,9},{13,14},{14,13},{17,18},{18,... | collective-permute-start | bytes 73736 | tf_op jit(solution)/shard_map/ppermute | solution.py:1254
  47.3 28.3 %collective-permute-start.6 = (bf16[1024,512]{1,0:T(8,128)(2,1)}, bf16[1024,512]{1,0:T(8,128)(2,1)}, u32[]{:S(2)}, u32[]{:S(2)}) collective-permute-start(bf16[1024,512]{1,0:T(8,128)(2,1)} %bitcast.9.rows_ref), channel_id=1, source_target_pairs={{1,2},{2,1},{5,6},{6,5},{9,10},{10,9},{13,14},{14,13},{17,18},{18,... | collective-permute-start | bytes 3145736 | tf_op jit(solution)/shard_map/ppermute | solution.py:1254
  49.0 26.6 %collective-permute-start.5 = (bf16[2,1024,256]{2,1,0:T(8,128)(2,1)}, bf16[2,1024,256]{2,1,0:T(8,128)(2,1)}, u32[]{:S(2)}, u32[]{:S(2)}) collective-permute-start(bf16[2,1024,256]{2,1,0:T(8,128)(2,1)} %get-tuple-element.441.own_ref), channel_id=1, source_target_pairs={{0,2},{2,0},{4,6},{6,4},{8,10},{10,8},{12,14},{14,12},{16,18},{18,... | collective-permute-start | bytes 3145736 | tf_op jit(solution)/shard_map/ppermute | solution.py:1242
  51.5 24.1 %collective-permute-start.7 = (bf16[512,512]{1,0:T(8,128)(2,1)}, bf16[512,512]{1,0:T(8,128)(2,1)}, u32[]{:S(2)}, u32[]{:S(2)}) collective-permute-start(bf16[512,512]{1,0:T(8,128)(2,1)} %fusion.9), channel_id=1, source_target_pairs={{0,1},{1,0},{2,3},{3,2},{4,5},{5,4},{6,7},{7,6},{8,9},{9,8},{10,11... | collective-permute-start | bytes 1572872 | tf_op jit(solution)/shard_map/ppermute | solution.py:1248
  75.6 34.6 %collective-permute-start.11 = (bf16[1152,512]{1,0:T(8,128)(2,1)}, bf16[1152,512]{1,0:T(8,128)(2,1)S(1)}, u32[]{:S(2)}, u32[]{:S(2)}) collective-permute-start(bf16[1152,512]{1,0:T(8,128)(2,1)} %constant_dynamic-slice_fusion.14), channel_id=1, source_target_pairs={{0,1},{1,0},{2,3},{3,2},{4,5},{5,4},{6,7},{7,6},{8,9},{9,8},{10,11... | collective-permute-start | bytes 3538952 | tf_op jit(solution)/shard_map/ppermute | solution.py:1248
  126.4 20.3 %collective-permute-start.14 = (bf16[384,512]{1,0:T(8,128)(2,1)S(1)}, bf16[384,512]{1,0:T(8,128)(2,1)S(1)}, u32[]{:S(2)}, u32[]{:S(2)}) collective-permute-start(bf16[384,512]{1,0:T(8,128)(2,1)S(1)} %collective-permute-done.12.near_ref.cross_near_ref.cq_near_ref), channel_id=1, source_target_pairs={{0,2},{2,0},{4,6},{6,4},{8,10},{10,8},{12,14},{14,12},{16,18},{18,... | collective-permute-start | bytes 1179656 | tf_op jit(solution)/shard_map/ppermute | solution.py:1242
  131.7 40.5 %collective-permute-start.17 = (bf16[1152,512]{1,0:T(8,128)(2,1)}, bf16[1152,512]{1,0:T(8,128)(2,1)}, u32[]{:S(2)}, u32[]{:S(2)}) collective-permute-start(bf16[1152,512]{1,0:T(8,128)(2,1)} %constant_dynamic-slice_fusion.12), channel_id=1, source_target_pairs={{0,1},{1,0},{2,3},{3,2},{4,5},{5,4},{6,7},{7,6},{8,9},{9,8},{10,11... | collective-permute-start | bytes 3538952 | tf_op jit(solution)/shard_map/ppermute | solution.py:1248
  154.6 17.6 %collective-permute-start.16 = (bf16[2,1024,256]{2,1,0:T(8,128)(2,1)}, bf16[2,1024,256]{2,1,0:T(8,128)(2,1)S(1)}, u32[]{:S(2)}, u32[]{:S(2)}) collective-permute-start(bf16[2,1024,256]{2,1,0:T(8,128)(2,1)} %get-tuple-element.499.own_ref), channel_id=1, source_target_pairs={{0,2},{2,0},{4,6},{6,4},{8,10},{10,8},{12,14},{14,12},{16,18},{18,... | collective-permute-start | bytes 3145736 | tf_op jit(solution)/shard_map/ppermute | solution.py:1242
  155.1 31.8 %collective-permute-start.18 = (bf16[1024,1024]{1,0:T(8,128)(2,1)S(1)}, bf16[1024,1024]{1,0:T(8,128)(2,1)S(1)}, u32[]{:S(2)}, u32[]{:S(2)}) collective-permute-start(bf16[1024,1024]{1,0:T(8,128)(2,1)S(1)} %copy-done.9), channel_id=1, source_target_pairs={{1,2},{2,1},{5,6},{6,5},{9,10},{10,9},{13,14},{14,13},{17,18},{18,... | collective-permute-start | bytes 6291464 | tf_op jit(solution)/shard_map/ppermute | solution.py:1254
  187.0 36.5 %collective-permute-start.20 = (bf16[1024,512]{1,0:T(8,128)(2,1)S(1)}, bf16[1024,512]{1,0:T(8,128)(2,1)S(1)}, u32[]{:S(2)}, u32[]{:S(2)}) collective-permute-start(bf16[1024,512]{1,0:T(8,128)(2,1)S(1)} %copy-done.4), channel_id=1, source_target_pairs={{1,2},{2,1},{5,6},{6,5},{9,10},{10,9},{13,14},{14,13},{17,18},{18,... | collective-permute-start | bytes 3145736 | tf_op jit(solution)/shard_map/ppermute | solution.py:1254
  223.5 28.4 %collective-permute-start.21 = (bf16[2,1152,512]{2,1,0:T(8,128)(2,1)}, bf16[2,1152,512]{2,1,0:T(8,128)(2,1)S(1)}, u32[]{:S(2)}, u32[]{:S(2)}) collective-permute-start(bf16[2,1152,512]{2,1,0:T(8,128)(2,1)} %get-tuple-element.523), channel_id=1, source_target_pairs={{0,2},{2,0},{4,6},{6,4},{8,10},{10,8},{12,14},{14,12},{16,18},{18,... | collective-permute-start | bytes 7077896 | tf_op jit(solution)/shard_map/ppermute | solution.py:1242
  226.0 25.8 %collective-permute-start.22 = (bf16[1024,512]{1,0:T(8,128)(2,1)}, bf16[1024,512]{1,0:T(8,128)(2,1)S(1)}, u32[]{:S(2)}, u32[]{:S(2)}) collective-permute-start(bf16[1024,512]{1,0:T(8,128)(2,1)} %get-tuple-element.756), channel_id=1, source_target_pairs={{1,2},{2,1},{5,6},{6,5},{9,10},{10,9},{13,14},{14,13},{17,18},{18,... | collective-permute-start | bytes 3145736 | tf_op jit(solution)/shard_map/ppermute | solution.py:1254
  253.7 29.5 %collective-permute-start.24 = (bf16[1152,512]{1,0:T(8,128)(2,1)S(1)}, bf16[1152,512]{1,0:T(8,128)(2,1)}, u32[]{:S(2)}, u32[]{:S(2)}) collective-permute-start(bf16[1152,512]{1,0:T(8,128)(2,1)S(1)} %fusion.4), channel_id=1, source_target_pairs={{0,1},{1,0},{2,3},{3,2},{4,5},{5,4},{6,7},{7,6},{8,9},{9,8},{10,11... | collective-permute-start | bytes 3538952 | tf_op jit(solution)/shard_map/ppermute | solution.py:1248
  256.6 25.1 %collective-permute-start.23 = (bf16[2,1024,256]{2,1,0:T(8,128)(2,1)}, bf16[2,1024,256]{2,1,0:T(8,128)(2,1)}, u32[]{:S(2)}, u32[]{:S(2)}) collective-permute-start(bf16[2,1024,256]{2,1,0:T(8,128)(2,1)} %get-tuple-element.537), channel_id=1, source_target_pairs={{0,2},{2,0},{4,6},{6,4},{8,10},{10,8},{12,14},{14,12},{16,18},{18,... | collective-permute-start | bytes 3145736 | tf_op jit(solution)/shard_map/ppermute | solution.py:1242
  285.2 33.1 %collective-permute-start.26 = (bf16[576,512]{1,0:T(8,128)(2,1)S(1)}, bf16[576,512]{1,0:T(8,128)(2,1)S(1)}, u32[]{:S(2)}, u32[]{:S(2)}) collective-permute-start(bf16[576,512]{1,0:T(8,128)(2,1)S(1)} %constant_dynamic-slice_fusion.11), channel_id=1, source_target_pairs={{0,4},{2,6},{4,0},{6,2},{8,12},{10,14},{12,8},{14,10},{16,20},{18,... | collective-permute-start | bytes 1769480 | tf_op jit(solution)/shard_map/ppermute | solution.py:1242
  333.7 33.8 %collective-permute-start.30 = (bf16[1408,512]{1,0:T(8,128)(2,1)}, bf16[1408,512]{1,0:T(8,128)(2,1)S(1)}, u32[]{:S(2)}, u32[]{:S(2)}) collective-permute-start(bf16[1408,512]{1,0:T(8,128)(2,1)} %fusion.2), channel_id=1, source_target_pairs={{0,1},{1,0},{2,3},{3,2},{4,5},{5,4},{6,7},{7,6},{8,9},{9,8},{10,11... | collective-permute-start | bytes 4325384 | tf_op jit(solution)/shard_map/ppermute | solution.py:1248
  334.7 28.2 %collective-permute-start.31 = (bf16[144,512]{1,0:T(8,128)(2,1)S(1)}, bf16[144,512]{1,0:T(8,128)(2,1)S(1)}, u32[]{:S(2)}, u32[]{:S(2)}) collective-permute-start(bf16[144,512]{1,0:T(8,128)(2,1)S(1)} %constant_dynamic-slice_fusion.9), channel_id=1, source_target_pairs={{0,16},{2,18},{4,20},{6,22},{8,24},{10,26},{12,28},{14,30},{16,0},... | collective-permute-start | bytes 442376 | tf_op jit(solution)/shard_map/ppermute | solution.py:1242
  337.3 25.6 %collective-permute-start.29 = (f32[24,512]{1,0:T(8,128)S(1)}, f32[24,512]{1,0:T(8,128)S(1)}, u32[]{:S(2)}, u32[]{:S(2)}) collective-permute-start(f32[24,512]{1,0:T(8,128)S(1)} %constant_dynamic-update-slice_fusion), channel_id=1, source_target_pairs={{0,2},{2,0},{4,6},{6,4},{8,10},{10,8},{12,14},{14,12},{16,18},{18,... | collective-permute-start | bytes 147464 | tf_op jit(solution)/shard_map/ppermute | solution.py:1242
  362.3 37.1 %collective-permute-start.32 = (bf16[2,1024,256]{2,1,0:T(8,128)(2,1)}, bf16[2,1024,256]{2,1,0:T(8,128)(2,1)}, u32[]{:S(2)}, u32[]{:S(2)}) collective-permute-start(bf16[2,1024,256]{2,1,0:T(8,128)(2,1)} %get-tuple-element.595), channel_id=1, source_target_pairs={{0,2},{2,0},{4,6},{6,4},{8,10},{10,8},{12,14},{14,12},{16,18},{18,... | collective-permute-start | bytes 3145736 | tf_op jit(solution)/shard_map/ppermute | solution.py:1242
  369.6 36.8 %collective-permute-start.34 = (bf16[704,512]{1,0:T(8,128)(2,1)S(1)}, bf16[704,512]{1,0:T(8,128)(2,1)S(1)}, u32[]{:S(2)}, u32[]{:S(2)}) collective-permute-start(bf16[704,512]{1,0:T(8,128)(2,1)S(1)} %constant_dynamic-slice_fusion.8), channel_id=1, source_target_pairs={{0,4},{2,6},{4,0},{6,2},{8,12},{10,14},{12,8},{14,10},{16,20},{18,... | collective-permute-start | bytes 2162696 | tf_op jit(solution)/shard_map/ppermute | solution.py:1242
  407.4 17.8 %collective-permute-start.37 = (bf16[352,512]{1,0:T(8,128)(2,1)S(1)}, bf16[352,512]{1,0:T(8,128)(2,1)S(1)}, u32[]{:S(2)}, u32[]{:S(2)}) collective-permute-start(bf16[352,512]{1,0:T(8,128)(2,1)S(1)} %constant_dynamic-slice_fusion.7), channel_id=1, source_target_pairs={{0,8},{2,10},{4,12},{6,14},{8,0},{10,2},{12,4},{14,6},{16,24},{18,... | collective-permute-start | bytes 1081352 | tf_op jit(solution)/shard_map/ppermute | solution.py:1242
  407.5 17.7 %collective-permute-start.38 = (bf16[2,144,512]{2,1,0:T(8,128)(2,1)}, bf16[2,144,512]{2,1,0:T(8,128)(2,1)S(1)}, u32[]{:S(2)}, u32[]{:S(2)}) collective-permute-start(bf16[2,144,512]{2,1,0:T(8,128)(2,1)} %pad_maximum_fusion.16), channel_id=1, source_target_pairs={{0,8},{2,10},{4,12},{6,14},{8,0},{10,2},{12,4},{14,6},{16,24},{18,... | collective-permute-start | bytes 884744 | tf_op jit(solution)/shard_map/ppermute | solution.py:1242
  426.9 17.8 %collective-permute-start.40 = (bf16[2,640,512]{2,1,0:T(8,128)(2,1)}, bf16[2,640,512]{2,1,0:T(8,128)(2,1)S(1)}, u32[]{:S(2)}, u32[]{:S(2)}) collective-permute-start(bf16[2,640,512]{2,1,0:T(8,128)(2,1)} %get-tuple-element.630), channel_id=1, source_target_pairs={{0,2},{2,0},{4,6},{6,4},{8,10},{10,8},{12,14},{14,12},{16,18},{18,... | collective-permute-start | bytes 3932168 | tf_op jit(solution)/shard_map/ppermute | solution.py:1242
  426.9 17.8 %collective-permute-start.41 = (bf16[1024,512]{1,0:T(8,128)(2,1)S(1)}, bf16[1024,512]{1,0:T(8,128)(2,1)}, u32[]{:S(2)}, u32[]{:S(2)}) collective-permute-start(bf16[1024,512]{1,0:T(8,128)(2,1)S(1)} %convert_element_type.295), channel_id=1, source_target_pairs={{1,2},{2,1},{5,6},{6,5},{9,10},{10,9},{13,14},{14,13},{17,18},{18,... | collective-permute-start | bytes 3145736 | tf_op jit(solution)/shard_map/ppermute | solution.py:1254
  449.0 18.9 %collective-permute-start.49 = (bf16[8,144,512]{2,1,0:T(8,128)(2,1)S(1)}, bf16[8,144,512]{2,1,0:T(8,128)(2,1)}, u32[]{:S(2)}, u32[]{:S(2)}) collective-permute-start(bf16[8,144,512]{2,1,0:T(8,128)(2,1)S(1)} %pad_maximum_fusion.5.mine_ref), channel_id=1, source_target_pairs={{0,2},{2,0},{4,6},{6,4},{8,10},{10,8},{12,14},{14,12},{16,18},{18,... | collective-permute-start | bytes 3538952 | tf_op jit(solution)/shard_map/ppermute | solution.py:1242
  449.9 18.0 %collective-permute-start.46 = (bf16[640,512]{1,0:T(8,128)(2,1)}, bf16[640,512]{1,0:T(8,128)(2,1)}, u32[]{:S(2)}, u32[]{:S(2)}) collective-permute-start(bf16[640,512]{1,0:T(8,128)(2,1)} %fusion.8), channel_id=1, source_target_pairs={{0,1},{1,0},{2,3},{3,2},{4,5},{5,4},{6,7},{7,6},{8,9},{9,8},{10,11... | collective-permute-start | bytes 1966088 | tf_op jit(solution)/shard_map/ppermute | solution.py:1248
  450.0 17.9 %collective-permute-start.48 = (bf16[1,176,512]{2,1,0:T(8,128)(2,1)S(1)}, bf16[1,176,512]{2,1,0:T(8,128)(2,1)S(1)}, u32[]{:S(2)}, u32[]{:S(2)}) collective-permute-start(bf16[1,176,512]{2,1,0:T(8,128)(2,1)S(1)} %fusion.11), channel_id=1, source_target_pairs={{0,16},{2,18},{4,20},{6,22},{8,24},{10,26},{12,28},{14,30},{16,0},... | collective-permute-start | bytes 540680 | tf_op jit(solution)/shard_map/ppermute | solution.py:1242
  453.0 18.5 %collective-permute-start.45 = (bf16[2,1024,128]{2,1,0:T(8,128)(2,1)}, bf16[2,1024,128]{2,1,0:T(8,128)(2,1)}, u32[]{:S(2)}, u32[]{:S(2)}) collective-permute-start(bf16[2,1024,128]{2,1,0:T(8,128)(2,1)} %get-tuple-element.646), channel_id=1, source_target_pairs={{0,2},{2,0},{4,6},{6,4},{8,10},{10,8},{12,14},{14,12},{16,18},{18,... | collective-permute-start | bytes 1572872 | tf_op jit(solution)/shard_map/ppermute | solution.py:1242
  482.3 18.2 %collective-permute-start.56 = (bf16[4,176,512]{2,1,0:T(8,128)(2,1)S(1)}, bf16[4,176,512]{2,1,0:T(8,128)(2,1)S(1)}, u32[]{:S(2)}, u32[]{:S(2)}) collective-permute-start(bf16[4,176,512]{2,1,0:T(8,128)(2,1)S(1)} %pad_maximum_fusion.9), channel_id=1, source_target_pairs={{0,4},{2,6},{4,0},{6,2},{8,12},{10,14},{12,8},{14,10},{16,20},{18,... | collective-permute-start | bytes 2162696 | tf_op jit(solution)/shard_map/ppermute | solution.py:1242
  531.3 23.7 %collective-permute-start.64 = (bf16[1024,512]{1,0:T(8,128)(2,1)}, bf16[1024,512]{1,0:T(8,128)(2,1)}, u32[]{:S(2)}, u32[]{:S(2)}) collective-permute-start(bf16[1024,512]{1,0:T(8,128)(2,1)} %convert_element_type.323), channel_id=1, source_target_pairs={{1,2},{2,1},{5,6},{6,5},{9,10},{10,9},{13,14},{14,13},{17,18},{18,... | collective-permute-start | bytes 3145736 | tf_op jit(solution)/shard_map/ppermute | solution.py:1254
  (128 other events, 1123.6 us)

commit v4 on v3

--- a/solution.py
+++ b/solution.py
@@ -5,6 +5,7 @@
 import jax.numpy as jnp
 from jax import lax
 from jax.experimental import pallas as pl
+from jax.experimental.layout import Layout, with_layout_constraint
 from jax.experimental.pallas import tpu as pltpu
 from jax.sharding import PartitionSpec as P
 
@@ -538,7 +539,11 @@
     return lane < DH, lane % DH
 
 
-def softmax_tasks(tasks, scores_of, after):
+def in_hbm(arrays):
+    return [pltpu.with_memory_space_constraint(a, pltpu.HBM) for a in arrays]
+
+
+def pipelined(tasks, scores_of, after):
     ahead = scores_of(*tasks[0])
     for i, task in enumerate(tasks):
         now = ahead
@@ -592,7 +597,7 @@
             total = total + dot_nn(values[head, :, key * chunk : (key + 1) * chunk], probs)
             state[head, query] = top, total
 
-        softmax_tasks(tasks, scores_of, after)
+        pipelined(tasks, scores_of, after)
         for query in range(n // rows):
             (top0, total0), (top1, total1) = state[0, query], state[1, query]
             out = jnp.concatenate([total0[:DH] / total0[DH:], total1[DH:] / total1[:DH]])
@@ -642,7 +647,7 @@
         compiler_params=pltpu.CompilerParams(vmem_limit_bytes=VMEM_BYTES),
         cost_estimate=COST,
         name="attention_causal" if causal else "attention",
-    )(core, q, own, got, hot, key_hot)
+    )(core, *in_hbm((q, own, got, hot, key_hot)))
 
 
 def backward_kernel(
@@ -715,7 +720,7 @@
             k_grads[head] = k_grads[head] + dot_nn(q_turned[:, here], score_grad)
             q_total[head, here, :] += dot_nn(score_grad, keys[head])
 
-        softmax_tasks(tasks, scores_of, after)
+        pipelined(tasks, scores_of, after)
         k_grad = jnp.concatenate([k_grads[0][:DH], k_grads[1][DH:]]).T
         v_grad = jnp.concatenate([v_grads[0][:DH], v_grads[1][DH:]]).T
         put((k_grad * math.log(2.0)).astype(BF), v_grad.astype(BF))
@@ -794,7 +799,7 @@
         compiler_params=pltpu.CompilerParams(vmem_limit_bytes=VMEM_BYTES),
         cost_estimate=COST,
         name="attention_causal_back" if causal else "attention_back",
-    )(core, q, own, got, hot, key_hot, grad, o, log)
+    )(core, *in_hbm((q, own, got, hot, key_hot, grad, o, log)))
 
 
 def fold_dot(x, w):
@@ -862,23 +867,49 @@
             yield which, ref[up : up + D, :], ref[down : down + D, :], up, down
 
 
-def ffn(low, own_ref, other_ref, begin):
-    total = 0.0
-    for _, up, down, _, _ in ffn_blocks(own_ref, other_ref, begin):
-        total = total + dot_nn(gelu(dot_nn(low, up)).astype(BF), down)
-    return total
-
-
-def ffn_back(low, out_low, own_ref, other_ref, begin, acc, shift):
-    total = 0.0
-    for which, up, down, up_at, down_at in ffn_blocks(own_ref, other_ref, begin):
-        active, slope = gelu_both(dot_nn(low, up))
-        hidden = (dot_nt(out_low, down) * slope).astype(BF)
+def ffn(low, own_ref, other_ref, begin, kept=None):
+    blocks = list(ffn_blocks(own_ref, other_ref, begin))
+    total = []
+
+    def after(hidden, j):
+        if kept is None:
+            active = gelu(hidden).astype(BF)
+        else:
+            active, slope = gelu_both(hidden)
+            active = active.astype(BF)
+            kept[0, :, j * D : (j + 1) * D] = active
+            kept[1, :, j * D : (j + 1) * D] = slope.astype(BF)
+        total.append(dot_nn(active, blocks[j][2]))
+
+    pipelined([(j,) for j in range(4)], lambda j: dot_nn(low, blocks[j][1]), after)
+    return sum(total)
+
+
+def ffn_back(low, out_low, own_ref, other_ref, begin, acc, shift, kept=None):
+    blocks = list(ffn_blocks(own_ref, other_ref, begin))
+    total = []
+
+    def products(j):
+        _, up, down, _, _ = blocks[j]
+        return None if kept is not None else dot_nn(low, up), dot_nt(out_low, down)
+
+    def after(got, j):
+        which, up, _, up_at, down_at = blocks[j]
+        hidden, active_grad = got
+        if kept is None:
+            active, slope = gelu_both(hidden)
+            active = active.astype(BF)
+        else:
+            active = kept[0, :, j * D : (j + 1) * D]
+            slope = kept[1, :, j * D : (j + 1) * D].astype(F32)
+        hidden_grad = (active_grad * slope).astype(BF)
         up_at, down_at = up_at + shift, down_at + shift
-        acc[which, down_at : down_at + D, :] += dot_tn(active.astype(BF), out_low)
-        acc[which, up_at : up_at + D, :] += dot_tn(low, hidden)
-        total = total + dot_nt(hidden, up)
-    return total
+        acc[which, down_at : down_at + D, :] += dot_tn(active, out_low)
+        acc[which, up_at : up_at + D, :] += dot_tn(low, hidden_grad)
+        total.append(dot_nt(hidden_grad, up))
+
+    pipelined([(j,) for j in range(4)], products, after)
+    return sum(total)
 
 
 def proj_back(o_refs, out_low, projs, acc, begin, o_grad_refs):
@@ -977,7 +1008,7 @@
     core_ref, o0_ref, o1_ref, sum_one_ref, start_ref, runs_ref, cot_ref, own_ref, near_ref, far_ref, small_ref,
     states_ref, start_grad_ref, sum_grad_ref, o0_grad_ref, o1_grad_ref,
     keep_ref, send_ref, small_grad_ref,
-    acc, small_acc, other_ref,
+    acc, small_acc, other_ref, kept,
 ):
     join(core_ref, (near_ref, far_ref, other_ref))
     first_step(acc, small_acc)
@@ -988,7 +1019,7 @@
     gain_two = small_ref[2:3, :]
     mixed, unit_two, scale_two = norm(sum_two, gain_two, small_ref[3:4, :])
     low = mixed.astype(BF)
-    sum_three = mixed + ffn(low, own_ref, other_ref, HALF)
+    sum_three = mixed + ffn(low, own_ref, other_ref, HALF, kept)
     gain_three = small_ref[4:5, :]
     last, unit_three, scale_three = norm(sum_three, gain_three, small_ref[5:6, :])
     weight = small_ref[6:7, :]
@@ -1002,7 +1033,7 @@
     small_acc[2:3, :] += over_rows(last_grad * unit_three)
     small_acc[3:4, :] += over_rows(last_grad)
     grad = norm_back(last_grad, unit_three, scale_three, gain_three)
-    grad = grad + ffn_back(low, grad.astype(BF), own_ref, other_ref, HALF, acc, 0)
+    grad = grad + ffn_back(low, grad.astype(BF), own_ref, other_ref, HALF, acc, 0, kept)
     small_acc[0:1, :] += over_rows(grad * unit_two)
     small_acc[1:2, :] += over_rows(grad)
     grad = norm_back(grad, unit_two, scale_two, gain_two)
@@ -1098,39 +1129,43 @@
 
 def own_qkv_back_kernel(
     core_ref, qa_ref, kva_ref, gota_ref, qb_ref, kvb_ref, gotb_ref, start_ref, base_ref, w_ref,
-    out_ref, keep_ref, send_ref,
+    out_ref, low_ref, keep_ref, send_ref,
     acc,
 ):
     first_step(acc)
     low = start_ref[...].astype(BF)
     parts = qkv_parts((qa_ref, kva_ref, gota_ref), (qb_ref, kvb_ref, gotb_ref))
-    out_ref[...] = base_ref[...] + qkv_back(low, parts, w_ref, acc, 0)
+    grad = base_ref[...] + qkv_back(low, parts, w_ref, acc, 0)
+    out_ref[...] = grad
+    low_ref[...] = grad.astype(BF)
     last_step(core_ref, acc, keep_ref, send_ref)
 
 
 def other_qkv_back_kernel(
     core_ref, qa_ref, kva_ref, gota_ref, qb_ref, kvb_ref, gotb_ref, start_ref, base_ref, near_ref, far_ref,
-    out_ref, keep_ref, send_ref,
+    out_ref, low_ref, keep_ref, send_ref,
     acc, other_ref,
 ):
     join(core_ref, (near_ref, far_ref, other_ref))
     own_qkv_back_kernel(
         core_ref, qa_ref, kva_ref, gota_ref, qb_ref, kvb_ref, gotb_ref, start_ref, base_ref, other_ref,
-        out_ref, keep_ref, send_ref, acc,
+        out_ref, low_ref, keep_ref, send_ref, acc,
     )
 
 
 def both_qkv_back_kernel(
     core_ref, q0_grad_ref, kv0_ref, got0_ref, q1_grad_ref, kv1_ref, got1_ref, start_ref, base_ref,
-    own_ref, near_ref, far_ref, more_keep_ref, more_send_ref,
-    out_ref, keep_ref, send_ref,
+    own_ref, near_ref, far_ref, more_keep_ref, more_send_ref, small_ref,
+    out_ref, low_ref, keep_ref, send_ref,
     acc, other_ref,
 ):
     first_step(acc)
     join(core_ref, (near_ref, far_ref, other_ref))
     low = start_ref[...].astype(BF)
     grad = base_ref[...] + qkv_back(low, qkv_parts((q0_grad_ref, kv0_ref, got0_ref)), own_ref, acc, 0)
-    out_ref[...] = grad + qkv_back(low, qkv_parts((q1_grad_ref, kv1_ref, got1_ref)), other_ref, acc, 1)
+    grad = grad + qkv_back(low, qkv_parts((q1_grad_ref, kv1_ref, got1_ref)), other_ref, acc, 1)
+    out_ref[...] = grad
+    low_ref[...] = grad.astype(BF)
 
     @pl.when(pl.program_id(0) == pl.num_programs(0) - 1)
     def _():
@@ -1139,8 +1174,11 @@
         for part, ref, more_ref in ends:
             here = pl.ds(pl.multiple_of(part * rows, 16), rows)
             for which in range(2):
+                after = rows + more_ref.shape[1]
                 ref[which, :rows, :] = acc[which, here, :].astype(BF)
-                ref[which, rows:, :] = more_ref[which]
+                ref[which, rows:after, :] = more_ref[which]
+                ref[which, after : after + 16, :] = small_ref[pl.ds(pl.multiple_of(part * 16, 16), 16), :].astype(BF)
+                ref[which, after + 16 :, :] = jnp.zeros((ref.shape[1] - after - 16, D), BF)
 
 
 def rows_call(kernel, name, core, by_rows, whole, row_outs, whole_outs=(), scratch=(), block=512):
@@ -1171,7 +1209,7 @@
         compiler_params=pltpu.CompilerParams(vmem_limit_bytes=VMEM_BYTES),
         cost_estimate=COST,
         name=name,
-    )(core, *by_rows, *arrays)
+    )(core, *in_hbm(by_rows), *arrays)
 
 
 def put_rows(out_ref, at, values):
@@ -1305,23 +1343,23 @@
     return sum(v.astype(F32) for v in values).astype(BF)
 
 
-def over_chips(at, total, steps, last_steps):
+def over_chips(at, total, last_steps=1, back_steps=(1, 1, 1)):
     for mask, bit in zip(at.masks, at.bits):
         rows = total.shape[0] // 2
         half = lax.dynamic_slice_in_dim(total, (1 - bit) * rows, rows, 0)
-        got = yield partial(at.flip, mask=mask), half, steps
+        got = yield partial(at.flip, mask=mask), half, 1
         total = plus(lax.dynamic_slice_in_dim(total, bit * rows, rows, 0), got)
     total = total[None]
-    for mask in at.masks[::-1]:
+    for mask, steps in zip(at.masks[::-1], back_steps):
         got = yield partial(at.flip, mask=mask), total, steps
         total = jnp.concatenate([total, got])
     return total, (yield at.core_swap, total, last_steps)
 
 
-def summed(at, keep, send, core_steps=1, y_steps=1, steps=1, last_steps=1):
-    got = yield at.core_swap, send, core_steps
-    near = yield at.y_swap, plus(keep[1], got[1]), y_steps
-    return (yield from over_chips(at, plus(keep[0], got[0], near), steps, last_steps))
+def summed(at, keep, send, back_steps=(1, 1, 1)):
+    got = yield at.core_swap, send, 1
+    near = yield at.y_swap, plus(keep[1], got[1]), 1
+    return (yield from over_chips(at, plus(keep[0], got[0], near), 1, back_steps))
 
 
 def summed_other(at, keep, got, y_steps):
@@ -1331,13 +1369,7 @@
 
 def summed_own(at, keep, send, near):
     got = yield at.core_swap, send, 1
-    return (yield from over_chips(at, plus(keep[0], got[0], near), 1, 1))
-
-
-def summed_small(at, values):
-    for mask in [1, *at.masks]:
-        values = values + (yield partial(at.flip, mask=mask), values, 1)
-    return values + (yield at.y_swap, values, 1)
+    return (yield from over_chips(at, plus(keep[0], got[0], near)))
 
 
 def rows_of(weight):
@@ -1391,15 +1423,25 @@
     half_low = ((n, HALF), BF)
     kv_low = ((2, n, HALF), BF)
 
+    def embedding():
+        place = at.core[0] * n + jnp.arange(n, dtype=jnp.int32)
+        return signal(place.astype(F32)) + signal(jnp.ones((1,), F32))
+
     ints = jnp.concatenate([source_segment[0], target_segment[0], running[0, 0], running[1, 0]])
-    w_enc_qkv = rows_of(enc_qkv)
-    flow.add("source", moved(at, source_rows[:, 0], 1))
-    flow.add("w_enc_qkv", gathered(at, w_enc_qkv))
     ints = ints.reshape(6, n)
-    flow.add("ints", moved(at, ints, 1))
-    (target_rows,) = flow.step((target_rows,))
-
-    w_dec_self = jnp.concatenate([rows_of(dec_qkv), rows_of(dec_proj)])
+    flow.add("source", moved(at, source_rows[:, 0], 3))
+    flow.add("ints", moved(at, ints, 2))
+    (enc_qkv_now,) = flow.step((enc_qkv,))
+    w_enc_qkv = rows_of(enc_qkv_now)
+    flow.add("w_enc_qkv", gathered(at, w_enc_qkv, 2, 1))
+    ints, dec_qkv_now = flow.step((ints, dec_qkv))
+    w_dec_self = jnp.concatenate([rows_of(dec_qkv_now), rows_of(dec_proj)])
+    ints, w_dec_self, embedding = flow.step((ints, w_dec_self, embedding()))
+    ints = jnp.where(at.stays, ints, flow.results["ints"])
+    runs = jnp.transpose(jnp.pad(ints[4:].astype(F32), ((0, 126), (0, 0))))
+    lane = jnp.arange(128, dtype=jnp.int32) % DH
+    source_hot, target_hot = (ints[:4].reshape(2, 2 * n, 1) == lane).astype(BF)
+
     w_enc = jnp.concatenate([rows_of(enc_proj), rows_of(enc_up), rows_of(enc_down)])
     w_cross = jnp.concatenate([rows_of(cross_query), rows_of(cross_kv)])
     w_dec = jnp.concatenate([rows_of(cross_proj), rows_of(dec_up), rows_of(dec_down)])
@@ -1413,17 +1455,11 @@
         [dec_gains[0], dec_shifts[0], dec_gains[1], dec_shifts[1], dec_gains[2], dec_shifts[2], halt_weight[1]]
     )
     small_dec = jnp.concatenate([small_dec, pad[:1]])
-    place = at.core[0] * n + jnp.arange(n, dtype=jnp.int32)
-    embedding = signal(place.astype(F32)) + signal(jnp.ones((1,), F32))
 
     flow.add("target", moved(at, target_rows[:, 0], 2))
     flow.add("w_dec_self", gathered(at, w_dec_self, 2, 1))
-    w_enc, w_cross, w_dec, embedding, cots = flow.step((w_enc, w_cross, w_dec, embedding, cots))
-    ints = jnp.where(at.stays, ints, flow.results["ints"])
-    runs = jnp.transpose(jnp.pad(ints[4:].astype(F32), ((0, 126), (0, 0))))
-    lane = jnp.arange(128, dtype=jnp.int32) % DH
-    source_hot, target_hot = (ints[:4].reshape(2, 2 * n, 1) == lane).astype(BF)
-    source_hot, target_hot = flow.step((source_hot, target_hot))
+    embedding, source_hot, target_hot = flow.step((embedding, source_hot, target_hot))
+    (embedding,) = flow.step((embedding,))
 
     def pre(rows, got, own, other):
         return rows_call(
@@ -1446,10 +1482,10 @@
     got0, got1 = at.core_swap(kv0), at.core_swap(kv1)
     enc_o0, enc_kept0 = attend(q0, kv0, got0, source_hot, source_hot)
     flow.add("w_enc", gathered(at, w_enc, 2, 1))
-    enc_o0, q1, kv1, got1 = flow.step((enc_o0, q1, kv1, got1))
+    enc_o0, q1, kv1, got1, w_enc, w_cross = flow.step((enc_o0, q1, kv1, got1, w_enc, w_cross))
     target = flow.results["target"]
     enc_o1, enc_kept1 = attend(q1, kv1, got1, source_hot, source_hot)
-    enc_o1, target = flow.step((enc_o1, target))
+    enc_o1, target, w_dec = flow.step((enc_o1, target, w_dec))
 
     w_dec_self_got = flow.results["w_dec_self"]
     dec_start, q0, q1, kv0, kv1 = pre(target_rows[:, 0], target, w_dec_self, w_dec_self_got)
@@ -1497,7 +1533,7 @@
         dec_post_kernel, "decoder_feed", at.core,
         [cross_o0, cross_o1, dec_sum_one, dec_start, runs, dec_cot], [w_dec, *w_dec_got, small_dec],
         [row_low, row, row, half_low, half_low], grad_outs(9 * HALF),
-        [*grad_scratch(9 * HALF), (w_dec.shape, BF)],
+        [*grad_scratch(9 * HALF), (w_dec.shape, BF), ((2, 512, 4 * D), BF)],
     )
     flow.add("dec", summed(at, *dec_parts))
     flow.add("dec_states", moved(at, dec_states, 1))
@@ -1530,25 +1566,24 @@
         [(w_cross, HALF, 0), *w_cross_got, *self_proj, small_dec],
         [row, half_low, half_low], grad_outs(2 * HALF), grad_scratch(2 * HALF),
     )
-    flow.add("small", summed_small(at, jnp.concatenate([small_enc_grad, small_one, small_two])))
-    enc_o1_grad, mid_parts = flow.step((enc_o1_grad, mid_parts))
+    smalls = jnp.concatenate([small_enc_grad, small_one, small_two, jnp.zeros((8, D), F32)])
+    enc_o1_grad, mid_parts, smalls = flow.step((enc_o1_grad, mid_parts, smalls))
 
     q1_grad, kv1_grad, kv1_send = attend_back(enc_kept1, enc_o1_grad)
+    q1_grad, kv1_grad, kv1_send, enc_o0_grad = flow.step((q1_grad, kv1_grad, kv1_send, enc_o0_grad))
     kv1_got = at.core_swap(kv1_send)
-    q1_grad, kv1_grad, enc_o0_grad = flow.step((q1_grad, kv1_grad, enc_o0_grad))
     q0_grad, kv0_grad, kv0_send = attend_back(enc_kept0, enc_o0_grad)
+    q0_grad, kv0_grad, kv0_send, kv1_got = flow.step((q0_grad, kv0_grad, kv0_send, kv1_got))
     kv0_got = at.core_swap(kv0_send)
-    q0_grad, kv0_grad, kv1_got, q1_grad = flow.step((q0_grad, kv0_grad, kv1_got, q1_grad))
-    source_grad, keep, send = rows_call(
+    source_grad, source_low, keep, send = rows_call(
         both_qkv_back_kernel, "project_back", at.core,
         [q0_grad, kv0_grad, kv0_got, q1_grad, kv1_grad, kv1_got, enc_start, enc_base],
-        [w_enc_qkv, *w_enc_qkv_got, *mid_parts], [row], [((2, 5 * HALF // 2, D), BF)] * 2,
+        [w_enc_qkv, *w_enc_qkv_got, *mid_parts, smalls], [row, row_low], [((2, 3 * HALF, D), BF)] * 2,
         [((2, 3 * HALF, D), F32), (w_enc_qkv.shape, BF)],
     )
-    source_low = source_grad.astype(BF)
-    flow.add("enc_qkv", summed(at, keep, send))
+    flow.add("enc_qkv", summed(at, keep, send, (1, 2, 1)))
     flow.add("source_grad", moved(at, source_low, 1))
-    (self_o1_grad,) = flow.step((self_o1_grad,))
+    self_o1_grad, source_grad = flow.step((self_o1_grad, source_grad))
 
     def heads_back(kept, grad):
         parts = []
@@ -1561,18 +1596,17 @@
     parts = heads_back(self_kept1, self_o1_grad)
     part_outs = [((1, 3 * HALF // 2, D), BF)] * 2
     part_scratch = [((1, 3 * HALF, D), F32)]
-    target_grad, keep1, send1 = rows_call(
+    target_grad, _, keep1, send1 = rows_call(
         other_qkv_back_kernel, "project_back", at.core, [*parts, dec_start, dec_base],
-        [*w_dec_self_got], [row], part_outs, [*part_scratch, (w_dec_self.shape, BF)],
+        [*w_dec_self_got], [row, row_low], part_outs, [*part_scratch, (w_dec_self.shape, BF)],
     )
     flow.add("dec_qkv_other", summed_other(at, keep1, at.core_swap(send1), 1))
     target_grad, self_o0_grad = flow.step((target_grad, self_o0_grad))
     parts = heads_back(self_kept0, self_o0_grad)
-    target_grad, keep0, send0 = rows_call(
+    target_grad, target_low, keep0, send0 = rows_call(
         own_qkv_back_kernel, "project_back", at.core, [*parts, dec_start, target_grad],
-        [(w_dec_self, 3 * HALF, 0)], [row], part_outs, part_scratch,
-    )
-    target_low = target_grad.astype(BF)
+        [(w_dec_self, 3 * HALF, 0)], [row, row_low], part_outs, part_scratch,
+    )
     flow.add("dec_qkv", summed_own(at, keep0, send0, flow.results["dec_qkv_other"]))
     flow.add("target_grad", moved(at, target_low, 2))
 
@@ -1586,15 +1620,17 @@
         return unpack(at.order, *done[name], [w.shape for w in weights], places)
 
     def home(values, name):
-        return jnp.where(at.stays, values, done[name].astype(values.dtype))[:, None]
+        values = jnp.where(at.stays, values, done[name].astype(values.dtype))[:, None]
+        return with_layout_constraint(values, Layout((0, 1, 2))) if values.dtype == F32 else values
 
     def mixed_weights(name):
         part, more = 3 * HALF // 2, HALF // 2
         places = []
         for c in range(2):
-            begin = c * (part + 2 * more)
+            begin = c * 3 * HALF
             places += [(0, begin, c * part, part), (1 + c, begin + part, 0, 2 * more)]
-        shapes = [enc_qkv.shape, cross_query.shape, dec_proj.shape]
+            places += [(3, begin + part + 2 * more, 16 * c, 16)]
+        shapes = [enc_qkv.shape, cross_query.shape, dec_proj.shape, (32, D)]
         return unpack(at.order, *done[name], shapes, places)
 
     target_grad, done["dec"] = flow.step((target_grad, done["dec"]))
@@ -1605,18 +1641,17 @@
     source_out = home(source_grad, "source_grad")
     source_out, enc_states, dec_states = flow.step((source_out, enc_states, dec_states))
     states_out = home(enc_states, "enc_states"), home(dec_states, "dec_states")
-    states_out, done["enc_qkv"] = flow.step((states_out, done["enc_qkv"]))
+    states_out, target_grad = flow.step((states_out, target_grad))
+    target_out = home(target_grad, "target_grad")
+    target_out, done["enc_qkv"] = flow.step((target_out, done["enc_qkv"]))
     mixed_grads = mixed_weights("enc_qkv")
-    mixed_grads, target_grad = flow.step((mixed_grads, target_grad))
-    target_out = home(target_grad, "target_grad")
-    (target_out,) = flow.step((target_out,))
+    (mixed_grads,) = flow.step((mixed_grads,))
     flow.finish()
     cross_proj_grad, dec_up_grad, dec_down_grad = dec_grads
     cross_kv_grad, enc_proj_grad, enc_up_grad, enc_down_grad = enc_grads
-    enc_qkv_grad, cross_query_grad, dec_proj_grad = mixed_grads
+    enc_qkv_grad, cross_query_grad, dec_proj_grad, small = mixed_grads
     (dec_qkv_grad,) = weights("dec_qkv", dec_qkv)
-    small = done["small"]
-    enc_small, one, two = small[:8], small[8:16], small[16:]
+    enc_small, one, two = small[:8], small[8:16], small[16:24]
     return (
         *states_out,
         source_out,

time: 604 us -> 587 us (0.972)
  other arithmetic: 53.1 us -> 43.1 us
    ppermute x56 -> x52, starting transfers between devices: 60 us -> 51.4 us  [flip(): lax.ppermute(values, 'dp', [(d, d ^ mask) for d in range(self.dp_size)])]
    unnamed x176 -> x164, local copies, waits for them, and re-layouts: 21.6 us -> 15 us
    broadcast_in_dim x0 -> x3, local copies, waits for them, and re-layouts: none -> 6.23 us  [the longest x2 6.23 us: home(): jnp.where(at.stays, values, done[name].astype(values.dtype))[:, None]]
    ppermute x56 -> x52, waiting for transfers between devices: 46.2 us -> 40.7 us  [flip(): lax.ppermute(values, 'dp', [(d, d ^ mask) for d in range(self.dp_size)])]
    ppermute x10 -> x9, starting transfers between devices: 12.8 us -> 17.6 us  [y_swap(): return lax.ppermute(values, 'mp', [(0, 1), (1, 0)])]
    ppermute x10 -> x9, waiting for transfers between devices: 21.9 us -> 26.1 us  [y_swap(): return lax.ppermute(values, 'mp', [(0, 1), (1, 0)])]
  transfers between devices with their start and end apart: 74 -> 69, of which waited for: 27 -> 26; matrix products, arithmetic and copies ran while one was open for 10% -> 8% of each run, Pallas kernels for 57% -> 59%
where the time goes in v4:
time: 587 us; the launch traced here: 581 us
  Pallas kernels  345 us (59%)
  starting transfers between devices  79.2 us (13%)
  waiting for transfers between devices  66.8 us (11%)
  local copies, waits for them, and re-layouts  44.8 us (8%)
  other arithmetic  43.1 us (7%)
    pallas_call x8, Pallas kernels, heads_backward(): pl.pallas_call(partial(backward_kernel, causal=causal), grid=(width // 12...  137 us
    pallas_call x10, Pallas kernels, rows_call(): pl.pallas_call(kernel, grid=(n // block,), in_specs=[pl.BlockSpec(memory_...  121 us
    pallas_call x6, Pallas kernels, heads_forward(): pl.pallas_call(partial(forward_kernel, causal=causal), grid=(width // 128...  73 us
    ppermute x52, starting transfers between devices, flip(): lax.ppermute(values, 'dp', [(d, d ^ mask) for d in range(self.dp_size)])  51.4 us
    ppermute x52, waiting for transfers between devices, flip(): lax.ppermute(values, 'dp', [(d, d ^ mask) for d in range(self.dp_size)])  40.7 us
    ppermute x9, waiting for transfers between devices, y_swap(): return lax.ppermute(values, 'mp', [(0, 1), (1, 0)])  26.1 us
    ppermute x9, starting transfers between devices, y_swap(): return lax.ppermute(values, 'mp', [(0, 1), (1, 0)])  17.6 us
    unnamed x164, local copies, waits for them, and re-layouts  15 us
  transfers between devices with their start and end apart: 69, of which 26 were waited for; matrix products, arithmetic and copies ran while one was open for 8% of the time, Pallas kernels for 59%

profile of v4, /device:TPU:0, one launch (start us, length us, event | category | flops | bytes accessed | tf_op | source)
XLA Modules:
  0.0 581.1 jit_solution(15052294253095390552)
XLA Ops:
  7.7 6.2 %collective-permute-start.2 = (bf16[384,512]{1,0:T(8,128)(2,1)}, bf16[384,512]{1,0:T(8,128)(2,1)S(1)}, u32[]{:S(2)}, u32[]{:S(2)}) collective-permute-start(bf16[384,512]{1,0:T(8,128)(2,1)} %constant_dynamic-slice_fusion.16), channel_id=1, source_target_pairs={{0,1},{1,0},{2,3},{3,2},{4,5},{5,4},{6,7},{7,6},{8,9},{9,8},{10,11... | collective-permute-start | bytes 1179656 | tf_op jit(solution)/shard_map/ppermute | solution.py:1286
  23.9 11.3 %collective-permute-done.2.near_ref = bf16[384,512]{1,0:T(8,128)(2,1)S(1)} collective-permute-done((bf16[384,512]{1,0:T(8,128)(2,1)}, bf16[384,512]{1,0:T(8,128)(2,1)S(1)}, u32[]{:S(2)}, u32[]{:S(2)}) %collective-permute-start.2) | collective-permute-done | bytes 393248 | tf_op jit(solution)/shard_map/ppermute | solution.py:1286
  39.8 5.3 project.2
  50.9 14.0 %attention.4 = (bf16[1024,256]{1,0:T(8,128)(2,1)}, f32[1024,256]{1,0:T(8,128)}) custom-call(s32[2]{0:T(128)} %get-tuple-element.857.core_ref, bf16[1024,256]{1,0:T(8,128)(2,1)} %get-tuple-element.443.q_ref, bf16[2,1024,256]{2,1,0:T(8,128)(2,1)} %get-tuple-element.444.own_ref, bf16[2,1024,256]{2,1,0:T(8,128)(2,1)} %collective-permute-done.4.got_ref, ...), custom_call_target="tpu_custom_call" | custom-call | flops 1 | bytes 1 | tf_op jit(solution)/shard_map/attention/pallas_call | solution.py:633
  66.3 14.6 %attention.5 = (bf16[1024,256]{1,0:T(8,128)(2,1)}, f32[1024,256]{1,0:T(8,128)}) custom-call(s32[2]{0:T(128)} %get-tuple-element.857.core_ref, bf16[1024,256]{1,0:T(8,128)(2,1)} %get-tuple-element.458.q_ref, bf16[2,1024,256]{2,1,0:T(8,128)(2,1)} %get-tuple-element.459.own_ref, bf16[2,1024,256]{2,1,0:T(8,128)(2,1)} %collective-permute-done.5.got_ref, ...), custom_call_target="tpu_custom_call" | custom-call | flops 1 | bytes 1 | tf_op jit(solution)/shard_map/attention/pallas_call | solution.py:633
  81.7 5.4 project.3
  91.0 8.4 %attention_causal.2 = (bf16[1024,256]{1,0:T(8,128)(2,1)}, f32[1024,256]{1,0:T(8,128)}) custom-call(s32[2]{0:T(128)} %get-tuple-element.857.core_ref, bf16[1024,256]{1,0:T(8,128)(2,1)} %get-tuple-element.469.q_ref, bf16[2,1024,256]{2,1,0:T(8,128)(2,1)} %get-tuple-element.470.own_ref, bf16[2,1024,256]{2,1,0:T(8,128)(2,1)} %copy-done.9, ...), custom_call_target="tpu_custom_call" | custom-call | flops 1 | bytes 1 | tf_op jit(solution)/shard_map/attention_causal/pallas_call | solution.py:633
  99.4 5.0 collective-permute-start.13
  109.6 8.1 %attention_causal.3 = (bf16[1024,256]{1,0:T(8,128)(2,1)}, f32[1024,256]{1,0:T(8,128)}) custom-call(s32[2]{0:T(128)} %get-tuple-element.857.core_ref, bf16[1024,256]{1,0:T(8,128)(2,1)} %get-tuple-element.483.q_ref, bf16[2,1024,256]{2,1,0:T(8,128)(2,1)} %get-tuple-element.484.own_ref, bf16[2,1024,256]{2,1,0:T(8,128)(2,1)} %copy-done.10, ...), custom_call_target="tpu_custom_call" | custom-call | flops 1 | bytes 1 | tf_op jit(solution)/shard_map/attention_causal/pallas_call | solution.py:633
  127.6 12.0 %encoder_feed.1 = (f32[1024,512]{1,0:T(8,128)}, f32[1024,512]{1,0:T(8,128)}, bf16[1024,512]{1,0:T(8,128)(2,1)}) custom-call(s32[2]{0:T(128)} %get-tuple-element.857.core_ref, bf16[1024,256]{1,0:T(8,128)(2,1)} %get-tuple-element.496.o0_ref.o_ref, bf16[1024,256]{1,0:T(8,128)(2,1)} %get-tuple-element.497.o1_ref.o_ref, ...), custom_call_target="tpu_custom_call" | custom-call | flops 1 | bytes 1 | tf_op jit(solution)/shard_map/encoder_feed/pallas_call | solution.py:1199
  140.4 7.0 %cross_project.1 = (f32[1024,512]{1,0:T(8,128)}, bf16[1024,256]{1,0:T(8,128)(2,1)}, bf16[1024,256]{1,0:T(8,128)(2,1)}, bf16[2,1024,256]{2,1,0:T(8,128)(2,1)}, bf16[2,1024,256]{2,1,0:T(8,128)(2,1)}) custom-call(s32[2]{0:T(128)} %get-tuple-element.857.core_ref, bf16[1024,256]{1,0:T(8,128)(2,1)} %get-tuple-element.482.o0_ref.o_ref, ...), custom_call_target="tpu_custom_call" | custom-call | flops 1 | bytes 1 | tf_op jit(solution)/shard_map/cross_project/pallas_call | solution.py:1199
  151.3 13.8 %attention.6 = (bf16[1024,256]{1,0:T(8,128)(2,1)}, f32[1024,256]{1,0:T(8,128)}) custom-call(s32[2]{0:T(128)} %get-tuple-element.857.core_ref, bf16[1024,256]{1,0:T(8,128)(2,1)} %get-tuple-element.510.q_ref, bf16[2,1024,256]{2,1,0:T(8,128)(2,1)} %get-tuple-element.511.own_ref, bf16[2,1024,256]{2,1,0:T(8,128)(2,1)} %copy-done.20, ...), custom_call_target="tpu_custom_call" | custom-call | flops 1 | bytes 1 | tf_op jit(solution)/shard_map/attention/pallas_call | solution.py:633
  166.3 14.0 %attention.7 = (bf16[1024,256]{1,0:T(8,128)(2,1)}, f32[1024,256]{1,0:T(8,128)}) custom-call(s32[2]{0:T(128)} %get-tuple-element.857.core_ref, bf16[1024,256]{1,0:T(8,128)(2,1)} %get-tuple-element.517.q_ref, bf16[2,1024,256]{2,1,0:T(8,128)(2,1)} %get-tuple-element.518.own_ref, bf16[2,1024,256]{2,1,0:T(8,128)(2,1)} %copy-done.19, ...), custom_call_target="tpu_custom_call" | custom-call | flops 1 | bytes 1 | tf_op jit(solution)/shard_map/attention/pallas_call | solution.py:633
  183.4 30.5 %decoder_feed.1 = (bf16[1024,512]{1,0:T(8,128)(2,1)}, f32[1024,512]{1,0:T(8,128)}, f32[1024,512]{1,0:T(8,128)}, bf16[1024,256]{1,0:T(8,128)(2,1)}, bf16[1024,256...) custom-call(s32[2]{0:T(128)} %get-tuple-element.857.core_ref, ...), custom_call_target="tpu_custom_call" | custom-call | flops 1 | bytes 1 | tf_op jit(solution)/shard_map/decoder_feed/pallas_call | solution.py:1199
  217.5 25.2 %attention_back.4 = (bf16[1024,256]{1,0:T(8,128)(2,1)}, bf16[2,1024,256]{2,1,0:T(8,128)(2,1)}, bf16[2,1024,256]{2,1,0:T(8,128)(2,1)}) custom-call(s32[2]{0:T(128)} %get-tuple-element.857.core_ref, bf16[1024,256]{1,0:T(8,128)(2,1)} %get-tuple-element.510.q_ref, bf16[2,1024,256]{2,1,0:T(8,128)(2,1)} %get-tuple-element.511.own_ref, ...), custom_call_target="tpu_custom_call" | custom-call | flops 1 | bytes 1 | tf_op jit(solution)/shard_map/attention_back/pallas_call | solution.py:776
  247.8 25.1 %attention_back.5 = (bf16[1024,256]{1,0:T(8,128)(2,1)}, bf16[2,1024,256]{2,1,0:T(8,128)(2,1)}, bf16[2,1024,256]{2,1,0:T(8,128)(2,1)}) custom-call(s32[2]{0:T(128)} %get-tuple-element.857.core_ref, bf16[1024,256]{1,0:T(8,128)(2,1)} %get-tuple-element.517.q_ref, bf16[2,1024,256]{2,1,0:T(8,128)(2,1)} %get-tuple-element.518.own_ref, ...), custom_call_target="tpu_custom_call" | custom-call | flops 1 | bytes 1 | tf_op jit(solution)/shard_map/attention_back/pallas_call | solution.py:776
  279.8 29.3 %encoder_feed_back.1 = (f32[1024,512]{1,0:T(8,128)}, bf16[1024,256]{1,0:T(8,128)(2,1)}, bf16[1024,256]{1,0:T(8,128)(2,1)}, bf16[2,1408,512]{2,1,0:T(8,128)(2,1)}...) custom-call(s32[2]{0:T(128)} %get-tuple-element.857.core_ref, bf16[2,1024,256]{2,1,0:T(8,128)(2,1)} %get-tuple-element.550.kv0_ref, ...), custom_call_target="tpu_custom_call" | custom-call | flops 1 | bytes 1 | tf_op jit(solution)/shard_map/encoder_feed_back/pallas_call | solution.py:1199
  312.1 9.3 %cross_project_back.1 = (f32[1024,512]{1,0:T(8,128)}, bf16[1024,256]{1,0:T(8,128)(2,1)}, bf16[1024,256]{1,0:T(8,128)(2,1)}, bf16[2,256,512]{2,1,0:T(8,128)(2,1)}...) custom-call(s32[2]{0:T(128)} %get-tuple-element.857.core_ref, bf16[1024,256]{1,0:T(8,128)(2,1)} %get-tuple-element.577.q0_grad_ref, ...), custom_call_target="tpu_custom_call" | custom-call | flops 1 | bytes 1 | tf_op jit(solution)/shard_map/cross_project_back/pallas_call | solution.py:1199
  330.6 25.0 %attention_back.6 = (bf16[1024,256]{1,0:T(8,128)(2,1)}, bf16[2,1024,256]{2,1,0:T(8,128)(2,1)}, bf16[2,1024,256]{2,1,0:T(8,128)(2,1)}) custom-call(s32[2]{0:T(128)} %get-tuple-element.857.core_ref, bf16[1024,256]{1,0:T(8,128)(2,1)} %get-tuple-element.458.q_ref, bf16[2,1024,256]{2,1,0:T(8,128)(2,1)} %get-tuple-element.459.own_ref, ...), custom_call_target="tpu_custom_call" | custom-call | flops 1 | bytes 1 | tf_op jit(solution)/shard_map/attention_back/pallas_call | solution.py:776
  355.6 4.7 collective-permute-done.29
  367.4 24.9 %attention_back.7 = (bf16[1024,256]{1,0:T(8,128)(2,1)}, bf16[2,1024,256]{2,1,0:T(8,128)(2,1)}, bf16[2,1024,256]{2,1,0:T(8,128)(2,1)}) custom-call(s32[2]{0:T(128)} %get-tuple-element.857.core_ref, bf16[1024,256]{1,0:T(8,128)(2,1)} %get-tuple-element.443.q_ref, bf16[2,1024,256]{2,1,0:T(8,128)(2,1)} %get-tuple-element.444.own_ref, ...), custom_call_target="tpu_custom_call" | custom-call | flops 1 | bytes 1 | tf_op jit(solution)/shard_map/attention_back/pallas_call | solution.py:776
  400.0 9.7 %project_back.3 = (f32[1024,512]{1,0:T(8,128)}, bf16[1024,512]{1,0:T(8,128)(2,1)}, bf16[2,768,512]{2,1,0:T(8,128)(2,1)}, bf16[2,768,512]{2,1,0:T(8,128)(2,1)}) custom-call(s32[2]{0:T(128)} %get-tuple-element.857.core_ref, bf16[1024,256]{1,0:T(8,128)(2,1)} %get-tuple-element.625.q0_grad_ref, bf16[2,1024,256]{2,1,0:T(8,128)(2,1)} %get-tuple-element.626.kv0_ref, ...), custom_call_target="tpu_custom_call" | custom-call | flops 1 | bytes 1 | tf_op jit(solution)/shard_map/project_back/pallas_call | solution.py:1199
  419.4 9.0 %attention_causal_back.4 = (bf16[1024,128]{1,0:T(8,128)(2,1)}, bf16[2,1024,128]{2,1,0:T(8,128)(2,1)}, bf16[2,1024,128]{2,1,0:T(8,128)(2,1)}) custom-call(s32[2]{0:T(128)} %get-tuple-element.857.core_ref, bf16[1024,256]{1,0:T(8,128)(2,1)} %get-tuple-element.483.q_ref, bf16[2,1024,256]{2,1,0:T(8,128)(2,1)} %get-tuple-element.484.own_ref, ...), custom_call_target="tpu_custom_call" | custom-call | flops 1 | bytes 1 | tf_op jit(solution)/shard_map/attention_causal_back/pallas_call | solution.py:776
  442.7 9.2 %attention_causal_back.5 = (bf16[1024,128]{1,0:T(8,128)(2,1)}, bf16[2,1024,128]{2,1,0:T(8,128)(2,1)}, bf16[2,1024,128]{2,1,0:T(8,128)(2,1)}) custom-call(s32[2]{0:T(128)} %get-tuple-element.857.core_ref, bf16[1024,256]{1,0:T(8,128)(2,1)} %get-tuple-element.483.q_ref, bf16[2,1024,256]{2,1,0:T(8,128)(2,1)} %get-tuple-element.484.own_ref, ...), custom_call_target="tpu_custom_call" | custom-call | flops 1 | bytes 1 | tf_op jit(solution)/shard_map/attention_causal_back/pallas_call | solution.py:776
  453.5 7.3 %collective-permute-done.42 = bf16[768,512]{1,0:T(8,128)(2,1)} collective-permute-done((bf16[768,512]{1,0:T(8,128)(2,1)}, bf16[768,512]{1,0:T(8,128)(2,1)}, u32[]{:S(2)}, u32[]{:S(2)}) %collective-permute-start.42) | collective-permute-done | bytes 786464 | tf_op jit(solution)/shard_map/ppermute | solution.py:1286
  466.1 6.1 %project_back.4 = (f32[1024,512]{1,0:T(8,128)}, bf16[1024,512]{1,0:T(8,128)(2,1)}, bf16[1,384,512]{2,1,0:T(8,128)(2,1)}, bf16[1,384,512]{2,1,0:T(8,128)(2,1)}) custom-call(s32[2]{0:T(128)} %get-tuple-element.857.core_ref, bf16[1024,128]{1,0:T(8,128)(2,1)} %get-tuple-element.661.qa_ref, bf16[2,1024,128]{2,1,0:T(8,128)(2,1)} %get-tuple-element.662.kva_ref, ...), custom_call_target="tpu_custom_call" | custom-call | flops 1 | bytes 1 | tf_op jit(solution)/shard_map/project_back/pallas_call | solution.py:1199
  480.8 9.2 %attention_causal_back.6 = (bf16[1024,128]{1,0:T(8,128)(2,1)}, bf16[2,1024,128]{2,1,0:T(8,128)(2,1)}, bf16[2,1024,128]{2,1,0:T(8,128)(2,1)}) custom-call(s32[2]{0:T(128)} %get-tuple-element.857.core_ref, bf16[1024,256]{1,0:T(8,128)(2,1)} %get-tuple-element.469.q_ref, bf16[2,1024,256]{2,1,0:T(8,128)(2,1)} %get-tuple-element.470.own_ref, ...), custom_call_target="tpu_custom_call" | custom-call | flops 1 | bytes 1 | tf_op jit(solution)/shard_map/attention_causal_back/pallas_call | solution.py:776
  490.1 5.5 collective-permute-done.51
  499.3 9.0 %attention_causal_back.7 = (bf16[1024,128]{1,0:T(8,128)(2,1)}, bf16[2,1024,128]{2,1,0:T(8,128)(2,1)}, bf16[2,1024,128]{2,1,0:T(8,128)(2,1)}) custom-call(s32[2]{0:T(128)} %get-tuple-element.857.core_ref, bf16[1024,256]{1,0:T(8,128)(2,1)} %get-tuple-element.469.q_ref, bf16[2,1024,256]{2,1,0:T(8,128)(2,1)} %get-tuple-element.470.own_ref, ...), custom_call_target="tpu_custom_call" | custom-call | flops 1 | bytes 1 | tf_op jit(solution)/shard_map/attention_causal_back/pallas_call | solution.py:776
  508.4 4.5 collective-permute-start.55
  515.4 5.9 %project_back.5 = (f32[1024,512]{1,0:T(8,128)}, bf16[1024,512]{1,0:T(8,128)(2,1)}, bf16[1,384,512]{2,1,0:T(8,128)(2,1)}, bf16[1,384,512]{2,1,0:T(8,128)(2,1)}) custom-call(s32[2]{0:T(128)} %get-tuple-element.857.core_ref, bf16[1024,128]{1,0:T(8,128)(2,1)} %get-tuple-element.704.qa_ref, bf16[2,1024,128]{2,1,0:T(8,128)(2,1)} %get-tuple-element.705.kva_ref, ...), custom_call_target="tpu_custom_call" | custom-call | flops 1 | bytes 1 | tf_op jit(solution)/shard_map/project_back/pallas_call | solution.py:1199
  531.4 4.9 unpack.5
  (409 shorter events, 199.3 us)
Async XLA Ops:
  3.1 17.4 %collective-permute-start = (s32[6,1024]{0,1:T(8,128)}, s32[6,1024]{0,1:T(8,128)S(1)}, u32[]{:S(2)}, u32[]{:S(2)}) collective-permute-start(s32[6,1024]{0,1:T(8,128)} %copy.46), channel_id=1, source_target_pairs={{1,2},{2,1},{5,6},{6,5},{9,10},{10,9},{13,14},{14,13},{17,18},{18,... | collective-permute-start | bytes 73736 | tf_op jit(solution)/shard_map/ppermute | solution.py:1292
  3.9 31.2 %collective-permute-start.1 = (bf16[1024,512]{1,0:T(8,128)(2,1)}, bf16[1024,512]{1,0:T(8,128)(2,1)}, u32[]{:S(2)}, u32[]{:S(2)}) collective-permute-start(bf16[1024,512]{1,0:T(8,128)(2,1)} %bitcast.70), channel_id=1, source_target_pairs={{1,2},{2,1},{5,6},{6,5},{9,10},{10,9},{13,14},{14,13},{17,18},{18,... | collective-permute-start | bytes 3145736 | tf_op jit(solution)/shard_map/ppermute | solution.py:1292
  7.7 27.4 %collective-permute-start.2 = (bf16[384,512]{1,0:T(8,128)(2,1)}, bf16[384,512]{1,0:T(8,128)(2,1)S(1)}, u32[]{:S(2)}, u32[]{:S(2)}) collective-permute-start(bf16[384,512]{1,0:T(8,128)(2,1)} %constant_dynamic-slice_fusion.16), channel_id=1, source_target_pairs={{0,1},{1,0},{2,3},{3,2},{4,5},{5,4},{6,7},{7,6},{8,9},{9,8},{10,11... | collective-permute-start | bytes 1179656 | tf_op jit(solution)/shard_map/ppermute | solution.py:1286
  37.2 28.0 %collective-permute-start.6 = (bf16[1024,512]{1,0:T(8,128)(2,1)S(1)}, bf16[1024,512]{1,0:T(8,128)(2,1)}, u32[]{:S(2)}, u32[]{:S(2)}) collective-permute-start(bf16[1024,512]{1,0:T(8,128)(2,1)S(1)} %bitcast.69), channel_id=1, source_target_pairs={{1,2},{2,1},{5,6},{6,5},{9,10},{10,9},{13,14},{14,13},{17,18},{18,... | collective-permute-start | bytes 3145736 | tf_op jit(solution)/shard_map/ppermute | solution.py:1292
  46.7 18.5 %collective-permute-start.5 = (bf16[2,1024,256]{2,1,0:T(8,128)(2,1)}, bf16[2,1024,256]{2,1,0:T(8,128)(2,1)}, u32[]{:S(2)}, u32[]{:S(2)}) collective-permute-start(bf16[2,1024,256]{2,1,0:T(8,128)(2,1)} %get-tuple-element.459.own_ref), channel_id=1, source_target_pairs={{0,2},{2,0},{4,6},{6,4},{8,10},{10,8},{12,14},{14,12},{16,18},{18,... | collective-permute-start | bytes 3145736 | tf_op jit(solution)/shard_map/ppermute | solution.py:1280
  48.2 16.9 %collective-permute-start.7 = (bf16[512,512]{1,0:T(8,128)(2,1)}, bf16[512,512]{1,0:T(8,128)(2,1)S(1)}, u32[]{:S(2)}, u32[]{:S(2)}) collective-permute-start(bf16[512,512]{1,0:T(8,128)(2,1)} %constant_dynamic-slice_fusion.15), channel_id=1, source_target_pairs={{0,1},{1,0},{2,3},{3,2},{4,5},{5,4},{6,7},{7,6},{8,9},{9,8},{10,11... | collective-permute-start | bytes 1572872 | tf_op jit(solution)/shard_map/ppermute | solution.py:1286
  65.2 15.7 %collective-permute-start.8 = (bf16[512,512]{1,0:T(8,128)(2,1)S(1)}, bf16[512,512]{1,0:T(8,128)(2,1)S(1)}, u32[]{:S(2)}, u32[]{:S(2)}) collective-permute-start(bf16[512,512]{1,0:T(8,128)(2,1)S(1)} %collective-permute-done.7.near_ref.proj_near_ref), channel_id=1, source_target_pairs={{0,2},{2,0},{4,6},{6,4},{8,10},{10,8},{12,14},{14,12},{16,18},{18,... | collective-permute-start | bytes 1572872 | tf_op jit(solution)/shard_map/ppermute | solution.py:1280
  65.4 34.0 %collective-permute-start.11 = (bf16[1152,512]{1,0:T(8,128)(2,1)}, bf16[1152,512]{1,0:T(8,128)(2,1)S(1)}, u32[]{:S(2)}, u32[]{:S(2)}) collective-permute-start(bf16[1152,512]{1,0:T(8,128)(2,1)} %constant_dynamic-slice_fusion.14), channel_id=1, source_target_pairs={{0,1},{1,0},{2,3},{3,2},{4,5},{5,4},{6,7},{7,6},{8,9},{9,8},{10,11... | collective-permute-start | bytes 3538952 | tf_op jit(solution)/shard_map/ppermute | solution.py:1286
  99.4 19.6 %collective-permute-start.13 = (bf16[1152,512]{1,0:T(8,128)(2,1)S(1)}, bf16[1152,512]{1,0:T(8,128)(2,1)S(1)}, u32[]{:S(2)}, u32[]{:S(2)}) collective-permute-start(bf16[1152,512]{1,0:T(8,128)(2,1)S(1)} %collective-permute-done.11.near_ref), channel_id=1, source_target_pairs={{0,2},{2,0},{4,6},{6,4},{8,10},{10,8},{12,14},{14,12},{16,18},{18,... | collective-permute-start | bytes 3538952 | tf_op jit(solution)/shard_map/ppermute | solution.py:1280
  119.1 20.5 %collective-permute-start.14 = (bf16[384,512]{1,0:T(8,128)(2,1)}, bf16[384,512]{1,0:T(8,128)(2,1)S(1)}, u32[]{:S(2)}, u32[]{:S(2)}) collective-permute-start(bf16[384,512]{1,0:T(8,128)(2,1)} %collective-permute-done.12.near_ref.cross_near_ref.cq_near_ref), channel_id=1, source_target_pairs={{0,2},{2,0},{4,6},{6,4},{8,10},{10,8},{12,14},{14,12},{16,18},{18,... | collective-permute-start | bytes 1179656 | tf_op jit(solution)/shard_map/ppermute | solution.py:1280
  125.9 39.2 %collective-permute-start.17 = (bf16[1152,512]{1,0:T(8,128)(2,1)}, bf16[1152,512]{1,0:T(8,128)(2,1)S(1)}, u32[]{:S(2)}, u32[]{:S(2)}) collective-permute-start(bf16[1152,512]{1,0:T(8,128)(2,1)} %constant_dynamic-slice_fusion.12), channel_id=1, source_target_pairs={{0,1},{1,0},{2,3},{3,2},{4,5},{5,4},{6,7},{7,6},{8,9},{9,8},{10,11... | collective-permute-start | bytes 3538952 | tf_op jit(solution)/shard_map/ppermute | solution.py:1286
  147.5 17.7 %collective-permute-start.16 = (bf16[2,1024,256]{2,1,0:T(8,128)(2,1)}, bf16[2,1024,256]{2,1,0:T(8,128)(2,1)S(1)}, u32[]{:S(2)}, u32[]{:S(2)}) collective-permute-start(bf16[2,1024,256]{2,1,0:T(8,128)(2,1)} %get-tuple-element.518.own_ref), channel_id=1, source_target_pairs={{0,2},{2,0},{4,6},{6,4},{8,10},{10,8},{12,14},{14,12},{16,18},{18,... | collective-permute-start | bytes 3145736 | tf_op jit(solution)/shard_map/ppermute | solution.py:1280
  148.0 32.4 %collective-permute-start.18 = (bf16[1024,1024]{1,0:T(8,128)(2,1)}, bf16[1024,1024]{1,0:T(8,128)(2,1)S(1)}, u32[]{:S(2)}, u32[]{:S(2)}) collective-permute-start(bf16[1024,1024]{1,0:T(8,128)(2,1)} %pad_maximum_fusion.2), channel_id=1, source_target_pairs={{1,2},{2,1},{5,6},{6,5},{9,10},{10,9},{13,14},{14,13},{17,18},{18,... | collective-permute-start | bytes 6291464 | tf_op jit(solution)/shard_map/ppermute | solution.py:1292
  180.4 33.6 %collective-permute-start.20 = (bf16[1024,512]{1,0:T(8,128)(2,1)S(1)}, bf16[1024,512]{1,0:T(8,128)(2,1)S(1)}, u32[]{:S(2)}, u32[]{:S(2)}) collective-permute-start(bf16[1024,512]{1,0:T(8,128)(2,1)S(1)} %copy-done.5), channel_id=1, source_target_pairs={{1,2},{2,1},{5,6},{6,5},{9,10},{10,9},{13,14},{14,13},{17,18},{18,... | collective-permute-start | bytes 3145736 | tf_op jit(solution)/shard_map/ppermute | solution.py:1292
  214.0 28.8 %collective-permute-start.21 = (bf16[2,1152,512]{2,1,0:T(8,128)(2,1)}, bf16[2,1152,512]{2,1,0:T(8,128)(2,1)S(1)}, u32[]{:S(2)}, u32[]{:S(2)}) collective-permute-start(bf16[2,1152,512]{2,1,0:T(8,128)(2,1)} %get-tuple-element.542), channel_id=1, source_target_pairs={{0,2},{2,0},{4,6},{6,4},{8,10},{10,8},{12,14},{14,12},{16,18},{18,... | collective-permute-start | bytes 7077896 | tf_op jit(solution)/shard_map/ppermute | solution.py:1280
  216.8 26.0 %collective-permute-start.22 = (bf16[1024,512]{1,0:T(8,128)(2,1)}, bf16[1024,512]{1,0:T(8,128)(2,1)S(1)}, u32[]{:S(2)}, u32[]{:S(2)}) collective-permute-start(bf16[1024,512]{1,0:T(8,128)(2,1)} %get-tuple-element.773), channel_id=1, source_target_pairs={{1,2},{2,1},{5,6},{6,5},{9,10},{10,9},{13,14},{14,13},{17,18},{18,... | collective-permute-start | bytes 3145736 | tf_op jit(solution)/shard_map/ppermute | solution.py:1292
  244.8 29.2 %collective-permute-start.24 = (bf16[1152,512]{1,0:T(8,128)(2,1)S(1)}, bf16[1152,512]{1,0:T(8,128)(2,1)}, u32[]{:S(2)}, u32[]{:S(2)}) collective-permute-start(bf16[1152,512]{1,0:T(8,128)(2,1)S(1)} %fusion.4), channel_id=1, source_target_pairs={{0,1},{1,0},{2,3},{3,2},{4,5},{5,4},{6,7},{7,6},{8,9},{9,8},{10,11... | collective-permute-start | bytes 3538952 | tf_op jit(solution)/shard_map/ppermute | solution.py:1286
  247.8 25.1 %collective-permute-start.23 = (bf16[2,1024,256]{2,1,0:T(8,128)(2,1)}, bf16[2,1024,256]{2,1,0:T(8,128)(2,1)}, u32[]{:S(2)}, u32[]{:S(2)}) collective-permute-start(bf16[2,1024,256]{2,1,0:T(8,128)(2,1)} %get-tuple-element.556), channel_id=1, source_target_pairs={{0,2},{2,0},{4,6},{6,4},{8,10},{10,8},{12,14},{14,12},{16,18},{18,... | collective-permute-start | bytes 3145736 | tf_op jit(solution)/shard_map/ppermute | solution.py:1280
  276.4 32.8 %collective-permute-start.26 = (bf16[576,512]{1,0:T(8,128)(2,1)S(1)}, bf16[576,512]{1,0:T(8,128)(2,1)S(1)}, u32[]{:S(2)}, u32[]{:S(2)}) collective-permute-start(bf16[576,512]{1,0:T(8,128)(2,1)S(1)} %constant_dynamic-slice_fusion.11), channel_id=1, source_target_pairs={{0,4},{2,6},{4,0},{6,2},{8,12},{10,14},{12,8},{14,10},{16,20},{18,... | collective-permute-start | bytes 1769480 | tf_op jit(solution)/shard_map/ppermute | solution.py:1280
  326.6 33.6 %collective-permute-start.29 = (bf16[1408,512]{1,0:T(8,128)(2,1)}, bf16[1408,512]{1,0:T(8,128)(2,1)S(1)}, u32[]{:S(2)}, u32[]{:S(2)}) collective-permute-start(bf16[1408,512]{1,0:T(8,128)(2,1)} %fusion.3), channel_id=1, source_target_pairs={{0,1},{1,0},{2,3},{3,2},{4,5},{5,4},{6,7},{7,6},{8,9},{9,8},{10,11... | collective-permute-start | bytes 4325384 | tf_op jit(solution)/shard_map/ppermute | solution.py:1286
  328.0 27.6 %collective-permute-start.30 = (bf16[144,512]{1,0:T(8,128)(2,1)S(1)}, bf16[144,512]{1,0:T(8,128)(2,1)S(1)}, u32[]{:S(2)}, u32[]{:S(2)}) collective-permute-start(bf16[144,512]{1,0:T(8,128)(2,1)S(1)} %constant_dynamic-slice_fusion.9), channel_id=1, source_target_pairs={{0,16},{2,18},{4,20},{6,22},{8,24},{10,26},{12,28},{14,30},{16,0},... | collective-permute-start | bytes 442376 | tf_op jit(solution)/shard_map/ppermute | solution.py:1280
  363.2 29.2 %collective-permute-start.31 = (bf16[2,1024,256]{2,1,0:T(8,128)(2,1)}, bf16[2,1024,256]{2,1,0:T(8,128)(2,1)S(1)}, u32[]{:S(2)}, u32[]{:S(2)}) collective-permute-start(bf16[2,1024,256]{2,1,0:T(8,128)(2,1)} %get-tuple-element.616), channel_id=1, source_target_pairs={{0,2},{2,0},{4,6},{6,4},{8,10},{10,8},{12,14},{14,12},{16,18},{18,... | collective-permute-start | bytes 3145736 | tf_op jit(solution)/shard_map/ppermute | solution.py:1280
  363.3 29.1 %collective-permute-start.32 = (bf16[704,512]{1,0:T(8,128)(2,1)}, bf16[704,512]{1,0:T(8,128)(2,1)S(1)}, u32[]{:S(2)}, u32[]{:S(2)}) collective-permute-start(bf16[704,512]{1,0:T(8,128)(2,1)} %constant_dynamic-slice_fusion.8), channel_id=1, source_target_pairs={{0,4},{2,6},{4,0},{6,2},{8,12},{10,14},{12,8},{14,10},{16,20},{18,... | collective-permute-start | bytes 2162696 | tf_op jit(solution)/shard_map/ppermute | solution.py:1280
  364.8 27.5 %collective-permute-start.33 = (bf16[1,144,512]{2,1,0:T(8,128)(2,1)S(1)}, bf16[1,144,512]{2,1,0:T(8,128)(2,1)S(1)}, u32[]{:S(2)}, u32[]{:S(2)}) collective-permute-start(bf16[1,144,512]{2,1,0:T(8,128)(2,1)S(1)} %fusion.11), channel_id=1, source_target_pairs={{0,16},{2,18},{4,20},{6,22},{8,24},{10,26},{12,28},{14,30},{16,0},... | collective-permute-start | bytes 442376 | tf_op jit(solution)/shard_map/ppermute | solution.py:1280
  396.1 17.4 %collective-permute-start.35 = (bf16[352,512]{1,0:T(8,128)(2,1)}, bf16[352,512]{1,0:T(8,128)(2,1)}, u32[]{:S(2)}, u32[]{:S(2)}) collective-permute-start(bf16[352,512]{1,0:T(8,128)(2,1)} %constant_dynamic-slice_fusion.7), channel_id=1, source_target_pairs={{0,8},{2,10},{4,12},{6,14},{8,0},{10,2},{12,4},{14,6},{16,24},{18,... | collective-permute-start | bytes 1081352 | tf_op jit(solution)/shard_map/ppermute | solution.py:1280
  396.5 16.9 %collective-permute-start.36 = (bf16[2,144,512]{2,1,0:T(8,128)(2,1)}, bf16[2,144,512]{2,1,0:T(8,128)(2,1)S(1)}, u32[]{:S(2)}, u32[]{:S(2)}) collective-permute-start(bf16[2,144,512]{2,1,0:T(8,128)(2,1)} %pad_maximum_fusion.16), channel_id=1, source_target_pairs={{0,8},{2,10},{4,12},{6,14},{8,0},{10,2},{12,4},{14,6},{16,24},{18,... | collective-permute-start | bytes 884744 | tf_op jit(solution)/shard_map/ppermute | solution.py:1280
  416.9 17.2 %collective-permute-start.37 = (bf16[2,768,512]{2,1,0:T(8,128)(2,1)}, bf16[2,768,512]{2,1,0:T(8,128)(2,1)S(1)}, u32[]{:S(2)}, u32[]{:S(2)}) collective-permute-start(bf16[2,768,512]{2,1,0:T(8,128)(2,1)} %get-tuple-element.649), channel_id=1, source_target_pairs={{0,2},{2,0},{4,6},{6,4},{8,10},{10,8},{12,14},{14,12},{16,18},{18,... | collective-permute-start | bytes 4718600 | tf_op jit(solution)/shard_map/ppermute | solution.py:1280
  416.9 17.2 %collective-permute-start.38 = (bf16[1024,512]{1,0:T(8,128)(2,1)}, bf16[1024,512]{1,0:T(8,128)(2,1)}, u32[]{:S(2)}, u32[]{:S(2)}) collective-permute-start(bf16[1024,512]{1,0:T(8,128)(2,1)} %get-tuple-element.650), channel_id=1, source_target_pairs={{1,2},{2,1},{5,6},{6,5},{9,10},{10,9},{13,14},{14,13},{17,18},{18,... | collective-permute-start | bytes 3145736 | tf_op jit(solution)/shard_map/ppermute | solution.py:1292
  440.1 20.7 %collective-permute-start.44 = (bf16[8,144,512]{2,1,0:T(8,128)(2,1)S(1)}, bf16[8,144,512]{2,1,0:T(8,128)(2,1)}, u32[]{:S(2)}, u32[]{:S(2)}) collective-permute-start(bf16[8,144,512]{2,1,0:T(8,128)(2,1)S(1)} %pad_maximum_fusion.4.mine_ref), channel_id=1, source_target_pairs={{0,2},{2,0},{4,6},{6,4},{8,10},{10,8},{12,14},{14,12},{16,18},{18,... | collective-permute-start | bytes 3538952 | tf_op jit(solution)/shard_map/ppermute | solution.py:1280
  441.0 19.8 %collective-permute-start.42 = (bf16[768,512]{1,0:T(8,128)(2,1)}, bf16[768,512]{1,0:T(8,128)(2,1)}, u32[]{:S(2)}, u32[]{:S(2)}) collective-permute-start(bf16[768,512]{1,0:T(8,128)(2,1)} %fusion.7), channel_id=1, source_target_pairs={{0,1},{1,0},{2,3},{3,2},{4,5},{5,4},{6,7},{7,6},{8,9},{9,8},{10,11... | collective-permute-start | bytes 2359304 | tf_op jit(solution)/shard_map/ppermute | solution.py:1286
  442.7 21.5 %collective-permute-start.41 = (bf16[2,1024,128]{2,1,0:T(8,128)(2,1)}, bf16[2,1024,128]{2,1,0:T(8,128)(2,1)}, u32[]{:S(2)}, u32[]{:S(2)}) collective-permute-start(bf16[2,1024,128]{2,1,0:T(8,128)(2,1)} %get-tuple-element.663), channel_id=1, source_target_pairs={{0,2},{2,0},{4,6},{6,4},{8,10},{10,8},{12,14},{14,12},{16,18},{18,... | collective-permute-start | bytes 1572872 | tf_op jit(solution)/shard_map/ppermute | solution.py:1280
  477.5 18.2 %collective-permute-start.51 = (bf16[4,176,512]{2,1,0:T(8,128)(2,1)S(1)}, bf16[4,176,512]{2,1,0:T(8,128)(2,1)S(1)}, u32[]{:S(2)}, u32[]{:S(2)}) collective-permute-start(bf16[4,176,512]{2,1,0:T(8,128)(2,1)S(1)} %pad_maximum_fusion.10), channel_id=1, source_target_pairs={{0,4},{2,6},{4,0},{6,2},{8,12},{10,14},{12,8},{14,10},{16,20},{18,... | collective-permute-start | bytes 2162696 | tf_op jit(solution)/shard_map/ppermute | solution.py:1280
  (119 other events, 1053.6 us)

commit v5 on v4

--- a/solution.py
+++ b/solution.py
@@ -1116,25 +1116,18 @@
     return grad
 
 
-def qkv_parts(*triples):
-    def beside(parts):
-        return parts[0] if len(parts) == 1 else jnp.concatenate(parts, axis=1)
-
-    return (
-        beside([q_ref[...] for q_ref, _, _ in triples]),
-        beside([kv_total(kv_ref, got_ref, 0) for _, kv_ref, got_ref in triples]),
-        beside([kv_total(kv_ref, got_ref, 1) for _, kv_ref, got_ref in triples]),
-    )
+def qkv_parts(q_ref, kv_ref, got_ref):
+    return q_ref[...], kv_total(kv_ref, got_ref, 0), kv_total(kv_ref, got_ref, 1)
 
 
 def own_qkv_back_kernel(
-    core_ref, qa_ref, kva_ref, gota_ref, qb_ref, kvb_ref, gotb_ref, start_ref, base_ref, w_ref,
+    core_ref, q_ref, kv_ref, got_ref, start_ref, base_ref, w_ref,
     out_ref, low_ref, keep_ref, send_ref,
     acc,
 ):
     first_step(acc)
     low = start_ref[...].astype(BF)
-    parts = qkv_parts((qa_ref, kva_ref, gota_ref), (qb_ref, kvb_ref, gotb_ref))
+    parts = qkv_parts(q_ref, kv_ref, got_ref)
     grad = base_ref[...] + qkv_back(low, parts, w_ref, acc, 0)
     out_ref[...] = grad
     low_ref[...] = grad.astype(BF)
@@ -1142,13 +1135,13 @@
 
 
 def other_qkv_back_kernel(
-    core_ref, qa_ref, kva_ref, gota_ref, qb_ref, kvb_ref, gotb_ref, start_ref, base_ref, near_ref, far_ref,
+    core_ref, q_ref, kv_ref, got_ref, start_ref, base_ref, near_ref, far_ref,
     out_ref, low_ref, keep_ref, send_ref,
     acc, other_ref,
 ):
     join(core_ref, (near_ref, far_ref, other_ref))
     own_qkv_back_kernel(
-        core_ref, qa_ref, kva_ref, gota_ref, qb_ref, kvb_ref, gotb_ref, start_ref, base_ref, other_ref,
+        core_ref, q_ref, kv_ref, got_ref, start_ref, base_ref, other_ref,
         out_ref, low_ref, keep_ref, send_ref, acc,
     )
 
@@ -1162,8 +1155,8 @@
     first_step(acc)
     join(core_ref, (near_ref, far_ref, other_ref))
     low = start_ref[...].astype(BF)
-    grad = base_ref[...] + qkv_back(low, qkv_parts((q0_grad_ref, kv0_ref, got0_ref)), own_ref, acc, 0)
-    grad = grad + qkv_back(low, qkv_parts((q1_grad_ref, kv1_ref, got1_ref)), other_ref, acc, 1)
+    grad = base_ref[...] + qkv_back(low, qkv_parts(q0_grad_ref, kv0_ref, got0_ref), own_ref, acc, 0)
+    grad = grad + qkv_back(low, qkv_parts(q1_grad_ref, kv1_ref, got1_ref), other_ref, acc, 1)
     out_ref[...] = grad
     low_ref[...] = grad.astype(BF)
 
@@ -1434,7 +1427,9 @@
     (enc_qkv_now,) = flow.step((enc_qkv,))
     w_enc_qkv = rows_of(enc_qkv_now)
     flow.add("w_enc_qkv", gathered(at, w_enc_qkv, 2, 1))
-    ints, dec_qkv_now = flow.step((ints, dec_qkv))
+    later = ints, dec_qkv, enc_up, cross_kv, dec_up, enc_cotangent, dec_cotangent, running, enc_gains, dec_gains
+    later = flow.step(later)
+    ints, dec_qkv_now, enc_up_now, cross_kv_now, dec_up_now, enc_cot, dec_cot, running, enc_gains, dec_gains = later
     w_dec_self = jnp.concatenate([rows_of(dec_qkv_now), rows_of(dec_proj)])
     ints, w_dec_self, embedding = flow.step((ints, w_dec_self, embedding()))
     ints = jnp.where(at.stays, ints, flow.results["ints"])
@@ -1442,10 +1437,10 @@
     lane = jnp.arange(128, dtype=jnp.int32) % DH
     source_hot, target_hot = (ints[:4].reshape(2, 2 * n, 1) == lane).astype(BF)
 
-    w_enc = jnp.concatenate([rows_of(enc_proj), rows_of(enc_up), rows_of(enc_down)])
-    w_cross = jnp.concatenate([rows_of(cross_query), rows_of(cross_kv)])
-    w_dec = jnp.concatenate([rows_of(cross_proj), rows_of(dec_up), rows_of(dec_down)])
-    cots = jnp.concatenate([enc_cotangent[:, 0].astype(BF), dec_cotangent[:, 0].astype(BF)], axis=1)
+    w_enc = jnp.concatenate([rows_of(enc_proj), rows_of(enc_up_now), rows_of(enc_down)])
+    w_cross = jnp.concatenate([rows_of(cross_query), rows_of(cross_kv_now)])
+    w_dec = jnp.concatenate([rows_of(cross_proj), rows_of(dec_up_now), rows_of(dec_down)])
+    cots = jnp.concatenate([enc_cot[:, 0].astype(BF), dec_cot[:, 0].astype(BF)], axis=1)
     pad = jnp.zeros((3, D), F32)
     small_enc = jnp.stack(
         [enc_gains[0], enc_shifts[0], enc_gains[1], enc_shifts[1], halt_weight[0]]
@@ -1456,9 +1451,10 @@
     )
     small_dec = jnp.concatenate([small_dec, pad[:1]])
 
-    flow.add("target", moved(at, target_rows[:, 0], 2))
     flow.add("w_dec_self", gathered(at, w_dec_self, 2, 1))
-    embedding, source_hot, target_hot = flow.step((embedding, source_hot, target_hot))
+    flow.add("target", moved(at, target_rows[:, 0], 3))
+    tables = embedding, source_hot, target_hot, w_enc, cots
+    embedding, source_hot, target_hot, w_enc, cots = flow.step(tables)
     (embedding,) = flow.step((embedding,))
 
     def pre(rows, got, own, other):
@@ -1471,24 +1467,20 @@
         o, log = heads_forward(at.core, q, kv, got, hot, key_hot, causal)
         return o, (q, kv, got, hot, key_hot, o, log)
 
-    def attend_back(kept, grad):
-        return heads_backward(at.core, kept, grad, False)
-
-    def attend_back_pair(kept, grad, pair):
-        return heads_backward(at.core, kept, grad, True, 128 * pair, 128)
+    def attend_back(kept, grad, causal=False):
+        return heads_backward(at.core, kept, grad, causal)
 
     w_enc_qkv_got = flow.results["w_enc_qkv"]
     enc_start, q0, q1, kv0, kv1 = pre(source_rows[:, 0], flow.results["source"], w_enc_qkv, w_enc_qkv_got)
     got0, got1 = at.core_swap(kv0), at.core_swap(kv1)
     enc_o0, enc_kept0 = attend(q0, kv0, got0, source_hot, source_hot)
     flow.add("w_enc", gathered(at, w_enc, 2, 1))
-    enc_o0, q1, kv1, got1, w_enc, w_cross = flow.step((enc_o0, q1, kv1, got1, w_enc, w_cross))
-    target = flow.results["target"]
+    enc_o0, q1, kv1, got1, w_cross = flow.step((enc_o0, q1, kv1, got1, w_cross))
     enc_o1, enc_kept1 = attend(q1, kv1, got1, source_hot, source_hot)
-    enc_o1, target, w_dec = flow.step((enc_o1, target, w_dec))
+    (enc_o1,) = flow.step((enc_o1,))
 
     w_dec_self_got = flow.results["w_dec_self"]
-    dec_start, q0, q1, kv0, kv1 = pre(target_rows[:, 0], target, w_dec_self, w_dec_self_got)
+    dec_start, q0, q1, kv0, kv1 = pre(target_rows[:, 0], flow.results["target"], w_dec_self, w_dec_self_got)
     got0, got1 = at.core_swap(kv0), at.core_swap(kv1)
     self_o0, self_kept0 = attend(q0, kv0, got0, target_hot, target_hot, True)
     flow.add("w_cross", gathered(at, w_cross))
@@ -1556,7 +1548,7 @@
         [row, half_low, half_low], grad_outs(11 * HALF),
         [*grad_scratch(11 * HALF), (w_cross.shape, BF), (w_enc.shape, BF)],
     )
-    flow.add("enc", summed(at, *enc_parts))
+    flow.add("enc", summed(at, *enc_parts, (1, 1, 2)))
     enc_o0_grad, enc_o1_grad, q0_grad = flow.step((enc_o0_grad, enc_o1_grad, q0_grad))
     (
         dec_base, self_o0_grad, self_o1_grad, *mid_parts, small_one,
@@ -1581,17 +1573,14 @@
         [w_enc_qkv, *w_enc_qkv_got, *mid_parts, smalls], [row, row_low], [((2, 3 * HALF, D), BF)] * 2,
         [((2, 3 * HALF, D), F32), (w_enc_qkv.shape, BF)],
     )
-    flow.add("enc_qkv", summed(at, keep, send, (1, 2, 1)))
+    flow.add("enc_qkv", summed(at, keep, send))
     flow.add("source_grad", moved(at, source_low, 1))
     self_o1_grad, source_grad = flow.step((self_o1_grad, source_grad))
 
     def heads_back(kept, grad):
-        parts = []
-        for pair in range(2):
-            q_grad, kv_grad, kv_send = attend_back_pair(kept, grad, pair)
-            grad, q_grad, kv_grad, kv_send = flow.step((grad, q_grad, kv_grad, kv_send))
-            parts += [q_grad, kv_grad, at.core_swap(kv_send)]
-        return parts
+        q_grad, kv_grad, kv_send = attend_back(kept, grad, True)
+        q_grad, kv_grad, kv_send = flow.step((q_grad, kv_grad, kv_send))
+        return q_grad, kv_grad, at.core_swap(kv_send)
 
     parts = heads_back(self_kept1, self_o1_grad)
     part_outs = [((1, 3 * HALF // 2, D), BF)] * 2
@@ -1629,29 +1618,39 @@
         for c in range(2):
             begin = c * 3 * HALF
             places += [(0, begin, c * part, part), (1 + c, begin + part, 0, 2 * more)]
-            places += [(3, begin + part + 2 * more, 16 * c, 16)]
-        shapes = [enc_qkv.shape, cross_query.shape, dec_proj.shape, (32, D)]
+        after = part + 2 * more
+        one, two = after + 8, 3 * HALF + after
+        for out, rows in (
+            (3, (after, after + 2)),
+            (4, (after + 1, after + 3)),
+            (5, (one, two, two + 2)),
+            (6, (one + 1, two + 1, two + 3)),
+            (7, (after + 4, two + 4)),
+        ):
+            places += [(out, row, at_row, 1) for at_row, row in enumerate(rows)]
+        shapes = [enc_qkv.shape, cross_query.shape, dec_proj.shape, (2, D), (2, D), (3, D), (3, D), (2, D)]
         return unpack(at.order, *done[name], shapes, places)
 
     target_grad, done["dec"] = flow.step((target_grad, done["dec"]))
     dec_grads = weights("dec", cross_proj, dec_up, dec_down)
-    dec_grads, done["enc"] = flow.step((dec_grads, done["enc"]))
+    dec_grads, source_grad = flow.step((dec_grads, source_grad))
+    source_out = home(source_grad, "source_grad")
+    (source_out,) = flow.step((source_out,))
     enc_grads = weights("enc", cross_kv, enc_proj, enc_up, enc_down)
-    enc_grads, source_grad = flow.step((enc_grads, source_grad))
-    source_out = home(source_grad, "source_grad")
-    source_out, enc_states, dec_states = flow.step((source_out, enc_states, dec_states))
+    enc_grads, enc_states, dec_states = flow.step((enc_grads, enc_states, dec_states))
     states_out = home(enc_states, "enc_states"), home(dec_states, "dec_states")
     states_out, target_grad = flow.step((states_out, target_grad))
     target_out = home(target_grad, "target_grad")
-    target_out, done["enc_qkv"] = flow.step((target_out, done["enc_qkv"]))
+    (target_out,) = flow.step((target_out,))
+    (target_out,) = flow.step((target_out,))
     mixed_grads = mixed_weights("enc_qkv")
     (mixed_grads,) = flow.step((mixed_grads,))
     flow.finish()
     cross_proj_grad, dec_up_grad, dec_down_grad = dec_grads
     cross_kv_grad, enc_proj_grad, enc_up_grad, enc_down_grad = enc_grads
-    enc_qkv_grad, cross_query_grad, dec_proj_grad, small = mixed_grads
+    enc_qkv_grad, cross_query_grad, dec_proj_grad, *small_grads = mixed_grads
     (dec_qkv_grad,) = weights("dec_qkv", dec_qkv)
-    enc_small, one, two = small[:8], small[8:16], small[16:24]
+    enc_gains_grad, enc_shifts_grad, dec_gains_grad, dec_shifts_grad, halt_grad = small_grads
     return (
         *states_out,
         source_out,
@@ -1660,8 +1659,8 @@
         enc_proj_grad,
         enc_up_grad,
         enc_down_grad,
-        enc_small[0:3:2],
-        enc_small[1:4:2],
+        enc_gains_grad,
+        enc_shifts_grad,
         dec_qkv_grad,
         dec_proj_grad,
         cross_query_grad,
@@ -1669,9 +1668,9 @@
         cross_proj_grad,
         dec_up_grad,
         dec_down_grad,
-        jnp.concatenate([one[0:1], two[0:3:2]]),
-        jnp.concatenate([one[1:2], two[1:4:2]]),
-        jnp.stack([enc_small[4], two[4]]),
+        dec_gains_grad,
+        dec_shifts_grad,
+        halt_grad,
     )
 
 

time: 587 us -> 581 us (0.990)
  waiting for transfers between devices: 66.8 us -> 46.7 us
  starting transfers between devices: 79.2 us -> 97.2 us
  Pallas kernels: 345 us -> 339 us
    ppermute x52 -> x50, starting transfers between devices: 51.4 us -> 72.4 us  [flip(): lax.ppermute(values, 'dp', [(d, d ^ mask) for d in range(self.dp_size)])]
    ppermute x52 -> x50, waiting for transfers between devices: 40.7 us -> 28.4 us  [flip(): lax.ppermute(values, 'dp', [(d, d ^ mask) for d in range(self.dp_size)])]
    ppermute x9, waiting for transfers between devices: 26.1 us -> 18.3 us  [y_swap(): return lax.ppermute(values, 'mp', [(0, 1), (1, 0)])]
    pallas_call x8 -> x6, Pallas kernels: 137 us -> 132 us  [heads_backward(): pl.pallas_call(partial(backward_kernel, causal=causal), grid=(width // 12...]
    unnamed x164 -> x172, local copies, waits for them, and re-layouts: 15 us -> 18.1 us
  transfers between devices with their start and end apart: 69 -> 67, of which waited for: 26 -> 22; matrix products, arithmetic and copies ran while one was open for 8% -> 8% of each run, Pallas kernels for 59% -> 58%
where the time goes in v5:
time: 581 us; the launch traced here: 573 us
  Pallas kernels  339 us (58%)
  starting transfers between devices  97.2 us (17%)
  waiting for transfers between devices  46.7 us (8%)
  local copies, waits for them, and re-layouts  46.1 us (8%)
  other arithmetic  41.2 us (7%)
    pallas_call x6, Pallas kernels, heads_backward(): pl.pallas_call(partial(backward_kernel, causal=causal), grid=(width // 12...  132 us
    pallas_call x10, Pallas kernels, rows_call(): pl.pallas_call(kernel, grid=(n // block,), in_specs=[pl.BlockSpec(memory_...  120 us
    ppermute x50, starting transfers between devices, flip(): lax.ppermute(values, 'dp', [(d, d ^ mask) for d in range(self.dp_size)])  72.4 us
    pallas_call x6, Pallas kernels, heads_forward(): pl.pallas_call(partial(forward_kernel, causal=causal), grid=(width // 128...  72.3 us
    ppermute x50, waiting for transfers between devices, flip(): lax.ppermute(values, 'dp', [(d, d ^ mask) for d in range(self.dp_size)])  28.4 us
    ppermute x9, waiting for transfers between devices, y_swap(): return lax.ppermute(values, 'mp', [(0, 1), (1, 0)])  18.3 us
    unnamed x172, local copies, waits for them, and re-layouts  18.1 us
    pallas_call x4, Pallas kernels, unpack(): pl.pallas_call(partial(unpack_kernel, places=places), in_specs=[pl.BlockS...  14.7 us
  transfers between devices with their start and end apart: 67, of which 22 were waited for; matrix products, arithmetic and copies ran while one was open for 8% of the time, Pallas kernels for 58%

profile of v5, /device:TPU:0, one launch (start us, length us, event | category | flops | bytes accessed | tf_op | source)
XLA Modules:
  0.0 572.7 jit_solution(1147604886116673485)
XLA Ops:
  8.4 5.5 collective-permute-start.2
  37.9 5.2 project.2
  50.0 14.1 %attention.4 = (bf16[1024,256]{1,0:T(8,128)(2,1)}, f32[1024,256]{1,0:T(8,128)}) custom-call(s32[2]{0:T(128)} %get-tuple-element.845.core_ref, bf16[1024,256]{1,0:T(8,128)(2,1)} %get-tuple-element.452.q_ref, bf16[2,1024,256]{2,1,0:T(8,128)(2,1)} %get-tuple-element.453.own_ref, bf16[2,1024,256]{2,1,0:T(8,128)(2,1)} %copy-done.17, ...), custom_call_target="tpu_custom_call" | custom-call | flops 1 | bytes 1 | tf_op jit(solution)/shard_map/attention/pallas_call | solution.py:633
  67.1 14.0 %attention.5 = (bf16[1024,256]{1,0:T(8,128)(2,1)}, f32[1024,256]{1,0:T(8,128)}) custom-call(s32[2]{0:T(128)} %get-tuple-element.845.core_ref, bf16[1024,256]{1,0:T(8,128)(2,1)} %get-tuple-element.467.q_ref, bf16[2,1024,256]{2,1,0:T(8,128)(2,1)} %get-tuple-element.468.own_ref, bf16[2,1024,256]{2,1,0:T(8,128)(2,1)} %collective-permute-done.5.got_ref, ...), custom_call_target="tpu_custom_call" | custom-call | flops 1 | bytes 1 | tf_op jit(solution)/shard_map/attention/pallas_call | solution.py:633
  82.3 5.4 project.3
  91.6 8.4 %attention_causal.2 = (bf16[1024,256]{1,0:T(8,128)(2,1)}, f32[1024,256]{1,0:T(8,128)}) custom-call(s32[2]{0:T(128)} %get-tuple-element.845.core_ref, bf16[1024,256]{1,0:T(8,128)(2,1)} %get-tuple-element.475.q_ref, bf16[2,1024,256]{2,1,0:T(8,128)(2,1)} %get-tuple-element.476.own_ref, bf16[2,1024,256]{2,1,0:T(8,128)(2,1)} %copy-done.15, ...), custom_call_target="tpu_custom_call" | custom-call | flops 1 | bytes 1 | tf_op jit(solution)/shard_map/attention_causal/pallas_call | solution.py:633
  100.0 5.0 collective-permute-start.13
  109.3 8.2 %attention_causal.3 = (bf16[1024,256]{1,0:T(8,128)(2,1)}, f32[1024,256]{1,0:T(8,128)}) custom-call(s32[2]{0:T(128)} %get-tuple-element.845.core_ref, bf16[1024,256]{1,0:T(8,128)(2,1)} %get-tuple-element.489.q_ref, bf16[2,1024,256]{2,1,0:T(8,128)(2,1)} %get-tuple-element.490.own_ref, bf16[2,1024,256]{2,1,0:T(8,128)(2,1)} %copy-done.16, ...), custom_call_target="tpu_custom_call" | custom-call | flops 1 | bytes 1 | tf_op jit(solution)/shard_map/attention_causal/pallas_call | solution.py:633
  118.3 4.4 collective-permute-start.14
  126.0 12.0 %encoder_feed.1 = (f32[1024,512]{1,0:T(8,128)}, f32[1024,512]{1,0:T(8,128)}, bf16[1024,512]{1,0:T(8,128)(2,1)}) custom-call(s32[2]{0:T(128)} %get-tuple-element.845.core_ref, bf16[1024,256]{1,0:T(8,128)(2,1)} %get-tuple-element.502.o0_ref.o_ref, bf16[1024,256]{1,0:T(8,128)(2,1)} %get-tuple-element.503.o1_ref.o_ref, ...), custom_call_target="tpu_custom_call" | custom-call | flops 1 | bytes 1 | tf_op jit(solution)/shard_map/encoder_feed/pallas_call | solution.py:1192
  138.8 7.0 %cross_project.1 = (f32[1024,512]{1,0:T(8,128)}, bf16[1024,256]{1,0:T(8,128)(2,1)}, bf16[1024,256]{1,0:T(8,128)(2,1)}, bf16[2,1024,256]{2,1,0:T(8,128)(2,1)}, bf16[2,1024,256]{2,1,0:T(8,128)(2,1)}) custom-call(s32[2]{0:T(128)} %get-tuple-element.845.core_ref, bf16[1024,256]{1,0:T(8,128)(2,1)} %get-tuple-element.488.o0_ref.o_ref, ...), custom_call_target="tpu_custom_call" | custom-call | flops 1 | bytes 1 | tf_op jit(solution)/shard_map/cross_project/pallas_call | solution.py:1192
  149.7 13.8 %attention.6 = (bf16[1024,256]{1,0:T(8,128)(2,1)}, f32[1024,256]{1,0:T(8,128)}) custom-call(s32[2]{0:T(128)} %get-tuple-element.845.core_ref, bf16[1024,256]{1,0:T(8,128)(2,1)} %get-tuple-element.518.q_ref, bf16[2,1024,256]{2,1,0:T(8,128)(2,1)} %get-tuple-element.519.own_ref, bf16[2,1024,256]{2,1,0:T(8,128)(2,1)} %copy-done.19, ...), custom_call_target="tpu_custom_call" | custom-call | flops 1 | bytes 1 | tf_op jit(solution)/shard_map/attention/pallas_call | solution.py:633
  164.6 13.8 %attention.7 = (bf16[1024,256]{1,0:T(8,128)(2,1)}, f32[1024,256]{1,0:T(8,128)}) custom-call(s32[2]{0:T(128)} %get-tuple-element.845.core_ref, bf16[1024,256]{1,0:T(8,128)(2,1)} %get-tuple-element.525.q_ref, bf16[2,1024,256]{2,1,0:T(8,128)(2,1)} %get-tuple-element.526.own_ref, bf16[2,1024,256]{2,1,0:T(8,128)(2,1)} %copy-done.18, ...), custom_call_target="tpu_custom_call" | custom-call | flops 1 | bytes 1 | tf_op jit(solution)/shard_map/attention/pallas_call | solution.py:633
  181.3 30.1 %decoder_feed.1 = (bf16[1024,512]{1,0:T(8,128)(2,1)}, f32[1024,512]{1,0:T(8,128)}, f32[1024,512]{1,0:T(8,128)}, bf16[1024,256]{1,0:T(8,128)(2,1)}, bf16[1024,256...) custom-call(s32[2]{0:T(128)} %get-tuple-element.845.core_ref, ...), custom_call_target="tpu_custom_call" | custom-call | flops 1 | bytes 1 | tf_op jit(solution)/shard_map/decoder_feed/pallas_call | solution.py:1192
  215.0 25.1 %attention_back.4 = (bf16[1024,256]{1,0:T(8,128)(2,1)}, bf16[2,1024,256]{2,1,0:T(8,128)(2,1)}, bf16[2,1024,256]{2,1,0:T(8,128)(2,1)}) custom-call(s32[2]{0:T(128)} %get-tuple-element.845.core_ref, bf16[1024,256]{1,0:T(8,128)(2,1)} %get-tuple-element.518.q_ref, bf16[2,1024,256]{2,1,0:T(8,128)(2,1)} %get-tuple-element.519.own_ref, ...), custom_call_target="tpu_custom_call" | custom-call | flops 1 | bytes 1 | tf_op jit(solution)/shard_map/attention_back/pallas_call | solution.py:776
  244.9 25.1 %attention_back.5 = (bf16[1024,256]{1,0:T(8,128)(2,1)}, bf16[2,1024,256]{2,1,0:T(8,128)(2,1)}, bf16[2,1024,256]{2,1,0:T(8,128)(2,1)}) custom-call(s32[2]{0:T(128)} %get-tuple-element.845.core_ref, bf16[1024,256]{1,0:T(8,128)(2,1)} %get-tuple-element.525.q_ref, bf16[2,1024,256]{2,1,0:T(8,128)(2,1)} %get-tuple-element.526.own_ref, ...), custom_call_target="tpu_custom_call" | custom-call | flops 1 | bytes 1 | tf_op jit(solution)/shard_map/attention_back/pallas_call | solution.py:776
  277.0 29.3 %encoder_feed_back.1 = (f32[1024,512]{1,0:T(8,128)}, bf16[1024,256]{1,0:T(8,128)(2,1)}, bf16[1024,256]{1,0:T(8,128)(2,1)}, bf16[2,1408,512]{2,1,0:T(8,128)(2,1)}...) custom-call(s32[2]{0:T(128)} %get-tuple-element.845.core_ref, bf16[2,1024,256]{2,1,0:T(8,128)(2,1)} %get-tuple-element.558.kv0_ref, ...), custom_call_target="tpu_custom_call" | custom-call | flops 1 | bytes 1 | tf_op jit(solution)/shard_map/encoder_feed_back/pallas_call | solution.py:1192
  311.1 9.3 %cross_project_back.1 = (f32[1024,512]{1,0:T(8,128)}, bf16[1024,256]{1,0:T(8,128)(2,1)}, bf16[1024,256]{1,0:T(8,128)(2,1)}, bf16[2,256,512]{2,1,0:T(8,128)(2,1)}...) custom-call(s32[2]{0:T(128)} %get-tuple-element.845.core_ref, bf16[1024,256]{1,0:T(8,128)(2,1)} %get-tuple-element.587.q0_grad_ref, ...), custom_call_target="tpu_custom_call" | custom-call | flops 1 | bytes 1 | tf_op jit(solution)/shard_map/cross_project_back/pallas_call | solution.py:1192
  329.3 25.1 %attention_back.6 = (bf16[1024,256]{1,0:T(8,128)(2,1)}, bf16[2,1024,256]{2,1,0:T(8,128)(2,1)}, bf16[2,1024,256]{2,1,0:T(8,128)(2,1)}) custom-call(s32[2]{0:T(128)} %get-tuple-element.845.core_ref, bf16[1024,256]{1,0:T(8,128)(2,1)} %get-tuple-element.467.q_ref, bf16[2,1024,256]{2,1,0:T(8,128)(2,1)} %get-tuple-element.468.own_ref, ...), custom_call_target="tpu_custom_call" | custom-call | flops 1 | bytes 1 | tf_op jit(solution)/shard_map/attention_back/pallas_call | solution.py:776
  354.4 4.8 collective-permute-done.29
  366.8 25.0 %attention_back.7 = (bf16[1024,256]{1,0:T(8,128)(2,1)}, bf16[2,1024,256]{2,1,0:T(8,128)(2,1)}, bf16[2,1024,256]{2,1,0:T(8,128)(2,1)}) custom-call(s32[2]{0:T(128)} %get-tuple-element.845.core_ref, bf16[1024,256]{1,0:T(8,128)(2,1)} %get-tuple-element.452.q_ref, bf16[2,1024,256]{2,1,0:T(8,128)(2,1)} %get-tuple-element.453.own_ref, ...), custom_call_target="tpu_custom_call" | custom-call | flops 1 | bytes 1 | tf_op jit(solution)/shard_map/attention_back/pallas_call | solution.py:776
  396.8 9.7 %project_back.3 = (f32[1024,512]{1,0:T(8,128)}, bf16[1024,512]{1,0:T(8,128)(2,1)}, bf16[2,768,512]{2,1,0:T(8,128)(2,1)}, bf16[2,768,512]{2,1,0:T(8,128)(2,1)}) custom-call(s32[2]{0:T(128)} %get-tuple-element.845.core_ref, bf16[1024,256]{1,0:T(8,128)(2,1)} %get-tuple-element.633.q0_grad_ref, bf16[2,1024,256]{2,1,0:T(8,128)(2,1)} %get-tuple-element.634.kv0_ref, ...), custom_call_target="tpu_custom_call" | custom-call | flops 1 | bytes 1 | tf_op jit(solution)/shard_map/project_back/pallas_call | solution.py:1192
  413.8 15.7 %attention_causal_back.2 = (bf16[1024,256]{1,0:T(8,128)(2,1)}, bf16[2,1024,256]{2,1,0:T(8,128)(2,1)}, bf16[2,1024,256]{2,1,0:T(8,128)(2,1)}) custom-call(s32[2]{0:T(128)} %get-tuple-element.845.core_ref, bf16[1024,256]{1,0:T(8,128)(2,1)} %get-tuple-element.489.q_ref, bf16[2,1024,256]{2,1,0:T(8,128)(2,1)} %get-tuple-element.490.own_ref, ...), custom_call_target="tpu_custom_call" | custom-call | flops 1 | bytes 1 | tf_op jit(solution)/shard_map/attention_causal_back/pallas_call | solution.py:776
  433.8 9.1 %collective-permute-start.44 = (bf16[8,144,512]{2,1,0:T(8,128)(2,1)S(1)}, bf16[8,144,512]{2,1,0:T(8,128)(2,1)S(1)}, u32[]{:S(2)}, u32[]{:S(2)}) collective-permute-start(bf16[8,144,512]{2,1,0:T(8,128)(2,1)S(1)} %pad_maximum_fusion.4.mine_ref), channel_id=1, source_target_pairs={{0,2},{2,0},{4,6},{6,4},{8,10},{10,8},{12,14},{14,12},{16,18},{18,... | collective-permute-start | bytes 3538952 | tf_op jit(solution)/shard_map/ppermute | solution.py:1273
  447.2 6.2 %project_back.4 = (f32[1024,512]{1,0:T(8,128)}, bf16[1024,512]{1,0:T(8,128)(2,1)}, bf16[1,384,512]{2,1,0:T(8,128)(2,1)}, bf16[1,384,512]{2,1,0:T(8,128)(2,1)}) custom-call(s32[2]{0:T(128)} %get-tuple-element.845.core_ref, bf16[1024,256]{1,0:T(8,128)(2,1)} %get-tuple-element.668.q_ref, bf16[2,1024,256]{2,1,0:T(8,128)(2,1)} %get-tuple-element.669.kv_ref, ...), custom_call_target="tpu_custom_call" | custom-call | flops 1 | bytes 1 | tf_op jit(solution)/shard_map/project_back/pallas_call | solution.py:1192
  454.5 8.7 %collective-permute-done.42 = bf16[768,512]{1,0:T(8,128)(2,1)} collective-permute-done((bf16[768,512]{1,0:T(8,128)(2,1)}, bf16[768,512]{1,0:T(8,128)(2,1)}, u32[]{:S(2)}, u32[]{:S(2)}) %collective-permute-start.42) | collective-permute-done | bytes 786464 | tf_op jit(solution)/shard_map/ppermute | solution.py:1279
  468.7 15.9 %attention_causal_back.3 = (bf16[1024,256]{1,0:T(8,128)(2,1)}, bf16[2,1024,256]{2,1,0:T(8,128)(2,1)}, bf16[2,1024,256]{2,1,0:T(8,128)(2,1)}) custom-call(s32[2]{0:T(128)} %get-tuple-element.845.core_ref, bf16[1024,256]{1,0:T(8,128)(2,1)} %get-tuple-element.475.q_ref, bf16[2,1024,256]{2,1,0:T(8,128)(2,1)} %get-tuple-element.476.own_ref, ...), custom_call_target="tpu_custom_call" | custom-call | flops 1 | bytes 1 | tf_op jit(solution)/shard_map/attention_causal_back/pallas_call | solution.py:776
  486.4 6.8 %collective-permute-start.49 = (bf16[2,1024,256]{2,1,0:T(8,128)(2,1)}, bf16[2,1024,256]{2,1,0:T(8,128)(2,1)S(1)}, u32[]{:S(2)}, u32[]{:S(2)}) collective-permute-start(bf16[2,1024,256]{2,1,0:T(8,128)(2,1)} %get-tuple-element.698), channel_id=1, source_target_pairs={{0,2},{2,0},{4,6},{6,4},{8,10},{10,8},{12,14},{14,12},{16,18},{18,... | collective-permute-start | bytes 3145736 | tf_op jit(solution)/shard_map/ppermute | solution.py:1273
  496.7 5.9 %project_back.5 = (f32[1024,512]{1,0:T(8,128)}, bf16[1024,512]{1,0:T(8,128)(2,1)}, bf16[1,384,512]{2,1,0:T(8,128)(2,1)}, bf16[1,384,512]{2,1,0:T(8,128)(2,1)}) custom-call(s32[2]{0:T(128)} %get-tuple-element.845.core_ref, bf16[1024,256]{1,0:T(8,128)(2,1)} %get-tuple-element.696.q_ref, bf16[2,1024,256]{2,1,0:T(8,128)(2,1)} %get-tuple-element.697.kv_ref, ...), custom_call_target="tpu_custom_call" | custom-call | flops 1 | bytes 1 | tf_op jit(solution)/shard_map/project_back/pallas_call | solution.py:1192
  532.1 4.7 unpack.5
  545.5 5.5 collective-permute-start.63
  556.8 4.6 collective-permute-done.64
  (401 shorter events, 186.6 us)
Async XLA Ops:
  3.1 22.2 %collective-permute-start = (s32[6,1024]{0,1:T(8,128)}, s32[6,1024]{0,1:T(8,128)}, u32[]{:S(2)}, u32[]{:S(2)}) collective-permute-start(s32[6,1024]{0,1:T(8,128)} %copy.46), channel_id=1, source_target_pairs={{1,2},{2,1},{5,6},{6,5},{9,10},{10,9},{13,14},{14,13},{17,18},{18,... | collective-permute-start | bytes 73736 | tf_op jit(solution)/shard_map/ppermute | solution.py:1285
  4.7 30.6 %collective-permute-start.1 = (bf16[1024,512]{1,0:T(8,128)(2,1)}, bf16[1024,512]{1,0:T(8,128)(2,1)}, u32[]{:S(2)}, u32[]{:S(2)}) collective-permute-start(bf16[1024,512]{1,0:T(8,128)(2,1)} %bitcast.70), channel_id=1, source_target_pairs={{1,2},{2,1},{5,6},{6,5},{9,10},{10,9},{13,14},{14,13},{17,18},{18,... | collective-permute-start | bytes 3145736 | tf_op jit(solution)/shard_map/ppermute | solution.py:1285
  8.4 26.8 %collective-permute-start.2 = (bf16[384,512]{1,0:T(8,128)(2,1)}, bf16[384,512]{1,0:T(8,128)(2,1)}, u32[]{:S(2)}, u32[]{:S(2)}) collective-permute-start(bf16[384,512]{1,0:T(8,128)(2,1)} %constant_dynamic-slice_fusion.16), channel_id=1, source_target_pairs={{0,1},{1,0},{2,3},{3,2},{4,5},{5,4},{6,7},{7,6},{8,9},{9,8},{10,11... | collective-permute-start | bytes 1179656 | tf_op jit(solution)/shard_map/ppermute | solution.py:1279
  43.3 20.8 %collective-permute-start.5 = (bf16[2,1024,256]{2,1,0:T(8,128)(2,1)}, bf16[2,1024,256]{2,1,0:T(8,128)(2,1)}, u32[]{:S(2)}, u32[]{:S(2)}) collective-permute-start(bf16[2,1024,256]{2,1,0:T(8,128)(2,1)} %get-tuple-element.468.own_ref), channel_id=1, source_target_pairs={{0,2},{2,0},{4,6},{6,4},{8,10},{10,8},{12,14},{14,12},{16,18},{18,... | collective-permute-start | bytes 3145736 | tf_op jit(solution)/shard_map/ppermute | solution.py:1273
  45.7 18.3 %collective-permute-start.6 = (bf16[512,512]{1,0:T(8,128)(2,1)}, bf16[512,512]{1,0:T(8,128)(2,1)S(1)}, u32[]{:S(2)}, u32[]{:S(2)}) collective-permute-start(bf16[512,512]{1,0:T(8,128)(2,1)} %constant_dynamic-slice_fusion.15), channel_id=1, source_target_pairs={{0,1},{1,0},{2,3},{3,2},{4,5},{5,4},{6,7},{7,6},{8,9},{9,8},{10,11... | collective-permute-start | bytes 1572872 | tf_op jit(solution)/shard_map/ppermute | solution.py:1279
  46.7 34.4 %collective-permute-start.7 = (bf16[1024,512]{1,0:T(8,128)(2,1)}, bf16[1024,512]{1,0:T(8,128)(2,1)S(1)}, u32[]{:S(2)}, u32[]{:S(2)}) collective-permute-start(bf16[1024,512]{1,0:T(8,128)(2,1)} %bitcast.68), channel_id=1, source_target_pairs={{1,2},{2,1},{5,6},{6,5},{9,10},{10,9},{13,14},{14,13},{17,18},{18,... | collective-permute-start | bytes 3145736 | tf_op jit(solution)/shard_map/ppermute | solution.py:1285
  64.1 17.1 %collective-permute-start.8 = (bf16[512,512]{1,0:T(8,128)(2,1)S(1)}, bf16[512,512]{1,0:T(8,128)(2,1)S(1)}, u32[]{:S(2)}, u32[]{:S(2)}) collective-permute-start(bf16[512,512]{1,0:T(8,128)(2,1)S(1)} %collective-permute-done.6.near_ref.proj_near_ref), channel_id=1, source_target_pairs={{0,2},{2,0},{4,6},{6,4},{8,10},{10,8},{12,14},{14,12},{16,18},{18,... | collective-permute-start | bytes 1572872 | tf_op jit(solution)/shard_map/ppermute | solution.py:1273
  66.6 33.4 %collective-permute-start.11 = (bf16[1152,512]{1,0:T(8,128)(2,1)}, bf16[1152,512]{1,0:T(8,128)(2,1)S(1)}, u32[]{:S(2)}, u32[]{:S(2)}) collective-permute-start(bf16[1152,512]{1,0:T(8,128)(2,1)} %constant_dynamic-slice_fusion.14), channel_id=1, source_target_pairs={{0,1},{1,0},{2,3},{3,2},{4,5},{5,4},{6,7},{7,6},{8,9},{9,8},{10,11... | collective-permute-start | bytes 3538952 | tf_op jit(solution)/shard_map/ppermute | solution.py:1279
  100.0 18.3 %collective-permute-start.13 = (bf16[1152,512]{1,0:T(8,128)(2,1)S(1)}, bf16[1152,512]{1,0:T(8,128)(2,1)S(1)}, u32[]{:S(2)}, u32[]{:S(2)}) collective-permute-start(bf16[1152,512]{1,0:T(8,128)(2,1)S(1)} %collective-permute-done.11.near_ref), channel_id=1, source_target_pairs={{0,2},{2,0},{4,6},{6,4},{8,10},{10,8},{12,14},{14,12},{16,18},{18,... | collective-permute-start | bytes 3538952 | tf_op jit(solution)/shard_map/ppermute | solution.py:1273
  118.3 19.7 %collective-permute-start.14 = (bf16[384,512]{1,0:T(8,128)(2,1)S(1)}, bf16[384,512]{1,0:T(8,128)(2,1)S(1)}, u32[]{:S(2)}, u32[]{:S(2)}) collective-permute-start(bf16[384,512]{1,0:T(8,128)(2,1)S(1)} %collective-permute-done.12.near_ref.cross_near_ref.cq_near_ref), channel_id=1, source_target_pairs={{0,2},{2,0},{4,6},{6,4},{8,10},{10,8},{12,14},{14,12},{16,18},{18,... | collective-permute-start | bytes 1179656 | tf_op jit(solution)/shard_map/ppermute | solution.py:1273
  124.1 39.4 %collective-permute-start.17 = (bf16[1152,512]{1,0:T(8,128)(2,1)}, bf16[1152,512]{1,0:T(8,128)(2,1)}, u32[]{:S(2)}, u32[]{:S(2)}) collective-permute-start(bf16[1152,512]{1,0:T(8,128)(2,1)} %constant_dynamic-slice_fusion.12), channel_id=1, source_target_pairs={{0,1},{1,0},{2,3},{3,2},{4,5},{5,4},{6,7},{7,6},{8,9},{9,8},{10,11... | collective-permute-start | bytes 3538952 | tf_op jit(solution)/shard_map/ppermute | solution.py:1279
  145.8 17.6 %collective-permute-start.16 = (bf16[2,1024,256]{2,1,0:T(8,128)(2,1)}, bf16[2,1024,256]{2,1,0:T(8,128)(2,1)S(1)}, u32[]{:S(2)}, u32[]{:S(2)}) collective-permute-start(bf16[2,1024,256]{2,1,0:T(8,128)(2,1)} %get-tuple-element.526.own_ref), channel_id=1, source_target_pairs={{0,2},{2,0},{4,6},{6,4},{8,10},{10,8},{12,14},{14,12},{16,18},{18,... | collective-permute-start | bytes 3145736 | tf_op jit(solution)/shard_map/ppermute | solution.py:1273
  146.3 32.1 %collective-permute-start.18 = (bf16[1024,1024]{1,0:T(8,128)(2,1)S(1)}, bf16[1024,1024]{1,0:T(8,128)(2,1)S(1)}, u32[]{:S(2)}, u32[]{:S(2)}) collective-permute-start(bf16[1024,1024]{1,0:T(8,128)(2,1)S(1)} %copy-done.9), channel_id=1, source_target_pairs={{1,2},{2,1},{5,6},{6,5},{9,10},{10,9},{13,14},{14,13},{17,18},{18,... | collective-permute-start | bytes 6291464 | tf_op jit(solution)/shard_map/ppermute | solution.py:1285
  178.4 33.0 %collective-permute-start.20 = (bf16[1024,512]{1,0:T(8,128)(2,1)S(1)}, bf16[1024,512]{1,0:T(8,128)(2,1)S(1)}, u32[]{:S(2)}, u32[]{:S(2)}) collective-permute-start(bf16[1024,512]{1,0:T(8,128)(2,1)S(1)} %copy-done.5), channel_id=1, source_target_pairs={{1,2},{2,1},{5,6},{6,5},{9,10},{10,9},{13,14},{14,13},{17,18},{18,... | collective-permute-start | bytes 3145736 | tf_op jit(solution)/shard_map/ppermute | solution.py:1285
  211.4 28.7 %collective-permute-start.21 = (bf16[2,1152,512]{2,1,0:T(8,128)(2,1)}, bf16[2,1152,512]{2,1,0:T(8,128)(2,1)S(1)}, u32[]{:S(2)}, u32[]{:S(2)}) collective-permute-start(bf16[2,1152,512]{2,1,0:T(8,128)(2,1)} %get-tuple-element.550), channel_id=1, source_target_pairs={{0,2},{2,0},{4,6},{6,4},{8,10},{10,8},{12,14},{14,12},{16,18},{18,... | collective-permute-start | bytes 7077896 | tf_op jit(solution)/shard_map/ppermute | solution.py:1273
  214.1 26.0 %collective-permute-start.22 = (bf16[1024,512]{1,0:T(8,128)(2,1)}, bf16[1024,512]{1,0:T(8,128)(2,1)S(1)}, u32[]{:S(2)}, u32[]{:S(2)}) collective-permute-start(bf16[1024,512]{1,0:T(8,128)(2,1)} %get-tuple-element.753), channel_id=1, source_target_pairs={{1,2},{2,1},{5,6},{6,5},{9,10},{10,9},{13,14},{14,13},{17,18},{18,... | collective-permute-start | bytes 3145736 | tf_op jit(solution)/shard_map/ppermute | solution.py:1285
  242.0 29.3 %collective-permute-start.24 = (bf16[1152,512]{1,0:T(8,128)(2,1)S(1)}, bf16[1152,512]{1,0:T(8,128)(2,1)}, u32[]{:S(2)}, u32[]{:S(2)}) collective-permute-start(bf16[1152,512]{1,0:T(8,128)(2,1)S(1)} %fusion.4), channel_id=1, source_target_pairs={{0,1},{1,0},{2,3},{3,2},{4,5},{5,4},{6,7},{7,6},{8,9},{9,8},{10,11... | collective-permute-start | bytes 3538952 | tf_op jit(solution)/shard_map/ppermute | solution.py:1279
  244.9 25.1 %collective-permute-start.23 = (bf16[2,1024,256]{2,1,0:T(8,128)(2,1)}, bf16[2,1024,256]{2,1,0:T(8,128)(2,1)}, u32[]{:S(2)}, u32[]{:S(2)}) collective-permute-start(bf16[2,1024,256]{2,1,0:T(8,128)(2,1)} %get-tuple-element.564), channel_id=1, source_target_pairs={{0,2},{2,0},{4,6},{6,4},{8,10},{10,8},{12,14},{14,12},{16,18},{18,... | collective-permute-start | bytes 3145736 | tf_op jit(solution)/shard_map/ppermute | solution.py:1273
  273.5 32.8 %collective-permute-start.26 = (bf16[576,512]{1,0:T(8,128)(2,1)S(1)}, bf16[576,512]{1,0:T(8,128)(2,1)S(1)}, u32[]{:S(2)}, u32[]{:S(2)}) collective-permute-start(bf16[576,512]{1,0:T(8,128)(2,1)S(1)} %constant_dynamic-slice_fusion.11), channel_id=1, source_target_pairs={{0,4},{2,6},{4,0},{6,2},{8,12},{10,14},{12,8},{14,10},{16,20},{18,... | collective-permute-start | bytes 1769480 | tf_op jit(solution)/shard_map/ppermute | solution.py:1273
  325.4 33.8 %collective-permute-start.29 = (bf16[1408,512]{1,0:T(8,128)(2,1)}, bf16[1408,512]{1,0:T(8,128)(2,1)}, u32[]{:S(2)}, u32[]{:S(2)}) collective-permute-start(bf16[1408,512]{1,0:T(8,128)(2,1)} %fusion.3), channel_id=1, source_target_pairs={{0,1},{1,0},{2,3},{3,2},{4,5},{5,4},{6,7},{7,6},{8,9},{9,8},{10,11... | collective-permute-start | bytes 4325384 | tf_op jit(solution)/shard_map/ppermute | solution.py:1279
  326.7 27.6 %collective-permute-start.30 = (bf16[144,512]{1,0:T(8,128)(2,1)S(1)}, bf16[144,512]{1,0:T(8,128)(2,1)S(1)}, u32[]{:S(2)}, u32[]{:S(2)}) collective-permute-start(bf16[144,512]{1,0:T(8,128)(2,1)S(1)} %constant_dynamic-slice_fusion.9), channel_id=1, source_target_pairs={{0,16},{2,18},{4,20},{6,22},{8,24},{10,26},{12,28},{14,30},{16,0},... | collective-permute-start | bytes 442376 | tf_op jit(solution)/shard_map/ppermute | solution.py:1273
  362.6 29.3 %collective-permute-start.31 = (bf16[2,1024,256]{2,1,0:T(8,128)(2,1)}, bf16[2,1024,256]{2,1,0:T(8,128)(2,1)}, u32[]{:S(2)}, u32[]{:S(2)}) collective-permute-start(bf16[2,1024,256]{2,1,0:T(8,128)(2,1)} %get-tuple-element.623), channel_id=1, source_target_pairs={{0,2},{2,0},{4,6},{6,4},{8,10},{10,8},{12,14},{14,12},{16,18},{18,... | collective-permute-start | bytes 3145736 | tf_op jit(solution)/shard_map/ppermute | solution.py:1273
  362.7 29.2 %collective-permute-start.32 = (bf16[704,512]{1,0:T(8,128)(2,1)}, bf16[704,512]{1,0:T(8,128)(2,1)S(1)}, u32[]{:S(2)}, u32[]{:S(2)}) collective-permute-start(bf16[704,512]{1,0:T(8,128)(2,1)} %constant_dynamic-slice_fusion.8), channel_id=1, source_target_pairs={{0,4},{2,6},{4,0},{6,2},{8,12},{10,14},{12,8},{14,10},{16,20},{18,... | collective-permute-start | bytes 2162696 | tf_op jit(solution)/shard_map/ppermute | solution.py:1273
  364.3 27.6 %collective-permute-start.33 = (bf16[1,144,512]{2,1,0:T(8,128)(2,1)S(1)}, bf16[1,144,512]{2,1,0:T(8,128)(2,1)S(1)}, u32[]{:S(2)}, u32[]{:S(2)}) collective-permute-start(bf16[1,144,512]{2,1,0:T(8,128)(2,1)S(1)} %fusion.11), channel_id=1, source_target_pairs={{0,16},{2,18},{4,20},{6,22},{8,24},{10,26},{12,28},{14,30},{16,0},... | collective-permute-start | bytes 442376 | tf_op jit(solution)/shard_map/ppermute | solution.py:1273
  393.0 17.2 %collective-permute-start.35 = (bf16[352,512]{1,0:T(8,128)(2,1)S(1)}, bf16[352,512]{1,0:T(8,128)(2,1)S(1)}, u32[]{:S(2)}, u32[]{:S(2)}) collective-permute-start(bf16[352,512]{1,0:T(8,128)(2,1)S(1)} %constant_dynamic-slice_fusion.7), channel_id=1, source_target_pairs={{0,8},{2,10},{4,12},{6,14},{8,0},{10,2},{12,4},{14,6},{16,24},{18,... | collective-permute-start | bytes 1081352 | tf_op jit(solution)/shard_map/ppermute | solution.py:1273
  411.1 18.4 %collective-permute-start.37 = (bf16[2,768,512]{2,1,0:T(8,128)(2,1)}, bf16[2,768,512]{2,1,0:T(8,128)(2,1)S(1)}, u32[]{:S(2)}, u32[]{:S(2)}) collective-permute-start(bf16[2,768,512]{2,1,0:T(8,128)(2,1)} %get-tuple-element.657), channel_id=1, source_target_pairs={{0,2},{2,0},{4,6},{6,4},{8,10},{10,8},{12,14},{14,12},{16,18},{18,... | collective-permute-start | bytes 4718600 | tf_op jit(solution)/shard_map/ppermute | solution.py:1273
  411.2 18.4 %collective-permute-start.38 = (bf16[1024,512]{1,0:T(8,128)(2,1)}, bf16[1024,512]{1,0:T(8,128)(2,1)}, u32[]{:S(2)}, u32[]{:S(2)}) collective-permute-start(bf16[1024,512]{1,0:T(8,128)(2,1)} %get-tuple-element.658), channel_id=1, source_target_pairs={{1,2},{2,1},{5,6},{6,5},{9,10},{10,9},{13,14},{14,13},{17,18},{18,... | collective-permute-start | bytes 3145736 | tf_op jit(solution)/shard_map/ppermute | solution.py:1285
  433.8 29.4 %collective-permute-start.44 = (bf16[8,144,512]{2,1,0:T(8,128)(2,1)S(1)}, bf16[8,144,512]{2,1,0:T(8,128)(2,1)S(1)}, u32[]{:S(2)}, u32[]{:S(2)}) collective-permute-start(bf16[8,144,512]{2,1,0:T(8,128)(2,1)S(1)} %pad_maximum_fusion.4.mine_ref), channel_id=1, source_target_pairs={{0,2},{2,0},{4,6},{6,4},{8,10},{10,8},{12,14},{14,12},{16,18},{18,... | collective-permute-start | bytes 3538952 | tf_op jit(solution)/shard_map/ppermute | solution.py:1273
  442.9 20.2 %collective-permute-start.42 = (bf16[768,512]{1,0:T(8,128)(2,1)}, bf16[768,512]{1,0:T(8,128)(2,1)}, u32[]{:S(2)}, u32[]{:S(2)}) collective-permute-start(bf16[768,512]{1,0:T(8,128)(2,1)} %fusion.7), channel_id=1, source_target_pairs={{0,1},{1,0},{2,3},{3,2},{4,5},{5,4},{6,7},{7,6},{8,9},{9,8},{10,11... | collective-permute-start | bytes 2359304 | tf_op jit(solution)/shard_map/ppermute | solution.py:1279
  466.4 18.2 %collective-permute-start.46 = (bf16[384,512]{1,0:T(8,128)(2,1)S(1)}, bf16[384,512]{1,0:T(8,128)(2,1)S(1)}, u32[]{:S(2)}, u32[]{:S(2)}) collective-permute-start(bf16[384,512]{1,0:T(8,128)(2,1)S(1)} %fusion.9), channel_id=1, source_target_pairs={{0,1},{1,0},{2,3},{3,2},{4,5},{5,4},{6,7},{7,6},{8,9},{9,8},{10,11... | collective-permute-start | bytes 1179656 | tf_op jit(solution)/shard_map/ppermute | solution.py:1279
  466.7 17.9 %collective-permute-start.47 = (bf16[384,512]{1,0:T(8,128)(2,1)}, bf16[384,512]{1,0:T(8,128)(2,1)S(1)}, u32[]{:S(2)}, u32[]{:S(2)}) collective-permute-start(bf16[384,512]{1,0:T(8,128)(2,1)} %constant_dynamic-slice_fusion.5), channel_id=1, source_target_pairs={{0,4},{2,6},{4,0},{6,2},{8,12},{10,14},{12,8},{14,10},{16,20},{18,... | collective-permute-start | bytes 1179656 | tf_op jit(solution)/shard_map/ppermute | solution.py:1273
  494.8 18.1 %collective-permute-start.51 = (bf16[4,176,512]{2,1,0:T(8,128)(2,1)}, bf16[4,176,512]{2,1,0:T(8,128)(2,1)S(1)}, u32[]{:S(2)}, u32[]{:S(2)}) collective-permute-start(bf16[4,176,512]{2,1,0:T(8,128)(2,1)} %pad_maximum_fusion.10), channel_id=1, source_target_pairs={{0,4},{2,6},{4,0},{6,2},{8,12},{10,14},{12,8},{14,10},{16,20},{18,... | collective-permute-start | bytes 2162696 | tf_op jit(solution)/shard_map/ppermute | solution.py:1273
  (121 other events, 1029.8 us)

commit v6 on v5

--- a/solution.py
+++ b/solution.py
@@ -1597,7 +1597,7 @@
         [(w_dec_self, 3 * HALF, 0)], [row, row_low], part_outs, part_scratch,
     )
     flow.add("dec_qkv", summed_own(at, keep0, send0, flow.results["dec_qkv_other"]))
-    flow.add("target_grad", moved(at, target_low, 2))
+    flow.add("target_grad", moved(at, target_low, 4))
 
     done = flow.results
 

time: 581 us -> 578 us (level)
  transfers between devices with their start and end apart: 67 -> 67, of which waited for: 22 -> 23; matrix products, arithmetic and copies ran while one was open for 8% -> 8% of each run, Pallas kernels for 58% -> 58%
where the time goes in v6:
time: 578 us; the launch traced here: 571 us
  Pallas kernels  339 us (59%)
  starting transfers between devices  94 us (16%)
  waiting for transfers between devices  49.3 us (9%)
  local copies, waits for them, and re-layouts  46.1 us (8%)
  other arithmetic  39.9 us (7%)
    pallas_call x6, Pallas kernels, heads_backward(): pl.pallas_call(partial(backward_kernel, causal=causal), grid=(width // 12...  132 us
    pallas_call x10, Pallas kernels, rows_call(): pl.pallas_call(kernel, grid=(n // block,), in_specs=[pl.BlockSpec(memory_...  120 us
    pallas_call x6, Pallas kernels, heads_forward(): pl.pallas_call(partial(forward_kernel, causal=causal), grid=(width // 128...  72.3 us
    ppermute x50, starting transfers between devices, flip(): lax.ppermute(values, 'dp', [(d, d ^ mask) for d in range(self.dp_size)])  70.4 us
    ppermute x50, waiting for transfers between devices, flip(): lax.ppermute(values, 'dp', [(d, d ^ mask) for d in range(self.dp_size)])  31 us
    ppermute x9, waiting for transfers between devices, y_swap(): return lax.ppermute(values, 'mp', [(0, 1), (1, 0)])  18.3 us
    unnamed x172, local copies, waits for them, and re-layouts  18.1 us
    pallas_call x4, Pallas kernels, unpack(): pl.pallas_call(partial(unpack_kernel, places=places), in_specs=[pl.BlockS...  14.7 us
  transfers between devices with their start and end apart: 67, of which 23 were waited for; matrix products, arithmetic and copies ran while one was open for 8% of the time, Pallas kernels for 58%

profile of v6, /device:TPU:0, one launch (start us, length us, event | category | flops | bytes accessed | tf_op | source)
XLA Modules:
  0.0 571.2 jit_solution(5929328229015713592)
XLA Ops:
  8.4 5.5 collective-permute-start.2
  37.9 5.2 project.2
  50.0 14.1 %attention.4 = (bf16[1024,256]{1,0:T(8,128)(2,1)}, f32[1024,256]{1,0:T(8,128)}) custom-call(s32[2]{0:T(128)} %get-tuple-element.845.core_ref, bf16[1024,256]{1,0:T(8,128)(2,1)} %get-tuple-element.452.q_ref, bf16[2,1024,256]{2,1,0:T(8,128)(2,1)} %get-tuple-element.453.own_ref, bf16[2,1024,256]{2,1,0:T(8,128)(2,1)} %copy-done.17, ...), custom_call_target="tpu_custom_call" | custom-call | flops 1 | bytes 1 | tf_op jit(solution)/shard_map/attention/pallas_call | solution.py:633
  67.1 14.0 %attention.5 = (bf16[1024,256]{1,0:T(8,128)(2,1)}, f32[1024,256]{1,0:T(8,128)}) custom-call(s32[2]{0:T(128)} %get-tuple-element.845.core_ref, bf16[1024,256]{1,0:T(8,128)(2,1)} %get-tuple-element.467.q_ref, bf16[2,1024,256]{2,1,0:T(8,128)(2,1)} %get-tuple-element.468.own_ref, bf16[2,1024,256]{2,1,0:T(8,128)(2,1)} %collective-permute-done.5.got_ref, ...), custom_call_target="tpu_custom_call" | custom-call | flops 1 | bytes 1 | tf_op jit(solution)/shard_map/attention/pallas_call | solution.py:633
  82.3 5.4 project.3
  91.6 8.4 %attention_causal.2 = (bf16[1024,256]{1,0:T(8,128)(2,1)}, f32[1024,256]{1,0:T(8,128)}) custom-call(s32[2]{0:T(128)} %get-tuple-element.845.core_ref, bf16[1024,256]{1,0:T(8,128)(2,1)} %get-tuple-element.475.q_ref, bf16[2,1024,256]{2,1,0:T(8,128)(2,1)} %get-tuple-element.476.own_ref, bf16[2,1024,256]{2,1,0:T(8,128)(2,1)} %copy-done.15, ...), custom_call_target="tpu_custom_call" | custom-call | flops 1 | bytes 1 | tf_op jit(solution)/shard_map/attention_causal/pallas_call | solution.py:633
  100.0 5.0 collective-permute-start.13
  109.3 8.2 %attention_causal.3 = (bf16[1024,256]{1,0:T(8,128)(2,1)}, f32[1024,256]{1,0:T(8,128)}) custom-call(s32[2]{0:T(128)} %get-tuple-element.845.core_ref, bf16[1024,256]{1,0:T(8,128)(2,1)} %get-tuple-element.489.q_ref, bf16[2,1024,256]{2,1,0:T(8,128)(2,1)} %get-tuple-element.490.own_ref, bf16[2,1024,256]{2,1,0:T(8,128)(2,1)} %copy-done.16, ...), custom_call_target="tpu_custom_call" | custom-call | flops 1 | bytes 1 | tf_op jit(solution)/shard_map/attention_causal/pallas_call | solution.py:633
  118.3 4.4 collective-permute-start.14
  126.0 12.0 %encoder_feed.1 = (f32[1024,512]{1,0:T(8,128)}, f32[1024,512]{1,0:T(8,128)}, bf16[1024,512]{1,0:T(8,128)(2,1)}) custom-call(s32[2]{0:T(128)} %get-tuple-element.845.core_ref, bf16[1024,256]{1,0:T(8,128)(2,1)} %get-tuple-element.502.o0_ref.o_ref, bf16[1024,256]{1,0:T(8,128)(2,1)} %get-tuple-element.503.o1_ref.o_ref, ...), custom_call_target="tpu_custom_call" | custom-call | flops 1 | bytes 1 | tf_op jit(solution)/shard_map/encoder_feed/pallas_call | solution.py:1192
  138.8 7.0 %cross_project.1 = (f32[1024,512]{1,0:T(8,128)}, bf16[1024,256]{1,0:T(8,128)(2,1)}, bf16[1024,256]{1,0:T(8,128)(2,1)}, bf16[2,1024,256]{2,1,0:T(8,128)(2,1)}, bf16[2,1024,256]{2,1,0:T(8,128)(2,1)}) custom-call(s32[2]{0:T(128)} %get-tuple-element.845.core_ref, bf16[1024,256]{1,0:T(8,128)(2,1)} %get-tuple-element.488.o0_ref.o_ref, ...), custom_call_target="tpu_custom_call" | custom-call | flops 1 | bytes 1 | tf_op jit(solution)/shard_map/cross_project/pallas_call | solution.py:1192
  149.7 13.8 %attention.6 = (bf16[1024,256]{1,0:T(8,128)(2,1)}, f32[1024,256]{1,0:T(8,128)}) custom-call(s32[2]{0:T(128)} %get-tuple-element.845.core_ref, bf16[1024,256]{1,0:T(8,128)(2,1)} %get-tuple-element.518.q_ref, bf16[2,1024,256]{2,1,0:T(8,128)(2,1)} %get-tuple-element.519.own_ref, bf16[2,1024,256]{2,1,0:T(8,128)(2,1)} %copy-done.19, ...), custom_call_target="tpu_custom_call" | custom-call | flops 1 | bytes 1 | tf_op jit(solution)/shard_map/attention/pallas_call | solution.py:633
  164.6 13.8 %attention.7 = (bf16[1024,256]{1,0:T(8,128)(2,1)}, f32[1024,256]{1,0:T(8,128)}) custom-call(s32[2]{0:T(128)} %get-tuple-element.845.core_ref, bf16[1024,256]{1,0:T(8,128)(2,1)} %get-tuple-element.525.q_ref, bf16[2,1024,256]{2,1,0:T(8,128)(2,1)} %get-tuple-element.526.own_ref, bf16[2,1024,256]{2,1,0:T(8,128)(2,1)} %copy-done.18, ...), custom_call_target="tpu_custom_call" | custom-call | flops 1 | bytes 1 | tf_op jit(solution)/shard_map/attention/pallas_call | solution.py:633
  181.3 30.1 %decoder_feed.1 = (bf16[1024,512]{1,0:T(8,128)(2,1)}, f32[1024,512]{1,0:T(8,128)}, f32[1024,512]{1,0:T(8,128)}, bf16[1024,256]{1,0:T(8,128)(2,1)}, bf16[1024,256...) custom-call(s32[2]{0:T(128)} %get-tuple-element.845.core_ref, ...), custom_call_target="tpu_custom_call" | custom-call | flops 1 | bytes 1 | tf_op jit(solution)/shard_map/decoder_feed/pallas_call | solution.py:1192
  215.0 25.1 %attention_back.4 = (bf16[1024,256]{1,0:T(8,128)(2,1)}, bf16[2,1024,256]{2,1,0:T(8,128)(2,1)}, bf16[2,1024,256]{2,1,0:T(8,128)(2,1)}) custom-call(s32[2]{0:T(128)} %get-tuple-element.845.core_ref, bf16[1024,256]{1,0:T(8,128)(2,1)} %get-tuple-element.518.q_ref, bf16[2,1024,256]{2,1,0:T(8,128)(2,1)} %get-tuple-element.519.own_ref, ...), custom_call_target="tpu_custom_call" | custom-call | flops 1 | bytes 1 | tf_op jit(solution)/shard_map/attention_back/pallas_call | solution.py:776
  244.9 25.1 %attention_back.5 = (bf16[1024,256]{1,0:T(8,128)(2,1)}, bf16[2,1024,256]{2,1,0:T(8,128)(2,1)}, bf16[2,1024,256]{2,1,0:T(8,128)(2,1)}) custom-call(s32[2]{0:T(128)} %get-tuple-element.845.core_ref, bf16[1024,256]{1,0:T(8,128)(2,1)} %get-tuple-element.525.q_ref, bf16[2,1024,256]{2,1,0:T(8,128)(2,1)} %get-tuple-element.526.own_ref, ...), custom_call_target="tpu_custom_call" | custom-call | flops 1 | bytes 1 | tf_op jit(solution)/shard_map/attention_back/pallas_call | solution.py:776
  277.0 29.3 %encoder_feed_back.1 = (f32[1024,512]{1,0:T(8,128)}, bf16[1024,256]{1,0:T(8,128)(2,1)}, bf16[1024,256]{1,0:T(8,128)(2,1)}, bf16[2,1408,512]{2,1,0:T(8,128)(2,1)}...) custom-call(s32[2]{0:T(128)} %get-tuple-element.845.core_ref, bf16[2,1024,256]{2,1,0:T(8,128)(2,1)} %get-tuple-element.558.kv0_ref, ...), custom_call_target="tpu_custom_call" | custom-call | flops 1 | bytes 1 | tf_op jit(solution)/shard_map/encoder_feed_back/pallas_call | solution.py:1192
  311.1 9.3 %cross_project_back.1 = (f32[1024,512]{1,0:T(8,128)}, bf16[1024,256]{1,0:T(8,128)(2,1)}, bf16[1024,256]{1,0:T(8,128)(2,1)}, bf16[2,256,512]{2,1,0:T(8,128)(2,1)}...) custom-call(s32[2]{0:T(128)} %get-tuple-element.845.core_ref, bf16[1024,256]{1,0:T(8,128)(2,1)} %get-tuple-element.587.q0_grad_ref, ...), custom_call_target="tpu_custom_call" | custom-call | flops 1 | bytes 1 | tf_op jit(solution)/shard_map/cross_project_back/pallas_call | solution.py:1192
  329.3 25.1 %attention_back.6 = (bf16[1024,256]{1,0:T(8,128)(2,1)}, bf16[2,1024,256]{2,1,0:T(8,128)(2,1)}, bf16[2,1024,256]{2,1,0:T(8,128)(2,1)}) custom-call(s32[2]{0:T(128)} %get-tuple-element.845.core_ref, bf16[1024,256]{1,0:T(8,128)(2,1)} %get-tuple-element.467.q_ref, bf16[2,1024,256]{2,1,0:T(8,128)(2,1)} %get-tuple-element.468.own_ref, ...), custom_call_target="tpu_custom_call" | custom-call | flops 1 | bytes 1 | tf_op jit(solution)/shard_map/attention_back/pallas_call | solution.py:776
  354.4 4.8 collective-permute-done.29
  366.8 25.0 %attention_back.7 = (bf16[1024,256]{1,0:T(8,128)(2,1)}, bf16[2,1024,256]{2,1,0:T(8,128)(2,1)}, bf16[2,1024,256]{2,1,0:T(8,128)(2,1)}) custom-call(s32[2]{0:T(128)} %get-tuple-element.845.core_ref, bf16[1024,256]{1,0:T(8,128)(2,1)} %get-tuple-element.452.q_ref, bf16[2,1024,256]{2,1,0:T(8,128)(2,1)} %get-tuple-element.453.own_ref, ...), custom_call_target="tpu_custom_call" | custom-call | flops 1 | bytes 1 | tf_op jit(solution)/shard_map/attention_back/pallas_call | solution.py:776
  396.8 9.7 %project_back.3 = (f32[1024,512]{1,0:T(8,128)}, bf16[1024,512]{1,0:T(8,128)(2,1)}, bf16[2,768,512]{2,1,0:T(8,128)(2,1)}, bf16[2,768,512]{2,1,0:T(8,128)(2,1)}) custom-call(s32[2]{0:T(128)} %get-tuple-element.845.core_ref, bf16[1024,256]{1,0:T(8,128)(2,1)} %get-tuple-element.633.q0_grad_ref, bf16[2,1024,256]{2,1,0:T(8,128)(2,1)} %get-tuple-element.634.kv0_ref, ...), custom_call_target="tpu_custom_call" | custom-call | flops 1 | bytes 1 | tf_op jit(solution)/shard_map/project_back/pallas_call | solution.py:1192
  413.8 15.7 %attention_causal_back.2 = (bf16[1024,256]{1,0:T(8,128)(2,1)}, bf16[2,1024,256]{2,1,0:T(8,128)(2,1)}, bf16[2,1024,256]{2,1,0:T(8,128)(2,1)}) custom-call(s32[2]{0:T(128)} %get-tuple-element.845.core_ref, bf16[1024,256]{1,0:T(8,128)(2,1)} %get-tuple-element.489.q_ref, bf16[2,1024,256]{2,1,0:T(8,128)(2,1)} %get-tuple-element.490.own_ref, ...), custom_call_target="tpu_custom_call" | custom-call | flops 1 | bytes 1 | tf_op jit(solution)/shard_map/attention_causal_back/pallas_call | solution.py:776
  433.8 9.1 %collective-permute-start.44 = (bf16[8,144,512]{2,1,0:T(8,128)(2,1)S(1)}, bf16[8,144,512]{2,1,0:T(8,128)(2,1)S(1)}, u32[]{:S(2)}, u32[]{:S(2)}) collective-permute-start(bf16[8,144,512]{2,1,0:T(8,128)(2,1)S(1)} %pad_maximum_fusion.4.mine_ref), channel_id=1, source_target_pairs={{0,2},{2,0},{4,6},{6,4},{8,10},{10,8},{12,14},{14,12},{16,18},{18,... | collective-permute-start | bytes 3538952 | tf_op jit(solution)/shard_map/ppermute | solution.py:1273
  447.2 6.2 %project_back.4 = (f32[1024,512]{1,0:T(8,128)}, bf16[1024,512]{1,0:T(8,128)(2,1)}, bf16[1,384,512]{2,1,0:T(8,128)(2,1)}, bf16[1,384,512]{2,1,0:T(8,128)(2,1)}) custom-call(s32[2]{0:T(128)} %get-tuple-element.845.core_ref, bf16[1024,256]{1,0:T(8,128)(2,1)} %get-tuple-element.668.q_ref, bf16[2,1024,256]{2,1,0:T(8,128)(2,1)} %get-tuple-element.669.kv_ref, ...), custom_call_target="tpu_custom_call" | custom-call | flops 1 | bytes 1 | tf_op jit(solution)/shard_map/project_back/pallas_call | solution.py:1192
  454.5 8.7 %collective-permute-done.42 = bf16[768,512]{1,0:T(8,128)(2,1)} collective-permute-done((bf16[768,512]{1,0:T(8,128)(2,1)}, bf16[768,512]{1,0:T(8,128)(2,1)}, u32[]{:S(2)}, u32[]{:S(2)}) %collective-permute-start.42) | collective-permute-done | bytes 786464 | tf_op jit(solution)/shard_map/ppermute | solution.py:1279
  468.7 15.9 %attention_causal_back.3 = (bf16[1024,256]{1,0:T(8,128)(2,1)}, bf16[2,1024,256]{2,1,0:T(8,128)(2,1)}, bf16[2,1024,256]{2,1,0:T(8,128)(2,1)}) custom-call(s32[2]{0:T(128)} %get-tuple-element.845.core_ref, bf16[1024,256]{1,0:T(8,128)(2,1)} %get-tuple-element.475.q_ref, bf16[2,1024,256]{2,1,0:T(8,128)(2,1)} %get-tuple-element.476.own_ref, ...), custom_call_target="tpu_custom_call" | custom-call | flops 1 | bytes 1 | tf_op jit(solution)/shard_map/attention_causal_back/pallas_call | solution.py:776
  486.4 6.8 %collective-permute-start.49 = (bf16[2,1024,256]{2,1,0:T(8,128)(2,1)}, bf16[2,1024,256]{2,1,0:T(8,128)(2,1)S(1)}, u32[]{:S(2)}, u32[]{:S(2)}) collective-permute-start(bf16[2,1024,256]{2,1,0:T(8,128)(2,1)} %get-tuple-element.698), channel_id=1, source_target_pairs={{0,2},{2,0},{4,6},{6,4},{8,10},{10,8},{12,14},{14,12},{16,18},{18,... | collective-permute-start | bytes 3145736 | tf_op jit(solution)/shard_map/ppermute | solution.py:1273
  496.7 6.1 %project_back.5 = (f32[1024,512]{1,0:T(8,128)}, bf16[1024,512]{1,0:T(8,128)(2,1)}, bf16[1,384,512]{2,1,0:T(8,128)(2,1)}, bf16[1,384,512]{2,1,0:T(8,128)(2,1)}) custom-call(s32[2]{0:T(128)} %get-tuple-element.845.core_ref, bf16[1024,256]{1,0:T(8,128)(2,1)} %get-tuple-element.696.q_ref, bf16[2,1024,256]{2,1,0:T(8,128)(2,1)} %get-tuple-element.697.kv_ref, ...), custom_call_target="tpu_custom_call" | custom-call | flops 1 | bytes 1 | tf_op jit(solution)/shard_map/project_back/pallas_call | solution.py:1192
  506.0 4.3 unpack.4
  530.2 4.7 unpack.5
  542.7 6.0 %collective-permute-done.61 = bf16[4,96,512]{2,1,0:T(8,128)(2,1)S(1)} collective-permute-done((bf16[4,96,512]{2,1,0:T(8,128)(2,1)S(1)}, bf16[4,96,512]{2,1,0:T(8,128)(2,1)S(1)}, u32[]{:S(2)}, u32[]{:S(2)}) %collective-permute-start.61) | collective-permute-done | bytes 393248 | tf_op jit(solution)/shard_map/ppermute | solution.py:1273
  (401 shorter events, 184.6 us)
Async XLA Ops:
  3.1 22.2 %collective-permute-start = (s32[6,1024]{0,1:T(8,128)}, s32[6,1024]{0,1:T(8,128)}, u32[]{:S(2)}, u32[]{:S(2)}) collective-permute-start(s32[6,1024]{0,1:T(8,128)} %copy.46), channel_id=1, source_target_pairs={{1,2},{2,1},{5,6},{6,5},{9,10},{10,9},{13,14},{14,13},{17,18},{18,... | collective-permute-start | bytes 73736 | tf_op jit(solution)/shard_map/ppermute | solution.py:1285
  4.7 30.6 %collective-permute-start.1 = (bf16[1024,512]{1,0:T(8,128)(2,1)}, bf16[1024,512]{1,0:T(8,128)(2,1)}, u32[]{:S(2)}, u32[]{:S(2)}) collective-permute-start(bf16[1024,512]{1,0:T(8,128)(2,1)} %bitcast.70), channel_id=1, source_target_pairs={{1,2},{2,1},{5,6},{6,5},{9,10},{10,9},{13,14},{14,13},{17,18},{18,... | collective-permute-start | bytes 3145736 | tf_op jit(solution)/shard_map/ppermute | solution.py:1285
  8.4 26.8 %collective-permute-start.2 = (bf16[384,512]{1,0:T(8,128)(2,1)}, bf16[384,512]{1,0:T(8,128)(2,1)}, u32[]{:S(2)}, u32[]{:S(2)}) collective-permute-start(bf16[384,512]{1,0:T(8,128)(2,1)} %constant_dynamic-slice_fusion.16), channel_id=1, source_target_pairs={{0,1},{1,0},{2,3},{3,2},{4,5},{5,4},{6,7},{7,6},{8,9},{9,8},{10,11... | collective-permute-start | bytes 1179656 | tf_op jit(solution)/shard_map/ppermute | solution.py:1279
  43.3 20.8 %collective-permute-start.5 = (bf16[2,1024,256]{2,1,0:T(8,128)(2,1)}, bf16[2,1024,256]{2,1,0:T(8,128)(2,1)}, u32[]{:S(2)}, u32[]{:S(2)}) collective-permute-start(bf16[2,1024,256]{2,1,0:T(8,128)(2,1)} %get-tuple-element.468.own_ref), channel_id=1, source_target_pairs={{0,2},{2,0},{4,6},{6,4},{8,10},{10,8},{12,14},{14,12},{16,18},{18,... | collective-permute-start | bytes 3145736 | tf_op jit(solution)/shard_map/ppermute | solution.py:1273
  45.7 18.3 %collective-permute-start.6 = (bf16[512,512]{1,0:T(8,128)(2,1)}, bf16[512,512]{1,0:T(8,128)(2,1)S(1)}, u32[]{:S(2)}, u32[]{:S(2)}) collective-permute-start(bf16[512,512]{1,0:T(8,128)(2,1)} %constant_dynamic-slice_fusion.15), channel_id=1, source_target_pairs={{0,1},{1,0},{2,3},{3,2},{4,5},{5,4},{6,7},{7,6},{8,9},{9,8},{10,11... | collective-permute-start | bytes 1572872 | tf_op jit(solution)/shard_map/ppermute | solution.py:1279
  46.7 34.4 %collective-permute-start.7 = (bf16[1024,512]{1,0:T(8,128)(2,1)}, bf16[1024,512]{1,0:T(8,128)(2,1)S(1)}, u32[]{:S(2)}, u32[]{:S(2)}) collective-permute-start(bf16[1024,512]{1,0:T(8,128)(2,1)} %bitcast.68), channel_id=1, source_target_pairs={{1,2},{2,1},{5,6},{6,5},{9,10},{10,9},{13,14},{14,13},{17,18},{18,... | collective-permute-start | bytes 3145736 | tf_op jit(solution)/shard_map/ppermute | solution.py:1285
  64.1 17.1 %collective-permute-start.8 = (bf16[512,512]{1,0:T(8,128)(2,1)S(1)}, bf16[512,512]{1,0:T(8,128)(2,1)S(1)}, u32[]{:S(2)}, u32[]{:S(2)}) collective-permute-start(bf16[512,512]{1,0:T(8,128)(2,1)S(1)} %collective-permute-done.6.near_ref.proj_near_ref), channel_id=1, source_target_pairs={{0,2},{2,0},{4,6},{6,4},{8,10},{10,8},{12,14},{14,12},{16,18},{18,... | collective-permute-start | bytes 1572872 | tf_op jit(solution)/shard_map/ppermute | solution.py:1273
  66.6 33.4 %collective-permute-start.11 = (bf16[1152,512]{1,0:T(8,128)(2,1)}, bf16[1152,512]{1,0:T(8,128)(2,1)S(1)}, u32[]{:S(2)}, u32[]{:S(2)}) collective-permute-start(bf16[1152,512]{1,0:T(8,128)(2,1)} %constant_dynamic-slice_fusion.14), channel_id=1, source_target_pairs={{0,1},{1,0},{2,3},{3,2},{4,5},{5,4},{6,7},{7,6},{8,9},{9,8},{10,11... | collective-permute-start | bytes 3538952 | tf_op jit(solution)/shard_map/ppermute | solution.py:1279
  100.0 18.3 %collective-permute-start.13 = (bf16[1152,512]{1,0:T(8,128)(2,1)S(1)}, bf16[1152,512]{1,0:T(8,128)(2,1)S(1)}, u32[]{:S(2)}, u32[]{:S(2)}) collective-permute-start(bf16[1152,512]{1,0:T(8,128)(2,1)S(1)} %collective-permute-done.11.near_ref), channel_id=1, source_target_pairs={{0,2},{2,0},{4,6},{6,4},{8,10},{10,8},{12,14},{14,12},{16,18},{18,... | collective-permute-start | bytes 3538952 | tf_op jit(solution)/shard_map/ppermute | solution.py:1273
  118.3 19.7 %collective-permute-start.14 = (bf16[384,512]{1,0:T(8,128)(2,1)S(1)}, bf16[384,512]{1,0:T(8,128)(2,1)S(1)}, u32[]{:S(2)}, u32[]{:S(2)}) collective-permute-start(bf16[384,512]{1,0:T(8,128)(2,1)S(1)} %collective-permute-done.12.near_ref.cross_near_ref.cq_near_ref), channel_id=1, source_target_pairs={{0,2},{2,0},{4,6},{6,4},{8,10},{10,8},{12,14},{14,12},{16,18},{18,... | collective-permute-start | bytes 1179656 | tf_op jit(solution)/shard_map/ppermute | solution.py:1273
  124.1 39.4 %collective-permute-start.17 = (bf16[1152,512]{1,0:T(8,128)(2,1)}, bf16[1152,512]{1,0:T(8,128)(2,1)}, u32[]{:S(2)}, u32[]{:S(2)}) collective-permute-start(bf16[1152,512]{1,0:T(8,128)(2,1)} %constant_dynamic-slice_fusion.12), channel_id=1, source_target_pairs={{0,1},{1,0},{2,3},{3,2},{4,5},{5,4},{6,7},{7,6},{8,9},{9,8},{10,11... | collective-permute-start | bytes 3538952 | tf_op jit(solution)/shard_map/ppermute | solution.py:1279
  145.8 17.6 %collective-permute-start.16 = (bf16[2,1024,256]{2,1,0:T(8,128)(2,1)}, bf16[2,1024,256]{2,1,0:T(8,128)(2,1)S(1)}, u32[]{:S(2)}, u32[]{:S(2)}) collective-permute-start(bf16[2,1024,256]{2,1,0:T(8,128)(2,1)} %get-tuple-element.526.own_ref), channel_id=1, source_target_pairs={{0,2},{2,0},{4,6},{6,4},{8,10},{10,8},{12,14},{14,12},{16,18},{18,... | collective-permute-start | bytes 3145736 | tf_op jit(solution)/shard_map/ppermute | solution.py:1273
  146.3 32.1 %collective-permute-start.18 = (bf16[1024,1024]{1,0:T(8,128)(2,1)S(1)}, bf16[1024,1024]{1,0:T(8,128)(2,1)S(1)}, u32[]{:S(2)}, u32[]{:S(2)}) collective-permute-start(bf16[1024,1024]{1,0:T(8,128)(2,1)S(1)} %copy-done.9), channel_id=1, source_target_pairs={{1,2},{2,1},{5,6},{6,5},{9,10},{10,9},{13,14},{14,13},{17,18},{18,... | collective-permute-start | bytes 6291464 | tf_op jit(solution)/shard_map/ppermute | solution.py:1285
  178.4 33.0 %collective-permute-start.20 = (bf16[1024,512]{1,0:T(8,128)(2,1)S(1)}, bf16[1024,512]{1,0:T(8,128)(2,1)S(1)}, u32[]{:S(2)}, u32[]{:S(2)}) collective-permute-start(bf16[1024,512]{1,0:T(8,128)(2,1)S(1)} %copy-done.5), channel_id=1, source_target_pairs={{1,2},{2,1},{5,6},{6,5},{9,10},{10,9},{13,14},{14,13},{17,18},{18,... | collective-permute-start | bytes 3145736 | tf_op jit(solution)/shard_map/ppermute | solution.py:1285
  211.4 28.7 %collective-permute-start.21 = (bf16[2,1152,512]{2,1,0:T(8,128)(2,1)}, bf16[2,1152,512]{2,1,0:T(8,128)(2,1)S(1)}, u32[]{:S(2)}, u32[]{:S(2)}) collective-permute-start(bf16[2,1152,512]{2,1,0:T(8,128)(2,1)} %get-tuple-element.550), channel_id=1, source_target_pairs={{0,2},{2,0},{4,6},{6,4},{8,10},{10,8},{12,14},{14,12},{16,18},{18,... | collective-permute-start | bytes 7077896 | tf_op jit(solution)/shard_map/ppermute | solution.py:1273
  214.1 26.0 %collective-permute-start.22 = (bf16[1024,512]{1,0:T(8,128)(2,1)}, bf16[1024,512]{1,0:T(8,128)(2,1)S(1)}, u32[]{:S(2)}, u32[]{:S(2)}) collective-permute-start(bf16[1024,512]{1,0:T(8,128)(2,1)} %get-tuple-element.752), channel_id=1, source_target_pairs={{1,2},{2,1},{5,6},{6,5},{9,10},{10,9},{13,14},{14,13},{17,18},{18,... | collective-permute-start | bytes 3145736 | tf_op jit(solution)/shard_map/ppermute | solution.py:1285
  242.0 29.3 %collective-permute-start.24 = (bf16[1152,512]{1,0:T(8,128)(2,1)S(1)}, bf16[1152,512]{1,0:T(8,128)(2,1)}, u32[]{:S(2)}, u32[]{:S(2)}) collective-permute-start(bf16[1152,512]{1,0:T(8,128)(2,1)S(1)} %fusion.4), channel_id=1, source_target_pairs={{0,1},{1,0},{2,3},{3,2},{4,5},{5,4},{6,7},{7,6},{8,9},{9,8},{10,11... | collective-permute-start | bytes 3538952 | tf_op jit(solution)/shard_map/ppermute | solution.py:1279
  244.9 25.1 %collective-permute-start.23 = (bf16[2,1024,256]{2,1,0:T(8,128)(2,1)}, bf16[2,1024,256]{2,1,0:T(8,128)(2,1)}, u32[]{:S(2)}, u32[]{:S(2)}) collective-permute-start(bf16[2,1024,256]{2,1,0:T(8,128)(2,1)} %get-tuple-element.564), channel_id=1, source_target_pairs={{0,2},{2,0},{4,6},{6,4},{8,10},{10,8},{12,14},{14,12},{16,18},{18,... | collective-permute-start | bytes 3145736 | tf_op jit(solution)/shard_map/ppermute | solution.py:1273
  273.5 32.8 %collective-permute-start.26 = (bf16[576,512]{1,0:T(8,128)(2,1)S(1)}, bf16[576,512]{1,0:T(8,128)(2,1)S(1)}, u32[]{:S(2)}, u32[]{:S(2)}) collective-permute-start(bf16[576,512]{1,0:T(8,128)(2,1)S(1)} %constant_dynamic-slice_fusion.11), channel_id=1, source_target_pairs={{0,4},{2,6},{4,0},{6,2},{8,12},{10,14},{12,8},{14,10},{16,20},{18,... | collective-permute-start | bytes 1769480 | tf_op jit(solution)/shard_map/ppermute | solution.py:1273
  325.4 33.8 %collective-permute-start.29 = (bf16[1408,512]{1,0:T(8,128)(2,1)}, bf16[1408,512]{1,0:T(8,128)(2,1)}, u32[]{:S(2)}, u32[]{:S(2)}) collective-permute-start(bf16[1408,512]{1,0:T(8,128)(2,1)} %fusion.3), channel_id=1, source_target_pairs={{0,1},{1,0},{2,3},{3,2},{4,5},{5,4},{6,7},{7,6},{8,9},{9,8},{10,11... | collective-permute-start | bytes 4325384 | tf_op jit(solution)/shard_map/ppermute | solution.py:1279
  326.7 27.6 %collective-permute-start.30 = (bf16[144,512]{1,0:T(8,128)(2,1)S(1)}, bf16[144,512]{1,0:T(8,128)(2,1)S(1)}, u32[]{:S(2)}, u32[]{:S(2)}) collective-permute-start(bf16[144,512]{1,0:T(8,128)(2,1)S(1)} %constant_dynamic-slice_fusion.9), channel_id=1, source_target_pairs={{0,16},{2,18},{4,20},{6,22},{8,24},{10,26},{12,28},{14,30},{16,0},... | collective-permute-start | bytes 442376 | tf_op jit(solution)/shard_map/ppermute | solution.py:1273
  362.6 29.3 %collective-permute-start.31 = (bf16[2,1024,256]{2,1,0:T(8,128)(2,1)}, bf16[2,1024,256]{2,1,0:T(8,128)(2,1)}, u32[]{:S(2)}, u32[]{:S(2)}) collective-permute-start(bf16[2,1024,256]{2,1,0:T(8,128)(2,1)} %get-tuple-element.623), channel_id=1, source_target_pairs={{0,2},{2,0},{4,6},{6,4},{8,10},{10,8},{12,14},{14,12},{16,18},{18,... | collective-permute-start | bytes 3145736 | tf_op jit(solution)/shard_map/ppermute | solution.py:1273
  362.7 29.2 %collective-permute-start.32 = (bf16[704,512]{1,0:T(8,128)(2,1)}, bf16[704,512]{1,0:T(8,128)(2,1)S(1)}, u32[]{:S(2)}, u32[]{:S(2)}) collective-permute-start(bf16[704,512]{1,0:T(8,128)(2,1)} %constant_dynamic-slice_fusion.8), channel_id=1, source_target_pairs={{0,4},{2,6},{4,0},{6,2},{8,12},{10,14},{12,8},{14,10},{16,20},{18,... | collective-permute-start | bytes 2162696 | tf_op jit(solution)/shard_map/ppermute | solution.py:1273
  364.3 27.6 %collective-permute-start.33 = (bf16[1,144,512]{2,1,0:T(8,128)(2,1)S(1)}, bf16[1,144,512]{2,1,0:T(8,128)(2,1)S(1)}, u32[]{:S(2)}, u32[]{:S(2)}) collective-permute-start(bf16[1,144,512]{2,1,0:T(8,128)(2,1)S(1)} %fusion.11), channel_id=1, source_target_pairs={{0,16},{2,18},{4,20},{6,22},{8,24},{10,26},{12,28},{14,30},{16,0},... | collective-permute-start | bytes 442376 | tf_op jit(solution)/shard_map/ppermute | solution.py:1273
  393.0 17.2 %collective-permute-start.35 = (bf16[352,512]{1,0:T(8,128)(2,1)S(1)}, bf16[352,512]{1,0:T(8,128)(2,1)S(1)}, u32[]{:S(2)}, u32[]{:S(2)}) collective-permute-start(bf16[352,512]{1,0:T(8,128)(2,1)S(1)} %constant_dynamic-slice_fusion.7), channel_id=1, source_target_pairs={{0,8},{2,10},{4,12},{6,14},{8,0},{10,2},{12,4},{14,6},{16,24},{18,... | collective-permute-start | bytes 1081352 | tf_op jit(solution)/shard_map/ppermute | solution.py:1273
  411.1 18.4 %collective-permute-start.37 = (bf16[2,768,512]{2,1,0:T(8,128)(2,1)}, bf16[2,768,512]{2,1,0:T(8,128)(2,1)S(1)}, u32[]{:S(2)}, u32[]{:S(2)}) collective-permute-start(bf16[2,768,512]{2,1,0:T(8,128)(2,1)} %get-tuple-element.657), channel_id=1, source_target_pairs={{0,2},{2,0},{4,6},{6,4},{8,10},{10,8},{12,14},{14,12},{16,18},{18,... | collective-permute-start | bytes 4718600 | tf_op jit(solution)/shard_map/ppermute | solution.py:1273
  411.2 18.4 %collective-permute-start.38 = (bf16[1024,512]{1,0:T(8,128)(2,1)}, bf16[1024,512]{1,0:T(8,128)(2,1)}, u32[]{:S(2)}, u32[]{:S(2)}) collective-permute-start(bf16[1024,512]{1,0:T(8,128)(2,1)} %get-tuple-element.658), channel_id=1, source_target_pairs={{1,2},{2,1},{5,6},{6,5},{9,10},{10,9},{13,14},{14,13},{17,18},{18,... | collective-permute-start | bytes 3145736 | tf_op jit(solution)/shard_map/ppermute | solution.py:1285
  433.8 29.4 %collective-permute-start.44 = (bf16[8,144,512]{2,1,0:T(8,128)(2,1)S(1)}, bf16[8,144,512]{2,1,0:T(8,128)(2,1)S(1)}, u32[]{:S(2)}, u32[]{:S(2)}) collective-permute-start(bf16[8,144,512]{2,1,0:T(8,128)(2,1)S(1)} %pad_maximum_fusion.4.mine_ref), channel_id=1, source_target_pairs={{0,2},{2,0},{4,6},{6,4},{8,10},{10,8},{12,14},{14,12},{16,18},{18,... | collective-permute-start | bytes 3538952 | tf_op jit(solution)/shard_map/ppermute | solution.py:1273
  442.9 20.2 %collective-permute-start.42 = (bf16[768,512]{1,0:T(8,128)(2,1)}, bf16[768,512]{1,0:T(8,128)(2,1)}, u32[]{:S(2)}, u32[]{:S(2)}) collective-permute-start(bf16[768,512]{1,0:T(8,128)(2,1)} %fusion.7), channel_id=1, source_target_pairs={{0,1},{1,0},{2,3},{3,2},{4,5},{5,4},{6,7},{7,6},{8,9},{9,8},{10,11... | collective-permute-start | bytes 2359304 | tf_op jit(solution)/shard_map/ppermute | solution.py:1279
  466.4 18.2 %collective-permute-start.46 = (bf16[384,512]{1,0:T(8,128)(2,1)S(1)}, bf16[384,512]{1,0:T(8,128)(2,1)S(1)}, u32[]{:S(2)}, u32[]{:S(2)}) collective-permute-start(bf16[384,512]{1,0:T(8,128)(2,1)S(1)} %fusion.9), channel_id=1, source_target_pairs={{0,1},{1,0},{2,3},{3,2},{4,5},{5,4},{6,7},{7,6},{8,9},{9,8},{10,11... | collective-permute-start | bytes 1179656 | tf_op jit(solution)/shard_map/ppermute | solution.py:1279
  466.7 17.9 %collective-permute-start.47 = (bf16[384,512]{1,0:T(8,128)(2,1)}, bf16[384,512]{1,0:T(8,128)(2,1)S(1)}, u32[]{:S(2)}, u32[]{:S(2)}) collective-permute-start(bf16[384,512]{1,0:T(8,128)(2,1)} %constant_dynamic-slice_fusion.5), channel_id=1, source_target_pairs={{0,4},{2,6},{4,0},{6,2},{8,12},{10,14},{12,8},{14,10},{16,20},{18,... | collective-permute-start | bytes 1179656 | tf_op jit(solution)/shard_map/ppermute | solution.py:1273
  494.8 18.1 %collective-permute-start.51 = (bf16[4,176,512]{2,1,0:T(8,128)(2,1)}, bf16[4,176,512]{2,1,0:T(8,128)(2,1)S(1)}, u32[]{:S(2)}, u32[]{:S(2)}) collective-permute-start(bf16[4,176,512]{2,1,0:T(8,128)(2,1)} %pad_maximum_fusion.10), channel_id=1, source_target_pairs={{0,4},{2,6},{4,0},{6,2},{8,12},{10,14},{12,8},{14,10},{16,20},{18,... | collective-permute-start | bytes 2162696 | tf_op jit(solution)/shard_map/ppermute | solution.py:1273
  (121 other events, 1026.4 us)
